TPU v7x, 32 devices: a whole 2x2x4 slice. The times are simulated.
32 devices in a mesh: acq: 4 (over y, x), pix: 8 (over z, core).
Axes of the slice: x: 2, y: 2, z: 4, core: 2. Of those that a mesh axis runs over, the one named last changes fastest.
Arguments:
- slc: bfloat16 [12, 2, 768, 3072], P('acq', None, 'pix')
- offsets: int32 [12, 768], P('acq', 'pix'), may hold values from -16 to 16
- weights: bfloat16 [12, 8], replicated, may hold values from -0.29882812 to 1
- pairs: int32 [60, 2], replicated, may hold values from 0 to 11, as said below
Outputs:
- coherence: float32 [2, 60, 192, 192], P(None, None, 'pix', 'acq')
Inputs may be any that keep to these rules, and one draw needn't show every extreme that they name: `pairs`: the two acquisitions of an interferogram differ.
All inputs are finite; a program needn't handle non-finite values.
Results may differ from a plain program's by a relative error of at most 0.0031.
Values may be sent and summed in bfloat16 or wider, within the bound.
No kernel may reach another device: no remote copies, remote signals or barrier semaphores. Data moves between devices by JAX's collectives and lax.ppermute only.
A program may use at most 64 MiB of HBM per device.

v0:
```python
import jax
import jax.numpy as jnp
from jax import lax
from jax.sharding import PartitionSpec as P

MAX_OFF = 16
LOOK_R = 4
LOOK_C = 16


def with_halo(array, sides, width):
    for axis, dim in sides:
        size, length = (lax.axis_size(axis), array.shape[dim])
        up = [(i, (i + 1) % size) for i in range(size - 1)]
        down = [(j, i) for i, j in up]
        last = lax.slice_in_dim(array, length - width, length, axis=dim)
        first = lax.slice_in_dim(array, 0, width, axis=dim)
        before = lax.ppermute(last, axis, up)
        after = lax.ppermute(first, axis, down)
        array = jnp.concatenate([before, array, after], axis=dim)
    return array


def resample(padded, line_off, kernel, halo, groups):
    lines = padded.shape[2] - 2 * halo
    taps = kernel.shape[1]
    source = jnp.arange(lines + 2 * halo, dtype=jnp.int32)
    target = jnp.arange(lines, dtype=jnp.int32)[None, :] + halo + line_off - (taps // 2 - 1)
    band = jnp.zeros((padded.shape[0], lines, lines + 2 * halo), jnp.float32)
    for k in range(taps):
        hit = (source[None, None, :] == (target + k)[:, :, None]).astype(jnp.float32)
        band = band + kernel[:, k].astype(jnp.float32)[:, None, None] * hit
    band = band.astype(jnp.bfloat16)
    width = padded.shape[3] // groups
    split = padded.reshape(padded.shape[0], padded.shape[1], padded.shape[2], groups, width)
    total = jnp.einsum("ars,axsgw->gaxrw", band, split, preferred_element_type=jnp.float32)
    return total.astype(jnp.bfloat16)


def interfere(block, pairs):
    blocks_r = block.shape[2]
    look_r = block.shape[3]
    width = block.shape[4]
    scale_look = 1.0 / (look_r * LOOK_C)

    def pool(field):
        shaped = field.reshape(blocks_r, look_r, width // LOOK_C, LOOK_C)
        return jnp.sum(shaped, axis=(1, 3)) * scale_look

    def power_one(field):
        wide = field.astype(jnp.float32)
        return pool(wide[0] * wide[0] + wide[1] * wide[1])

    power = lax.map(power_one, block)
    power_first = jnp.take(power, pairs[:, 0], axis=0)
    power_second = jnp.take(power, pairs[:, 1], axis=0)

    def one_pair(pair):
        first = lax.dynamic_index_in_dim(block, pair[0], 0, False).astype(jnp.float32)
        second = lax.dynamic_index_in_dim(block, pair[1], 0, False).astype(jnp.float32)
        real_look = pool(first[0] * second[0] + first[1] * second[1])
        imag_look = pool(first[1] * second[0] - first[0] * second[1])
        return (real_look, imag_look)

    real_all, imag_all = lax.map(one_pair, pairs)
    scale = jnp.sqrt((power_first + 1e-06) * (power_second + 1e-06))
    return jnp.stack([real_all / scale, imag_all / scale])


def local(slc, offsets, weights, pairs):
    acq_local = slc.shape[0]
    lines = slc.shape[2]
    halo = MAX_OFF + weights.shape[1] // 2
    groups = lax.axis_size("acq")
    start = lax.axis_index("acq") * acq_local
    kernel = lax.dynamic_slice_in_dim(weights, start, acq_local, 0)
    padded = with_halo(slc, (("pix", 2),), halo)
    resampled = resample(padded, offsets, kernel, halo, groups)
    shaped = resampled.reshape(groups, acq_local, 2, lines // LOOK_R, LOOK_R, resampled.shape[4])
    return interfere(
        lax.all_to_all(shaped, "acq", split_axis=0, concat_axis=1, tiled=True)[0], pairs
    )


def solution(mesh):
    placed = (P("acq", None, "pix", None), P("acq", "pix"), P(), P())
    return jax.shard_map(
        local, mesh=mesh, in_specs=placed, out_specs=P(None, None, "pix", "acq"), check_vma=False
    )
```

profile of v0, /device:TPU:9, one launch (start us, length us, event | category | flops | bytes accessed | tf_op | source)
XLA Modules:
  0.0 524.6 jit_solution(3721894150896704940)
XLA Ops:
  0.0 3.0 fusion.30
  3.0 3.8 collective-permute-start
  6.8 1.9 collective-permute-start.1
  9.5 7.6 %collective-permute-done = bf16[3,2,20,3072]{3,2,1,0:T(8,128)(2,1)} collective-permute-done((bf16[3,2,20,3072]{3,2,1,0:T(8,128)(2,1)}, bf16[3,2,20,3072]{3,2,1,0:T(8,128)(2,1)}, u32[]{:S(2)}, u32[]{:S(2)}) %collective-permute-start) | collective-permute-done | bytes 737312 | tf_op jit(solution)/shard_map/ppermute | solution.py:18
  17.1 4.4 collective-permute-done.1
  21.5 3.2 pad_maximum_fusion
  24.7 3.2 convert_bitcast_fusion
  27.9 5.7 %reshape.150 = bf16[4,3,2,24,4,768]{5,4,3,0,2,1:T(4,128)(2,1)S(1)} reshape(bf16[4,3,2,96,768]{4,3,0,2,1:T(8,128)(2,1)} %convert_bitcast_fusion) | data formatting | bytes 7077888 | tf_op jit(solution)/shard_map/reshape | solution.py:79
  33.5 3.5 copy.12
  37.1 4.8 all-to-all-start
  42.0 39.7 %all-to-all-done = bf16[4,3,2,24,4,768]{5,4,3,2,1,0:T(4,128)(2,1)} async-done(((bf16[4,3,2,24,4,768]{5,4,3,2,1,0:T(4,128)(2,1)}), bf16[4,3,2,24,4,768]{5,4,3,2,1,0:T(4,128)(2,1)}, u32[]{:S(2)}, u32[]{:S(2)}) %all-to-all-start) | async-done | bytes 3538976 | tf_op jit(solution)/shard_map/all_to_all | solution.py:81
  81.7 418.8 %while.22 = (s32[]{:T(128)}, f32[60,24,48]{2,1,0:T(8,128)S(1)}, f32[60,24,48]{2,1,0:T(8,128)S(1)}, s32[60,2]{0,1:T(2,128)S(1)}, bf16[12,2,24,4,768]{4,3,2,1,0:T(...) while((s32[]{:T(128)}, f32[60,24,48]{2,1,0:T(8,128)S(1)}, f32[60,24,48]{2,1,0:T(8,128)S(1)}, ...), condition=%wide.region_5.6_spmd, body=%wide.region_0.5_spmd.sunk | while | flops 884744 | bytes 3597529 | solution.py:65
  86.1 1.2 dynamic-slice_convert_fusion.5
  93.0 1.2 dynamic-slice_convert_fusion.5
  100.0 1.2 dynamic-slice_convert_fusion.5
  107.0 1.2 dynamic-slice_convert_fusion.5
  114.0 1.2 dynamic-slice_convert_fusion.5
  121.0 1.2 dynamic-slice_convert_fusion.5
  127.9 1.2 dynamic-slice_convert_fusion.5
  134.9 1.2 dynamic-slice_convert_fusion.5
  141.9 1.2 dynamic-slice_convert_fusion.5
  148.9 1.2 dynamic-slice_convert_fusion.5
  155.9 1.2 dynamic-slice_convert_fusion.5
  162.8 1.2 dynamic-slice_convert_fusion.5
  169.8 1.2 dynamic-slice_convert_fusion.5
  176.8 1.2 dynamic-slice_convert_fusion.5
  183.8 1.2 dynamic-slice_convert_fusion.5
  190.8 1.2 dynamic-slice_convert_fusion.5
  197.7 1.2 dynamic-slice_convert_fusion.5
  204.7 1.2 dynamic-slice_convert_fusion.5
  211.7 1.2 dynamic-slice_convert_fusion.5
  218.7 1.2 dynamic-slice_convert_fusion.5
  225.7 1.2 dynamic-slice_convert_fusion.5
  232.6 1.2 dynamic-slice_convert_fusion.5
  239.6 1.2 dynamic-slice_convert_fusion.5
  246.6 1.2 dynamic-slice_convert_fusion.5
  253.6 1.2 dynamic-slice_convert_fusion.5
  260.6 1.2 dynamic-slice_convert_fusion.5
  267.5 1.2 dynamic-slice_convert_fusion.5
  274.5 1.2 dynamic-slice_convert_fusion.5
  281.5 1.2 dynamic-slice_convert_fusion.5
  288.5 1.2 dynamic-slice_convert_fusion.5
  295.5 1.2 dynamic-slice_convert_fusion.5
  302.4 1.2 dynamic-slice_convert_fusion.5
  309.4 1.2 dynamic-slice_convert_fusion.5
  316.4 1.2 dynamic-slice_convert_fusion.5
  500.5 20.7 %while.23 = (s32[]{:T(128)}, f32[12,24,48]{2,1,0:T(8,128)S(1)}, bf16[12,2,24,4,768]{4,3,2,1,0:T(4,128)(2,1)}, s32[]{:T(128)}, f32[]{:T(128)}) while((s32[]{:T(128)}, f32[12,24,48]{2,1,0:T(8,128)S(1)}, bf16[12,2,24,4,768]{4,3,2,1,0:T(4,128)(2,1)}, s32[]{:T(128)}, f32[]{:T(128)}) %tuple.67), condition=%wide.region_9.10_spmd, body=%wide.region_6.9_spmd.sunk | while | flops 442370 | bytes 1798729 | solution.py:54
  523.0 1.6 copy.13
  (586 shorter events, 171.9 us)
Async XLA Ops:
  0.0 8.7 %copy-start = (bf16[12,8]{0,1:T(8,128)(2,1)S(1)}, bf16[12,8]{0,1:T(8,128)(2,1)}, u32[]{:S(2)}) copy-start(bf16[12,8]{0,1:T(8,128)(2,1)} %param.12) | copy-start | bytes 580
  0.0 21.5 %copy-start.1 = (bf16[3,2,96,3072]{3,2,1,0:T(8,128)(2,1)S(1)}, bf16[3,2,96,3072]{3,2,1,0:T(8,128)(2,1)}, u32[]{:S(2)}) copy-start(bf16[3,2,96,3072]{3,2,1,0:T(8,128)(2,1)} %param.10) | copy-start | bytes 10616836
  3.0 14.0 %collective-permute-start = (bf16[3,2,20,3072]{3,2,1,0:T(8,128)(2,1)}, bf16[3,2,20,3072]{3,2,1,0:T(8,128)(2,1)}, u32[]{:S(2)}, u32[]{:S(2)}) collective-permute-start(bf16[3,2,20,3072]{3,2,1,0:T(8,128)(2,1)} %get-tuple-element.84), channel_id=1, source_target_pairs={{0,1},{1,2},{2,3},{3,4},{4,5},{5,6},{6,7},{8,9},{9,10},{10,11},{11... | collective-permute-start | bytes 2211848 | tf_op jit(solution)/shard_map/ppermute | solution.py:18
  6.8 14.7 %collective-permute-start.1 = (bf16[3,2,20,3072]{3,2,1,0:T(8,128)(2,1)}, bf16[3,2,20,3072]{3,2,1,0:T(8,128)(2,1)}, u32[]{:S(2)}, u32[]{:S(2)}) collective-permute-start(bf16[3,2,20,3072]{3,2,1,0:T(8,128)(2,1)} %get-tuple-element.85), channel_id=1, source_target_pairs={{1,0},{2,1},{3,2},{4,3},{5,4},{6,5},{7,6},{9,8},{10,9},{11,10},{12... | collective-permute-start | bytes 2211848 | tf_op jit(solution)/shard_map/ppermute | solution.py:19
  37.1 4.9 copy-start.2
  37.1 44.6 %all-to-all-start = ((bf16[4,3,2,24,4,768]{5,4,3,2,1,0:T(4,128)(2,1)}), bf16[4,3,2,24,4,768]{5,4,3,2,1,0:T(4,128)(2,1)}, u32[]{:S(2)}, u32[]{:S(2)}) async-start(bf16[4,3,2,24,4,768]{5,4,3,2,1,0:T(4,128)(2,1)} %copy.12), calls=%async_computation | async-start | bytes 7077888 | tf_op jit(solution)/shard_map/all_to_all | solution.py:81
where the time goes:
time: 530 us; the launch traced here: 525 us
  loops' own time  229 us (43%)
  other arithmetic  149 us (28%)
  local copies, waits for them, and re-layouts  81.3 us (15%)
  waiting for transfers between devices  51.6 us (10%)
  starting transfers between devices  10.5 us (2%)
    another operation x1, loops' own time, interfere(): real_all, imag_all = lax.map(one_pair, pairs)  229 us
    convert_element_type x60, other arithmetic, one_pair(): lax.dynamic_index_in_dim(block, pair[0], 0, False).astype(jnp.float32)  72.5 us
    reduce_sum x204, other arithmetic, pool(): return jnp.sum(shaped, axis=(1, 3)) * scale_look  58.9 us
    all_to_all x1, waiting for transfers between devices, local(): lax.all_to_all(shaped, 'acq', split_axis=0, concat_axis=1, tiled=True)[0]  39.7 us
    slice x60, local copies, waits for them, and re-layouts, one_pair(): pair[0]  32.3 us
    reduce_sum x132, local copies, waits for them, and re-layouts, pool(): return jnp.sum(shaped, axis=(1, 3)) * scale_look  29.5 us
    convert_element_type x12, other arithmetic, power_one(): wide = field.astype(jnp.float32)  12.1 us
  transfers between devices with their start and end apart: 3, of which 3 were waited for; matrix products, arithmetic and copies ran while one was open for 0% of the time, Pallas kernels for 0%

commit v1 on v0

v1 whole, which is shorter than its diff:
```python
import functools

import jax
import jax.numpy as jnp
from jax import lax
from jax.experimental import pallas as pl
from jax.experimental.pallas import tpu as pltpu
from jax.sharding import PartitionSpec as P

LOOK_R = 4
LOOK_C = 16
CHUNK = 32
VMEM_BYTES = 48 * 1024 * 1024


def resample_kernel(first, group, kernel, off, top, mid, low, *rest):
    outs, band = rest[:-1], rest[-1]
    acq = top.shape[0]
    taps = kernel.shape[1]
    rows = 3 * CHUNK
    step = pl.program_id(0)

    @pl.when(step == 0)
    def _():
        source = lax.broadcasted_iota(jnp.int32, (rows, CHUNK), 0)
        target = lax.broadcasted_iota(jnp.int32, (rows, CHUNK), 1)
        base = source - target - (CHUNK - (taps // 2 - 1))
        row = lax.broadcasted_iota(jnp.int32, (CHUNK, CHUNK), 0)
        col = lax.broadcasted_iota(jnp.int32, (CHUNK, CHUNK), 1)
        blocks = CHUNK // LOOK_R
        order = jnp.where(col == (row % blocks) * LOOK_R + row // blocks, 1.0, 0.0).astype(jnp.bfloat16)
        for a in range(acq):
            tap = base - off[a : a + 1, first : first + CHUNK]
            total = jnp.zeros((rows, CHUNK), jnp.float32)
            for k in range(taps):
                total = jnp.where(tap == k, kernel[group[0] * acq + a, k], total)
            turned = lax.dot_general(
                order, total.astype(jnp.bfloat16), (((1,), (1,)), ((), ())),
                preferred_element_type=jnp.float32,
            )
            band[a] = turned.astype(jnp.bfloat16)

    for s, out in enumerate(outs):

        @pl.when(step == s)
        def _(out=out):
            for a in range(acq):
                for x in range(2):
                    lines = jnp.concatenate([top[a, x], mid[a, x], low[a, x]], axis=0)
                    total = jnp.dot(band[a], lines, preferred_element_type=jnp.float32)
                    out[a, x] = total.astype(jnp.bfloat16)


def resample(first, group, kernel, offsets, parts, groups):
    acq, cols = parts[0][0].shape[0], parts[0][0].shape[3]
    width = cols // groups
    shape = (acq, 2, CHUNK, width)

    def source(index):
        return pl.BlockSpec(shape, lambda t, g: (0, 0, index, t ^ g[0]))

    return pl.pallas_call(
        functools.partial(resample_kernel, first),
        grid_spec=pltpu.PrefetchScalarGridSpec(
            num_scalar_prefetch=1,
            grid=(groups,),
            in_specs=[
                pl.BlockSpec(memory_space=pltpu.SMEM),
                pl.BlockSpec(offsets.shape, lambda t, g: (0, 0)),
                *[source(index) for _, index in parts],
            ],
            out_specs=[pl.BlockSpec(shape, lambda t, g: (0, 0, 0, 0))] * groups,
            scratch_shapes=[pltpu.VMEM((acq, CHUNK, 3 * CHUNK), jnp.bfloat16)],
        ),
        out_shape=[jax.ShapeDtypeStruct(shape, jnp.bfloat16)] * groups,
        compiler_params=pltpu.CompilerParams(vmem_limit_bytes=VMEM_BYTES),
        cost_estimate=pl.CostEstimate(
            flops=2 * acq * 2 * CHUNK * 3 * CHUNK * cols,
            bytes_accessed=acq * 2 * 4 * CHUNK * cols * 2,
            transcendentals=0,
        ),
        name="resample",
    )(group, kernel, offsets, *[array for array, _ in parts])


def interfere_kernel(groups, pairs, *rest):
    blocks, (out, wide, high, low, pooled, inverse) = rest[:groups], rest[-6:]
    acq, _, lines, width = blocks[0].shape
    looks = lines // LOOK_R
    count = pairs.shape[0]
    windows = width // LOOK_C

    for r, block in enumerate(blocks):
        for a in range(acq):
            for x in range(2):
                wide[r * acq + a, x] = block[a, x].astype(jnp.float32) * 0.125

    col = lax.broadcasted_iota(jnp.int32, (width, windows), 0)
    window = lax.broadcasted_iota(jnp.int32, (width, windows), 1)
    pool = jnp.where(col // LOOK_C == window, 1.0, 0.0).astype(jnp.bfloat16)

    def split(field):
        first = field.astype(jnp.bfloat16)
        return first, (field - first.astype(jnp.float32)).astype(jnp.bfloat16)

    def gather(first, second):
        return jnp.dot(first, pool, preferred_element_type=jnp.float32) + jnp.dot(
            second, pool, preferred_element_type=jnp.float32
        )

    def power_two(i, carry):
        fields = []
        for u in range(2):
            total = 0.0
            for j in range(LOOK_R):
                for x in range(2):
                    value = wide[2 * i + u, x, j * looks : (j + 1) * looks, :]
                    total = total + value * value
            fields.append(total)
        first, second = split(jnp.concatenate(fields, axis=0))
        at = pl.multiple_of(i * 2 * looks, 2 * looks)
        high[pl.ds(at, 2 * looks), :] = first
        low[pl.ds(at, 2 * looks), :] = second
        return carry

    total_acq = groups * acq
    lax.fori_loop(0, total_acq // 2, power_two, 0)
    power = gather(high[: total_acq * looks, :], low[: total_acq * looks, :])
    inverse[...] = lax.rsqrt(power + 1e-6).reshape(total_acq, looks, windows)

    def one_pair(p, carry):
        m, s = pairs[p, 0], pairs[p, 1]
        real, imag = 0.0, 0.0
        for j in range(LOOK_R):
            at = slice(j * looks, (j + 1) * looks)
            m0, m1, s0, s1 = wide[m, 0, at, :], wide[m, 1, at, :], wide[s, 0, at, :], wide[s, 1, at, :]
            real = real + (m0 * s0 + m1 * s1)
            imag = imag + (m1 * s0 - m0 * s1)
        first, second = split(jnp.concatenate([real, imag], axis=0))
        at = pl.multiple_of(p * 2 * looks, 2 * looks)
        high[pl.ds(at, 2 * looks), :] = first
        low[pl.ds(at, 2 * looks), :] = second
        return carry

    lax.fori_loop(0, count, one_pair, 0, unroll=2)
    pooled[...] = gather(high[: count * 2 * looks, :], low[: count * 2 * looks, :]).reshape(
        count, 2, looks, windows
    )

    def scale_pair(p, carry):
        scale = inverse[pairs[p, 0]] * inverse[pairs[p, 1]]
        for x in range(2):
            out[x, p] = pooled[p, x] * scale
        return carry

    lax.fori_loop(0, count, scale_pair, 0, unroll=4)


def interfere(place, chunks, pairs, blocks, before):
    groups = len(blocks)
    acq, _, lines, width = blocks[0].shape
    looks, windows, count = lines // LOOK_R, width // LOOK_C, pairs.shape[0]
    rows = max(count * 2, groups * acq) * looks
    whole = pl.BlockSpec(blocks[0].shape, lambda t: (0, 0, 0, 0))
    extra = [] if before is None else [before]
    return pl.pallas_call(
        functools.partial(interfere_kernel, groups),
        grid=(1,),
        in_specs=[pl.BlockSpec(memory_space=pltpu.SMEM)]
        + [whole] * groups
        + [pl.BlockSpec(memory_space=pl.ANY)] * len(extra),
        out_specs=pl.BlockSpec((2, count, looks, windows), lambda t: (0, 0, place, 0)),
        out_shape=jax.ShapeDtypeStruct((2, count, chunks * looks, windows), jnp.float32),
        scratch_shapes=[
            pltpu.VMEM((groups * acq, 2, lines, width), jnp.float32),
            pltpu.VMEM((rows, width), jnp.bfloat16),
            pltpu.VMEM((rows, width), jnp.bfloat16),
            pltpu.VMEM((count, 2, looks, windows), jnp.float32),
            pltpu.VMEM((groups * acq, looks, windows), jnp.float32),
        ],
        input_output_aliases={} if before is None else {1 + groups: 0},
        compiler_params=pltpu.CompilerParams(vmem_limit_bytes=VMEM_BYTES),
        cost_estimate=pl.CostEstimate(
            flops=count * 8 * lines * width,
            bytes_accessed=groups * acq * 2 * lines * width * 2,
            transcendentals=0,
        ),
        name="interfere",
    )(pairs, *blocks, *extra)


def local(slc, offsets, weights, pairs):
    acq, _, lines, cols = slc.shape
    groups = lax.axis_size("acq")
    size = lax.axis_size("pix")
    mine = lax.axis_index("acq")
    group = jnp.reshape(mine, (1,)).astype(jnp.int32)
    kernel = weights.astype(jnp.float32)
    placed = ((pairs // acq) ^ mine) * acq + pairs % acq
    chunks = lines // CHUNK
    last = chunks - 1

    up = [(i, i + 1) for i in range(size - 1)]
    down = [(j, i) for i, j in up]
    above = lax.ppermute(slc[:, :, lines - CHUNK :], "pix", up)
    below = lax.ppermute(slc[:, :, :CHUNK], "pix", down)

    def piece(index):
        if index < 0:
            return (above, 0)
        return (below, 0) if index > last else (slc, index)

    result = None
    held = []
    for c in [*range(1, last), 0, last]:
        parts = [piece(c - 1), piece(c), piece(c + 1)]
        blocks = resample(c * CHUNK, group, kernel, offsets, parts, groups)
        moved = [blocks[0]]
        for s in range(1, groups):
            moved.append(lax.ppermute(blocks[s], "acq", [(i, i ^ s) for i in range(groups)]))
        held.append((c, moved))
    for c, moved in held:
        result = interfere(c, chunks, placed, moved, result)
    return result


def solution(mesh):
    placed = (P("acq", None, "pix", None), P("acq", "pix"), P(), P())
    return jax.shard_map(
        local, mesh=mesh, in_specs=placed, out_specs=P(None, None, "pix", "acq"), check_vma=False
    )
```

time: 530 us -> 72.7 us (0.14)
  the two profiles are of different devices: /device:TPU:9 before, /device:TPU:16 now
where the time goes in v1:
time: 72.7 us; the launch traced here: 72.3 us
  Pallas kernels  26.1 us (36%)
  waiting for transfers between devices  16.4 us (23%)
  starting transfers between devices  16.1 us (22%)
  local copies, waits for them, and re-layouts  13.5 us (19%)
    pallas_call x3, Pallas kernels, interfere(): pl.pallas_call(functools.partial(interfere_kernel, groups), grid=(1,), in...  15.8 us
    ppermute x9, starting transfers between devices, local(): lax.ppermute(blocks[s], 'acq', [(i, i ^ s) for i in range(groups)])  10.5 us
    pallas_call x3, Pallas kernels, resample(): pl.pallas_call(functools.partial(resample_kernel, first), grid_spec=pltpu...  10.3 us
    ppermute x9, waiting for transfers between devices, local(): lax.ppermute(blocks[s], 'acq', [(i, i ^ s) for i in range(groups)])  10.1 us
    unnamed x38, local copies, waits for them, and re-layouts  8.36 us
    ppermute x1, waiting for transfers between devices, local(): above = lax.ppermute(slc[:, :, lines - CHUNK:], 'pix', up)  6.24 us
    ppermute x1, starting transfers between devices, local(): below = lax.ppermute(slc[:, :, :CHUNK], 'pix', down)  3.64 us
    slice x1, local copies, waits for them, and re-layouts, local(): above = lax.ppermute(slc[:, :, lines - CHUNK:], 'pix', up)  3.36 us
  transfers between devices with their start and end apart: 11, of which 2 were waited for; matrix products, arithmetic and copies ran while one was open for 1% of the time, Pallas kernels for 29%

profile of v1, /device:TPU:16, one launch (start us, length us, event | category | flops | bytes accessed | tf_op | source)
XLA Modules:
  0.0 72.3 jit_solution(16264764837662642544)
XLA Ops:
  0.0 3.4 %fusion.2 = (bf16[3,2,32,3072]{3,2,1,0:T(8,128)(2,1)}, bf16[3,2,32,3072]{3,2,1,0:T(8,128)(2,1)}) fusion(bf16[3,2,96,3072]{3,2,1,0:T(8,128)(2,1)} %low.3), kind=kLoop, calls=%fused_computation.7 | loop fusion | bytes 4718592 | tf_op jit(solution)/shard_map/slice | solution.py:205
  3.4 1.9 %collective-permute-start.4 = (bf16[3,2,32,3072]{3,2,1,0:T(8,128)(2,1)}, bf16[3,2,32,3072]{3,2,1,0:T(8,128)(2,1)}, u32[]{:S(2)}, u32[]{:S(2)}) collective-permute-start(bf16[3,2,32,3072]{3,2,1,0:T(8,128)(2,1)} %get-tuple-element.31), channel_id=1, source_target_pairs={{0,1},{1,2},{2,3},{3,4},{4,5},{5,6},{6,7},{8,9},{9,10},{10,11},{11... | collective-permute-start | bytes 3538952 | tf_op jit(solution)/shard_map/ppermute | solution.py:205
  5.3 3.6 %collective-permute-start = (bf16[3,2,32,3072]{3,2,1,0:T(8,128)(2,1)}, bf16[3,2,32,3072]{3,2,1,0:T(8,128)(2,1)}, u32[]{:S(2)}, u32[]{:S(2)}) collective-permute-start(bf16[3,2,32,3072]{3,2,1,0:T(8,128)(2,1)} %get-tuple-element.32), channel_id=1, source_target_pairs={{1,0},{2,1},{3,2},{4,3},{5,4},{6,5},{7,6},{9,8},{10,9},{11,10},{12... | collective-permute-start | bytes 3538952 | tf_op jit(solution)/shard_map/ppermute | solution.py:206
  8.9 0.0 copy-done.17
  9.0 0.1 copy.20
  9.0 0.0 copy-done
  9.1 2.3 %resample.5 = (bf16[3,2,32,768]{3,2,1,0:T(8,128)(2,1)S(1)}, bf16[3,2,32,768]{3,2,1,0:T(8,128)(2,1)S(1)}, bf16[3,2,32,768]{3,2,1,0:T(8,128)(2,1)S(1)}, bf16[3,2,32,768]{3,2,1,0:T(8,128)(2,1)S(1)}) custom-call(s32[1]{0:T(128)} %bitcast.group, f32[12,8]{1,0:T(8,128)S(1)} %convert_element_type.3.kernel, s32[3,96]{1,0:T(4,128)S(1)} %copy-done.15, ...), custom_call_target="tpu_custom_call" | custom-call | flops 113246208 | bytes 4718592 | tf_op jit(solution)/shard_map/resample/pallas_call | solution.py:62
  11.4 0.0 copy-start.7
  11.4 1.6 %collective-permute-start.8 = (bf16[3,2,32,768]{3,2,1,0:T(8,128)(2,1)S(1)}, bf16[3,2,32,768]{3,2,1,0:T(8,128)(2,1)S(1)}, u32[]{:S(2)}, u32[]{:S(2)}) collective-permute-start(bf16[3,2,32,768]{3,2,1,0:T(8,128)(2,1)S(1)} %get-tuple-element.26), channel_id=1, source_target_pairs={{0,8},{8,0},{16,24},{24,16},{1,9},{9,1},{17,25},{25,17},{2,10},{10... | collective-permute-start | bytes 884744 | tf_op jit(solution)/shard_map/ppermute | solution.py:220
  13.0 1.5 %collective-permute-start.9 = (bf16[3,2,32,768]{3,2,1,0:T(8,128)(2,1)S(1)}, bf16[3,2,32,768]{3,2,1,0:T(8,128)(2,1)S(1)}, u32[]{:S(2)}, u32[]{:S(2)}) collective-permute-start(bf16[3,2,32,768]{3,2,1,0:T(8,128)(2,1)S(1)} %get-tuple-element.27), channel_id=1, source_target_pairs={{0,16},{8,24},{16,0},{24,8},{1,17},{9,25},{17,1},{25,9},{2,18},{10... | collective-permute-start | bytes 884744 | tf_op jit(solution)/shard_map/ppermute | solution.py:220
  14.5 0.5 collective-permute-start.10
  15.0 6.2 %collective-permute-done.4.top = bf16[3,2,32,3072]{3,2,1,0:T(8,128)(2,1)} collective-permute-done((bf16[3,2,32,3072]{3,2,1,0:T(8,128)(2,1)}, bf16[3,2,32,3072]{3,2,1,0:T(8,128)(2,1)}, u32[]{:S(2)}, u32[]{:S(2)}) %collective-permute-start.4) | collective-permute-done | bytes 1179680 | tf_op jit(solution)/shard_map/ppermute | solution.py:205
  21.2 3.8 %resample.4 = (bf16[3,2,32,768]{3,2,1,0:T(8,128)(2,1)S(1)}, bf16[3,2,32,768]{3,2,1,0:T(8,128)(2,1)S(1)}, bf16[3,2,32,768]{3,2,1,0:T(8,128)(2,1)}, bf16[3,2,32,768]{3,2,1,0:T(8,128)(2,1)}) custom-call(s32[1]{0:T(128)} %bitcast.group, f32[12,8]{1,0:T(8,128)S(1)} %convert_element_type.3.kernel, s32[3,96]{1,0:T(4,128)S(1)} %copy-done.15, ...), custom_call_target="tpu_custom_call" | custom-call | flops 113246208 | bytes 4718592 | tf_op jit(solution)/shard_map/resample/pallas_call | solution.py:62
  25.0 0.7 %copy-done.3 = bf16[3,2,32,768]{3,2,1,0:T(8,128)(2,1)} copy-done((bf16[3,2,32,768]{3,2,1,0:T(8,128)(2,1)}, bf16[3,2,32,768]{3,2,1,0:T(8,128)(2,1)S(1)}, u32[]{:S(2)}) %copy-start.3) | copy-done | bytes 294936
  25.8 1.5 %collective-permute-start.5 = (bf16[3,2,32,768]{3,2,1,0:T(8,128)(2,1)S(1)}, bf16[3,2,32,768]{3,2,1,0:T(8,128)(2,1)S(1)}, u32[]{:S(2)}, u32[]{:S(2)}) collective-permute-start(bf16[3,2,32,768]{3,2,1,0:T(8,128)(2,1)S(1)} %get-tuple-element.22), channel_id=1, source_target_pairs={{0,8},{8,0},{16,24},{24,16},{1,9},{9,1},{17,25},{25,17},{2,10},{10... | collective-permute-start | bytes 884744 | tf_op jit(solution)/shard_map/ppermute | solution.py:220
  27.3 0.0 collective-permute-done.low
  27.3 4.1 %resample.3 = (bf16[3,2,32,768]{3,2,1,0:T(8,128)(2,1)S(1)}, bf16[3,2,32,768]{3,2,1,0:T(8,128)(2,1)}, bf16[3,2,32,768]{3,2,1,0:T(8,128)(2,1)}, bf16[3,2,32,768]{3,2,1,0:T(8,128)(2,1)}) custom-call(s32[1]{0:T(128)} %bitcast.group, f32[12,8]{1,0:T(8,128)S(1)} %convert_element_type.3.kernel, s32[3,96]{1,0:T(4,128)S(1)} %copy-done.15, ...), custom_call_target="tpu_custom_call" | custom-call | flops 113246208 | bytes 4718592 | tf_op jit(solution)/shard_map/resample/pallas_call | solution.py:62
  31.4 0.7 copy-done.1
  32.1 0.5 collective-permute-start.1
  32.7 0.0 collective-permute-done.8.rest_1_
  32.7 0.7 copy-done.9
  33.4 1.5 %collective-permute-start.2 = (bf16[3,2,32,768]{3,2,1,0:T(8,128)(2,1)}, bf16[3,2,32,768]{3,2,1,0:T(8,128)(2,1)S(1)}, u32[]{:S(2)}, u32[]{:S(2)}) collective-permute-start(bf16[3,2,32,768]{3,2,1,0:T(8,128)(2,1)} %get-tuple-element.19), channel_id=1, source_target_pairs={{0,16},{8,24},{16,0},{24,8},{1,17},{9,25},{17,1},{25,9},{2,18},{10... | collective-permute-start | bytes 884744 | tf_op jit(solution)/shard_map/ppermute | solution.py:220
  34.9 0.0 collective-permute-done.9.rest_2_
  34.9 0.7 copy-done.11
  35.6 1.4 %collective-permute-start.3 = (bf16[3,2,32,768]{3,2,1,0:T(8,128)(2,1)}, bf16[3,2,32,768]{3,2,1,0:T(8,128)(2,1)S(1)}, u32[]{:S(2)}, u32[]{:S(2)}) collective-permute-start(bf16[3,2,32,768]{3,2,1,0:T(8,128)(2,1)} %get-tuple-element.20), channel_id=1, source_target_pairs={{0,24},{8,16},{16,8},{24,0},{1,25},{9,17},{17,9},{25,1},{2,26},{10... | collective-permute-start | bytes 884744 | tf_op jit(solution)/shard_map/ppermute | solution.py:220
  37.0 0.0 collective-permute-done.10.rest_3_
  37.1 0.7 copy-done.13
  37.8 1.5 %collective-permute-start.6 = (bf16[3,2,32,768]{3,2,1,0:T(8,128)(2,1)}, bf16[3,2,32,768]{3,2,1,0:T(8,128)(2,1)S(1)}, u32[]{:S(2)}, u32[]{:S(2)}) collective-permute-start(bf16[3,2,32,768]{3,2,1,0:T(8,128)(2,1)} %get-tuple-element.23), channel_id=1, source_target_pairs={{0,16},{8,24},{16,0},{24,8},{1,17},{9,25},{17,1},{25,9},{2,18},{10... | collective-permute-start | bytes 884744 | tf_op jit(solution)/shard_map/ppermute | solution.py:220
  39.3 0.0 collective-permute-done.5.rest_1_
  39.3 0.7 copy-done.5
  40.0 0.5 collective-permute-start.7
  40.5 0.1 copy.15
  40.6 0.1 copy.18
  40.7 0.1 copy.19
  40.9 1.0 %copy-done.8 = bf16[3,2,32,768]{3,2,1,0:T(8,128)(2,1)S(1)} copy-done((bf16[3,2,32,768]{3,2,1,0:T(8,128)(2,1)S(1)}, bf16[3,2,32,768]{3,2,1,0:T(8,128)(2,1)}, u32[]{:S(2)}) %copy-start.8) | copy-done | bytes 294936
  41.8 1.0 %copy-done.10 = bf16[3,2,32,768]{3,2,1,0:T(8,128)(2,1)S(1)} copy-done((bf16[3,2,32,768]{3,2,1,0:T(8,128)(2,1)S(1)}, bf16[3,2,32,768]{3,2,1,0:T(8,128)(2,1)}, u32[]{:S(2)}) %copy-start.10) | copy-done | bytes 294936
  42.8 1.0 %copy-done.12 = bf16[3,2,32,768]{3,2,1,0:T(8,128)(2,1)S(1)} copy-done((bf16[3,2,32,768]{3,2,1,0:T(8,128)(2,1)S(1)}, bf16[3,2,32,768]{3,2,1,0:T(8,128)(2,1)}, u32[]{:S(2)}) %copy-start.12) | copy-done | bytes 294936
  43.7 1.0 %copy-done.14 = bf16[3,2,32,768]{3,2,1,0:T(8,128)(2,1)S(1)} copy-done((bf16[3,2,32,768]{3,2,1,0:T(8,128)(2,1)S(1)}, bf16[3,2,32,768]{3,2,1,0:T(8,128)(2,1)}, u32[]{:S(2)}) %copy-start.14) | copy-done | bytes 294936
  44.7 5.3 %interfere.3.rest_4_ = f32[2,60,24,48]{3,2,1,0:T(8,128)S(1)} custom-call(s32[60,2]{1,0:T(8,128)S(1)} %fusion.pairs, bf16[3,2,32,768]{3,2,1,0:T(8,128)(2,1)S(1)} %copy-done.8, bf16[3,2,32,768]{3,2,1,0:T(8,128)(2,1)S(1)} %copy-done.10, bf16[3,2,32,768]{3,2,1,0:T(8,128)(2,1)S(1)} %copy-done.12, bf16[3,2,32,768]{3,2,1,0:T(8,128)(2,1)S(1)} %copy-done.14), custom_call_target="tpu_custom_call" | custom-call | flops 11796480 | bytes 1179648 | tf_op jit(solution)/shard_map/interfere/pallas_call | solution.py:166
  50.0 10.1 %collective-permute-done.6.rest_2_ = bf16[3,2,32,768]{3,2,1,0:T(8,128)(2,1)S(1)} collective-permute-done((bf16[3,2,32,768]{3,2,1,0:T(8,128)(2,1)}, bf16[3,2,32,768]{3,2,1,0:T(8,128)(2,1)S(1)}, u32[]{:S(2)}, u32[]{:S(2)}) %collective-permute-start.6) | collective-permute-done | bytes 294944 | tf_op jit(solution)/shard_map/ppermute | solution.py:220
  60.1 0.0 collective-permute-done.7.rest_3_
  60.1 0.0 copy-done.6
  60.1 5.3 %interfere.4.rest_4_ = f32[2,60,24,48]{3,2,1,0:T(8,128)S(1)} custom-call(s32[60,2]{1,0:T(8,128)S(1)} %fusion.pairs, bf16[3,2,32,768]{3,2,1,0:T(8,128)(2,1)S(1)} %copy-done.4, bf16[3,2,32,768]{3,2,1,0:T(8,128)(2,1)S(1)} %copy-done.6, bf16[3,2,32,768]{3,2,1,0:T(8,128)(2,1)S(1)} %collective-permute-done.6.rest_2_, ...), custom_call_target="tpu_custom_call", output_to_operand_aliasing={{}: (5, {})} | custom-call | flops 11796480 | bytes 1179648 | tf_op jit(solution)/shard_map/interfere/pallas_call | solution.py:166
  65.4 0.0 collective-permute-done.1.rest_1_
  65.4 0.0 collective-permute-done.2.rest_2_
  65.4 0.0 collective-permute-done.3.rest_3_
  65.5 5.3 %interfere.5 = f32[2,60,24,48]{3,2,1,0:T(8,128)S(1)} custom-call(s32[60,2]{1,0:T(8,128)S(1)} %fusion.pairs, bf16[3,2,32,768]{3,2,1,0:T(8,128)(2,1)S(1)} %copy-done.2, bf16[3,2,32,768]{3,2,1,0:T(8,128)(2,1)S(1)} %collective-permute-done.1.rest_1_, bf16[3,2,32,768]{3,2,1,0:T(8,128)(2,1)S(1)} %collective-permute-done.2.rest_2_, ...), custom_call_target="tpu_custom_call", output_to_operand_aliasing={{}: (5, {})} | custom-call | flops 11796480 | bytes 1179648 | tf_op jit(solution)/shard_map/interfere/pallas_call | solution.py:166
  70.8 1.6 %copy.21 = f32[2,60,24,48]{1,3,2,0:T(8,128)} copy(f32[2,60,24,48]{3,2,1,0:T(8,128)S(1)} %interfere.5) | data formatting | bytes 1105920 | tf_op jit(solution)/shard_map/interfere/pallas_call | solution.py:166
  (25 shorter events, 0.1 us)
Async XLA Ops:
  0.0 8.9 %copy-start.17 = (bf16[12,8]{0,1:T(8,128)(2,1)S(1)}, bf16[12,8]{0,1:T(8,128)(2,1)}, u32[]{:S(2)}) copy-start(bf16[12,8]{0,1:T(8,128)(2,1)} %param.6) | copy-start | bytes 580
  0.0 9.0 %copy-start.15 = (s32[3,96]{1,0:T(4,128)S(1)}, s32[3,96]{1,0:T(4,128)}, u32[]{:S(2)}) copy-start(s32[3,96]{1,0:T(4,128)} %off.5) | copy-start | bytes 3460
  0.0 9.0 %copy-start = (bf16[3,2,96,3072]{3,2,1,0:T(8,128)(2,1)S(1)}, bf16[3,2,96,3072]{3,2,1,0:T(8,128)(2,1)}, u32[]{:S(2)}) copy-start(bf16[3,2,96,3072]{3,2,1,0:T(8,128)(2,1)} %low.3) | copy-start | bytes 10616836
  3.4 17.8 %collective-permute-start.4 = (bf16[3,2,32,3072]{3,2,1,0:T(8,128)(2,1)}, bf16[3,2,32,3072]{3,2,1,0:T(8,128)(2,1)}, u32[]{:S(2)}, u32[]{:S(2)}) collective-permute-start(bf16[3,2,32,3072]{3,2,1,0:T(8,128)(2,1)} %get-tuple-element.31), channel_id=1, source_target_pairs={{0,1},{1,2},{2,3},{3,4},{4,5},{5,6},{6,7},{8,9},{9,10},{10,11},{11... | collective-permute-start | bytes 3538952 | tf_op jit(solution)/shard_map/ppermute | solution.py:205
  5.3 22.0 %collective-permute-start = (bf16[3,2,32,3072]{3,2,1,0:T(8,128)(2,1)}, bf16[3,2,32,3072]{3,2,1,0:T(8,128)(2,1)}, u32[]{:S(2)}, u32[]{:S(2)}) collective-permute-start(bf16[3,2,32,3072]{3,2,1,0:T(8,128)(2,1)} %get-tuple-element.32), channel_id=1, source_target_pairs={{1,0},{2,1},{3,2},{4,3},{5,4},{6,5},{7,6},{9,8},{10,9},{11,10},{12... | collective-permute-start | bytes 3538952 | tf_op jit(solution)/shard_map/ppermute | solution.py:206
  11.4 13.7 %copy-start.7 = (bf16[3,2,32,768]{3,2,1,0:T(8,128)(2,1)}, bf16[3,2,32,768]{3,2,1,0:T(8,128)(2,1)S(1)}, u32[]{:S(2)}) copy-start(bf16[3,2,32,768]{3,2,1,0:T(8,128)(2,1)S(1)} %get-tuple-element.25.rest_0_) | copy-start | bytes 884740
  11.4 21.3 %collective-permute-start.8 = (bf16[3,2,32,768]{3,2,1,0:T(8,128)(2,1)S(1)}, bf16[3,2,32,768]{3,2,1,0:T(8,128)(2,1)S(1)}, u32[]{:S(2)}, u32[]{:S(2)}) collective-permute-start(bf16[3,2,32,768]{3,2,1,0:T(8,128)(2,1)S(1)} %get-tuple-element.26), channel_id=1, source_target_pairs={{0,8},{8,0},{16,24},{24,16},{1,9},{9,1},{17,25},{25,17},{2,10},{10... | collective-permute-start | bytes 884744 | tf_op jit(solution)/shard_map/ppermute | solution.py:220
  13.0 21.9 %collective-permute-start.9 = (bf16[3,2,32,768]{3,2,1,0:T(8,128)(2,1)S(1)}, bf16[3,2,32,768]{3,2,1,0:T(8,128)(2,1)S(1)}, u32[]{:S(2)}, u32[]{:S(2)}) collective-permute-start(bf16[3,2,32,768]{3,2,1,0:T(8,128)(2,1)S(1)} %get-tuple-element.27), channel_id=1, source_target_pairs={{0,16},{8,24},{16,0},{24,8},{1,17},{9,25},{17,1},{25,9},{2,18},{10... | collective-permute-start | bytes 884744 | tf_op jit(solution)/shard_map/ppermute | solution.py:220
  14.5 22.6 %collective-permute-start.10 = (bf16[3,2,32,768]{3,2,1,0:T(8,128)(2,1)S(1)}, bf16[3,2,32,768]{3,2,1,0:T(8,128)(2,1)S(1)}, u32[]{:S(2)}, u32[]{:S(2)}) collective-permute-start(bf16[3,2,32,768]{3,2,1,0:T(8,128)(2,1)S(1)} %get-tuple-element.28), channel_id=1, source_target_pairs={{0,24},{8,16},{16,8},{24,0},{1,25},{9,17},{17,9},{25,1},{2,26},{10... | collective-permute-start | bytes 884744 | tf_op jit(solution)/shard_map/ppermute | solution.py:220
  25.0 0.7 %copy-start.3 = (bf16[3,2,32,768]{3,2,1,0:T(8,128)(2,1)}, bf16[3,2,32,768]{3,2,1,0:T(8,128)(2,1)S(1)}, u32[]{:S(2)}) copy-start(bf16[3,2,32,768]{3,2,1,0:T(8,128)(2,1)S(1)} %get-tuple-element.21.rest_0_) | copy-start | bytes 884740
  25.8 14.7 %copy-start.16 = (s32[60,2]{0,1:T(2,128)S(1)}, s32[60,2]{0,1:T(2,128)}, u32[]{:S(2)}) copy-start(s32[60,2]{0,1:T(2,128)} %param.7) | copy-start | bytes 1444
  25.8 13.5 %collective-permute-start.5 = (bf16[3,2,32,768]{3,2,1,0:T(8,128)(2,1)S(1)}, bf16[3,2,32,768]{3,2,1,0:T(8,128)(2,1)S(1)}, u32[]{:S(2)}, u32[]{:S(2)}) collective-permute-start(bf16[3,2,32,768]{3,2,1,0:T(8,128)(2,1)S(1)} %get-tuple-element.22), channel_id=1, source_target_pairs={{0,8},{8,0},{16,24},{24,16},{1,9},{9,1},{17,25},{25,17},{2,10},{10... | collective-permute-start | bytes 884744 | tf_op jit(solution)/shard_map/ppermute | solution.py:220
  31.4 0.7 copy-start.1
  32.1 33.3 %collective-permute-start.1 = (bf16[3,2,32,768]{3,2,1,0:T(8,128)(2,1)}, bf16[3,2,32,768]{3,2,1,0:T(8,128)(2,1)S(1)}, u32[]{:S(2)}, u32[]{:S(2)}) collective-permute-start(bf16[3,2,32,768]{3,2,1,0:T(8,128)(2,1)} %get-tuple-element.18), channel_id=1, source_target_pairs={{0,8},{8,0},{16,24},{24,16},{1,9},{9,1},{17,25},{25,17},{2,10},{10... | collective-permute-start | bytes 884744 | tf_op jit(solution)/shard_map/ppermute | solution.py:220
  32.7 0.7 copy-start.9
  33.4 32.1 %collective-permute-start.2 = (bf16[3,2,32,768]{3,2,1,0:T(8,128)(2,1)}, bf16[3,2,32,768]{3,2,1,0:T(8,128)(2,1)S(1)}, u32[]{:S(2)}, u32[]{:S(2)}) collective-permute-start(bf16[3,2,32,768]{3,2,1,0:T(8,128)(2,1)} %get-tuple-element.19), channel_id=1, source_target_pairs={{0,16},{8,24},{16,0},{24,8},{1,17},{9,25},{17,1},{25,9},{2,18},{10... | collective-permute-start | bytes 884744 | tf_op jit(solution)/shard_map/ppermute | solution.py:220
  34.9 0.7 copy-start.11
  35.6 29.8 %collective-permute-start.3 = (bf16[3,2,32,768]{3,2,1,0:T(8,128)(2,1)}, bf16[3,2,32,768]{3,2,1,0:T(8,128)(2,1)S(1)}, u32[]{:S(2)}, u32[]{:S(2)}) collective-permute-start(bf16[3,2,32,768]{3,2,1,0:T(8,128)(2,1)} %get-tuple-element.20), channel_id=1, source_target_pairs={{0,24},{8,16},{16,8},{24,0},{1,25},{9,17},{17,9},{25,1},{2,26},{10... | collective-permute-start | bytes 884744 | tf_op jit(solution)/shard_map/ppermute | solution.py:220
  37.0 0.7 copy-start.13
  37.8 22.4 %collective-permute-start.6 = (bf16[3,2,32,768]{3,2,1,0:T(8,128)(2,1)}, bf16[3,2,32,768]{3,2,1,0:T(8,128)(2,1)S(1)}, u32[]{:S(2)}, u32[]{:S(2)}) collective-permute-start(bf16[3,2,32,768]{3,2,1,0:T(8,128)(2,1)} %get-tuple-element.23), channel_id=1, source_target_pairs={{0,16},{8,24},{16,0},{24,8},{1,17},{9,25},{17,1},{25,9},{2,18},{10... | collective-permute-start | bytes 884744 | tf_op jit(solution)/shard_map/ppermute | solution.py:220
  39.3 0.7 copy-start.5
  40.0 20.1 %collective-permute-start.7 = (bf16[3,2,32,768]{3,2,1,0:T(8,128)(2,1)}, bf16[3,2,32,768]{3,2,1,0:T(8,128)(2,1)S(1)}, u32[]{:S(2)}, u32[]{:S(2)}) collective-permute-start(bf16[3,2,32,768]{3,2,1,0:T(8,128)(2,1)} %get-tuple-element.24), channel_id=1, source_target_pairs={{0,24},{8,16},{16,8},{24,0},{1,25},{9,17},{17,9},{25,1},{2,26},{10... | collective-permute-start | bytes 884744 | tf_op jit(solution)/shard_map/ppermute | solution.py:220
  40.9 1.0 %copy-start.8 = (bf16[3,2,32,768]{3,2,1,0:T(8,128)(2,1)S(1)}, bf16[3,2,32,768]{3,2,1,0:T(8,128)(2,1)}, u32[]{:S(2)}) copy-start(bf16[3,2,32,768]{3,2,1,0:T(8,128)(2,1)} %copy-done.7) | copy-start | bytes 884740
  41.8 1.0 %copy-start.10 = (bf16[3,2,32,768]{3,2,1,0:T(8,128)(2,1)S(1)}, bf16[3,2,32,768]{3,2,1,0:T(8,128)(2,1)}, u32[]{:S(2)}) copy-start(bf16[3,2,32,768]{3,2,1,0:T(8,128)(2,1)} %copy-done.9) | copy-start | bytes 884740
  42.8 1.0 %copy-start.12 = (bf16[3,2,32,768]{3,2,1,0:T(8,128)(2,1)S(1)}, bf16[3,2,32,768]{3,2,1,0:T(8,128)(2,1)}, u32[]{:S(2)}) copy-start(bf16[3,2,32,768]{3,2,1,0:T(8,128)(2,1)} %copy-done.11) | copy-start | bytes 884740
  43.7 1.0 %copy-start.14 = (bf16[3,2,32,768]{3,2,1,0:T(8,128)(2,1)S(1)}, bf16[3,2,32,768]{3,2,1,0:T(8,128)(2,1)}, u32[]{:S(2)}) copy-start(bf16[3,2,32,768]{3,2,1,0:T(8,128)(2,1)} %copy-done.13) | copy-start | bytes 884740
  44.7 15.4 %copy-start.4 = (bf16[3,2,32,768]{3,2,1,0:T(8,128)(2,1)S(1)}, bf16[3,2,32,768]{3,2,1,0:T(8,128)(2,1)}, u32[]{:S(2)}) copy-start(bf16[3,2,32,768]{3,2,1,0:T(8,128)(2,1)} %copy-done.3) | copy-start | bytes 884740
  44.7 15.4 %copy-start.6 = (bf16[3,2,32,768]{3,2,1,0:T(8,128)(2,1)S(1)}, bf16[3,2,32,768]{3,2,1,0:T(8,128)(2,1)}, u32[]{:S(2)}) copy-start(bf16[3,2,32,768]{3,2,1,0:T(8,128)(2,1)} %copy-done.5) | copy-start | bytes 884740
  60.1 5.3 %copy-start.2 = (bf16[3,2,32,768]{3,2,1,0:T(8,128)(2,1)S(1)}, bf16[3,2,32,768]{3,2,1,0:T(8,128)(2,1)}, u32[]{:S(2)}) copy-start(bf16[3,2,32,768]{3,2,1,0:T(8,128)(2,1)} %copy-done.1) | copy-start | bytes 884740

commit v2 on v0

v2 whole, which is shorter than its diff:
```python
import functools

import jax
import jax.numpy as jnp
from jax import lax
from jax.experimental import pallas as pl
from jax.experimental.pallas import tpu as pltpu
from jax.sharding import PartitionSpec as P

LOOK_R = 4
LOOK_C = 16
CHUNK = 32
HALO = 24
TILE = 16
MIB = 1024 * 1024


def build_bands(first, sources, group, kernel, off, band):
    acq, taps = off.shape[0], kernel.shape[0]
    rows = sum(count for _, count in sources)
    index = lax.broadcasted_iota(jnp.int32, (rows, CHUNK), 0)
    source = jnp.zeros((rows, CHUNK), jnp.int32)
    at = 0
    for begin, count in sources:
        source = jnp.where(index >= at, index + (begin - at), source)
        at += count
    target = first + lax.broadcasted_iota(jnp.int32, (rows, CHUNK), 1)
    base = source - target + (taps // 2 - 1)
    row = lax.broadcasted_iota(jnp.int32, (CHUNK, CHUNK), 0)
    col = lax.broadcasted_iota(jnp.int32, (CHUNK, CHUNK), 1)
    blocks = CHUNK // LOOK_R
    order = jnp.where(col == (row % blocks) * LOOK_R + row // blocks, 1.0, 0.0).astype(jnp.bfloat16)
    for a in range(acq):
        tap = base - off[a : a + 1, first : first + CHUNK]
        total = jnp.zeros((rows, CHUNK), jnp.float32)
        for k in range(taps):
            total = jnp.where(tap == k, kernel[k, group[0] * acq + a], total)
        turned = lax.dot_general(
            order, total.astype(jnp.bfloat16), (((1,), (1,)), ((), ())),
            preferred_element_type=jnp.float32,
        )
        band[a] = turned.astype(jnp.bfloat16)


def first_kernel(first, groups, group, kernel, off, slc, *rest):
    outs, (head, tail, slab, band, sems) = rest[:groups], rest[groups:]
    acq, _, lines, cols = slc.shape
    width = cols // groups

    def columns(s):
        return pl.ds(pl.multiple_of((group[0] ^ s) * width, width), width)

    order = [*range(1, groups), 0]
    copies = {}
    for s in order:
        at = columns(s)
        copies[s] = pltpu.make_async_copy(slc.at[:, :, :, at], slab.at[:, :, :, at], sems.at[s])
        copies[s].start()
    build_bands(first, [(0, lines)], group, kernel, off, band)
    for s in order:
        copies[s].wait()
        at = columns(s)
        for a in range(acq):
            for x in range(2):
                total = jnp.dot(band[a], slab[a, x, :, at], preferred_element_type=jnp.float32)
                outs[s][a, x] = total.astype(jnp.bfloat16)
    head[...] = slab[:, :, :HALO, :]
    tail[...] = slab[:, :, lines - HALO :, :]


def edge_kernel(first, groups, begin, count, halo_at, group, kernel, off, slab, halo, *rest):
    outs, band = rest[:groups], rest[groups]
    acq, _, _, cols = slab.shape
    width = cols // groups
    build_bands(first, [(begin, count), (halo_at, HALO)], group, kernel, off, band)
    for s in [*range(1, groups), 0]:
        at = pl.ds(pl.multiple_of((group[0] ^ s) * width, width), width)
        for a in range(acq):
            for x in range(2):
                lines = jnp.concatenate(
                    [slab[a, x, begin : begin + count, at], halo[a, x, :, at]], axis=0
                )
                total = jnp.dot(band[a], lines, preferred_element_type=jnp.float32)
                outs[s][a, x] = total.astype(jnp.bfloat16)


SMEM = pl.BlockSpec(memory_space=pltpu.SMEM)
VMEM = pl.BlockSpec(memory_space=pltpu.VMEM)
ANY = pl.BlockSpec(memory_space=pl.ANY)


def resample_cost(acq, cols, rows):
    return pl.CostEstimate(
        flops=2 * acq * 2 * CHUNK * rows * cols,
        bytes_accessed=acq * 2 * (rows + CHUNK) * cols * 2,
        transcendentals=0,
    )


def resample_first(first, group, kernel, offsets, slc, groups):
    acq, _, lines, cols = slc.shape
    piece = pltpu.VMEM((acq, 2, CHUNK, cols // groups), jnp.bfloat16)
    halo = pltpu.VMEM((acq, 2, HALO, cols), jnp.bfloat16)
    slab = pltpu.VMEM(slc.shape, jnp.bfloat16)
    return pl.pallas_call(
        functools.partial(first_kernel, first, groups),
        in_specs=[SMEM, SMEM, VMEM, ANY],
        out_specs=[VMEM] * (groups + 3),
        out_shape=[piece] * groups + [halo, halo, slab],
        scratch_shapes=[
            pltpu.VMEM((acq, CHUNK, lines), jnp.bfloat16),
            pltpu.SemaphoreType.DMA((groups,)),
        ],
        compiler_params=pltpu.CompilerParams(vmem_limit_bytes=16 * MIB),
        cost_estimate=resample_cost(acq, cols, lines),
        name="resample_first",
    )(group, kernel, offsets, slc)


def resample_edge(first, begin, count, halo_at, group, kernel, offsets, slab, halo, groups):
    acq, _, lines, cols = slab.shape
    piece = pltpu.VMEM((acq, 2, CHUNK, cols // groups), jnp.bfloat16)
    return pl.pallas_call(
        functools.partial(edge_kernel, first, groups, begin, count, halo_at),
        in_specs=[SMEM, SMEM, VMEM, VMEM, VMEM],
        out_specs=[VMEM] * groups,
        out_shape=[piece] * groups,
        scratch_shapes=[pltpu.VMEM((acq, CHUNK, count + HALO), jnp.bfloat16)],
        compiler_params=pltpu.CompilerParams(vmem_limit_bytes=16 * MIB),
        cost_estimate=resample_cost(acq, cols, count + HALO),
        name="resample_edge",
    )(group, kernel, offsets, slab, halo)


def interfere_kernel(groups, place, batch, group, pairs, *rest):
    blocks, (out, wide, high, low, flat, inverse, slab, sem) = rest[:groups], rest[-8:]
    acq, _, lines, width = blocks[0].shape
    looks = lines // LOOK_R
    count = pairs.shape[1]
    windows = width // LOOK_C
    both = 2 * looks
    total_acq = groups * acq

    for r, block in enumerate(blocks):
        for a in range(acq):
            for x in range(2):
                wide[(group[0] ^ r) * acq + a, x] = block[a, x].astype(jnp.float32) * 0.125

    col = lax.broadcasted_iota(jnp.int32, (width, windows), 0)
    window = lax.broadcasted_iota(jnp.int32, (width, windows), 1)
    pool = jnp.where(col // LOOK_C == window, 1.0, 0.0).astype(jnp.bfloat16)

    def put(at, field):
        first = field.astype(jnp.bfloat16)
        high[at : at + both, :] = first
        low[at : at + both, :] = (field - first.astype(jnp.float32)).astype(jnp.bfloat16)

    def gather(rows):
        return jnp.dot(high[:rows, :], pool, preferred_element_type=jnp.float32) + jnp.dot(
            low[:rows, :], pool, preferred_element_type=jnp.float32
        )

    for i in range(0, total_acq, 2):
        fields = []
        for u in (i, i + 1):
            total = 0.0
            for j in range(LOOK_R):
                for x in range(2):
                    value = wide[u, x, j * looks : (j + 1) * looks, :]
                    total = total + value * value
            fields.append(total)
        put(i * looks, jnp.concatenate(fields, axis=0))
    power = gather(total_acq * looks)
    inverse[...] = lax.rsqrt(power + 1e-6).reshape(total_acq, looks, windows)

    def products(i):
        for u in range(batch):
            m, s = pairs[0, i * batch + u], pairs[1, i * batch + u]
            real, imag = 0.0, 0.0
            for j in range(LOOK_R):
                at = slice(j * looks, (j + 1) * looks)
                m0, m1, s0, s1 = wide[m, 0, at, :], wide[m, 1, at, :], wide[s, 0, at, :], wide[s, 1, at, :]
                real = real + (m0 * s0 + m1 * s1)
                imag = imag + (m1 * s0 - m0 * s1)
            put(u * both, jnp.concatenate([real, imag], axis=0))

    def settle(i):
        pooled = gather(batch * both)
        for u in range(batch):
            p = i * batch + u
            scale = inverse[pairs[0, p]] * inverse[pairs[1, p]]
            scaled = pooled[u * both : (u + 1) * both] * jnp.concatenate([scale, scale], axis=0)
            flat[pl.ds(pl.multiple_of(p * both, both), both), :] = scaled

    def turn(i, carry):
        settle(i - 1)
        products(i)
        return carry

    products(0)
    lax.fori_loop(1, count // batch, turn, 0)
    settle(count // batch - 1)

    for x in range(2):
        for g in range(looks):
            slab[x, g] = flat[pl.ds(x * looks + g, count, stride=both), :].T
    copy = pltpu.make_async_copy(slab, out.at[:, pl.ds(place * looks, looks)], sem)
    copy.start()
    copy.wait()


def interfere(place, chunks, group, pairs, blocks, before):
    groups = len(blocks)
    acq, _, lines, width = blocks[0].shape
    looks, windows, count = lines // LOOK_R, width // LOOK_C, pairs.shape[1]
    batch = max(b for b in range(1, 7) if count % b == 0)
    rows = max(batch * 2, groups * acq) * looks
    extra = [] if before is None else [before]
    return pl.pallas_call(
        functools.partial(interfere_kernel, groups, place, batch),
        in_specs=[SMEM, SMEM] + [VMEM] * groups + [ANY] * len(extra),
        out_specs=ANY,
        out_shape=pltpu.HBM((2, chunks * looks, windows, count), jnp.float32),
        scratch_shapes=[
            pltpu.VMEM((groups * acq, 2, lines, width), jnp.float32),
            pltpu.VMEM((rows, width), jnp.bfloat16),
            pltpu.VMEM((rows, width), jnp.bfloat16),
            pltpu.VMEM((count * 2 * looks, windows), jnp.float32),
            pltpu.VMEM((groups * acq, looks, windows), jnp.float32),
            pltpu.VMEM((2, looks, windows, count), jnp.float32),
            pltpu.SemaphoreType.DMA,
        ],
        input_output_aliases={} if before is None else {2 + groups: 0},
        compiler_params=pltpu.CompilerParams(vmem_limit_bytes=16 * MIB),
        cost_estimate=pl.CostEstimate(
            flops=count * 8 * lines * width,
            bytes_accessed=groups * acq * 2 * lines * width * 2,
            transcendentals=0,
        ),
        name="interfere",
    )(group, pairs, *blocks, *extra)


def local(slc, offsets, weights, pairs):
    acq, _, lines, cols = slc.shape
    groups = lax.axis_size("acq")
    size = lax.axis_size("pix")
    group = jnp.reshape(lax.axis_index("acq"), (1,)).astype(jnp.int32)
    kernel = weights.T.astype(jnp.float32)
    turned = pairs.T
    chunks = lines // CHUNK
    reach = CHUNK + TILE * 2

    up = [(i, i + 1) for i in range(size - 1)]
    down = [(j, i) for i, j in up]

    def send(blocks):
        moved = [blocks[0]]
        for s in range(1, groups):
            moved.append(lax.ppermute(blocks[s], "acq", [(i, i ^ s) for i in range(groups)]))
        return moved

    slc = pltpu.with_memory_space_constraint(slc, pltpu.HBM)
    *blocks, head, tail, slab = resample_first(CHUNK, group, kernel, offsets, slc, groups)
    above = lax.ppermute(tail, "pix", up)
    below = lax.ppermute(head, "pix", down)
    middle = send(blocks)
    top = send(
        resample_edge(0, 0, reach, -HALO, group, kernel, offsets, slab, above, groups)
    )
    bottom = send(
        resample_edge(
            lines - CHUNK, lines - reach, reach, lines, group, kernel, offsets, slab, below, groups
        )
    )
    result = None
    for place, moved in ((1, middle), (0, top), (2, bottom)):
        result = interfere(place, chunks, group, turned, moved, result)
    return jnp.transpose(result, (0, 3, 1, 2))


def solution(mesh):
    placed = (P("acq", None, "pix", None), P("acq", "pix"), P(), P())
    return jax.shard_map(
        local, mesh=mesh, in_specs=placed, out_specs=P(None, None, "pix", "acq"), check_vma=False
    )
```

time: 530 us -> 57.7 us (0.11)
  loops' own time: 229 us -> 0 us
  other arithmetic: 149 us -> 0.68 us
  local copies, waits for them, and re-layouts: 81.3 us -> 0.68 us
  waiting for transfers between devices: 51.6 us -> 16.4 us
  Pallas kernels: 0 us -> 23 us
  starting transfers between devices: 10.5 us -> 15.8 us
    another operation x2 -> x0, loops' own time: 229 us -> none  [the longest x1 229 us: interfere(): real_all, imag_all = lax.map(one_pair, pairs)]
    convert_element_type x73 -> x1, other arithmetic: 84.6 us -> 0.68 us  [local(): kernel = weights.T.astype(jnp.float32)]
    reduce_sum x204 -> x0, other arithmetic: 58.9 us -> none  [pool(): return jnp.sum(shaped, axis=(1, 3)) * scale_look]
    all_to_all x1 -> x0, waiting for transfers between devices: 39.7 us -> none  [local(): lax.all_to_all(shaped, 'acq', split_axis=0, concat_axis=1, tiled=True)[0]]
    slice x61 -> x0, local copies, waits for them, and re-layouts: 35.3 us -> none  [the longest x60 32.3 us: one_pair(): pair[0]]
    reduce_sum x132 -> x0, local copies, waits for them, and re-layouts: 29.5 us -> none  [pool(): return jnp.sum(shaped, axis=(1, 3)) * scale_look]
    pallas_call x0 -> x6, Pallas kernels: none -> 23 us  [the longest x3 17.1 us: interfere(): pl.pallas_call(functools.partial(interfere_kernel, groups, place, batch),...]
    ppermute x2 -> x11, starting transfers between devices: 5.68 us -> 15.8 us  [the longest x9 10.1 us: send(): lax.ppermute(blocks[s], 'acq', [(i, i ^ s) for i in range(groups)])]
  transfers between devices with their start and end apart: 3 -> 11, of which waited for: 3 -> 5; matrix products, arithmetic and copies ran while one was open for 0% -> 0% of each run, Pallas kernels for 0% -> 25%
where the time goes in v2:
time: 57.7 us; the launch traced here: 56.7 us
  Pallas kernels  23 us (40%)
  waiting for transfers between devices  16.4 us (28%)
  starting transfers between devices  15.8 us (27%)
  other arithmetic  0.68 us (1%)
  local copies, waits for them, and re-layouts  0.68 us (1%)
    pallas_call x3, Pallas kernels, interfere(): pl.pallas_call(functools.partial(interfere_kernel, groups, place, batch),...  17.1 us
    ppermute x9, waiting for transfers between devices, send(): lax.ppermute(blocks[s], 'acq', [(i, i ^ s) for i in range(groups)])  10.3 us
    ppermute x9, starting transfers between devices, send(): lax.ppermute(blocks[s], 'acq', [(i, i ^ s) for i in range(groups)])  10.1 us
    ppermute x1, waiting for transfers between devices, local(): above = lax.ppermute(tail, 'pix', up)  5.32 us
    ppermute x1, starting transfers between devices, local(): above = lax.ppermute(tail, 'pix', up)  3.77 us
    pallas_call x1, Pallas kernels, resample_first(): pl.pallas_call(functools.partial(first_kernel, first, groups), in_specs=[...  3.12 us
    pallas_call x2, Pallas kernels, resample_edge(): pl.pallas_call(functools.partial(edge_kernel, first, groups, begin, count...  2.77 us
    ppermute x1, starting transfers between devices, local(): below = lax.ppermute(head, 'pix', down)  1.92 us
  transfers between devices with their start and end apart: 11, of which 5 were waited for; matrix products, arithmetic and copies ran while one was open for 0% of the time, Pallas kernels for 25%

profile of v2, /device:TPU:9, one launch (start us, length us, event | category | flops | bytes accessed | tf_op | source)
XLA Modules:
  0.0 56.7 jit_solution(3300618092887384253)
XLA Ops:
  0.0 0.7 %convert_bitcast_fusion.kernel = f32[8,12]{1,0:T(8,128)S(1)} fusion(bf16[12,8]{0,1:T(8,128)(2,1)} %param.6), kind=kLoop, calls=%fused_computation | loop fusion | flops 96 | bytes 576 | tf_op jit(solution)/shard_map/convert_element_type | solution.py:249
  0.7 0.0 copy-start
  0.7 0.7 %copy-done = s32[3,96]{1,0:T(4,128)S(1)} copy-done((s32[3,96]{1,0:T(4,128)S(1)}, s32[3,96]{1,0:T(4,128)}, u32[]{:S(2)}) %copy-start) | copy-done | bytes 1176
  1.4 3.1 %resample_first.1 = (bf16[3,2,32,768]{3,2,1,0:T(8,128)(2,1)S(1)}, bf16[3,2,32,768]{3,2,1,0:T(8,128)(2,1)S(1)}, bf16[3,2,32,768]{3,2,1,0:T(8,128)(2,1)S(1)}, bf16...) custom-call(s32[1]{0:T(128)} %bitcast.group, ...), custom_call_target="tpu_custom_call" | custom-call | flops 113246208 | bytes 4718592 | tf_op jit(solution)/shard_map/resample_first/pallas_call | solution.py:105
  4.5 3.8 %collective-permute-start.4 = (bf16[3,2,24,3072]{3,2,1,0:T(8,128)(2,1)S(1)}, bf16[3,2,24,3072]{3,2,1,0:T(8,128)(2,1)S(1)}, u32[]{:S(2)}, u32[]{:S(2)}) collective-permute-start(bf16[3,2,24,3072]{3,2,1,0:T(8,128)(2,1)S(1)} %get-tuple-element.26), channel_id=1, source_target_pairs={{0,1},{1,2},{2,3},{3,4},{4,5},{5,6},{6,7},{8,9},{9,10},{10,11},{11... | collective-permute-start | bytes 2654216 | tf_op jit(solution)/shard_map/ppermute | solution.py:265
  8.3 1.9 %collective-permute-start = (bf16[3,2,24,3072]{3,2,1,0:T(8,128)(2,1)S(1)}, bf16[3,2,24,3072]{3,2,1,0:T(8,128)(2,1)S(1)}, u32[]{:S(2)}, u32[]{:S(2)}) collective-permute-start(bf16[3,2,24,3072]{3,2,1,0:T(8,128)(2,1)S(1)} %get-tuple-element.21), channel_id=1, source_target_pairs={{1,0},{2,1},{3,2},{4,3},{5,4},{6,5},{7,6},{9,8},{10,9},{11,10},{12... | collective-permute-start | bytes 2654216 | tf_op jit(solution)/shard_map/ppermute | solution.py:266
  10.2 1.3 %collective-permute-start.8 = (bf16[3,2,32,768]{3,2,1,0:T(8,128)(2,1)S(1)}, bf16[3,2,32,768]{3,2,1,0:T(8,128)(2,1)S(1)}, u32[]{:S(2)}, u32[]{:S(2)}) collective-permute-start(bf16[3,2,32,768]{3,2,1,0:T(8,128)(2,1)S(1)} %get-tuple-element.32), channel_id=1, source_target_pairs={{0,8},{8,0},{16,24},{24,16},{1,9},{9,1},{17,25},{25,17},{2,10},{10... | collective-permute-start | bytes 884744 | tf_op jit(solution)/shard_map/ppermute | solution.py:260
  11.5 1.2 %collective-permute-start.9 = (bf16[3,2,32,768]{3,2,1,0:T(8,128)(2,1)S(1)}, bf16[3,2,32,768]{3,2,1,0:T(8,128)(2,1)S(1)}, u32[]{:S(2)}, u32[]{:S(2)}) collective-permute-start(bf16[3,2,32,768]{3,2,1,0:T(8,128)(2,1)S(1)} %get-tuple-element.33), channel_id=1, source_target_pairs={{0,16},{8,24},{16,0},{24,8},{1,17},{9,25},{17,1},{25,9},{2,18},{10... | collective-permute-start | bytes 884744 | tf_op jit(solution)/shard_map/ppermute | solution.py:260
  12.7 0.2 collective-permute-start.10
  12.9 5.3 %collective-permute-done.4.halo = bf16[3,2,24,3072]{3,2,1,0:T(8,128)(2,1)S(1)} collective-permute-done((bf16[3,2,24,3072]{3,2,1,0:T(8,128)(2,1)S(1)}, bf16[3,2,24,3072]{3,2,1,0:T(8,128)(2,1)S(1)}, u32[]{:S(2)}, u32[]{:S(2)}) %collective-permute-start.4) | collective-permute-done | bytes 884768 | tf_op jit(solution)/shard_map/ppermute | solution.py:265
  18.2 1.4 %resample_edge.3 = (bf16[3,2,32,768]{3,2,1,0:T(8,128)(2,1)S(1)}, bf16[3,2,32,768]{3,2,1,0:T(8,128)(2,1)S(1)}, bf16[3,2,32,768]{3,2,1,0:T(8,128)(2,1)S(1)}, bf16[3,2,32,768]{3,2,1,0:T(8,128)(2,1)S(1)}) custom-call(s32[1]{0:T(128)} %bitcast.group, f32[8,12]{1,0:T(8,128)S(1)} %convert_bitcast_fusion.kernel, s32[3,96]{1,0:T(4,128)S(1)} %copy-done, ...), custom_call_target="tpu_custom_call" | custom-call | flops 103809024 | bytes 4423680 | tf_op jit(solution)/shard_map/resample_edge/pallas_call | solution.py:123
  19.6 1.3 %collective-permute-start.5 = (bf16[3,2,32,768]{3,2,1,0:T(8,128)(2,1)S(1)}, bf16[3,2,32,768]{3,2,1,0:T(8,128)(2,1)S(1)}, u32[]{:S(2)}, u32[]{:S(2)}) collective-permute-start(bf16[3,2,32,768]{3,2,1,0:T(8,128)(2,1)S(1)} %get-tuple-element.28), channel_id=1, source_target_pairs={{0,8},{8,0},{16,24},{24,16},{1,9},{9,1},{17,25},{25,17},{2,10},{10... | collective-permute-start | bytes 884744 | tf_op jit(solution)/shard_map/ppermute | solution.py:260
  20.9 0.0 collective-permute-done.8.rest_1_
  20.9 1.2 %collective-permute-start.6 = (bf16[3,2,32,768]{3,2,1,0:T(8,128)(2,1)S(1)}, bf16[3,2,32,768]{3,2,1,0:T(8,128)(2,1)S(1)}, u32[]{:S(2)}, u32[]{:S(2)}) collective-permute-start(bf16[3,2,32,768]{3,2,1,0:T(8,128)(2,1)S(1)} %get-tuple-element.29), channel_id=1, source_target_pairs={{0,16},{8,24},{16,0},{24,8},{1,17},{9,25},{17,1},{25,9},{2,18},{10... | collective-permute-start | bytes 884744 | tf_op jit(solution)/shard_map/ppermute | solution.py:260
  22.1 0.8 %collective-permute-done.halo = bf16[3,2,24,3072]{3,2,1,0:T(8,128)(2,1)S(1)} collective-permute-done((bf16[3,2,24,3072]{3,2,1,0:T(8,128)(2,1)S(1)}, bf16[3,2,24,3072]{3,2,1,0:T(8,128)(2,1)S(1)}, u32[]{:S(2)}, u32[]{:S(2)}) %collective-permute-start) | collective-permute-done | bytes 884768 | tf_op jit(solution)/shard_map/ppermute | solution.py:266
  22.9 0.0 copy-start.1
  22.9 2.2 %collective-permute-start.7 = (bf16[3,2,32,768]{3,2,1,0:T(8,128)(2,1)S(1)}, bf16[3,2,32,768]{3,2,1,0:T(8,128)(2,1)S(1)}, u32[]{:S(2)}, u32[]{:S(2)}) collective-permute-start(bf16[3,2,32,768]{3,2,1,0:T(8,128)(2,1)S(1)} %get-tuple-element.30), channel_id=1, source_target_pairs={{0,24},{8,16},{16,8},{24,0},{1,25},{9,17},{17,9},{25,1},{2,26},{10... | collective-permute-start | bytes 884744 | tf_op jit(solution)/shard_map/ppermute | solution.py:260
  25.1 1.4 %resample_edge.2 = (bf16[3,2,32,768]{3,2,1,0:T(8,128)(2,1)S(1)}, bf16[3,2,32,768]{3,2,1,0:T(8,128)(2,1)S(1)}, bf16[3,2,32,768]{3,2,1,0:T(8,128)(2,1)S(1)}, bf16[3,2,32,768]{3,2,1,0:T(8,128)(2,1)S(1)}) custom-call(s32[1]{0:T(128)} %bitcast.group, f32[8,12]{1,0:T(8,128)S(1)} %convert_bitcast_fusion.kernel, s32[3,96]{1,0:T(4,128)S(1)} %copy-done, ...), custom_call_target="tpu_custom_call" | custom-call | flops 103809024 | bytes 4423680 | tf_op jit(solution)/shard_map/resample_edge/pallas_call | solution.py:123
  26.5 0.0 collective-permute-done.9.rest_2_
  26.5 0.3 collective-permute-start.1
  26.8 0.0 collective-permute-done.10.rest_3_
  26.8 0.2 collective-permute-start.2
  27.1 3.9 %collective-permute-done.5.rest_1_ = bf16[3,2,32,768]{3,2,1,0:T(8,128)(2,1)S(1)} collective-permute-done((bf16[3,2,32,768]{3,2,1,0:T(8,128)(2,1)S(1)}, bf16[3,2,32,768]{3,2,1,0:T(8,128)(2,1)S(1)}, u32[]{:S(2)}, u32[]{:S(2)}) %collective-permute-start.5) | collective-permute-done | bytes 294944 | tf_op jit(solution)/shard_map/ppermute | solution.py:260
  31.0 2.2 %collective-permute-start.3 = (bf16[3,2,32,768]{3,2,1,0:T(8,128)(2,1)S(1)}, bf16[3,2,32,768]{3,2,1,0:T(8,128)(2,1)S(1)}, u32[]{:S(2)}, u32[]{:S(2)}) collective-permute-start(bf16[3,2,32,768]{3,2,1,0:T(8,128)(2,1)S(1)} %get-tuple-element.25), channel_id=1, source_target_pairs={{0,24},{8,16},{16,8},{24,0},{1,25},{9,17},{17,9},{25,1},{2,26},{10... | collective-permute-start | bytes 884744 | tf_op jit(solution)/shard_map/ppermute | solution.py:260
  33.1 0.0 copy-done.1
  33.1 5.7 %interfere.3.rest_4_ = f32[2,24,48,60]{3,2,1,0:T(8,128)} custom-call(s32[1]{0:T(128)} %bitcast.group, s32[2,60]{1,0:T(2,128)S(1)} %bitcast.5, bf16[3,2,32,768]{3,2,1,0:T(8,128)(2,1)S(1)} %get-tuple-element.31.rest_0_, bf16[3,2,32,768]{3,2,1,0:T(8,128)(2,1)S(1)} %collective-permute-done.8.rest_1_, bf16[3,2,32,768]{3,2,1,0:T(8,128)(2,1)S(1)} %collective-permute-done.9.rest_2_, ...), custom_call_target="tpu_custom_call" | custom-call | flops 11796480 | bytes 1179648 | tf_op jit(solution)/shard_map/interfere/pallas_call | solution.py:219
  38.8 0.0 collective-permute-done.6.rest_2_
  38.9 0.0 collective-permute-done.7.rest_3_
  38.9 5.7 %interfere.4.rest_4_ = f32[2,24,48,60]{3,2,1,0:T(8,128)} custom-call(s32[1]{0:T(128)} %bitcast.group, s32[2,60]{1,0:T(2,128)S(1)} %bitcast.6, bf16[3,2,32,768]{3,2,1,0:T(8,128)(2,1)S(1)} %get-tuple-element.27.rest_0_, bf16[3,2,32,768]{3,2,1,0:T(8,128)(2,1)S(1)} %collective-permute-done.5.rest_1_, ...), custom_call_target="tpu_custom_call", output_to_operand_aliasing={{}: (6, {})} | custom-call | flops 11796480 | bytes 1179648 | tf_op jit(solution)/shard_map/interfere/pallas_call | solution.py:219
  44.6 0.0 collective-permute-done.1.rest_1_
  44.6 2.1 %collective-permute-done.2.rest_2_ = bf16[3,2,32,768]{3,2,1,0:T(8,128)(2,1)S(1)} collective-permute-done((bf16[3,2,32,768]{3,2,1,0:T(8,128)(2,1)S(1)}, bf16[3,2,32,768]{3,2,1,0:T(8,128)(2,1)S(1)}, u32[]{:S(2)}, u32[]{:S(2)}) %collective-permute-start.2) | collective-permute-done | bytes 294944 | tf_op jit(solution)/shard_map/ppermute | solution.py:260
  46.7 4.3 %collective-permute-done.3.rest_3_ = bf16[3,2,32,768]{3,2,1,0:T(8,128)(2,1)S(1)} collective-permute-done((bf16[3,2,32,768]{3,2,1,0:T(8,128)(2,1)S(1)}, bf16[3,2,32,768]{3,2,1,0:T(8,128)(2,1)S(1)}, u32[]{:S(2)}, u32[]{:S(2)}) %collective-permute-start.3) | collective-permute-done | bytes 294944 | tf_op jit(solution)/shard_map/ppermute | solution.py:260
  51.0 5.7 %interfere.5 = f32[2,24,48,60]{3,2,1,0:T(8,128)} custom-call(s32[1]{0:T(128)} %bitcast.group, s32[2,60]{1,0:T(2,128)S(1)} %bitcast.7, bf16[3,2,32,768]{3,2,1,0:T(8,128)(2,1)S(1)} %get-tuple-element.22.rest_0_, bf16[3,2,32,768]{3,2,1,0:T(8,128)(2,1)S(1)} %collective-permute-done.1.rest_1_, ...), custom_call_target="tpu_custom_call", output_to_operand_aliasing={{}: (6, {})} | custom-call | flops 11796480 | bytes 1179648 | tf_op jit(solution)/shard_map/interfere/pallas_call | solution.py:219
Async XLA Ops:
  0.7 0.7 %copy-start = (s32[3,96]{1,0:T(4,128)S(1)}, s32[3,96]{1,0:T(4,128)}, u32[]{:S(2)}) copy-start(s32[3,96]{1,0:T(4,128)} %off.5) | copy-start | bytes 3460
  4.5 13.7 %collective-permute-start.4 = (bf16[3,2,24,3072]{3,2,1,0:T(8,128)(2,1)S(1)}, bf16[3,2,24,3072]{3,2,1,0:T(8,128)(2,1)S(1)}, u32[]{:S(2)}, u32[]{:S(2)}) collective-permute-start(bf16[3,2,24,3072]{3,2,1,0:T(8,128)(2,1)S(1)} %get-tuple-element.26), channel_id=1, source_target_pairs={{0,1},{1,2},{2,3},{3,4},{4,5},{5,6},{6,7},{8,9},{9,10},{10,11},{11... | collective-permute-start | bytes 2654216 | tf_op jit(solution)/shard_map/ppermute | solution.py:265
  8.3 14.7 %collective-permute-start = (bf16[3,2,24,3072]{3,2,1,0:T(8,128)(2,1)S(1)}, bf16[3,2,24,3072]{3,2,1,0:T(8,128)(2,1)S(1)}, u32[]{:S(2)}, u32[]{:S(2)}) collective-permute-start(bf16[3,2,24,3072]{3,2,1,0:T(8,128)(2,1)S(1)} %get-tuple-element.21), channel_id=1, source_target_pairs={{1,0},{2,1},{3,2},{4,3},{5,4},{6,5},{7,6},{9,8},{10,9},{11,10},{12... | collective-permute-start | bytes 2654216 | tf_op jit(solution)/shard_map/ppermute | solution.py:266
  10.2 10.7 %collective-permute-start.8 = (bf16[3,2,32,768]{3,2,1,0:T(8,128)(2,1)S(1)}, bf16[3,2,32,768]{3,2,1,0:T(8,128)(2,1)S(1)}, u32[]{:S(2)}, u32[]{:S(2)}) collective-permute-start(bf16[3,2,32,768]{3,2,1,0:T(8,128)(2,1)S(1)} %get-tuple-element.32), channel_id=1, source_target_pairs={{0,8},{8,0},{16,24},{24,16},{1,9},{9,1},{17,25},{25,17},{2,10},{10... | collective-permute-start | bytes 884744 | tf_op jit(solution)/shard_map/ppermute | solution.py:260
  11.5 15.1 %collective-permute-start.9 = (bf16[3,2,32,768]{3,2,1,0:T(8,128)(2,1)S(1)}, bf16[3,2,32,768]{3,2,1,0:T(8,128)(2,1)S(1)}, u32[]{:S(2)}, u32[]{:S(2)}) collective-permute-start(bf16[3,2,32,768]{3,2,1,0:T(8,128)(2,1)S(1)} %get-tuple-element.33), channel_id=1, source_target_pairs={{0,16},{8,24},{16,0},{24,8},{1,17},{9,25},{17,1},{25,9},{2,18},{10... | collective-permute-start | bytes 884744 | tf_op jit(solution)/shard_map/ppermute | solution.py:260
  12.7 14.1 %collective-permute-start.10 = (bf16[3,2,32,768]{3,2,1,0:T(8,128)(2,1)S(1)}, bf16[3,2,32,768]{3,2,1,0:T(8,128)(2,1)S(1)}, u32[]{:S(2)}, u32[]{:S(2)}) collective-permute-start(bf16[3,2,32,768]{3,2,1,0:T(8,128)(2,1)S(1)} %get-tuple-element.34), channel_id=1, source_target_pairs={{0,24},{8,16},{16,8},{24,0},{1,25},{9,17},{17,9},{25,1},{2,26},{10... | collective-permute-start | bytes 884744 | tf_op jit(solution)/shard_map/ppermute | solution.py:260
  19.6 11.4 %collective-permute-start.5 = (bf16[3,2,32,768]{3,2,1,0:T(8,128)(2,1)S(1)}, bf16[3,2,32,768]{3,2,1,0:T(8,128)(2,1)S(1)}, u32[]{:S(2)}, u32[]{:S(2)}) collective-permute-start(bf16[3,2,32,768]{3,2,1,0:T(8,128)(2,1)S(1)} %get-tuple-element.28), channel_id=1, source_target_pairs={{0,8},{8,0},{16,24},{24,16},{1,9},{9,1},{17,25},{25,17},{2,10},{10... | collective-permute-start | bytes 884744 | tf_op jit(solution)/shard_map/ppermute | solution.py:260
  20.9 18.0 %collective-permute-start.6 = (bf16[3,2,32,768]{3,2,1,0:T(8,128)(2,1)S(1)}, bf16[3,2,32,768]{3,2,1,0:T(8,128)(2,1)S(1)}, u32[]{:S(2)}, u32[]{:S(2)}) collective-permute-start(bf16[3,2,32,768]{3,2,1,0:T(8,128)(2,1)S(1)} %get-tuple-element.29), channel_id=1, source_target_pairs={{0,16},{8,24},{16,0},{24,8},{1,17},{9,25},{17,1},{25,9},{2,18},{10... | collective-permute-start | bytes 884744 | tf_op jit(solution)/shard_map/ppermute | solution.py:260
  22.9 10.2 %copy-start.1 = (s32[60,2]{0,1:T(2,128)S(1)}, s32[60,2]{0,1:T(2,128)}, u32[]{:S(2)}) copy-start(s32[60,2]{0,1:T(2,128)} %param.7) | copy-start | bytes 1444
  22.9 15.9 %collective-permute-start.7 = (bf16[3,2,32,768]{3,2,1,0:T(8,128)(2,1)S(1)}, bf16[3,2,32,768]{3,2,1,0:T(8,128)(2,1)S(1)}, u32[]{:S(2)}, u32[]{:S(2)}) collective-permute-start(bf16[3,2,32,768]{3,2,1,0:T(8,128)(2,1)S(1)} %get-tuple-element.30), channel_id=1, source_target_pairs={{0,24},{8,16},{16,8},{24,0},{1,25},{9,17},{17,9},{25,1},{2,26},{10... | collective-permute-start | bytes 884744 | tf_op jit(solution)/shard_map/ppermute | solution.py:260
  26.5 18.1 %collective-permute-start.1 = (bf16[3,2,32,768]{3,2,1,0:T(8,128)(2,1)S(1)}, bf16[3,2,32,768]{3,2,1,0:T(8,128)(2,1)S(1)}, u32[]{:S(2)}, u32[]{:S(2)}) collective-permute-start(bf16[3,2,32,768]{3,2,1,0:T(8,128)(2,1)S(1)} %get-tuple-element.23), channel_id=1, source_target_pairs={{0,8},{8,0},{16,24},{24,16},{1,9},{9,1},{17,25},{25,17},{2,10},{10... | collective-permute-start | bytes 884744 | tf_op jit(solution)/shard_map/ppermute | solution.py:260
  26.8 19.9 %collective-permute-start.2 = (bf16[3,2,32,768]{3,2,1,0:T(8,128)(2,1)S(1)}, bf16[3,2,32,768]{3,2,1,0:T(8,128)(2,1)S(1)}, u32[]{:S(2)}, u32[]{:S(2)}) collective-permute-start(bf16[3,2,32,768]{3,2,1,0:T(8,128)(2,1)S(1)} %get-tuple-element.24), channel_id=1, source_target_pairs={{0,16},{8,24},{16,0},{24,8},{1,17},{9,25},{17,1},{25,9},{2,18},{10... | collective-permute-start | bytes 884744 | tf_op jit(solution)/shard_map/ppermute | solution.py:260
  31.0 20.0 %collective-permute-start.3 = (bf16[3,2,32,768]{3,2,1,0:T(8,128)(2,1)S(1)}, bf16[3,2,32,768]{3,2,1,0:T(8,128)(2,1)S(1)}, u32[]{:S(2)}, u32[]{:S(2)}) collective-permute-start(bf16[3,2,32,768]{3,2,1,0:T(8,128)(2,1)S(1)} %get-tuple-element.25), channel_id=1, source_target_pairs={{0,24},{8,16},{16,8},{24,0},{1,25},{9,17},{17,9},{25,1},{2,26},{10... | collective-permute-start | bytes 884744 | tf_op jit(solution)/shard_map/ppermute | solution.py:260

commit v3 on v2

--- a/solution.py
+++ b/solution.py
@@ -43,14 +43,14 @@
 
 
 def first_kernel(first, groups, group, kernel, off, slc, *rest):
-    outs, (head, tail, slab, band, sems) = rest[:groups], rest[groups:]
+    outs, head, tail, slab, band, sems = rest
     acq, _, lines, cols = slc.shape
     width = cols // groups
 
     def columns(s):
-        return pl.ds(pl.multiple_of((group[0] ^ s) * width, width), width)
-
-    order = [*range(1, groups), 0]
+        return slice(s * width, (s + 1) * width)
+
+    order = range(groups)
     copies = {}
     for s in order:
         at = columns(s)
@@ -63,25 +63,25 @@
         for a in range(acq):
             for x in range(2):
                 total = jnp.dot(band[a], slab[a, x, :, at], preferred_element_type=jnp.float32)
-                outs[s][a, x] = total.astype(jnp.bfloat16)
+                outs[s, a, x] = total.astype(jnp.bfloat16)
     head[...] = slab[:, :, :HALO, :]
     tail[...] = slab[:, :, lines - HALO :, :]
 
 
 def edge_kernel(first, groups, begin, count, halo_at, group, kernel, off, slab, halo, *rest):
-    outs, band = rest[:groups], rest[groups]
+    outs, band = rest
     acq, _, _, cols = slab.shape
     width = cols // groups
     build_bands(first, [(begin, count), (halo_at, HALO)], group, kernel, off, band)
-    for s in [*range(1, groups), 0]:
-        at = pl.ds(pl.multiple_of((group[0] ^ s) * width, width), width)
+    for s in range(groups):
+        at = slice(s * width, (s + 1) * width)
         for a in range(acq):
             for x in range(2):
                 lines = jnp.concatenate(
                     [slab[a, x, begin : begin + count, at], halo[a, x, :, at]], axis=0
                 )
                 total = jnp.dot(band[a], lines, preferred_element_type=jnp.float32)
-                outs[s][a, x] = total.astype(jnp.bfloat16)
+                outs[s, a, x] = total.astype(jnp.bfloat16)
 
 
 SMEM = pl.BlockSpec(memory_space=pltpu.SMEM)
@@ -99,14 +99,14 @@
 
 def resample_first(first, group, kernel, offsets, slc, groups):
     acq, _, lines, cols = slc.shape
-    piece = pltpu.VMEM((acq, 2, CHUNK, cols // groups), jnp.bfloat16)
+    piece = pltpu.VMEM((groups, acq, 2, CHUNK, cols // groups), jnp.bfloat16)
     halo = pltpu.VMEM((acq, 2, HALO, cols), jnp.bfloat16)
     slab = pltpu.VMEM(slc.shape, jnp.bfloat16)
     return pl.pallas_call(
         functools.partial(first_kernel, first, groups),
         in_specs=[SMEM, SMEM, VMEM, ANY],
-        out_specs=[VMEM] * (groups + 3),
-        out_shape=[piece] * groups + [halo, halo, slab],
+        out_specs=[VMEM] * 4,
+        out_shape=[piece, halo, halo, slab],
         scratch_shapes=[
             pltpu.VMEM((acq, CHUNK, lines), jnp.bfloat16),
             pltpu.SemaphoreType.DMA((groups,)),
@@ -119,12 +119,12 @@
 
 def resample_edge(first, begin, count, halo_at, group, kernel, offsets, slab, halo, groups):
     acq, _, lines, cols = slab.shape
-    piece = pltpu.VMEM((acq, 2, CHUNK, cols // groups), jnp.bfloat16)
+    piece = pltpu.VMEM((groups, acq, 2, CHUNK, cols // groups), jnp.bfloat16)
     return pl.pallas_call(
         functools.partial(edge_kernel, first, groups, begin, count, halo_at),
         in_specs=[SMEM, SMEM, VMEM, VMEM, VMEM],
-        out_specs=[VMEM] * groups,
-        out_shape=[piece] * groups,
+        out_specs=VMEM,
+        out_shape=piece,
         scratch_shapes=[pltpu.VMEM((acq, CHUNK, count + HALO), jnp.bfloat16)],
         compiler_params=pltpu.CompilerParams(vmem_limit_bytes=16 * MIB),
         cost_estimate=resample_cost(acq, cols, count + HALO),
@@ -132,19 +132,19 @@
     )(group, kernel, offsets, slab, halo)
 
 
-def interfere_kernel(groups, place, batch, group, pairs, *rest):
-    blocks, (out, wide, high, low, flat, inverse, slab, sem) = rest[:groups], rest[-8:]
-    acq, _, lines, width = blocks[0].shape
+def interfere_kernel(place, batch, pairs, blocks, *rest):
+    (out, wide, high, low, flat, inverse, slab, sem) = rest[-8:]
+    groups, acq, _, lines, width = blocks.shape
     looks = lines // LOOK_R
     count = pairs.shape[1]
     windows = width // LOOK_C
     both = 2 * looks
     total_acq = groups * acq
 
-    for r, block in enumerate(blocks):
+    for r in range(groups):
         for a in range(acq):
             for x in range(2):
-                wide[(group[0] ^ r) * acq + a, x] = block[a, x].astype(jnp.float32) * 0.125
+                wide[r * acq + a, x] = blocks[r, a, x].astype(jnp.float32) * 0.125
 
     col = lax.broadcasted_iota(jnp.int32, (width, windows), 0)
     window = lax.broadcasted_iota(jnp.int32, (width, windows), 1)
@@ -209,16 +209,15 @@
     copy.wait()
 
 
-def interfere(place, chunks, group, pairs, blocks, before):
-    groups = len(blocks)
-    acq, _, lines, width = blocks[0].shape
+def interfere(place, chunks, pairs, blocks, before):
+    groups, acq, _, lines, width = blocks.shape
     looks, windows, count = lines // LOOK_R, width // LOOK_C, pairs.shape[1]
     batch = max(b for b in range(1, 7) if count % b == 0)
     rows = max(batch * 2, groups * acq) * looks
     extra = [] if before is None else [before]
     return pl.pallas_call(
-        functools.partial(interfere_kernel, groups, place, batch),
-        in_specs=[SMEM, SMEM] + [VMEM] * groups + [ANY] * len(extra),
+        functools.partial(interfere_kernel, place, batch),
+        in_specs=[SMEM, VMEM] + [ANY] * len(extra),
         out_specs=ANY,
         out_shape=pltpu.HBM((2, chunks * looks, windows, count), jnp.float32),
         scratch_shapes=[
@@ -230,7 +229,7 @@
             pltpu.VMEM((2, looks, windows, count), jnp.float32),
             pltpu.SemaphoreType.DMA,
         ],
-        input_output_aliases={} if before is None else {2 + groups: 0},
+        input_output_aliases={} if before is None else {2: 0},
         compiler_params=pltpu.CompilerParams(vmem_limit_bytes=16 * MIB),
         cost_estimate=pl.CostEstimate(
             flops=count * 8 * lines * width,
@@ -238,7 +237,7 @@
             transcendentals=0,
         ),
         name="interfere",
-    )(group, pairs, *blocks, *extra)
+    )(pairs, blocks, *extra)
 
 
 def local(slc, offsets, weights, pairs):
@@ -255,16 +254,13 @@
     down = [(j, i) for i, j in up]
 
     def send(blocks):
-        moved = [blocks[0]]
-        for s in range(1, groups):
-            moved.append(lax.ppermute(blocks[s], "acq", [(i, i ^ s) for i in range(groups)]))
-        return moved
+        return lax.all_to_all(blocks, "acq", split_axis=0, concat_axis=0, tiled=True)
 
     slc = pltpu.with_memory_space_constraint(slc, pltpu.HBM)
-    *blocks, head, tail, slab = resample_first(CHUNK, group, kernel, offsets, slc, groups)
+    blocks, head, tail, slab = resample_first(CHUNK, group, kernel, offsets, slc, groups)
+    middle = send(blocks)
     above = lax.ppermute(tail, "pix", up)
     below = lax.ppermute(head, "pix", down)
-    middle = send(blocks)
     top = send(
         resample_edge(0, 0, reach, -HALO, group, kernel, offsets, slab, above, groups)
     )
@@ -275,7 +271,7 @@
     )
     result = None
     for place, moved in ((1, middle), (0, top), (2, bottom)):
-        result = interfere(place, chunks, group, turned, moved, result)
+        result = interfere(place, chunks, turned, moved, result)
     return jnp.transpose(result, (0, 3, 1, 2))
 
 

time: 57.7 us -> 76.1 us (1.32)
  the two profiles are of different devices: /device:TPU:9 before, /device:TPU:0 now
where the time goes in v3:
time: 76.1 us; the launch traced here: 75.5 us
  Pallas kernels  27 us (35%)
  waiting for transfers between devices  26.1 us (34%)
  starting transfers between devices  17 us (22%)
  local copies, waits for them, and re-layouts  4.65 us (6%)
    all_to_all x3, waiting for transfers between devices, send(): lax.all_to_all(blocks, 'acq', split_axis=0, concat_axis=0, tiled=True)  26.1 us
    pallas_call x3, Pallas kernels, interfere(): pl.pallas_call(functools.partial(interfere_kernel, place, batch), in_spec...  19.2 us
    all_to_all x3, starting transfers between devices, send(): lax.all_to_all(blocks, 'acq', split_axis=0, concat_axis=0, tiled=True)  12.5 us
    unnamed x14, local copies, waits for them, and re-layouts  4.65 us
    pallas_call x2, Pallas kernels, resample_edge(): pl.pallas_call(functools.partial(edge_kernel, first, groups, begin, count...  3.94 us
    pallas_call x1, Pallas kernels, resample_first(): pl.pallas_call(functools.partial(first_kernel, first, groups), in_specs=[...  3.86 us
    ppermute x1, starting transfers between devices, local(): above = lax.ppermute(tail, 'pix', up)  3.27 us
  transfers between devices with their start and end apart: 5, of which 3 were waited for; matrix products, arithmetic and copies ran while one was open for 0% of the time, Pallas kernels for 23%

profile of v3, /device:TPU:0, one launch (start us, length us, event | category | flops | bytes accessed | tf_op | source)
XLA Modules:
  0.0 75.5 jit_solution(9439569336969478255)
XLA Ops:
  0.0 0.7 convert_bitcast_fusion.kernel
  0.7 0.0 copy-start.3
  0.7 0.7 copy-done.3
  1.4 3.9 %resample_first.1 = (bf16[4,3,2,32,768]{4,3,2,1,0:T(8,128)(2,1)S(1)}, bf16[3,2,24,3072]{3,2,1,0:T(8,128)(2,1)S(1)}, bf16[3,2,24,3072]{3,2,1,0:T(8,128)(2,1)}, bf16[3,2,96,3072]{3,2,1,0:T(8,128)(2,1)S(1)}) custom-call(s32[1]{0:T(128)} %bitcast.1.group, f32[8,12]{1,0:T(8,128)S(1)} %convert_bitcast_fusion.kernel, s32[3,96]{1,0:T(4,128)S(1)} %copy-done.3, ...), custom_call_target="tpu_custom_call" | custom-call | flops 113246208 | bytes 4718592 | tf_op jit(solution)/shard_map/resample_first/pallas_call | solution.py:105
  5.2 0.0 copy-start.2
  5.2 1.0 %copy-done.2 = bf16[4,3,2,32,768]{4,3,2,1,0:T(8,128)(2,1)} copy-done((bf16[4,3,2,32,768]{4,3,2,1,0:T(8,128)(2,1)}, bf16[4,3,2,32,768]{4,3,2,1,0:T(8,128)(2,1)S(1)}, u32[]{:S(2)}) %copy-start.2) | copy-done | bytes 1179672
  6.2 0.0 copy-start.6
  6.3 0.9 %copy-done.6 = bf16[3,2,24,3072]{3,2,1,0:T(8,128)(2,1)} copy-done((bf16[3,2,24,3072]{3,2,1,0:T(8,128)(2,1)}, bf16[3,2,24,3072]{3,2,1,0:T(8,128)(2,1)S(1)}, u32[]{:S(2)}) %copy-start.6) | copy-done | bytes 884760
  7.2 3.3 %collective-permute-start.1 = (bf16[3,2,24,3072]{3,2,1,0:T(8,128)(2,1)}, bf16[3,2,24,3072]{3,2,1,0:T(8,128)(2,1)}, u32[]{:S(2)}, u32[]{:S(2)}) collective-permute-start(bf16[3,2,24,3072]{3,2,1,0:T(8,128)(2,1)} %get-tuple-element.11), channel_id=1, source_target_pairs={{0,1},{1,2},{2,3},{3,4},{4,5},{5,6},{6,7},{8,9},{9,10},{10,11},{11... | collective-permute-start | bytes 2654216 | tf_op jit(solution)/shard_map/ppermute | solution.py:262
  10.4 0.0 copy-start.4
  10.4 4.7 %all-to-all-start.2 = ((bf16[4,3,2,32,768]{4,3,2,1,0:T(8,128)(2,1)}), bf16[4,3,2,32,768]{4,3,2,1,0:T(8,128)(2,1)}, u32[]{:S(2)}, u32[]{:S(2)}) async-start(bf16[4,3,2,32,768]{4,3,2,1,0:T(8,128)(2,1)} %copy-done.2), calls=%async_computation.2 | async-start | bytes 2359296 | tf_op jit(solution)/shard_map/all_to_all | solution.py:257
  15.1 1.3 %collective-permute-start = (bf16[3,2,24,3072]{3,2,1,0:T(8,128)(2,1)}, bf16[3,2,24,3072]{3,2,1,0:T(8,128)(2,1)}, u32[]{:S(2)}, u32[]{:S(2)}) collective-permute-start(bf16[3,2,24,3072]{3,2,1,0:T(8,128)(2,1)} %copy-done.6), channel_id=1, source_target_pairs={{1,0},{2,1},{3,2},{4,3},{5,4},{6,5},{7,6},{9,8},{10,9},{11,10},{12... | collective-permute-start | bytes 2654216 | tf_op jit(solution)/shard_map/ppermute | solution.py:263
  16.4 0.0 collective-permute-done.1.halo
  16.4 0.0 copy-done.4
  16.4 1.9 %resample_edge.3 = bf16[4,3,2,32,768]{4,3,2,1,0:T(8,128)(2,1)S(1)} custom-call(s32[1]{0:T(128)} %bitcast.1.group, f32[8,12]{1,0:T(8,128)S(1)} %convert_bitcast_fusion.kernel, s32[3,96]{1,0:T(4,128)S(1)} %copy-done.4, bf16[3,2,96,3072]{3,2,1,0:T(8,128)(2,1)S(1)} %get-tuple-element.9.slab, bf16[3,2,24,3072]{3,2,1,0:T(8,128)(2,1)} %collective-permute-done.1.halo), custom_call_target="tpu_custom_call" | custom-call | flops 103809024 | bytes 4423680 | tf_op jit(solution)/shard_map/resample_edge/pallas_call | solution.py:123
  18.4 0.0 copy-start
  18.4 1.0 %copy-done = bf16[4,3,2,32,768]{4,3,2,1,0:T(8,128)(2,1)} copy-done((bf16[4,3,2,32,768]{4,3,2,1,0:T(8,128)(2,1)}, bf16[4,3,2,32,768]{4,3,2,1,0:T(8,128)(2,1)S(1)}, u32[]{:S(2)}) %copy-start) | copy-done | bytes 1179672
  19.4 12.0 %all-to-all-done.2.blocks = bf16[4,3,2,32,768]{4,3,2,1,0:T(8,128)(2,1)} async-done(((bf16[4,3,2,32,768]{4,3,2,1,0:T(8,128)(2,1)}), bf16[4,3,2,32,768]{4,3,2,1,0:T(8,128)(2,1)}, u32[]{:S(2)}, u32[]{:S(2)}) %all-to-all-start.2) | async-done | bytes 1179680 | tf_op jit(solution)/shard_map/all_to_all | solution.py:257
  31.4 4.3 %all-to-all-start.1 = ((bf16[4,3,2,32,768]{4,3,2,1,0:T(8,128)(2,1)}), bf16[4,3,2,32,768]{4,3,2,1,0:T(8,128)(2,1)}, u32[]{:S(2)}, u32[]{:S(2)}) async-start(bf16[4,3,2,32,768]{4,3,2,1,0:T(8,128)(2,1)} %copy-done), calls=%async_computation.1 | async-start | bytes 2359296 | tf_op jit(solution)/shard_map/all_to_all | solution.py:257
  35.7 0.0 collective-permute-done.halo
  35.7 2.0 %resample_edge.2 = bf16[4,3,2,32,768]{4,3,2,1,0:T(8,128)(2,1)S(1)} custom-call(s32[1]{0:T(128)} %bitcast.1.group, f32[8,12]{1,0:T(8,128)S(1)} %convert_bitcast_fusion.kernel, s32[3,96]{1,0:T(4,128)S(1)} %copy-done.4, bf16[3,2,96,3072]{3,2,1,0:T(8,128)(2,1)S(1)} %get-tuple-element.9.slab, bf16[3,2,24,3072]{3,2,1,0:T(8,128)(2,1)} %collective-permute-done.halo), custom_call_target="tpu_custom_call" | custom-call | flops 103809024 | bytes 4423680 | tf_op jit(solution)/shard_map/resample_edge/pallas_call | solution.py:123
  37.7 0.0 copy-start.1
  37.7 1.0 %copy-done.1 = bf16[4,3,2,32,768]{4,3,2,1,0:T(8,128)(2,1)} copy-done((bf16[4,3,2,32,768]{4,3,2,1,0:T(8,128)(2,1)}, bf16[4,3,2,32,768]{4,3,2,1,0:T(8,128)(2,1)S(1)}, u32[]{:S(2)}) %copy-start.1) | copy-done | bytes 1179672
  38.7 0.0 copy-start.5
  38.7 12.6 %all-to-all-done.1.blocks = bf16[4,3,2,32,768]{4,3,2,1,0:T(8,128)(2,1)} async-done(((bf16[4,3,2,32,768]{4,3,2,1,0:T(8,128)(2,1)}), bf16[4,3,2,32,768]{4,3,2,1,0:T(8,128)(2,1)}, u32[]{:S(2)}, u32[]{:S(2)}) %all-to-all-start.1) | async-done | bytes 1179680 | tf_op jit(solution)/shard_map/all_to_all | solution.py:257
  51.3 3.5 %all-to-all-start = ((bf16[4,3,2,32,768]{4,3,2,1,0:T(8,128)(2,1)}), bf16[4,3,2,32,768]{4,3,2,1,0:T(8,128)(2,1)S(1)}, u32[]{:S(2)}, u32[]{:S(2)}) async-start(bf16[4,3,2,32,768]{4,3,2,1,0:T(8,128)(2,1)} %copy-done.1), calls=%async_computation | async-start | bytes 2359296 | tf_op jit(solution)/shard_map/all_to_all | solution.py:257
  54.9 0.0 copy-done.5
  54.9 6.6 %interfere.3.rest_0_ = f32[2,24,48,60]{3,2,1,0:T(8,128)} custom-call(s32[2,60]{1,0:T(2,128)S(1)} %bitcast.5, bf16[4,3,2,32,768]{4,3,2,1,0:T(8,128)(2,1)} %all-to-all-done.2.blocks), custom_call_target="tpu_custom_call" | custom-call | flops 11796480 | bytes 1179648 | tf_op jit(solution)/shard_map/interfere/pallas_call | solution.py:218
  61.5 6.6 %interfere.4.rest_0_ = f32[2,24,48,60]{3,2,1,0:T(8,128)} custom-call(s32[2,60]{1,0:T(2,128)S(1)} %bitcast.6, bf16[4,3,2,32,768]{4,3,2,1,0:T(8,128)(2,1)} %all-to-all-done.1.blocks, f32[2,24,48,60]{3,2,1,0:T(8,128)} %interfere.3.rest_0_), custom_call_target="tpu_custom_call", output_to_operand_aliasing={{}: (2, {})} | custom-call | flops 11796480 | bytes 1179648 | tf_op jit(solution)/shard_map/interfere/pallas_call | solution.py:218
  68.2 1.4 %all-to-all-done.blocks = bf16[4,3,2,32,768]{4,3,2,1,0:T(8,128)(2,1)S(1)} async-done(((bf16[4,3,2,32,768]{4,3,2,1,0:T(8,128)(2,1)}), bf16[4,3,2,32,768]{4,3,2,1,0:T(8,128)(2,1)S(1)}, u32[]{:S(2)}, u32[]{:S(2)}) %all-to-all-start) | async-done | bytes 1179680 | tf_op jit(solution)/shard_map/all_to_all | solution.py:257
  69.6 5.9 %interfere.5 = f32[2,24,48,60]{3,2,1,0:T(8,128)} custom-call(s32[2,60]{1,0:T(2,128)S(1)} %bitcast.7, bf16[4,3,2,32,768]{4,3,2,1,0:T(8,128)(2,1)S(1)} %all-to-all-done.blocks, f32[2,24,48,60]{3,2,1,0:T(8,128)} %interfere.4.rest_0_), custom_call_target="tpu_custom_call", output_to_operand_aliasing={{}: (2, {})} | custom-call | flops 11796480 | bytes 1179648 | tf_op jit(solution)/shard_map/interfere/pallas_call | solution.py:218
Async XLA Ops:
  0.7 0.7 copy-start.3
  5.2 1.0 %copy-start.2 = (bf16[4,3,2,32,768]{4,3,2,1,0:T(8,128)(2,1)}, bf16[4,3,2,32,768]{4,3,2,1,0:T(8,128)(2,1)S(1)}, u32[]{:S(2)}) copy-start(bf16[4,3,2,32,768]{4,3,2,1,0:T(8,128)(2,1)S(1)} %get-tuple-element.12) | copy-start | bytes 3538948
  6.2 0.9 %copy-start.6 = (bf16[3,2,24,3072]{3,2,1,0:T(8,128)(2,1)}, bf16[3,2,24,3072]{3,2,1,0:T(8,128)(2,1)S(1)}, u32[]{:S(2)}) copy-start(bf16[3,2,24,3072]{3,2,1,0:T(8,128)(2,1)S(1)} %get-tuple-element.10) | copy-start | bytes 2654212
  7.2 9.2 %collective-permute-start.1 = (bf16[3,2,24,3072]{3,2,1,0:T(8,128)(2,1)}, bf16[3,2,24,3072]{3,2,1,0:T(8,128)(2,1)}, u32[]{:S(2)}, u32[]{:S(2)}) collective-permute-start(bf16[3,2,24,3072]{3,2,1,0:T(8,128)(2,1)} %get-tuple-element.11), channel_id=1, source_target_pairs={{0,1},{1,2},{2,3},{3,4},{4,5},{5,6},{6,7},{8,9},{9,10},{10,11},{11... | collective-permute-start | bytes 2654216 | tf_op jit(solution)/shard_map/ppermute | solution.py:262
  10.4 6.0 %copy-start.4 = (s32[3,96]{1,0:T(4,128)S(1)}, s32[3,96]{1,0:T(4,128)}, u32[]{:S(2)}) copy-start(s32[3,96]{1,0:T(4,128)} %off.5) | copy-start | bytes 3460
  10.4 21.0 %all-to-all-start.2 = ((bf16[4,3,2,32,768]{4,3,2,1,0:T(8,128)(2,1)}), bf16[4,3,2,32,768]{4,3,2,1,0:T(8,128)(2,1)}, u32[]{:S(2)}, u32[]{:S(2)}) async-start(bf16[4,3,2,32,768]{4,3,2,1,0:T(8,128)(2,1)} %copy-done.2), calls=%async_computation.2 | async-start | bytes 2359296 | tf_op jit(solution)/shard_map/all_to_all | solution.py:257
  15.1 20.6 %collective-permute-start = (bf16[3,2,24,3072]{3,2,1,0:T(8,128)(2,1)}, bf16[3,2,24,3072]{3,2,1,0:T(8,128)(2,1)}, u32[]{:S(2)}, u32[]{:S(2)}) collective-permute-start(bf16[3,2,24,3072]{3,2,1,0:T(8,128)(2,1)} %copy-done.6), channel_id=1, source_target_pairs={{1,0},{2,1},{3,2},{4,3},{5,4},{6,5},{7,6},{9,8},{10,9},{11,10},{12... | collective-permute-start | bytes 2654216 | tf_op jit(solution)/shard_map/ppermute | solution.py:263
  18.4 1.0 %copy-start = (bf16[4,3,2,32,768]{4,3,2,1,0:T(8,128)(2,1)}, bf16[4,3,2,32,768]{4,3,2,1,0:T(8,128)(2,1)S(1)}, u32[]{:S(2)}) copy-start(bf16[4,3,2,32,768]{4,3,2,1,0:T(8,128)(2,1)S(1)} %resample_edge.3) | copy-start | bytes 3538948
  31.4 19.9 %all-to-all-start.1 = ((bf16[4,3,2,32,768]{4,3,2,1,0:T(8,128)(2,1)}), bf16[4,3,2,32,768]{4,3,2,1,0:T(8,128)(2,1)}, u32[]{:S(2)}, u32[]{:S(2)}) async-start(bf16[4,3,2,32,768]{4,3,2,1,0:T(8,128)(2,1)} %copy-done), calls=%async_computation.1 | async-start | bytes 2359296 | tf_op jit(solution)/shard_map/all_to_all | solution.py:257
  37.7 1.0 %copy-start.1 = (bf16[4,3,2,32,768]{4,3,2,1,0:T(8,128)(2,1)}, bf16[4,3,2,32,768]{4,3,2,1,0:T(8,128)(2,1)S(1)}, u32[]{:S(2)}) copy-start(bf16[4,3,2,32,768]{4,3,2,1,0:T(8,128)(2,1)S(1)} %resample_edge.2) | copy-start | bytes 3538948
  38.7 16.1 %copy-start.5 = (s32[60,2]{0,1:T(2,128)S(1)}, s32[60,2]{0,1:T(2,128)}, u32[]{:S(2)}) copy-start(s32[60,2]{0,1:T(2,128)} %param.7) | copy-start | bytes 1444
  51.3 18.3 %all-to-all-start = ((bf16[4,3,2,32,768]{4,3,2,1,0:T(8,128)(2,1)}), bf16[4,3,2,32,768]{4,3,2,1,0:T(8,128)(2,1)S(1)}, u32[]{:S(2)}, u32[]{:S(2)}) async-start(bf16[4,3,2,32,768]{4,3,2,1,0:T(8,128)(2,1)} %copy-done.1), calls=%async_computation | async-start | bytes 2359296 | tf_op jit(solution)/shard_map/all_to_all | solution.py:257

commit v4 on v2

v4 whole, which is shorter than its diff:
```python
import functools

import jax
import jax.numpy as jnp
from jax import lax
from jax.experimental import pallas as pl
from jax.experimental.pallas import tpu as pltpu
from jax.sharding import PartitionSpec as P

LOOK_R = 4
LOOK_C = 16
CHUNK = 32
HALO = 24
TILE = 16
LANES = 128
MIB = 1024 * 1024


def build_bands(first, sources, group, kernel, off, band):
    acq, taps = off.shape[0], kernel.shape[0]
    gains = kernel[...].astype(jnp.float32)
    lane = lax.broadcasted_iota(jnp.int32, gains.shape, 1)
    rows = sum(count for _, count in sources)
    index = lax.broadcasted_iota(jnp.int32, (rows, CHUNK), 0)
    source = jnp.zeros((rows, CHUNK), jnp.int32)
    at = 0
    for begin, count in sources:
        source = jnp.where(index >= at, index + (begin - at), source)
        at += count
    target = first + lax.broadcasted_iota(jnp.int32, (rows, CHUNK), 1)
    base = source - target + (taps // 2 - 1)
    row = lax.broadcasted_iota(jnp.int32, (CHUNK, CHUNK), 0)
    col = lax.broadcasted_iota(jnp.int32, (CHUNK, CHUNK), 1)
    blocks = CHUNK // LOOK_R
    order = jnp.where(col == (row % blocks) * LOOK_R + row // blocks, 1.0, 0.0).astype(jnp.bfloat16)
    for a in range(acq):
        tap = base - off[a : a + 1, first : first + CHUNK]
        total = jnp.zeros((rows, CHUNK), jnp.float32)
        gain = jnp.sum(jnp.where(lane == group[0] * acq + a, gains, 0.0), axis=1, keepdims=True)
        for k in range(taps):
            total = jnp.where(tap == k, gain[k : k + 1, :], total)
        turned = lax.dot_general(
            order, total.astype(jnp.bfloat16), (((1,), (1,)), ((), ())),
            preferred_element_type=jnp.float32,
        )
        band[a] = turned.astype(jnp.bfloat16)


def first_kernel(first, groups, group, kernel, off, slc, *rest):
    outs, (head, tail, slab, band, gains, shifts, sems) = rest[:groups], rest[groups:]
    acq, _, lines, cols = slc.shape
    width = cols // groups

    def columns(s):
        return pl.ds(pl.multiple_of((group[0] ^ s) * width, width), width)

    order = [*range(1, groups), 0]
    small = [
        pltpu.make_async_copy(kernel, gains, sems.at[groups]),
        pltpu.make_async_copy(off, shifts, sems.at[groups + 1]),
    ]
    for copy in small:
        copy.start()
    copies = {}
    for s in order:
        at = columns(s)
        copies[s] = pltpu.make_async_copy(slc.at[:, :, :, at], slab.at[:, :, :, at], sems.at[s])
        copies[s].start()
    for copy in small:
        copy.wait()
    build_bands(first, [(0, lines)], group, gains, shifts, band)
    for s in order:
        copies[s].wait()
        at = columns(s)
        for a in range(acq):
            for x in range(2):
                total = jnp.dot(band[a], slab[a, x, :, at], preferred_element_type=jnp.float32)
                outs[s][a, x] = total.astype(jnp.bfloat16)
    head[...] = slab[:, :, :HALO, :]
    tail[...] = slab[:, :, lines - HALO :, :]


def edge_kernel(first, groups, begin, count, halo_at, group, kernel, off, slab, halo, *rest):
    outs, band = rest[:groups], rest[groups]
    acq, _, _, cols = slab.shape
    width = cols // groups
    build_bands(first, [(begin, count), (halo_at, HALO)], group, kernel, off, band)
    for s in [*range(1, groups), 0]:
        at = pl.ds(pl.multiple_of((group[0] ^ s) * width, width), width)
        for a in range(acq):
            for x in range(2):
                lines = jnp.concatenate(
                    [slab[a, x, begin : begin + count, at], halo[a, x, :, at]], axis=0
                )
                total = jnp.dot(band[a], lines, preferred_element_type=jnp.float32)
                outs[s][a, x] = total.astype(jnp.bfloat16)


SMEM = pl.BlockSpec(memory_space=pltpu.SMEM)
VMEM = pl.BlockSpec(memory_space=pltpu.VMEM)
ANY = pl.BlockSpec(memory_space=pl.ANY)


def resample_cost(acq, cols, rows):
    return pl.CostEstimate(
        flops=2 * acq * 2 * CHUNK * rows * cols,
        bytes_accessed=acq * 2 * (rows + CHUNK) * cols * 2,
        transcendentals=0,
    )


def resample_first(first, group, kernel, offsets, slc, groups):
    acq, _, lines, cols = slc.shape
    piece = pltpu.VMEM((acq, 2, CHUNK, cols // groups), jnp.bfloat16)
    halo = pltpu.VMEM((acq, 2, HALO, cols), jnp.bfloat16)
    slab = pltpu.VMEM(slc.shape, jnp.bfloat16)
    return pl.pallas_call(
        functools.partial(first_kernel, first, groups),
        in_specs=[SMEM, ANY, ANY, ANY],
        out_specs=[VMEM] * (groups + 3),
        out_shape=[piece] * groups + [halo, halo, slab],
        scratch_shapes=[
            pltpu.VMEM((acq, CHUNK, lines), jnp.bfloat16),
            pltpu.VMEM(kernel.shape, kernel.dtype),
            pltpu.VMEM(offsets.shape, offsets.dtype),
            pltpu.SemaphoreType.DMA((groups + 2,)),
        ],
        compiler_params=pltpu.CompilerParams(vmem_limit_bytes=16 * MIB),
        cost_estimate=resample_cost(acq, cols, lines),
        name="resample_first",
    )(group, kernel, offsets, slc)


def resample_edge(first, begin, count, halo_at, group, kernel, offsets, slab, halo, groups):
    acq, _, lines, cols = slab.shape
    piece = pltpu.VMEM((acq, 2, CHUNK, cols // groups), jnp.bfloat16)
    return pl.pallas_call(
        functools.partial(edge_kernel, first, groups, begin, count, halo_at),
        in_specs=[SMEM, VMEM, VMEM, VMEM, VMEM],
        out_specs=[VMEM] * groups,
        out_shape=[piece] * groups,
        scratch_shapes=[pltpu.VMEM((acq, CHUNK, count + HALO), jnp.bfloat16)],
        compiler_params=pltpu.CompilerParams(vmem_limit_bytes=16 * MIB),
        cost_estimate=resample_cost(acq, cols, count + HALO),
        name="resample_edge",
    )(group, kernel, offsets, slab, halo)


def interfere_kernel(groups, place, table, *rest):
    blocks, (out, parts, terms, pooled, flat, inverse, slab, sem) = rest[:groups], rest[-8:]
    acq, _, lines, width = blocks[0].shape
    looks = lines // LOOK_R
    count = table.shape[1]
    windows = width // LOOK_C
    both = 2 * looks
    total_acq = groups * acq
    slots = total_acq * (total_acq - 1) // 2
    tiles = width // LANES

    def pool(tile):
        row = lax.broadcasted_iota(jnp.int32, (2 * LANES, windows), 0)
        window = lax.broadcasted_iota(jnp.int32, (2 * LANES, windows), 1)
        wanted = tile * (LANES // LOOK_C) + (row % LANES) // LOOK_C
        return jnp.where(wanted == window, 1.0, 0.0).astype(jnp.bfloat16)

    def put(row, field):
        first = field.astype(jnp.bfloat16)
        terms[row : row + both, :LANES] = first
        terms[row : row + both, LANES:] = (field - first.astype(jnp.float32)).astype(jnp.bfloat16)

    def settle(tile):
        pooled[...] += jnp.dot(terms[...], pool(tile), preferred_element_type=jnp.float32)

    def unpack(tile):
        at = pl.ds(pl.multiple_of(tile * LANES, LANES), LANES)
        for r, block in enumerate(blocks):
            for a in range(acq):
                real = block[a, 0, :, at].astype(jnp.float32) * 0.125
                imag = block[a, 1, :, at].astype(jnp.float32) * 0.125
                parts[r * acq + a, 0] = real
                parts[r * acq + a, 1] = imag
                parts[r * acq + a, 2] = real + imag
                parts[r * acq + a, 3] = real - imag

    def cross(pairs):
        sums = {pair: [0.0, 0.0, 0.0] for pair in pairs}
        for j in range(LOOK_R):
            at = slice(j * looks, (j + 1) * looks)
            left = {i: [parts[i, c, at, :] for c in (2, 0, 1)] for i in sorted({i for i, _ in pairs})}
            right = {i: [parts[i, c, at, :] for c in (0, 2, 3)] for i in sorted({i for _, i in pairs})}
            for pair in pairs:
                for t in range(3):
                    sums[pair][t] = sums[pair][t] + left[pair[0]][t] * right[pair[1]][t]
        for i, k in pairs:
            one, two, three = sums[i, k]
            slot = i * (2 * total_acq - i - 1) // 2 + k - i - 1
            put(slot * both, jnp.concatenate([one - three, one - two], axis=0))

    def powers(members):
        fields = []
        for i in members:
            total = 0.0
            for j in range(LOOK_R):
                for c in range(2):
                    value = parts[i, c, j * looks : (j + 1) * looks, :]
                    total = total + value * value
            fields.append(total)
        put(slots * both + members[0] * looks, jnp.concatenate(fields, axis=0))

    def work(tile):
        unpack(tile)
        for r in range(groups):
            for q in range(r, groups):
                cross(
                    [
                        (i, k)
                        for i in range(r * acq, (r + 1) * acq)
                        for k in range(q * acq, (q + 1) * acq)
                        if i < k
                    ]
                )
        for i in range(0, total_acq, 2):
            powers((i, i + 1))

    def turn(tile, carry):
        settle(tile - 1)
        work(tile)
        return carry

    pooled[...] = jnp.zeros(pooled.shape, jnp.float32)
    work(0)
    lax.fori_loop(1, tiles, turn, 0)
    settle(tiles - 1)

    inverse[...] = lax.rsqrt(pooled[slots * both :, :] + 1e-6)

    def select(p, carry):
        at = pl.multiple_of(table[0, p] * both, both)
        m = pl.multiple_of(table[1, p] * looks, looks)
        s = pl.multiple_of(table[2, p] * looks, looks)
        scale = inverse[pl.ds(m, looks), :] * inverse[pl.ds(s, looks), :]
        turned = scale * table[3, p].astype(jnp.float32)
        value = pooled[pl.ds(at, both), :] * jnp.concatenate([scale, turned], axis=0)
        flat[pl.ds(pl.multiple_of(p * both, both), both), :] = value
        return carry

    lax.fori_loop(0, count, select, 0, unroll=max(b for b in range(1, 7) if count % b == 0))
    for x in range(2):
        for g in range(looks):
            slab[x, g] = flat[pl.ds(x * looks + g, count, stride=both), :].T
    copy = pltpu.make_async_copy(slab, out.at[:, pl.ds(place * looks, looks)], sem)
    copy.start()
    copy.wait()


def interfere(place, chunks, table, blocks, before):
    groups = len(blocks)
    acq, _, lines, width = blocks[0].shape
    looks, windows, count = lines // LOOK_R, width // LOOK_C, table.shape[1]
    total = groups * acq
    rows = (total * (total - 1) + total) * looks
    extra = [] if before is None else [before]
    return pl.pallas_call(
        functools.partial(interfere_kernel, groups, place),
        in_specs=[SMEM] + [VMEM] * groups + [ANY] * len(extra),
        out_specs=ANY,
        out_shape=pltpu.HBM((2, chunks * looks, windows, count), jnp.float32),
        scratch_shapes=[
            pltpu.VMEM((total, 4, lines, LANES), jnp.float32),
            pltpu.VMEM((rows, 2 * LANES), jnp.bfloat16),
            pltpu.VMEM((rows, windows), jnp.float32),
            pltpu.VMEM((count * 2 * looks, windows), jnp.float32),
            pltpu.VMEM((total * looks, windows), jnp.float32),
            pltpu.VMEM((2, looks, windows, count), jnp.float32),
            pltpu.SemaphoreType.DMA,
        ],
        input_output_aliases={} if before is None else {1 + groups: 0},
        compiler_params=pltpu.CompilerParams(vmem_limit_bytes=16 * MIB),
        cost_estimate=pl.CostEstimate(
            flops=count * 8 * lines * width,
            bytes_accessed=groups * acq * 2 * lines * width * 2,
            transcendentals=0,
        ),
        name="interfere",
    )(table, *blocks, *extra)


def pair_table(pairs, groups, acq, mine):
    total = groups * acq
    near = ((pairs // acq) ^ mine) * acq + pairs % acq
    m, s = near[:, 0], near[:, 1]
    low, high = jnp.minimum(m, s), jnp.maximum(m, s)
    slot = low * (2 * total - low - 1) // 2 + high - low - 1
    return jnp.stack([slot, m, s, jnp.where(m < s, 1, -1)]).astype(jnp.int32)


def local(slc, offsets, weights, pairs):
    acq, _, lines, cols = slc.shape
    groups = lax.axis_size("acq")
    size = lax.axis_size("pix")
    group = jnp.reshape(lax.axis_index("acq"), (1,)).astype(jnp.int32)
    kernel = weights.T
    table = pair_table(pairs, groups, acq, group[0])
    chunks = lines // CHUNK
    reach = CHUNK + TILE * 2

    up = [(i, i + 1) for i in range(size - 1)]
    down = [(j, i) for i, j in up]

    def send(blocks):
        moved = [blocks[0]]
        for s in range(1, groups):
            moved.append(lax.ppermute(blocks[s], "acq", [(i, i ^ s) for i in range(groups)]))
        return moved

    *blocks, head, tail, slab = resample_first(
        CHUNK, group, *[pltpu.with_memory_space_constraint(t, pltpu.HBM) for t in (kernel, offsets, slc)], groups
    )
    above = lax.ppermute(tail, "pix", up)
    below = lax.ppermute(head, "pix", down)
    middle = send(blocks)
    top = send(
        resample_edge(0, 0, reach, -HALO, group, kernel, offsets, slab, above, groups)
    )
    late = resample_edge(
        lines - CHUNK, lines - reach, reach, lines, group, kernel, offsets, slab, below, groups
    )
    late, middle = lax.optimization_barrier((late, middle))
    bottom = send(late)
    result = None
    for place, moved in ((1, middle), (0, top), (2, bottom)):
        result = interfere(place, chunks, table, moved, result)
    return jnp.transpose(result, (0, 3, 1, 2))


def solution(mesh):
    placed = (P("acq", None, "pix", None), P("acq", "pix"), P(), P())
    return jax.shard_map(
        local, mesh=mesh, in_specs=placed, out_specs=P(None, None, "pix", "acq"), check_vma=False
    )
```

time: 57.7 us -> 63.3 us (1.097)
  the two profiles are of different devices: /device:TPU:9 before, /device:TPU:16 now
where the time goes in v4:
time: 63.3 us; the launch traced here: 63.2 us
  waiting for transfers between devices  25.6 us (40%)
  Pallas kernels  20.1 us (32%)
  starting transfers between devices  17.3 us (27%)
    ppermute x9, waiting for transfers between devices, send(): lax.ppermute(blocks[s], 'acq', [(i, i ^ s) for i in range(groups)])  20.3 us
    pallas_call x3, Pallas kernels, interfere(): pl.pallas_call(functools.partial(interfere_kernel, groups, place), in_spe...  16 us
    ppermute x9, starting transfers between devices, send(): lax.ppermute(blocks[s], 'acq', [(i, i ^ s) for i in range(groups)])  11.7 us
    ppermute x1, waiting for transfers between devices, local(): above = lax.ppermute(tail, 'pix', up)  5.23 us
    ppermute x1, starting transfers between devices, local(): below = lax.ppermute(head, 'pix', down)  3.64 us
    pallas_call x1, Pallas kernels, resample_first(): pl.pallas_call(functools.partial(first_kernel, first, groups), in_specs=[...  2.46 us
    ppermute x1, starting transfers between devices, local(): above = lax.ppermute(tail, 'pix', up)  1.92 us
    pallas_call x2, Pallas kernels, resample_edge(): pl.pallas_call(functools.partial(edge_kernel, first, groups, begin, count...  1.68 us
  transfers between devices with their start and end apart: 11, of which 5 were waited for; matrix products, arithmetic and copies ran while one was open for 0% of the time, Pallas kernels for 20%

profile of v4, /device:TPU:16, one launch (start us, length us, event | category | flops | bytes accessed | tf_op | source)
XLA Modules:
  0.0 63.2 jit_solution(1897643288829224116)
XLA Ops:
  0.0 0.0 copy-start
  0.0 0.0 copy-start.1
  0.0 2.5 %resample_first.1 = (bf16[3,2,32,768]{3,2,1,0:T(8,128)(2,1)S(1)}, bf16[3,2,32,768]{3,2,1,0:T(8,128)(2,1)S(1)}, bf16[3,2,32,768]{3,2,1,0:T(8,128)(2,1)S(1)}, bf16...) custom-call(s32[1]{0:T(128)} %bitcast.2.group, ...), custom_call_target="tpu_custom_call" | custom-call | flops 113246208 | bytes 4718592 | tf_op jit(solution)/shard_map/resample_first/pallas_call | solution.py:117
  2.5 1.9 %collective-permute-start.7 = (bf16[3,2,24,3072]{3,2,1,0:T(8,128)(2,1)S(1)}, bf16[3,2,24,3072]{3,2,1,0:T(8,128)(2,1)S(1)}, u32[]{:S(2)}, u32[]{:S(2)}) collective-permute-start(bf16[3,2,24,3072]{3,2,1,0:T(8,128)(2,1)S(1)} %get-tuple-element.42), channel_id=1, source_target_pairs={{0,1},{1,2},{2,3},{3,4},{4,5},{5,6},{6,7},{8,9},{9,10},{10,11},{11... | collective-permute-start | bytes 2654216 | tf_op jit(solution)/shard_map/ppermute | solution.py:319
  4.4 3.6 %collective-permute-start = (bf16[3,2,24,3072]{3,2,1,0:T(8,128)(2,1)S(1)}, bf16[3,2,24,3072]{3,2,1,0:T(8,128)(2,1)S(1)}, u32[]{:S(2)}, u32[]{:S(2)}) collective-permute-start(bf16[3,2,24,3072]{3,2,1,0:T(8,128)(2,1)S(1)} %get-tuple-element.29), channel_id=1, source_target_pairs={{1,0},{2,1},{3,2},{4,3},{5,4},{6,5},{7,6},{9,8},{10,9},{11,10},{12... | collective-permute-start | bytes 2654216 | tf_op jit(solution)/shard_map/ppermute | solution.py:320
  8.1 1.6 %collective-permute-start.1 = (bf16[3,2,32,768]{3,2,1,0:T(8,128)(2,1)S(1)}, bf16[3,2,32,768]{3,2,1,0:T(8,128)(2,1)S(1)}, u32[]{:S(2)}, u32[]{:S(2)}) collective-permute-start(bf16[3,2,32,768]{3,2,1,0:T(8,128)(2,1)S(1)} %get-tuple-element.35), channel_id=1, source_target_pairs={{0,8},{8,0},{16,24},{24,16},{1,9},{9,1},{17,25},{25,17},{2,10},{10... | collective-permute-start | bytes 884744 | tf_op jit(solution)/shard_map/ppermute | solution.py:313
  9.6 1.5 %collective-permute-start.2 = (bf16[3,2,32,768]{3,2,1,0:T(8,128)(2,1)S(1)}, bf16[3,2,32,768]{3,2,1,0:T(8,128)(2,1)S(1)}, u32[]{:S(2)}, u32[]{:S(2)}) collective-permute-start(bf16[3,2,32,768]{3,2,1,0:T(8,128)(2,1)S(1)} %get-tuple-element.36), channel_id=1, source_target_pairs={{0,16},{8,24},{16,0},{24,8},{1,17},{9,25},{17,1},{25,9},{2,18},{10... | collective-permute-start | bytes 884744 | tf_op jit(solution)/shard_map/ppermute | solution.py:313
  11.1 0.5 collective-permute-start.3
  11.6 5.2 %collective-permute-done.7.halo = bf16[3,2,24,3072]{3,2,1,0:T(8,128)(2,1)S(1)} collective-permute-done((bf16[3,2,24,3072]{3,2,1,0:T(8,128)(2,1)S(1)}, bf16[3,2,24,3072]{3,2,1,0:T(8,128)(2,1)S(1)}, u32[]{:S(2)}, u32[]{:S(2)}) %collective-permute-start.7) | collective-permute-done | bytes 884768 | tf_op jit(solution)/shard_map/ppermute | solution.py:319
  16.8 0.0 copy-done
  16.8 0.0 copy-done.1
  16.8 0.0 copy-start.2
  16.8 0.8 %resample_edge.3 = (bf16[3,2,32,768]{3,2,1,0:T(8,128)(2,1)S(1)}, bf16[3,2,32,768]{3,2,1,0:T(8,128)(2,1)S(1)}, bf16[3,2,32,768]{3,2,1,0:T(8,128)(2,1)S(1)}, bf16[3,2,32,768]{3,2,1,0:T(8,128)(2,1)S(1)}) custom-call(s32[1]{0:T(128)} %bitcast.2.group, bf16[8,12]{1,0:T(8,128)(2,1)S(1)} %bitcast.16, s32[3,96]{1,0:T(4,128)S(1)} %copy-done.1, ...), custom_call_target="tpu_custom_call" | custom-call | flops 103809024 | bytes 4423680 | tf_op jit(solution)/shard_map/resample_edge/pallas_call | solution.py:137
  17.7 1.6 %collective-permute-start.8 = (bf16[3,2,32,768]{3,2,1,0:T(8,128)(2,1)S(1)}, bf16[3,2,32,768]{3,2,1,0:T(8,128)(2,1)S(1)}, u32[]{:S(2)}, u32[]{:S(2)}) collective-permute-start(bf16[3,2,32,768]{3,2,1,0:T(8,128)(2,1)S(1)} %get-tuple-element.44), channel_id=1, source_target_pairs={{0,8},{8,0},{16,24},{24,16},{1,9},{9,1},{17,25},{25,17},{2,10},{10... | collective-permute-start | bytes 884744 | tf_op jit(solution)/shard_map/ppermute | solution.py:313
  19.3 0.0 copy-done.2
  19.3 0.0 collective-permute-done.halo
  19.3 0.8 %resample_edge.2 = (bf16[3,2,32,768]{3,2,1,0:T(8,128)(2,1)S(1)}, bf16[3,2,32,768]{3,2,1,0:T(8,128)(2,1)S(1)}, bf16[3,2,32,768]{3,2,1,0:T(8,128)(2,1)S(1)}, bf16[3,2,32,768]{3,2,1,0:T(8,128)(2,1)S(1)}) custom-call(s32[1]{0:T(128)} %bitcast.2.group, bf16[8,12]{1,0:T(8,128)(2,1)S(1)} %bitcast.17, s32[3,96]{1,0:T(4,128)S(1)} %copy-done.1, ...), custom_call_target="tpu_custom_call" | custom-call | flops 103809024 | bytes 4423680 | tf_op jit(solution)/shard_map/resample_edge/pallas_call | solution.py:137
  20.1 0.0 collective-permute-done.1.rest_1_
  20.2 3.6 %collective-permute-done.2.rest_2_ = bf16[3,2,32,768]{3,2,1,0:T(8,128)(2,1)S(1)} collective-permute-done((bf16[3,2,32,768]{3,2,1,0:T(8,128)(2,1)S(1)}, bf16[3,2,32,768]{3,2,1,0:T(8,128)(2,1)S(1)}, u32[]{:S(2)}, u32[]{:S(2)}) %collective-permute-start.2) | collective-permute-done | bytes 294944 | tf_op jit(solution)/shard_map/ppermute | solution.py:313
  23.7 1.6 %collective-permute-done.3.rest_3_ = bf16[3,2,32,768]{3,2,1,0:T(8,128)(2,1)S(1)} collective-permute-done((bf16[3,2,32,768]{3,2,1,0:T(8,128)(2,1)S(1)}, bf16[3,2,32,768]{3,2,1,0:T(8,128)(2,1)S(1)}, u32[]{:S(2)}, u32[]{:S(2)}) %collective-permute-start.3) | collective-permute-done | bytes 294944 | tf_op jit(solution)/shard_map/ppermute | solution.py:313
  25.3 1.4 %collective-permute-start.4 = (bf16[3,2,32,768]{3,2,1,0:T(8,128)(2,1)S(1)}, bf16[3,2,32,768]{3,2,1,0:T(8,128)(2,1)S(1)}, u32[]{:S(2)}, u32[]{:S(2)}) collective-permute-start(bf16[3,2,32,768]{3,2,1,0:T(8,128)(2,1)S(1)} %get-tuple-element.39), channel_id=1, source_target_pairs={{0,8},{8,0},{16,24},{24,16},{1,9},{9,1},{17,25},{25,17},{2,10},{10... | collective-permute-start | bytes 884744 | tf_op jit(solution)/shard_map/ppermute | solution.py:313
  26.8 0.6 collective-permute-start.5
  27.3 1.5 %collective-permute-start.6 = (bf16[3,2,32,768]{3,2,1,0:T(8,128)(2,1)S(1)}, bf16[3,2,32,768]{3,2,1,0:T(8,128)(2,1)S(1)}, u32[]{:S(2)}, u32[]{:S(2)}) collective-permute-start(bf16[3,2,32,768]{3,2,1,0:T(8,128)(2,1)S(1)} %get-tuple-element.41), channel_id=1, source_target_pairs={{0,24},{8,16},{16,8},{24,0},{1,25},{9,17},{17,9},{25,1},{2,26},{10... | collective-permute-start | bytes 884744 | tf_op jit(solution)/shard_map/ppermute | solution.py:313
  28.8 0.7 %collective-permute-start.9 = (bf16[3,2,32,768]{3,2,1,0:T(8,128)(2,1)S(1)}, bf16[3,2,32,768]{3,2,1,0:T(8,128)(2,1)S(1)}, u32[]{:S(2)}, u32[]{:S(2)}) collective-permute-start(bf16[3,2,32,768]{3,2,1,0:T(8,128)(2,1)S(1)} %get-tuple-element.45), channel_id=1, source_target_pairs={{0,16},{8,24},{16,0},{24,8},{1,17},{9,25},{17,1},{25,9},{2,18},{10... | collective-permute-start | bytes 884744 | tf_op jit(solution)/shard_map/ppermute | solution.py:313
  29.5 1.1 %collective-permute-done.8.rest_1_ = bf16[3,2,32,768]{3,2,1,0:T(8,128)(2,1)S(1)} collective-permute-done((bf16[3,2,32,768]{3,2,1,0:T(8,128)(2,1)S(1)}, bf16[3,2,32,768]{3,2,1,0:T(8,128)(2,1)S(1)}, u32[]{:S(2)}, u32[]{:S(2)}) %collective-permute-start.8) | collective-permute-done | bytes 294944 | tf_op jit(solution)/shard_map/ppermute | solution.py:313
  30.7 2.4 %collective-permute-start.10 = (bf16[3,2,32,768]{3,2,1,0:T(8,128)(2,1)S(1)}, bf16[3,2,32,768]{3,2,1,0:T(8,128)(2,1)S(1)}, u32[]{:S(2)}, u32[]{:S(2)}) collective-permute-start(bf16[3,2,32,768]{3,2,1,0:T(8,128)(2,1)S(1)} %get-tuple-element.46), channel_id=1, source_target_pairs={{0,24},{8,16},{16,8},{24,0},{1,25},{9,17},{17,9},{25,1},{2,26},{10... | collective-permute-start | bytes 884744 | tf_op jit(solution)/shard_map/ppermute | solution.py:313
  33.1 5.3 %interfere.3.rest_4_ = f32[2,24,48,60]{3,2,1,0:T(8,128)} custom-call(s32[4,60]{1,0:T(4,128)S(1)} %pad_add_fusion.table, bf16[3,2,32,768]{3,2,1,0:T(8,128)(2,1)S(1)} %get-tuple-element.47.rest_0_, bf16[3,2,32,768]{3,2,1,0:T(8,128)(2,1)S(1)} %collective-permute-done.1.rest_1_, bf16[3,2,32,768]{3,2,1,0:T(8,128)(2,1)S(1)} %collective-permute-done.2.rest_2_, ...), custom_call_target="tpu_custom_call" | custom-call | flops 11796480 | bytes 1179648 | tf_op jit(solution)/shard_map/interfere/pallas_call | solution.py:263
  38.4 14.0 %collective-permute-done.9.rest_2_ = bf16[3,2,32,768]{3,2,1,0:T(8,128)(2,1)S(1)} collective-permute-done((bf16[3,2,32,768]{3,2,1,0:T(8,128)(2,1)S(1)}, bf16[3,2,32,768]{3,2,1,0:T(8,128)(2,1)S(1)}, u32[]{:S(2)}, u32[]{:S(2)}) %collective-permute-start.9) | collective-permute-done | bytes 294944 | tf_op jit(solution)/shard_map/ppermute | solution.py:313
  52.5 0.0 collective-permute-done.10.rest_3_
  52.5 5.3 %interfere.4.rest_4_ = f32[2,24,48,60]{3,2,1,0:T(8,128)} custom-call(s32[4,60]{1,0:T(4,128)S(1)} %pad_add_fusion.table, bf16[3,2,32,768]{3,2,1,0:T(8,128)(2,1)S(1)} %get-tuple-element.43.rest_0_, bf16[3,2,32,768]{3,2,1,0:T(8,128)(2,1)S(1)} %collective-permute-done.8.rest_1_, ...), custom_call_target="tpu_custom_call", output_to_operand_aliasing={{}: (5, {})} | custom-call | flops 11796480 | bytes 1179648 | tf_op jit(solution)/shard_map/interfere/pallas_call | solution.py:263
  57.8 0.0 collective-permute-done.4.rest_1_
  57.8 0.0 collective-permute-done.5.rest_2_
  57.8 0.0 collective-permute-done.6.rest_3_
  57.8 5.3 %interfere.5 = f32[2,24,48,60]{3,2,1,0:T(8,128)} custom-call(s32[4,60]{1,0:T(4,128)S(1)} %pad_add_fusion.table, bf16[3,2,32,768]{3,2,1,0:T(8,128)(2,1)S(1)} %get-tuple-element.38.rest_0_, bf16[3,2,32,768]{3,2,1,0:T(8,128)(2,1)S(1)} %collective-permute-done.4.rest_1_, ...), custom_call_target="tpu_custom_call", output_to_operand_aliasing={{}: (5, {})} | custom-call | flops 11796480 | bytes 1179648 | tf_op jit(solution)/shard_map/interfere/pallas_call | solution.py:263
  (4 shorter events, 0.1 us)
Async XLA Ops:
  0.0 16.8 %copy-start = (bf16[12,8]{0,1:T(8,128)(2,1)S(1)}, bf16[12,8]{0,1:T(8,128)(2,1)}, u32[]{:S(2)}) copy-start(bf16[12,8]{0,1:T(8,128)(2,1)} %param.6) | copy-start | bytes 580
  0.0 16.8 %copy-start.1 = (s32[3,96]{1,0:T(4,128)S(1)}, s32[3,96]{1,0:T(4,128)}, u32[]{:S(2)}) copy-start(s32[3,96]{1,0:T(4,128)} %off.5) | copy-start | bytes 3460
  2.5 14.4 %collective-permute-start.7 = (bf16[3,2,24,3072]{3,2,1,0:T(8,128)(2,1)S(1)}, bf16[3,2,24,3072]{3,2,1,0:T(8,128)(2,1)S(1)}, u32[]{:S(2)}, u32[]{:S(2)}) collective-permute-start(bf16[3,2,24,3072]{3,2,1,0:T(8,128)(2,1)S(1)} %get-tuple-element.42), channel_id=1, source_target_pairs={{0,1},{1,2},{2,3},{3,4},{4,5},{5,6},{6,7},{8,9},{9,10},{10,11},{11... | collective-permute-start | bytes 2654216 | tf_op jit(solution)/shard_map/ppermute | solution.py:319
  4.4 14.9 %collective-permute-start = (bf16[3,2,24,3072]{3,2,1,0:T(8,128)(2,1)S(1)}, bf16[3,2,24,3072]{3,2,1,0:T(8,128)(2,1)S(1)}, u32[]{:S(2)}, u32[]{:S(2)}) collective-permute-start(bf16[3,2,24,3072]{3,2,1,0:T(8,128)(2,1)S(1)} %get-tuple-element.29), channel_id=1, source_target_pairs={{1,0},{2,1},{3,2},{4,3},{5,4},{6,5},{7,6},{9,8},{10,9},{11,10},{12... | collective-permute-start | bytes 2654216 | tf_op jit(solution)/shard_map/ppermute | solution.py:320
  8.1 12.1 %collective-permute-start.1 = (bf16[3,2,32,768]{3,2,1,0:T(8,128)(2,1)S(1)}, bf16[3,2,32,768]{3,2,1,0:T(8,128)(2,1)S(1)}, u32[]{:S(2)}, u32[]{:S(2)}) collective-permute-start(bf16[3,2,32,768]{3,2,1,0:T(8,128)(2,1)S(1)} %get-tuple-element.35), channel_id=1, source_target_pairs={{0,8},{8,0},{16,24},{24,16},{1,9},{9,1},{17,25},{25,17},{2,10},{10... | collective-permute-start | bytes 884744 | tf_op jit(solution)/shard_map/ppermute | solution.py:313
  9.6 14.1 %collective-permute-start.2 = (bf16[3,2,32,768]{3,2,1,0:T(8,128)(2,1)S(1)}, bf16[3,2,32,768]{3,2,1,0:T(8,128)(2,1)S(1)}, u32[]{:S(2)}, u32[]{:S(2)}) collective-permute-start(bf16[3,2,32,768]{3,2,1,0:T(8,128)(2,1)S(1)} %get-tuple-element.36), channel_id=1, source_target_pairs={{0,16},{8,24},{16,0},{24,8},{1,17},{9,25},{17,1},{25,9},{2,18},{10... | collective-permute-start | bytes 884744 | tf_op jit(solution)/shard_map/ppermute | solution.py:313
  11.1 14.2 %collective-permute-start.3 = (bf16[3,2,32,768]{3,2,1,0:T(8,128)(2,1)S(1)}, bf16[3,2,32,768]{3,2,1,0:T(8,128)(2,1)S(1)}, u32[]{:S(2)}, u32[]{:S(2)}) collective-permute-start(bf16[3,2,32,768]{3,2,1,0:T(8,128)(2,1)S(1)} %get-tuple-element.37), channel_id=1, source_target_pairs={{0,24},{8,16},{16,8},{24,0},{1,25},{9,17},{17,9},{25,1},{2,26},{10... | collective-permute-start | bytes 884744 | tf_op jit(solution)/shard_map/ppermute | solution.py:313
  16.8 2.4 %copy-start.2 = (s32[60,2]{0,1:T(2,128)S(1)}, s32[60,2]{0,1:T(2,128)}, u32[]{:S(2)}) copy-start(s32[60,2]{0,1:T(2,128)} %param.7) | copy-start | bytes 1444
  17.7 13.0 %collective-permute-start.8 = (bf16[3,2,32,768]{3,2,1,0:T(8,128)(2,1)S(1)}, bf16[3,2,32,768]{3,2,1,0:T(8,128)(2,1)S(1)}, u32[]{:S(2)}, u32[]{:S(2)}) collective-permute-start(bf16[3,2,32,768]{3,2,1,0:T(8,128)(2,1)S(1)} %get-tuple-element.44), channel_id=1, source_target_pairs={{0,8},{8,0},{16,24},{24,16},{1,9},{9,1},{17,25},{25,17},{2,10},{10... | collective-permute-start | bytes 884744 | tf_op jit(solution)/shard_map/ppermute | solution.py:313
  25.3 32.5 %collective-permute-start.4 = (bf16[3,2,32,768]{3,2,1,0:T(8,128)(2,1)S(1)}, bf16[3,2,32,768]{3,2,1,0:T(8,128)(2,1)S(1)}, u32[]{:S(2)}, u32[]{:S(2)}) collective-permute-start(bf16[3,2,32,768]{3,2,1,0:T(8,128)(2,1)S(1)} %get-tuple-element.39), channel_id=1, source_target_pairs={{0,8},{8,0},{16,24},{24,16},{1,9},{9,1},{17,25},{25,17},{2,10},{10... | collective-permute-start | bytes 884744 | tf_op jit(solution)/shard_map/ppermute | solution.py:313
  26.8 31.0 %collective-permute-start.5 = (bf16[3,2,32,768]{3,2,1,0:T(8,128)(2,1)S(1)}, bf16[3,2,32,768]{3,2,1,0:T(8,128)(2,1)S(1)}, u32[]{:S(2)}, u32[]{:S(2)}) collective-permute-start(bf16[3,2,32,768]{3,2,1,0:T(8,128)(2,1)S(1)} %get-tuple-element.40), channel_id=1, source_target_pairs={{0,16},{8,24},{16,0},{24,8},{1,17},{9,25},{17,1},{25,9},{2,18},{10... | collective-permute-start | bytes 884744 | tf_op jit(solution)/shard_map/ppermute | solution.py:313
  27.3 30.5 %collective-permute-start.6 = (bf16[3,2,32,768]{3,2,1,0:T(8,128)(2,1)S(1)}, bf16[3,2,32,768]{3,2,1,0:T(8,128)(2,1)S(1)}, u32[]{:S(2)}, u32[]{:S(2)}) collective-permute-start(bf16[3,2,32,768]{3,2,1,0:T(8,128)(2,1)S(1)} %get-tuple-element.41), channel_id=1, source_target_pairs={{0,24},{8,16},{16,8},{24,0},{1,25},{9,17},{17,9},{25,1},{2,26},{10... | collective-permute-start | bytes 884744 | tf_op jit(solution)/shard_map/ppermute | solution.py:313
  28.8 23.6 %collective-permute-start.9 = (bf16[3,2,32,768]{3,2,1,0:T(8,128)(2,1)S(1)}, bf16[3,2,32,768]{3,2,1,0:T(8,128)(2,1)S(1)}, u32[]{:S(2)}, u32[]{:S(2)}) collective-permute-start(bf16[3,2,32,768]{3,2,1,0:T(8,128)(2,1)S(1)} %get-tuple-element.45), channel_id=1, source_target_pairs={{0,16},{8,24},{16,0},{24,8},{1,17},{9,25},{17,1},{25,9},{2,18},{10... | collective-permute-start | bytes 884744 | tf_op jit(solution)/shard_map/ppermute | solution.py:313
  30.7 21.8 %collective-permute-start.10 = (bf16[3,2,32,768]{3,2,1,0:T(8,128)(2,1)S(1)}, bf16[3,2,32,768]{3,2,1,0:T(8,128)(2,1)S(1)}, u32[]{:S(2)}, u32[]{:S(2)}) collective-permute-start(bf16[3,2,32,768]{3,2,1,0:T(8,128)(2,1)S(1)} %get-tuple-element.46), channel_id=1, source_target_pairs={{0,24},{8,16},{16,8},{24,0},{1,25},{9,17},{17,9},{25,1},{2,26},{10... | collective-permute-start | bytes 884744 | tf_op jit(solution)/shard_map/ppermute | solution.py:313

commit v5 on v4

--- a/solution.py
+++ b/solution.py
@@ -147,29 +147,20 @@
 
 
 def interfere_kernel(groups, place, table, *rest):
-    blocks, (out, parts, terms, pooled, flat, inverse, slab, sem) = rest[:groups], rest[-8:]
+    blocks, (out, parts, halves, pooled, flat, inverse, turned, slab, sem) = rest[:groups], rest[-9:]
     acq, _, lines, width = blocks[0].shape
     looks = lines // LOOK_R
     count = table.shape[1]
-    windows = width // LOOK_C
-    both = 2 * looks
-    total_acq = groups * acq
-    slots = total_acq * (total_acq - 1) // 2
+    total = groups * acq
+    slots = total * (total - 1) // 2
     tiles = width // LANES
-
-    def pool(tile):
-        row = lax.broadcasted_iota(jnp.int32, (2 * LANES, windows), 0)
-        window = lax.broadcasted_iota(jnp.int32, (2 * LANES, windows), 1)
-        wanted = tile * (LANES // LOOK_C) + (row % LANES) // LOOK_C
-        return jnp.where(wanted == window, 1.0, 0.0).astype(jnp.bfloat16)
-
-    def put(row, field):
-        first = field.astype(jnp.bfloat16)
-        terms[row : row + both, :LANES] = first
-        terms[row : row + both, LANES:] = (field - first.astype(jnp.float32)).astype(jnp.bfloat16)
-
-    def settle(tile):
-        pooled[...] += jnp.dot(terms[...], pool(tile), preferred_element_type=jnp.float32)
+    lane = lax.broadcasted_iota(jnp.int32, (looks, LANES), 1)
+    steps = [LOOK_C >> (level + 1) for level in range(LOOK_C.bit_length() - 1)]
+
+    def merge(one, two, step):
+        left = one + pltpu.roll(one, LANES - step, 1)
+        right = two + pltpu.roll(two, step, 1)
+        return jnp.where((lane & step) == 0, left, right)
 
     def unpack(tile):
         at = pl.ds(pl.multiple_of(tile * LANES, LANES), LANES)
@@ -182,7 +173,7 @@
                 parts[r * acq + a, 2] = real + imag
                 parts[r * acq + a, 3] = real - imag
 
-    def cross(pairs):
+    def cross(tile, pairs):
         sums = {pair: [0.0, 0.0, 0.0] for pair in pairs}
         for j in range(LOOK_R):
             at = slice(j * looks, (j + 1) * looks)
@@ -193,61 +184,63 @@
                     sums[pair][t] = sums[pair][t] + left[pair[0]][t] * right[pair[1]][t]
         for i, k in pairs:
             one, two, three = sums[i, k]
-            slot = i * (2 * total_acq - i - 1) // 2 + k - i - 1
-            put(slot * both, jnp.concatenate([one - three, one - two], axis=0))
-
-    def powers(members):
-        fields = []
-        for i in members:
-            total = 0.0
-            for j in range(LOOK_R):
-                for c in range(2):
-                    value = parts[i, c, j * looks : (j + 1) * looks, :]
-                    total = total + value * value
-            fields.append(total)
-        put(slots * both + members[0] * looks, jnp.concatenate(fields, axis=0))
-
-    def work(tile):
+            slot = i * (2 * total - i - 1) // 2 + k - i - 1
+            halves[tile, slot] = merge(one - three, one - two, steps[0])
+
+    def power(tile, i):
+        field = 0.0
+        for j in range(LOOK_R):
+            for c in range(2):
+                value = parts[i, c, j * looks : (j + 1) * looks, :]
+                field = field + value * value
+        halves[tile, slots + i] = merge(field, field, steps[0])
+
+    def work(tile, carry):
         unpack(tile)
         for r in range(groups):
             for q in range(r, groups):
-                cross(
-                    [
-                        (i, k)
-                        for i in range(r * acq, (r + 1) * acq)
-                        for k in range(q * acq, (q + 1) * acq)
-                        if i < k
-                    ]
-                )
-        for i in range(0, total_acq, 2):
-            powers((i, i + 1))
-
-    def turn(tile, carry):
-        settle(tile - 1)
-        work(tile)
+                first = range(r * acq, (r + 1) * acq)
+                second = range(q * acq, (q + 1) * acq)
+                cross(tile, [(i, k) for i in first for k in second if i < k])
+        for i in range(total):
+            power(tile, i)
         return carry
 
-    pooled[...] = jnp.zeros(pooled.shape, jnp.float32)
-    work(0)
-    lax.fori_loop(1, tiles, turn, 0)
-    settle(tiles - 1)
-
-    inverse[...] = lax.rsqrt(pooled[slots * both :, :] + 1e-6)
+    def fold(slot):
+        fields = [halves[tile, slot] for tile in range(tiles)]
+        for step in steps[1:]:
+            fields = [
+                merge(fields[i], fields[min(i + 1, len(fields) - 1)], step)
+                for i in range(0, len(fields), 2)
+            ]
+        return fields[0]
+
+    def fold_slots(b, carry):
+        for u in range(acq):
+            pooled[b * acq + u] = fold(b * acq + u)
+        return carry
+
+    lax.fori_loop(0, tiles, work, 0)
+    for i in range(total):
+        inverse[i] = lax.rsqrt(fold(slots + i) + 1e-6)
+    lax.fori_loop(0, slots // acq, fold_slots, 0)
 
     def select(p, carry):
-        at = pl.multiple_of(table[0, p] * both, both)
-        m = pl.multiple_of(table[1, p] * looks, looks)
-        s = pl.multiple_of(table[2, p] * looks, looks)
-        scale = inverse[pl.ds(m, looks), :] * inverse[pl.ds(s, looks), :]
-        turned = scale * table[3, p].astype(jnp.float32)
-        value = pooled[pl.ds(at, both), :] * jnp.concatenate([scale, turned], axis=0)
-        flat[pl.ds(pl.multiple_of(p * both, both), both), :] = value
+        sign = table[3, p].astype(jnp.float32)
+        scale = inverse[table[1, p]] * inverse[table[2, p]]
+        value = pooled[table[0, p]] * scale
+        at = pl.multiple_of(p * looks, looks)
+        flat[pl.ds(at, looks), :] = jnp.where((lane & steps[0]) == 0, value, value * sign)
         return carry
 
     lax.fori_loop(0, count, select, 0, unroll=max(b for b in range(1, 7) if count % b == 0))
-    for x in range(2):
-        for g in range(looks):
-            slab[x, g] = flat[pl.ds(x * looks + g, count, stride=both), :].T
+    span = LANES // LOOK_C
+    for g in range(looks):
+        turned[g] = flat[pl.ds(g, count, stride=looks), :].T
+        for x in range(2):
+            for tile in range(tiles):
+                t = x * steps[0] + sum(((tile >> n) & 1) * step for n, step in enumerate(steps[1:]))
+                slab[x, g, tile * span : (tile + 1) * span, :] = turned[g, pl.ds(t, span, stride=LOOK_C), :]
     copy = pltpu.make_async_copy(slab, out.at[:, pl.ds(place * looks, looks)], sem)
     copy.start()
     copy.wait()
@@ -258,7 +251,7 @@
     acq, _, lines, width = blocks[0].shape
     looks, windows, count = lines // LOOK_R, width // LOOK_C, table.shape[1]
     total = groups * acq
-    rows = (total * (total - 1) + total) * looks
+    rows = total * (total - 1) // 2 + total
     extra = [] if before is None else [before]
     return pl.pallas_call(
         functools.partial(interfere_kernel, groups, place),
@@ -267,10 +260,11 @@
         out_shape=pltpu.HBM((2, chunks * looks, windows, count), jnp.float32),
         scratch_shapes=[
             pltpu.VMEM((total, 4, lines, LANES), jnp.float32),
-            pltpu.VMEM((rows, 2 * LANES), jnp.bfloat16),
-            pltpu.VMEM((rows, windows), jnp.float32),
-            pltpu.VMEM((count * 2 * looks, windows), jnp.float32),
-            pltpu.VMEM((total * looks, windows), jnp.float32),
+            pltpu.VMEM((width // LANES, rows, looks, LANES), jnp.float32),
+            pltpu.VMEM((rows, looks, LANES), jnp.float32),
+            pltpu.VMEM((count * looks, LANES), jnp.float32),
+            pltpu.VMEM((total, looks, LANES), jnp.float32),
+            pltpu.VMEM((looks, LANES, count), jnp.float32),
             pltpu.VMEM((2, looks, windows, count), jnp.float32),
             pltpu.SemaphoreType.DMA,
         ],
@@ -278,7 +272,7 @@
         compiler_params=pltpu.CompilerParams(vmem_limit_bytes=16 * MIB),
         cost_estimate=pl.CostEstimate(
             flops=count * 8 * lines * width,
-            bytes_accessed=groups * acq * 2 * lines * width * 2,
+            bytes_accessed=groups * acq * 2 * lines * width * 2 * 12,
             transcendentals=0,
         ),
         name="interfere",
@@ -318,6 +312,7 @@
     )
     above = lax.ppermute(tail, "pix", up)
     below = lax.ppermute(head, "pix", down)
+    above, below = lax.optimization_barrier((above, below))
     middle = send(blocks)
     top = send(
         resample_edge(0, 0, reach, -HALO, group, kernel, offsets, slab, above, groups)
@@ -325,7 +320,6 @@
     late = resample_edge(
         lines - CHUNK, lines - reach, reach, lines, group, kernel, offsets, slab, below, groups
     )
-    late, middle = lax.optimization_barrier((late, middle))
     bottom = send(late)
     result = None
     for place, moved in ((1, middle), (0, top), (2, bottom)):

time: 63.3 us -> 62.6 us (0.989)
  the two profiles are of different devices: /device:TPU:16 before, /device:TPU:9 now
where the time goes in v5:
time: 62.6 us; the launch traced here: 61.6 us
  Pallas kernels  32.6 us (52%)
  starting transfers between devices  15.9 us (25%)
  waiting for transfers between devices  13 us (21%)
    pallas_call x3, Pallas kernels, interfere(): pl.pallas_call(functools.partial(interfere_kernel, groups, place), in_spe...  28.5 us
    ppermute x9, starting transfers between devices, send(): lax.ppermute(blocks[s], 'acq', [(i, i ^ s) for i in range(groups)])  10.2 us
    ppermute x1, waiting for transfers between devices, local(): above = lax.ppermute(tail, 'pix', up)  5.32 us
    ppermute x1, waiting for transfers between devices, local(): below = lax.ppermute(head, 'pix', down)  4.69 us
    ppermute x1, starting transfers between devices, local(): above = lax.ppermute(tail, 'pix', up)  3.77 us
    ppermute x9, waiting for transfers between devices, send(): lax.ppermute(blocks[s], 'acq', [(i, i ^ s) for i in range(groups)])  2.98 us
    pallas_call x1, Pallas kernels, resample_first(): pl.pallas_call(functools.partial(first_kernel, first, groups), in_specs=[...  2.46 us
    ppermute x1, starting transfers between devices, local(): below = lax.ppermute(head, 'pix', down)  1.92 us
  transfers between devices with their start and end apart: 11, of which 3 were waited for; matrix products, arithmetic and copies ran while one was open for 0% of the time, Pallas kernels for 34%

profile of v5, /device:TPU:9, one launch (start us, length us, event | category | flops | bytes accessed | tf_op | source)
XLA Modules:
  0.0 61.6 jit_solution(17036260916025201976)
XLA Ops:
  0.0 0.0 copy-start
  0.0 0.0 copy-start.1
  0.0 2.5 %resample_first.1 = (bf16[3,2,32,768]{3,2,1,0:T(8,128)(2,1)S(1)}, bf16[3,2,32,768]{3,2,1,0:T(8,128)(2,1)S(1)}, bf16[3,2,32,768]{3,2,1,0:T(8,128)(2,1)S(1)}, bf16...) custom-call(s32[1]{0:T(128)} %bitcast.2.group, ...), custom_call_target="tpu_custom_call" | custom-call | flops 113246208 | bytes 4718592 | tf_op jit(solution)/shard_map/resample_first/pallas_call | solution.py:117
  2.5 3.8 %collective-permute-start = (bf16[3,2,24,3072]{3,2,1,0:T(8,128)(2,1)S(1)}, bf16[3,2,24,3072]{3,2,1,0:T(8,128)(2,1)S(1)}, u32[]{:S(2)}, u32[]{:S(2)}) collective-permute-start(bf16[3,2,24,3072]{3,2,1,0:T(8,128)(2,1)S(1)} %get-tuple-element.23), channel_id=1, source_target_pairs={{0,1},{1,2},{2,3},{3,4},{4,5},{5,6},{6,7},{8,9},{9,10},{10,11},{11... | collective-permute-start | bytes 2654216 | tf_op jit(solution)/shard_map/ppermute | solution.py:313
  6.2 1.9 %collective-permute-start.1 = (bf16[3,2,24,3072]{3,2,1,0:T(8,128)(2,1)S(1)}, bf16[3,2,24,3072]{3,2,1,0:T(8,128)(2,1)S(1)}, u32[]{:S(2)}, u32[]{:S(2)}) collective-permute-start(bf16[3,2,24,3072]{3,2,1,0:T(8,128)(2,1)S(1)} %get-tuple-element.24), channel_id=1, source_target_pairs={{1,0},{2,1},{3,2},{4,3},{5,4},{6,5},{7,6},{9,8},{10,9},{11,10},{12... | collective-permute-start | bytes 2654216 | tf_op jit(solution)/shard_map/ppermute | solution.py:314
  8.2 2.2 %collective-permute-start.10 = (bf16[3,2,32,768]{3,2,1,0:T(8,128)(2,1)S(1)}, bf16[3,2,32,768]{3,2,1,0:T(8,128)(2,1)S(1)}, u32[]{:S(2)}, u32[]{:S(2)}) collective-permute-start(bf16[3,2,32,768]{3,2,1,0:T(8,128)(2,1)S(1)} %get-tuple-element.38), channel_id=1, source_target_pairs={{0,24},{8,16},{16,8},{24,0},{1,25},{9,17},{17,9},{25,1},{2,26},{10... | collective-permute-start | bytes 884744 | tf_op jit(solution)/shard_map/ppermute | solution.py:307
  10.4 0.3 collective-permute-start.8
  10.7 0.2 collective-permute-start.9
  10.9 5.3 %collective-permute-done.halo = bf16[3,2,24,3072]{3,2,1,0:T(8,128)(2,1)S(1)} collective-permute-done((bf16[3,2,24,3072]{3,2,1,0:T(8,128)(2,1)S(1)}, bf16[3,2,24,3072]{3,2,1,0:T(8,128)(2,1)S(1)}, u32[]{:S(2)}, u32[]{:S(2)}) %collective-permute-start) | collective-permute-done | bytes 884768 | tf_op jit(solution)/shard_map/ppermute | solution.py:313
  16.2 4.7 %collective-permute-done.1.halo = bf16[3,2,24,3072]{3,2,1,0:T(8,128)(2,1)S(1)} collective-permute-done((bf16[3,2,24,3072]{3,2,1,0:T(8,128)(2,1)S(1)}, bf16[3,2,24,3072]{3,2,1,0:T(8,128)(2,1)S(1)}, u32[]{:S(2)}, u32[]{:S(2)}) %collective-permute-start.1) | collective-permute-done | bytes 884768 | tf_op jit(solution)/shard_map/ppermute | solution.py:314
  20.9 0.0 copy-done
  20.9 0.0 copy-done.1
  20.9 0.0 copy-start.2
  20.9 0.8 %resample_edge.3 = (bf16[3,2,32,768]{3,2,1,0:T(8,128)(2,1)S(1)}, bf16[3,2,32,768]{3,2,1,0:T(8,128)(2,1)S(1)}, bf16[3,2,32,768]{3,2,1,0:T(8,128)(2,1)S(1)}, bf16[3,2,32,768]{3,2,1,0:T(8,128)(2,1)S(1)}) custom-call(s32[1]{0:T(128)} %bitcast.2.group, bf16[8,12]{1,0:T(8,128)(2,1)S(1)} %bitcast.16, s32[3,96]{1,0:T(4,128)S(1)} %copy-done.1, ...), custom_call_target="tpu_custom_call" | custom-call | flops 103809024 | bytes 4423680 | tf_op jit(solution)/shard_map/resample_edge/pallas_call | solution.py:137
  21.8 1.3 %collective-permute-start.5 = (bf16[3,2,32,768]{3,2,1,0:T(8,128)(2,1)S(1)}, bf16[3,2,32,768]{3,2,1,0:T(8,128)(2,1)S(1)}, u32[]{:S(2)}, u32[]{:S(2)}) collective-permute-start(bf16[3,2,32,768]{3,2,1,0:T(8,128)(2,1)S(1)} %get-tuple-element.32), channel_id=1, source_target_pairs={{0,8},{8,0},{16,24},{24,16},{1,9},{9,1},{17,25},{25,17},{2,10},{10... | collective-permute-start | bytes 884744 | tf_op jit(solution)/shard_map/ppermute | solution.py:307
  23.0 0.0 copy-done.2
  23.1 1.3 %collective-permute-start.6 = (bf16[3,2,32,768]{3,2,1,0:T(8,128)(2,1)S(1)}, bf16[3,2,32,768]{3,2,1,0:T(8,128)(2,1)S(1)}, u32[]{:S(2)}, u32[]{:S(2)}) collective-permute-start(bf16[3,2,32,768]{3,2,1,0:T(8,128)(2,1)S(1)} %get-tuple-element.33), channel_id=1, source_target_pairs={{0,16},{8,24},{16,0},{24,8},{1,17},{9,25},{17,1},{25,9},{2,18},{10... | collective-permute-start | bytes 884744 | tf_op jit(solution)/shard_map/ppermute | solution.py:307
  24.4 0.8 %resample_edge.2 = (bf16[3,2,32,768]{3,2,1,0:T(8,128)(2,1)S(1)}, bf16[3,2,32,768]{3,2,1,0:T(8,128)(2,1)S(1)}, bf16[3,2,32,768]{3,2,1,0:T(8,128)(2,1)S(1)}, bf16[3,2,32,768]{3,2,1,0:T(8,128)(2,1)S(1)}) custom-call(s32[1]{0:T(128)} %bitcast.2.group, bf16[8,12]{1,0:T(8,128)(2,1)S(1)} %bitcast.17, s32[3,96]{1,0:T(4,128)S(1)} %copy-done.1, ...), custom_call_target="tpu_custom_call" | custom-call | flops 103809024 | bytes 4423680 | tf_op jit(solution)/shard_map/resample_edge/pallas_call | solution.py:137
  25.2 0.0 collective-permute-done.10.rest_3_
  25.2 0.3 collective-permute-start.7
  25.5 0.0 collective-permute-done.8.rest_1_
  25.5 1.2 %collective-permute-start.2 = (bf16[3,2,32,768]{3,2,1,0:T(8,128)(2,1)S(1)}, bf16[3,2,32,768]{3,2,1,0:T(8,128)(2,1)S(1)}, u32[]{:S(2)}, u32[]{:S(2)}) collective-permute-start(bf16[3,2,32,768]{3,2,1,0:T(8,128)(2,1)S(1)} %get-tuple-element.27), channel_id=1, source_target_pairs={{0,8},{8,0},{16,24},{24,16},{1,9},{9,1},{17,25},{25,17},{2,10},{10... | collective-permute-start | bytes 884744 | tf_op jit(solution)/shard_map/ppermute | solution.py:307
  26.7 0.0 collective-permute-done.9.rest_2_
  26.7 1.2 %collective-permute-start.3 = (bf16[3,2,32,768]{3,2,1,0:T(8,128)(2,1)S(1)}, bf16[3,2,32,768]{3,2,1,0:T(8,128)(2,1)S(1)}, u32[]{:S(2)}, u32[]{:S(2)}) collective-permute-start(bf16[3,2,32,768]{3,2,1,0:T(8,128)(2,1)S(1)} %get-tuple-element.28), channel_id=1, source_target_pairs={{0,16},{8,24},{16,0},{24,8},{1,17},{9,25},{17,1},{25,9},{2,18},{10... | collective-permute-start | bytes 884744 | tf_op jit(solution)/shard_map/ppermute | solution.py:307
  28.0 3.0 %collective-permute-done.5.rest_1_ = bf16[3,2,32,768]{3,2,1,0:T(8,128)(2,1)S(1)} collective-permute-done((bf16[3,2,32,768]{3,2,1,0:T(8,128)(2,1)S(1)}, bf16[3,2,32,768]{3,2,1,0:T(8,128)(2,1)S(1)}, u32[]{:S(2)}, u32[]{:S(2)}) %collective-permute-start.5) | collective-permute-done | bytes 294944 | tf_op jit(solution)/shard_map/ppermute | solution.py:307
  30.9 2.2 %collective-permute-start.4 = (bf16[3,2,32,768]{3,2,1,0:T(8,128)(2,1)S(1)}, bf16[3,2,32,768]{3,2,1,0:T(8,128)(2,1)S(1)}, u32[]{:S(2)}, u32[]{:S(2)}) collective-permute-start(bf16[3,2,32,768]{3,2,1,0:T(8,128)(2,1)S(1)} %get-tuple-element.29), channel_id=1, source_target_pairs={{0,24},{8,16},{16,8},{24,0},{1,25},{9,17},{17,9},{25,1},{2,26},{10... | collective-permute-start | bytes 884744 | tf_op jit(solution)/shard_map/ppermute | solution.py:307
  33.1 9.5 %interfere.3.rest_4_ = f32[2,24,48,60]{3,2,1,0:T(8,128)} custom-call(s32[4,60]{1,0:T(4,128)S(1)} %pad_add_fusion.table, bf16[3,2,32,768]{3,2,1,0:T(8,128)(2,1)S(1)} %get-tuple-element.35.rest_0_, bf16[3,2,32,768]{3,2,1,0:T(8,128)(2,1)S(1)} %collective-permute-done.8.rest_1_, bf16[3,2,32,768]{3,2,1,0:T(8,128)(2,1)S(1)} %collective-permute-done.9.rest_2_, ...), custom_call_target="tpu_custom_call" | custom-call | flops 11796480 | bytes 14155776 | tf_op jit(solution)/shard_map/interfere/pallas_call | solution.py:256
  42.6 0.0 collective-permute-done.6.rest_2_
  42.6 0.0 collective-permute-done.7.rest_3_
  42.6 9.5 %interfere.4.rest_4_ = f32[2,24,48,60]{3,2,1,0:T(8,128)} custom-call(s32[4,60]{1,0:T(4,128)S(1)} %pad_add_fusion.table, bf16[3,2,32,768]{3,2,1,0:T(8,128)(2,1)S(1)} %get-tuple-element.31.rest_0_, bf16[3,2,32,768]{3,2,1,0:T(8,128)(2,1)S(1)} %collective-permute-done.5.rest_1_, ...), custom_call_target="tpu_custom_call", output_to_operand_aliasing={{}: (5, {})} | custom-call | flops 11796480 | bytes 14155776 | tf_op jit(solution)/shard_map/interfere/pallas_call | solution.py:256
  52.1 0.0 collective-permute-done.2.rest_1_
  52.1 0.0 collective-permute-done.3.rest_2_
  52.1 0.0 collective-permute-done.4.rest_3_
  52.1 9.5 %interfere.5 = f32[2,24,48,60]{3,2,1,0:T(8,128)} custom-call(s32[4,60]{1,0:T(4,128)S(1)} %pad_add_fusion.table, bf16[3,2,32,768]{3,2,1,0:T(8,128)(2,1)S(1)} %get-tuple-element.26.rest_0_, bf16[3,2,32,768]{3,2,1,0:T(8,128)(2,1)S(1)} %collective-permute-done.2.rest_1_, ...), custom_call_target="tpu_custom_call", output_to_operand_aliasing={{}: (5, {})} | custom-call | flops 11796480 | bytes 14155776 | tf_op jit(solution)/shard_map/interfere/pallas_call | solution.py:256
  (4 shorter events, 0.1 us)
Async XLA Ops:
  0.0 20.9 %copy-start = (bf16[12,8]{0,1:T(8,128)(2,1)S(1)}, bf16[12,8]{0,1:T(8,128)(2,1)}, u32[]{:S(2)}) copy-start(bf16[12,8]{0,1:T(8,128)(2,1)} %param.6) | copy-start | bytes 580
  0.0 20.9 %copy-start.1 = (s32[3,96]{1,0:T(4,128)S(1)}, s32[3,96]{1,0:T(4,128)}, u32[]{:S(2)}) copy-start(s32[3,96]{1,0:T(4,128)} %off.5) | copy-start | bytes 3460
  2.5 13.7 %collective-permute-start = (bf16[3,2,24,3072]{3,2,1,0:T(8,128)(2,1)S(1)}, bf16[3,2,24,3072]{3,2,1,0:T(8,128)(2,1)S(1)}, u32[]{:S(2)}, u32[]{:S(2)}) collective-permute-start(bf16[3,2,24,3072]{3,2,1,0:T(8,128)(2,1)S(1)} %get-tuple-element.23), channel_id=1, source_target_pairs={{0,1},{1,2},{2,3},{3,4},{4,5},{5,6},{6,7},{8,9},{9,10},{10,11},{11... | collective-permute-start | bytes 2654216 | tf_op jit(solution)/shard_map/ppermute | solution.py:313
  6.2 14.7 %collective-permute-start.1 = (bf16[3,2,24,3072]{3,2,1,0:T(8,128)(2,1)S(1)}, bf16[3,2,24,3072]{3,2,1,0:T(8,128)(2,1)S(1)}, u32[]{:S(2)}, u32[]{:S(2)}) collective-permute-start(bf16[3,2,24,3072]{3,2,1,0:T(8,128)(2,1)S(1)} %get-tuple-element.24), channel_id=1, source_target_pairs={{1,0},{2,1},{3,2},{4,3},{5,4},{6,5},{7,6},{9,8},{10,9},{11,10},{12... | collective-permute-start | bytes 2654216 | tf_op jit(solution)/shard_map/ppermute | solution.py:314
  8.2 17.0 %collective-permute-start.10 = (bf16[3,2,32,768]{3,2,1,0:T(8,128)(2,1)S(1)}, bf16[3,2,32,768]{3,2,1,0:T(8,128)(2,1)S(1)}, u32[]{:S(2)}, u32[]{:S(2)}) collective-permute-start(bf16[3,2,32,768]{3,2,1,0:T(8,128)(2,1)S(1)} %get-tuple-element.38), channel_id=1, source_target_pairs={{0,24},{8,16},{16,8},{24,0},{1,25},{9,17},{17,9},{25,1},{2,26},{10... | collective-permute-start | bytes 884744 | tf_op jit(solution)/shard_map/ppermute | solution.py:307
  10.4 15.1 %collective-permute-start.8 = (bf16[3,2,32,768]{3,2,1,0:T(8,128)(2,1)S(1)}, bf16[3,2,32,768]{3,2,1,0:T(8,128)(2,1)S(1)}, u32[]{:S(2)}, u32[]{:S(2)}) collective-permute-start(bf16[3,2,32,768]{3,2,1,0:T(8,128)(2,1)S(1)} %get-tuple-element.36), channel_id=1, source_target_pairs={{0,8},{8,0},{16,24},{24,16},{1,9},{9,1},{17,25},{25,17},{2,10},{10... | collective-permute-start | bytes 884744 | tf_op jit(solution)/shard_map/ppermute | solution.py:307
  10.7 16.1 %collective-permute-start.9 = (bf16[3,2,32,768]{3,2,1,0:T(8,128)(2,1)S(1)}, bf16[3,2,32,768]{3,2,1,0:T(8,128)(2,1)S(1)}, u32[]{:S(2)}, u32[]{:S(2)}) collective-permute-start(bf16[3,2,32,768]{3,2,1,0:T(8,128)(2,1)S(1)} %get-tuple-element.37), channel_id=1, source_target_pairs={{0,16},{8,24},{16,0},{24,8},{1,17},{9,25},{17,1},{25,9},{2,18},{10... | collective-permute-start | bytes 884744 | tf_op jit(solution)/shard_map/ppermute | solution.py:307
  20.9 2.1 %copy-start.2 = (s32[60,2]{0,1:T(2,128)S(1)}, s32[60,2]{0,1:T(2,128)}, u32[]{:S(2)}) copy-start(s32[60,2]{0,1:T(2,128)} %param.7) | copy-start | bytes 1444
  21.8 9.2 %collective-permute-start.5 = (bf16[3,2,32,768]{3,2,1,0:T(8,128)(2,1)S(1)}, bf16[3,2,32,768]{3,2,1,0:T(8,128)(2,1)S(1)}, u32[]{:S(2)}, u32[]{:S(2)}) collective-permute-start(bf16[3,2,32,768]{3,2,1,0:T(8,128)(2,1)S(1)} %get-tuple-element.32), channel_id=1, source_target_pairs={{0,8},{8,0},{16,24},{24,16},{1,9},{9,1},{17,25},{25,17},{2,10},{10... | collective-permute-start | bytes 884744 | tf_op jit(solution)/shard_map/ppermute | solution.py:307
  23.1 19.5 %collective-permute-start.6 = (bf16[3,2,32,768]{3,2,1,0:T(8,128)(2,1)S(1)}, bf16[3,2,32,768]{3,2,1,0:T(8,128)(2,1)S(1)}, u32[]{:S(2)}, u32[]{:S(2)}) collective-permute-start(bf16[3,2,32,768]{3,2,1,0:T(8,128)(2,1)S(1)} %get-tuple-element.33), channel_id=1, source_target_pairs={{0,16},{8,24},{16,0},{24,8},{1,17},{9,25},{17,1},{25,9},{2,18},{10... | collective-permute-start | bytes 884744 | tf_op jit(solution)/shard_map/ppermute | solution.py:307
  25.2 17.4 %collective-permute-start.7 = (bf16[3,2,32,768]{3,2,1,0:T(8,128)(2,1)S(1)}, bf16[3,2,32,768]{3,2,1,0:T(8,128)(2,1)S(1)}, u32[]{:S(2)}, u32[]{:S(2)}) collective-permute-start(bf16[3,2,32,768]{3,2,1,0:T(8,128)(2,1)S(1)} %get-tuple-element.34), channel_id=1, source_target_pairs={{0,24},{8,16},{16,8},{24,0},{1,25},{9,17},{17,9},{25,1},{2,26},{10... | collective-permute-start | bytes 884744 | tf_op jit(solution)/shard_map/ppermute | solution.py:307
  25.5 26.6 %collective-permute-start.2 = (bf16[3,2,32,768]{3,2,1,0:T(8,128)(2,1)S(1)}, bf16[3,2,32,768]{3,2,1,0:T(8,128)(2,1)S(1)}, u32[]{:S(2)}, u32[]{:S(2)}) collective-permute-start(bf16[3,2,32,768]{3,2,1,0:T(8,128)(2,1)S(1)} %get-tuple-element.27), channel_id=1, source_target_pairs={{0,8},{8,0},{16,24},{24,16},{1,9},{9,1},{17,25},{25,17},{2,10},{10... | collective-permute-start | bytes 884744 | tf_op jit(solution)/shard_map/ppermute | solution.py:307
  26.7 25.4 %collective-permute-start.3 = (bf16[3,2,32,768]{3,2,1,0:T(8,128)(2,1)S(1)}, bf16[3,2,32,768]{3,2,1,0:T(8,128)(2,1)S(1)}, u32[]{:S(2)}, u32[]{:S(2)}) collective-permute-start(bf16[3,2,32,768]{3,2,1,0:T(8,128)(2,1)S(1)} %get-tuple-element.28), channel_id=1, source_target_pairs={{0,16},{8,24},{16,0},{24,8},{1,17},{9,25},{17,1},{25,9},{2,18},{10... | collective-permute-start | bytes 884744 | tf_op jit(solution)/shard_map/ppermute | solution.py:307
  30.9 21.2 %collective-permute-start.4 = (bf16[3,2,32,768]{3,2,1,0:T(8,128)(2,1)S(1)}, bf16[3,2,32,768]{3,2,1,0:T(8,128)(2,1)S(1)}, u32[]{:S(2)}, u32[]{:S(2)}) collective-permute-start(bf16[3,2,32,768]{3,2,1,0:T(8,128)(2,1)S(1)} %get-tuple-element.29), channel_id=1, source_target_pairs={{0,24},{8,16},{16,8},{24,0},{1,25},{9,17},{17,9},{25,1},{2,26},{10... | collective-permute-start | bytes 884744 | tf_op jit(solution)/shard_map/ppermute | solution.py:307

commit v6 on v4

--- a/solution.py
+++ b/solution.py
@@ -18,7 +18,7 @@
 
 def build_bands(first, sources, group, kernel, off, band):
     acq, taps = off.shape[0], kernel.shape[0]
-    gains = kernel[...].astype(jnp.float32)
+    gains = kernel[...].astype(jnp.float32) * 0.125
     lane = lax.broadcasted_iota(jnp.int32, gains.shape, 1)
     rows = sum(count for _, count in sources)
     index = lax.broadcasted_iota(jnp.int32, (rows, CHUNK), 0)
@@ -146,16 +146,20 @@
     )(group, kernel, offsets, slab, halo)
 
 
-def interfere_kernel(groups, place, table, *rest):
-    blocks, (out, parts, terms, pooled, flat, inverse, slab, sem) = rest[:groups], rest[-8:]
+def slot_of(low, high):
+    return high * (high - 1) // 2 + low
+
+
+def look_sums(blocks, begin, parts, terms, sums, slot_rows, power_rows):
     acq, _, lines, width = blocks[0].shape
     looks = lines // LOOK_R
-    count = table.shape[1]
     windows = width // LOOK_C
     both = 2 * looks
-    total_acq = groups * acq
-    slots = total_acq * (total_acq - 1) // 2
     tiles = width // LANES
+    total, fresh = len(blocks) * acq, begin * acq
+    base = slot_of(0, fresh)
+    split = (slot_of(0, total) - base) * both
+    used = split + (total - fresh) * looks
 
     def pool(tile):
         row = lax.broadcasted_iota(jnp.int32, (2 * LANES, windows), 0)
@@ -169,70 +173,89 @@
         terms[row : row + both, LANES:] = (field - first.astype(jnp.float32)).astype(jnp.bfloat16)
 
     def settle(tile):
-        pooled[...] += jnp.dot(terms[...], pool(tile), preferred_element_type=jnp.float32)
+        result = jnp.dot(terms[...], pool(tile), preferred_element_type=jnp.float32)
+        sums[slot_rows : slot_rows + split, :] += result[:split]
+        sums[power_rows : power_rows + used - split, :] += result[split:used]
 
     def unpack(tile):
         at = pl.ds(pl.multiple_of(tile * LANES, LANES), LANES)
         for r, block in enumerate(blocks):
             for a in range(acq):
-                real = block[a, 0, :, at].astype(jnp.float32) * 0.125
-                imag = block[a, 1, :, at].astype(jnp.float32) * 0.125
+                real = block[a, 0, :, at].astype(jnp.float32)
+                imag = block[a, 1, :, at].astype(jnp.float32)
                 parts[r * acq + a, 0] = real
                 parts[r * acq + a, 1] = imag
                 parts[r * acq + a, 2] = real + imag
                 parts[r * acq + a, 3] = real - imag
 
     def cross(pairs):
-        sums = {pair: [0.0, 0.0, 0.0] for pair in pairs}
+        totals = {pair: [0.0, 0.0, 0.0] for pair in pairs}
         for j in range(LOOK_R):
             at = slice(j * looks, (j + 1) * looks)
             left = {i: [parts[i, c, at, :] for c in (2, 0, 1)] for i in sorted({i for i, _ in pairs})}
             right = {i: [parts[i, c, at, :] for c in (0, 2, 3)] for i in sorted({i for _, i in pairs})}
             for pair in pairs:
                 for t in range(3):
-                    sums[pair][t] = sums[pair][t] + left[pair[0]][t] * right[pair[1]][t]
+                    totals[pair][t] = totals[pair][t] + left[pair[0]][t] * right[pair[1]][t]
         for i, k in pairs:
-            one, two, three = sums[i, k]
-            slot = i * (2 * total_acq - i - 1) // 2 + k - i - 1
-            put(slot * both, jnp.concatenate([one - three, one - two], axis=0))
+            one, two, three = totals[i, k]
+            put((slot_of(i, k) - base) * both, jnp.concatenate([one - three, one - two], axis=0))
 
     def powers(members):
         fields = []
         for i in members:
-            total = 0.0
+            field = 0.0
             for j in range(LOOK_R):
                 for c in range(2):
                     value = parts[i, c, j * looks : (j + 1) * looks, :]
-                    total = total + value * value
-            fields.append(total)
-        put(slots * both + members[0] * looks, jnp.concatenate(fields, axis=0))
+                    field = field + value * value
+            fields.append(field)
+        put(split + (members[0] - fresh) * looks, jnp.concatenate(fields, axis=0))
 
     def work(tile):
         unpack(tile)
-        for r in range(groups):
-            for q in range(r, groups):
-                cross(
-                    [
-                        (i, k)
-                        for i in range(r * acq, (r + 1) * acq)
-                        for k in range(q * acq, (q + 1) * acq)
-                        if i < k
-                    ]
-                )
-        for i in range(0, total_acq, 2):
-            powers((i, i + 1))
+        for q in range(begin, len(blocks)):
+            for r in range(q + 1):
+                first = range(r * acq, (r + 1) * acq)
+                second = range(q * acq, (q + 1) * acq)
+                cross([(i, k) for i in first for k in second if i < k])
+        for i in range(fresh, total, 2):
+            powers((i, min(i + 1, total - 1)))
 
     def turn(tile, carry):
         settle(tile - 1)
         work(tile)
         return carry
 
-    pooled[...] = jnp.zeros(pooled.shape, jnp.float32)
     work(0)
     lax.fori_loop(1, tiles, turn, 0)
     settle(tiles - 1)
 
-    inverse[...] = lax.rsqrt(pooled[slots * both :, :] + 1e-6)
+
+def near_kernel(groups, *rest):
+    blocks, (sums, parts, terms) = rest[:groups], rest[groups:]
+    acq, _, lines, _ = blocks[0].shape
+    looks = lines // LOOK_R
+    sums[...] = jnp.zeros(sums.shape, jnp.float32)
+    look_sums(blocks, 0, parts, terms, sums, 0, slot_of(0, groups * acq) * 2 * looks)
+
+
+def interfere_kernel(groups, known, place, table, *rest):
+    blocks, rest = rest[:groups], rest[groups:]
+    out, parts, terms, sums, flat, inverse, slab, sem = rest[-8:]
+    acq, _, lines, width = blocks[0].shape
+    looks = lines // LOOK_R
+    count = table.shape[1]
+    both = 2 * looks
+    total, fresh = groups * acq, known * acq
+    start, split = slot_of(0, fresh) * both, slot_of(0, total) * both
+    sums[...] = jnp.zeros(sums.shape, jnp.float32)
+    if known:
+        near = rest[0]
+        sums[:start, :] = near[:start, :]
+        sums[split : split + fresh * looks, :] = near[start : start + fresh * looks, :]
+    look_sums(blocks, known, parts, terms, sums, start, split + fresh * looks)
+    inverse[...] = lax.rsqrt(sums[split : split + total * looks, :] + 1e-6)
 
     def select(p, carry):
         at = pl.multiple_of(table[0, p] * both, both)
@@ -240,7 +263,7 @@
         s = pl.multiple_of(table[2, p] * looks, looks)
         scale = inverse[pl.ds(m, looks), :] * inverse[pl.ds(s, looks), :]
         turned = scale * table[3, p].astype(jnp.float32)
-        value = pooled[pl.ds(at, both), :] * jnp.concatenate([scale, turned], axis=0)
+        value = sums[pl.ds(at, both), :] * jnp.concatenate([scale, turned], axis=0)
         flat[pl.ds(pl.multiple_of(p * both, both), both), :] = value
         return carry
 
@@ -253,44 +276,71 @@
     copy.wait()
 
 
-def interfere(place, chunks, table, blocks, before):
+def work_space(groups, known, acq, lines, looks):
+    total, fresh = groups * acq, known * acq
+    count = total - fresh
+    rows = (slot_of(0, total) - slot_of(0, fresh)) * 2 * looks + (count + count % 2) * looks
+    return [
+        pltpu.VMEM((total, 4, lines, LANES), jnp.float32),
+        pltpu.VMEM((rows, 2 * LANES), jnp.bfloat16),
+    ]
+
+
+def interfere_cost(pairs, acq, lines, width):
+    return pl.CostEstimate(
+        flops=pairs * 8 * lines * width,
+        bytes_accessed=acq * 2 * lines * width * 2 * 12,
+        transcendentals=0,
+    )
+
+
+def interfere_near(blocks):
+    groups = len(blocks)
+    acq, _, lines, width = blocks[0].shape
+    looks, windows, total = lines // LOOK_R, width // LOOK_C, groups * acq
+    return pl.pallas_call(
+        functools.partial(near_kernel, groups),
+        in_specs=[VMEM] * groups,
+        out_specs=VMEM,
+        out_shape=pltpu.VMEM(((slot_of(0, total) * 2 + total) * looks, windows), jnp.float32),
+        scratch_shapes=work_space(groups, 0, acq, lines, looks),
+        compiler_params=pltpu.CompilerParams(vmem_limit_bytes=16 * MIB),
+        cost_estimate=interfere_cost(slot_of(0, total), total, lines, width),
+        name="interfere_near",
+    )(*blocks)
+
+
+def interfere(place, chunks, table, blocks, near, known, before):
     groups = len(blocks)
     acq, _, lines, width = blocks[0].shape
     looks, windows, count = lines // LOOK_R, width // LOOK_C, table.shape[1]
     total = groups * acq
-    rows = (total * (total - 1) + total) * looks
+    near = [] if near is None else [near]
     extra = [] if before is None else [before]
     return pl.pallas_call(
-        functools.partial(interfere_kernel, groups, place),
-        in_specs=[SMEM] + [VMEM] * groups + [ANY] * len(extra),
+        functools.partial(interfere_kernel, groups, known, place),
+        in_specs=[SMEM] + [VMEM] * (groups + len(near)) + [ANY] * len(extra),
         out_specs=ANY,
         out_shape=pltpu.HBM((2, chunks * looks, windows, count), jnp.float32),
-        scratch_shapes=[
-            pltpu.VMEM((total, 4, lines, LANES), jnp.float32),
-            pltpu.VMEM((rows, 2 * LANES), jnp.bfloat16),
-            pltpu.VMEM((rows, windows), jnp.float32),
+        scratch_shapes=work_space(groups, known, acq, lines, looks)
+        + [
+            pltpu.VMEM(((slot_of(0, total) * 2 + total) * looks, windows), jnp.float32),
             pltpu.VMEM((count * 2 * looks, windows), jnp.float32),
             pltpu.VMEM((total * looks, windows), jnp.float32),
             pltpu.VMEM((2, looks, windows, count), jnp.float32),
             pltpu.SemaphoreType.DMA,
         ],
-        input_output_aliases={} if before is None else {1 + groups: 0},
+        input_output_aliases={} if before is None else {1 + groups + len(near): 0},
         compiler_params=pltpu.CompilerParams(vmem_limit_bytes=16 * MIB),
-        cost_estimate=pl.CostEstimate(
-            flops=count * 8 * lines * width,
-            bytes_accessed=groups * acq * 2 * lines * width * 2,
-            transcendentals=0,
-        ),
+        cost_estimate=interfere_cost(count, total, lines, width),
         name="interfere",
-    )(table, *blocks, *extra)
+    )(table, *blocks, *near, *extra)
 
 
 def pair_table(pairs, groups, acq, mine):
-    total = groups * acq
-    near = ((pairs // acq) ^ mine) * acq + pairs % acq
-    m, s = near[:, 0], near[:, 1]
-    low, high = jnp.minimum(m, s), jnp.maximum(m, s)
-    slot = low * (2 * total - low - 1) // 2 + high - low - 1
+    close = ((pairs // acq) ^ mine) * acq + pairs % acq
+    m, s = close[:, 0], close[:, 1]
+    slot = slot_of(jnp.minimum(m, s), jnp.maximum(m, s))
     return jnp.stack([slot, m, s, jnp.where(m < s, 1, -1)]).astype(jnp.int32)
 
 
@@ -318,6 +368,7 @@
     )
     above = lax.ppermute(tail, "pix", up)
     below = lax.ppermute(head, "pix", down)
+    above, below = lax.optimization_barrier((above, below))
     middle = send(blocks)
     top = send(
         resample_edge(0, 0, reach, -HALO, group, kernel, offsets, slab, above, groups)
@@ -325,11 +376,14 @@
     late = resample_edge(
         lines - CHUNK, lines - reach, reach, lines, group, kernel, offsets, slab, below, groups
     )
-    late, middle = lax.optimization_barrier((late, middle))
     bottom = send(late)
     result = None
-    for place, moved in ((1, middle), (0, top), (2, bottom)):
-        result = interfere(place, chunks, table, moved, result)
+    for place, moved, known in ((1, middle, 0), (0, top, 0), (2, bottom, groups - 1)):
+        near = None
+        if known:
+            mine, result = lax.optimization_barrier((moved[0], result))
+            near = interfere_near([mine, *moved[1:known]])
+        result = interfere(place, chunks, table, moved, near, known, result)
     return jnp.transpose(result, (0, 3, 1, 2))
 
 

time: 63.3 us -> 56.4 us (0.89)
  the two profiles are of different devices: /device:TPU:16 before, /device:TPU:9 now
where the time goes in v6:
time: 56.4 us; the launch traced here: 56.3 us
  Pallas kernels  21.1 us (37%)
  waiting for transfers between devices  19.1 us (34%)
  starting transfers between devices  15.9 us (28%)
    pallas_call x3, Pallas kernels, interfere(): pl.pallas_call(functools.partial(interfere_kernel, groups, known, place),...  14.6 us
    ppermute x9, starting transfers between devices, send(): lax.ppermute(blocks[s], 'acq', [(i, i ^ s) for i in range(groups)])  10.2 us
    ppermute x9, waiting for transfers between devices, send(): lax.ppermute(blocks[s], 'acq', [(i, i ^ s) for i in range(groups)])  9.13 us
    ppermute x1, waiting for transfers between devices, local(): above = lax.ppermute(tail, 'pix', up)  5.32 us
    ppermute x1, waiting for transfers between devices, local(): below = lax.ppermute(head, 'pix', down)  4.69 us
    ppermute x1, starting transfers between devices, local(): above = lax.ppermute(tail, 'pix', up)  3.77 us
    pallas_call x1, Pallas kernels, resample_first(): pl.pallas_call(functools.partial(first_kernel, first, groups), in_specs=[...  2.46 us
    pallas_call x1, Pallas kernels, interfere_near(): pl.pallas_call(functools.partial(near_kernel, groups), in_specs=[VMEM] *...  2.3 us
  transfers between devices with their start and end apart: 11, of which 4 were waited for; matrix products, arithmetic and copies ran while one was open for 0% of the time, Pallas kernels for 26%

profile of v6, /device:TPU:9, one launch (start us, length us, event | category | flops | bytes accessed | tf_op | source)
XLA Modules:
  0.0 56.3 jit_solution(13828308292071710645)
XLA Ops:
  0.0 0.0 copy-start
  0.0 0.0 copy-start.1
  0.0 2.5 %resample_first.1 = (bf16[3,2,32,768]{3,2,1,0:T(8,128)(2,1)S(1)}, bf16[3,2,32,768]{3,2,1,0:T(8,128)(2,1)S(1)}, bf16[3,2,32,768]{3,2,1,0:T(8,128)(2,1)S(1)}, bf16...) custom-call(s32[1]{0:T(128)} %bitcast.2.group, ...), custom_call_target="tpu_custom_call" | custom-call | flops 113246208 | bytes 4718592 | tf_op jit(solution)/shard_map/resample_first/pallas_call | solution.py:117
  2.5 3.8 %collective-permute-start = (bf16[3,2,24,3072]{3,2,1,0:T(8,128)(2,1)S(1)}, bf16[3,2,24,3072]{3,2,1,0:T(8,128)(2,1)S(1)}, u32[]{:S(2)}, u32[]{:S(2)}) collective-permute-start(bf16[3,2,24,3072]{3,2,1,0:T(8,128)(2,1)S(1)} %get-tuple-element.25), channel_id=1, source_target_pairs={{0,1},{1,2},{2,3},{3,4},{4,5},{5,6},{6,7},{8,9},{9,10},{10,11},{11... | collective-permute-start | bytes 2654216 | tf_op jit(solution)/shard_map/ppermute | solution.py:369
  6.2 1.9 %collective-permute-start.1 = (bf16[3,2,24,3072]{3,2,1,0:T(8,128)(2,1)S(1)}, bf16[3,2,24,3072]{3,2,1,0:T(8,128)(2,1)S(1)}, u32[]{:S(2)}, u32[]{:S(2)}) collective-permute-start(bf16[3,2,24,3072]{3,2,1,0:T(8,128)(2,1)S(1)} %get-tuple-element.26), channel_id=1, source_target_pairs={{1,0},{2,1},{3,2},{4,3},{5,4},{6,5},{7,6},{9,8},{10,9},{11,10},{12... | collective-permute-start | bytes 2654216 | tf_op jit(solution)/shard_map/ppermute | solution.py:370
  8.2 2.2 %collective-permute-start.10 = (bf16[3,2,32,768]{3,2,1,0:T(8,128)(2,1)S(1)}, bf16[3,2,32,768]{3,2,1,0:T(8,128)(2,1)S(1)}, u32[]{:S(2)}, u32[]{:S(2)}) collective-permute-start(bf16[3,2,32,768]{3,2,1,0:T(8,128)(2,1)S(1)} %get-tuple-element.40), channel_id=1, source_target_pairs={{0,24},{8,16},{16,8},{24,0},{1,25},{9,17},{17,9},{25,1},{2,26},{10... | collective-permute-start | bytes 884744 | tf_op jit(solution)/shard_map/ppermute | solution.py:363
  10.4 0.3 collective-permute-start.8
  10.7 0.2 collective-permute-start.9
  10.9 5.3 %collective-permute-done.halo = bf16[3,2,24,3072]{3,2,1,0:T(8,128)(2,1)S(1)} collective-permute-done((bf16[3,2,24,3072]{3,2,1,0:T(8,128)(2,1)S(1)}, bf16[3,2,24,3072]{3,2,1,0:T(8,128)(2,1)S(1)}, u32[]{:S(2)}, u32[]{:S(2)}) %collective-permute-start) | collective-permute-done | bytes 884768 | tf_op jit(solution)/shard_map/ppermute | solution.py:369
  16.2 4.7 %collective-permute-done.1.halo = bf16[3,2,24,3072]{3,2,1,0:T(8,128)(2,1)S(1)} collective-permute-done((bf16[3,2,24,3072]{3,2,1,0:T(8,128)(2,1)S(1)}, bf16[3,2,24,3072]{3,2,1,0:T(8,128)(2,1)S(1)}, u32[]{:S(2)}, u32[]{:S(2)}) %collective-permute-start.1) | collective-permute-done | bytes 884768 | tf_op jit(solution)/shard_map/ppermute | solution.py:370
  20.9 0.0 copy-done
  20.9 0.0 copy-done.1
  20.9 0.0 copy-start.2
  20.9 0.8 %resample_edge.3 = (bf16[3,2,32,768]{3,2,1,0:T(8,128)(2,1)S(1)}, bf16[3,2,32,768]{3,2,1,0:T(8,128)(2,1)S(1)}, bf16[3,2,32,768]{3,2,1,0:T(8,128)(2,1)S(1)}, bf16[3,2,32,768]{3,2,1,0:T(8,128)(2,1)S(1)}) custom-call(s32[1]{0:T(128)} %bitcast.2.group, bf16[8,12]{1,0:T(8,128)(2,1)S(1)} %bitcast.16, s32[3,96]{1,0:T(4,128)S(1)} %copy-done.1, ...), custom_call_target="tpu_custom_call" | custom-call | flops 103809024 | bytes 4423680 | tf_op jit(solution)/shard_map/resample_edge/pallas_call | solution.py:137
  21.8 1.3 %collective-permute-start.5 = (bf16[3,2,32,768]{3,2,1,0:T(8,128)(2,1)S(1)}, bf16[3,2,32,768]{3,2,1,0:T(8,128)(2,1)S(1)}, u32[]{:S(2)}, u32[]{:S(2)}) collective-permute-start(bf16[3,2,32,768]{3,2,1,0:T(8,128)(2,1)S(1)} %get-tuple-element.34), channel_id=1, source_target_pairs={{0,8},{8,0},{16,24},{24,16},{1,9},{9,1},{17,25},{25,17},{2,10},{10... | collective-permute-start | bytes 884744 | tf_op jit(solution)/shard_map/ppermute | solution.py:363
  23.0 0.0 copy-done.2
  23.1 1.3 %collective-permute-start.6 = (bf16[3,2,32,768]{3,2,1,0:T(8,128)(2,1)S(1)}, bf16[3,2,32,768]{3,2,1,0:T(8,128)(2,1)S(1)}, u32[]{:S(2)}, u32[]{:S(2)}) collective-permute-start(bf16[3,2,32,768]{3,2,1,0:T(8,128)(2,1)S(1)} %get-tuple-element.35), channel_id=1, source_target_pairs={{0,16},{8,24},{16,0},{24,8},{1,17},{9,25},{17,1},{25,9},{2,18},{10... | collective-permute-start | bytes 884744 | tf_op jit(solution)/shard_map/ppermute | solution.py:363
  24.4 0.8 %resample_edge.2 = (bf16[3,2,32,768]{3,2,1,0:T(8,128)(2,1)S(1)}, bf16[3,2,32,768]{3,2,1,0:T(8,128)(2,1)S(1)}, bf16[3,2,32,768]{3,2,1,0:T(8,128)(2,1)S(1)}, bf16[3,2,32,768]{3,2,1,0:T(8,128)(2,1)S(1)}) custom-call(s32[1]{0:T(128)} %bitcast.2.group, bf16[8,12]{1,0:T(8,128)(2,1)S(1)} %bitcast.17, s32[3,96]{1,0:T(4,128)S(1)} %copy-done.1, ...), custom_call_target="tpu_custom_call" | custom-call | flops 103809024 | bytes 4423680 | tf_op jit(solution)/shard_map/resample_edge/pallas_call | solution.py:137
  25.2 0.0 collective-permute-done.10.rest_3_
  25.2 0.3 collective-permute-start.7
  25.5 0.0 collective-permute-done.8.rest_1_
  25.5 1.2 %collective-permute-start.2 = (bf16[3,2,32,768]{3,2,1,0:T(8,128)(2,1)S(1)}, bf16[3,2,32,768]{3,2,1,0:T(8,128)(2,1)S(1)}, u32[]{:S(2)}, u32[]{:S(2)}) collective-permute-start(bf16[3,2,32,768]{3,2,1,0:T(8,128)(2,1)S(1)} %get-tuple-element.29), channel_id=1, source_target_pairs={{0,8},{8,0},{16,24},{24,16},{1,9},{9,1},{17,25},{25,17},{2,10},{10... | collective-permute-start | bytes 884744 | tf_op jit(solution)/shard_map/ppermute | solution.py:363
  26.7 0.0 collective-permute-done.9.rest_2_
  26.7 1.2 %collective-permute-start.3 = (bf16[3,2,32,768]{3,2,1,0:T(8,128)(2,1)S(1)}, bf16[3,2,32,768]{3,2,1,0:T(8,128)(2,1)S(1)}, u32[]{:S(2)}, u32[]{:S(2)}) collective-permute-start(bf16[3,2,32,768]{3,2,1,0:T(8,128)(2,1)S(1)} %get-tuple-element.30), channel_id=1, source_target_pairs={{0,16},{8,24},{16,0},{24,8},{1,17},{9,25},{17,1},{25,9},{2,18},{10... | collective-permute-start | bytes 884744 | tf_op jit(solution)/shard_map/ppermute | solution.py:363
  28.0 3.0 %collective-permute-done.5.rest_1_ = bf16[3,2,32,768]{3,2,1,0:T(8,128)(2,1)S(1)} collective-permute-done((bf16[3,2,32,768]{3,2,1,0:T(8,128)(2,1)S(1)}, bf16[3,2,32,768]{3,2,1,0:T(8,128)(2,1)S(1)}, u32[]{:S(2)}, u32[]{:S(2)}) %collective-permute-start.5) | collective-permute-done | bytes 294944 | tf_op jit(solution)/shard_map/ppermute | solution.py:363
  30.9 2.2 %collective-permute-start.4 = (bf16[3,2,32,768]{3,2,1,0:T(8,128)(2,1)S(1)}, bf16[3,2,32,768]{3,2,1,0:T(8,128)(2,1)S(1)}, u32[]{:S(2)}, u32[]{:S(2)}) collective-permute-start(bf16[3,2,32,768]{3,2,1,0:T(8,128)(2,1)S(1)} %get-tuple-element.31), channel_id=1, source_target_pairs={{0,24},{8,16},{16,8},{24,0},{1,25},{9,17},{17,9},{25,1},{2,26},{10... | collective-permute-start | bytes 884744 | tf_op jit(solution)/shard_map/ppermute | solution.py:363
  33.1 5.3 %interfere.3.rest_4_ = f32[2,24,48,60]{3,2,1,0:T(8,128)} custom-call(s32[4,60]{1,0:T(4,128)S(1)} %pad_add_fusion.table, bf16[3,2,32,768]{3,2,1,0:T(8,128)(2,1)S(1)} %get-tuple-element.37.rest_0_, bf16[3,2,32,768]{3,2,1,0:T(8,128)(2,1)S(1)} %collective-permute-done.8.rest_1_, bf16[3,2,32,768]{3,2,1,0:T(8,128)(2,1)S(1)} %collective-permute-done.9.rest_2_, ...), custom_call_target="tpu_custom_call" | custom-call | flops 11796480 | bytes 14155776 | tf_op jit(solution)/shard_map/interfere/pallas_call | solution.py:320
  38.4 0.0 collective-permute-done.6.rest_2_
  38.5 0.0 collective-permute-done.7.rest_3_
  38.5 5.3 %interfere.4.rest_5_ = f32[2,24,48,60]{3,2,1,0:T(8,128)} custom-call(s32[4,60]{1,0:T(4,128)S(1)} %pad_add_fusion.table, bf16[3,2,32,768]{3,2,1,0:T(8,128)(2,1)S(1)} %get-tuple-element.33.rest_0_, bf16[3,2,32,768]{3,2,1,0:T(8,128)(2,1)S(1)} %collective-permute-done.5.rest_1_, ...), custom_call_target="tpu_custom_call", output_to_operand_aliasing={{}: (5, {})} | custom-call | flops 11796480 | bytes 14155776 | tf_op jit(solution)/shard_map/interfere/pallas_call | solution.py:320
  43.8 0.0 collective-permute-done.2.rest_1_
  43.8 6.1 %collective-permute-done.3.rest_2_ = bf16[3,2,32,768]{3,2,1,0:T(8,128)(2,1)S(1)} collective-permute-done((bf16[3,2,32,768]{3,2,1,0:T(8,128)(2,1)S(1)}, bf16[3,2,32,768]{3,2,1,0:T(8,128)(2,1)S(1)}, u32[]{:S(2)}, u32[]{:S(2)}) %collective-permute-start.3) | collective-permute-done | bytes 294944 | tf_op jit(solution)/shard_map/ppermute | solution.py:363
  49.9 2.3 %interfere_near.1.rest_4_ = f32[648,48]{1,0:T(8,128)S(1)} custom-call(bf16[3,2,32,768]{3,2,1,0:T(8,128)(2,1)S(1)} %get-tuple-element.41.rest_0_, bf16[3,2,32,768]{3,2,1,0:T(8,128)(2,1)S(1)} %collective-permute-done.2.rest_1_, bf16[3,2,32,768]{3,2,1,0:T(8,128)(2,1)S(1)} %collective-permute-done.3.rest_2_), custom_call_target="tpu_custom_call" | custom-call | flops 7077888 | bytes 10616832 | tf_op jit(solution)/shard_map/interfere_near/pallas_call | solution.py:301
  52.2 0.0 collective-permute-done.4.rest_3_
  52.3 4.0 %interfere.5 = f32[2,24,48,60]{3,2,1,0:T(8,128)} custom-call(s32[4,60]{1,0:T(4,128)S(1)} %pad_add_fusion.table, bf16[3,2,32,768]{3,2,1,0:T(8,128)(2,1)S(1)} %get-tuple-element.41.rest_0_, bf16[3,2,32,768]{3,2,1,0:T(8,128)(2,1)S(1)} %collective-permute-done.2.rest_1_, ...), custom_call_target="tpu_custom_call", output_to_operand_aliasing={{}: (6, {})} | custom-call | flops 11796480 | bytes 14155776 | tf_op jit(solution)/shard_map/interfere/pallas_call | solution.py:320
  (4 shorter events, 0.1 us)
Async XLA Ops:
  0.0 20.9 %copy-start = (bf16[12,8]{0,1:T(8,128)(2,1)S(1)}, bf16[12,8]{0,1:T(8,128)(2,1)}, u32[]{:S(2)}) copy-start(bf16[12,8]{0,1:T(8,128)(2,1)} %param.6) | copy-start | bytes 580
  0.0 20.9 %copy-start.1 = (s32[3,96]{1,0:T(4,128)S(1)}, s32[3,96]{1,0:T(4,128)}, u32[]{:S(2)}) copy-start(s32[3,96]{1,0:T(4,128)} %off.5) | copy-start | bytes 3460
  2.5 13.7 %collective-permute-start = (bf16[3,2,24,3072]{3,2,1,0:T(8,128)(2,1)S(1)}, bf16[3,2,24,3072]{3,2,1,0:T(8,128)(2,1)S(1)}, u32[]{:S(2)}, u32[]{:S(2)}) collective-permute-start(bf16[3,2,24,3072]{3,2,1,0:T(8,128)(2,1)S(1)} %get-tuple-element.25), channel_id=1, source_target_pairs={{0,1},{1,2},{2,3},{3,4},{4,5},{5,6},{6,7},{8,9},{9,10},{10,11},{11... | collective-permute-start | bytes 2654216 | tf_op jit(solution)/shard_map/ppermute | solution.py:369
  6.2 14.7 %collective-permute-start.1 = (bf16[3,2,24,3072]{3,2,1,0:T(8,128)(2,1)S(1)}, bf16[3,2,24,3072]{3,2,1,0:T(8,128)(2,1)S(1)}, u32[]{:S(2)}, u32[]{:S(2)}) collective-permute-start(bf16[3,2,24,3072]{3,2,1,0:T(8,128)(2,1)S(1)} %get-tuple-element.26), channel_id=1, source_target_pairs={{1,0},{2,1},{3,2},{4,3},{5,4},{6,5},{7,6},{9,8},{10,9},{11,10},{12... | collective-permute-start | bytes 2654216 | tf_op jit(solution)/shard_map/ppermute | solution.py:370
  8.2 17.0 %collective-permute-start.10 = (bf16[3,2,32,768]{3,2,1,0:T(8,128)(2,1)S(1)}, bf16[3,2,32,768]{3,2,1,0:T(8,128)(2,1)S(1)}, u32[]{:S(2)}, u32[]{:S(2)}) collective-permute-start(bf16[3,2,32,768]{3,2,1,0:T(8,128)(2,1)S(1)} %get-tuple-element.40), channel_id=1, source_target_pairs={{0,24},{8,16},{16,8},{24,0},{1,25},{9,17},{17,9},{25,1},{2,26},{10... | collective-permute-start | bytes 884744 | tf_op jit(solution)/shard_map/ppermute | solution.py:363
  10.4 15.1 %collective-permute-start.8 = (bf16[3,2,32,768]{3,2,1,0:T(8,128)(2,1)S(1)}, bf16[3,2,32,768]{3,2,1,0:T(8,128)(2,1)S(1)}, u32[]{:S(2)}, u32[]{:S(2)}) collective-permute-start(bf16[3,2,32,768]{3,2,1,0:T(8,128)(2,1)S(1)} %get-tuple-element.38), channel_id=1, source_target_pairs={{0,8},{8,0},{16,24},{24,16},{1,9},{9,1},{17,25},{25,17},{2,10},{10... | collective-permute-start | bytes 884744 | tf_op jit(solution)/shard_map/ppermute | solution.py:363
  10.7 16.1 %collective-permute-start.9 = (bf16[3,2,32,768]{3,2,1,0:T(8,128)(2,1)S(1)}, bf16[3,2,32,768]{3,2,1,0:T(8,128)(2,1)S(1)}, u32[]{:S(2)}, u32[]{:S(2)}) collective-permute-start(bf16[3,2,32,768]{3,2,1,0:T(8,128)(2,1)S(1)} %get-tuple-element.39), channel_id=1, source_target_pairs={{0,16},{8,24},{16,0},{24,8},{1,17},{9,25},{17,1},{25,9},{2,18},{10... | collective-permute-start | bytes 884744 | tf_op jit(solution)/shard_map/ppermute | solution.py:363
  20.9 2.1 %copy-start.2 = (s32[60,2]{0,1:T(2,128)S(1)}, s32[60,2]{0,1:T(2,128)}, u32[]{:S(2)}) copy-start(s32[60,2]{0,1:T(2,128)} %param.7) | copy-start | bytes 1444
  21.8 9.2 %collective-permute-start.5 = (bf16[3,2,32,768]{3,2,1,0:T(8,128)(2,1)S(1)}, bf16[3,2,32,768]{3,2,1,0:T(8,128)(2,1)S(1)}, u32[]{:S(2)}, u32[]{:S(2)}) collective-permute-start(bf16[3,2,32,768]{3,2,1,0:T(8,128)(2,1)S(1)} %get-tuple-element.34), channel_id=1, source_target_pairs={{0,8},{8,0},{16,24},{24,16},{1,9},{9,1},{17,25},{25,17},{2,10},{10... | collective-permute-start | bytes 884744 | tf_op jit(solution)/shard_map/ppermute | solution.py:363
  23.1 15.4 %collective-permute-start.6 = (bf16[3,2,32,768]{3,2,1,0:T(8,128)(2,1)S(1)}, bf16[3,2,32,768]{3,2,1,0:T(8,128)(2,1)S(1)}, u32[]{:S(2)}, u32[]{:S(2)}) collective-permute-start(bf16[3,2,32,768]{3,2,1,0:T(8,128)(2,1)S(1)} %get-tuple-element.35), channel_id=1, source_target_pairs={{0,16},{8,24},{16,0},{24,8},{1,17},{9,25},{17,1},{25,9},{2,18},{10... | collective-permute-start | bytes 884744 | tf_op jit(solution)/shard_map/ppermute | solution.py:363
  25.2 13.2 %collective-permute-start.7 = (bf16[3,2,32,768]{3,2,1,0:T(8,128)(2,1)S(1)}, bf16[3,2,32,768]{3,2,1,0:T(8,128)(2,1)S(1)}, u32[]{:S(2)}, u32[]{:S(2)}) collective-permute-start(bf16[3,2,32,768]{3,2,1,0:T(8,128)(2,1)S(1)} %get-tuple-element.36), channel_id=1, source_target_pairs={{0,24},{8,16},{16,8},{24,0},{1,25},{9,17},{17,9},{25,1},{2,26},{10... | collective-permute-start | bytes 884744 | tf_op jit(solution)/shard_map/ppermute | solution.py:363
  25.5 18.3 %collective-permute-start.2 = (bf16[3,2,32,768]{3,2,1,0:T(8,128)(2,1)S(1)}, bf16[3,2,32,768]{3,2,1,0:T(8,128)(2,1)S(1)}, u32[]{:S(2)}, u32[]{:S(2)}) collective-permute-start(bf16[3,2,32,768]{3,2,1,0:T(8,128)(2,1)S(1)} %get-tuple-element.29), channel_id=1, source_target_pairs={{0,8},{8,0},{16,24},{24,16},{1,9},{9,1},{17,25},{25,17},{2,10},{10... | collective-permute-start | bytes 884744 | tf_op jit(solution)/shard_map/ppermute | solution.py:363
  26.7 23.2 %collective-permute-start.3 = (bf16[3,2,32,768]{3,2,1,0:T(8,128)(2,1)S(1)}, bf16[3,2,32,768]{3,2,1,0:T(8,128)(2,1)S(1)}, u32[]{:S(2)}, u32[]{:S(2)}) collective-permute-start(bf16[3,2,32,768]{3,2,1,0:T(8,128)(2,1)S(1)} %get-tuple-element.30), channel_id=1, source_target_pairs={{0,16},{8,24},{16,0},{24,8},{1,17},{9,25},{17,1},{25,9},{2,18},{10... | collective-permute-start | bytes 884744 | tf_op jit(solution)/shard_map/ppermute | solution.py:363
  30.9 21.3 %collective-permute-start.4 = (bf16[3,2,32,768]{3,2,1,0:T(8,128)(2,1)S(1)}, bf16[3,2,32,768]{3,2,1,0:T(8,128)(2,1)S(1)}, u32[]{:S(2)}, u32[]{:S(2)}) collective-permute-start(bf16[3,2,32,768]{3,2,1,0:T(8,128)(2,1)S(1)} %get-tuple-element.31), channel_id=1, source_target_pairs={{0,24},{8,16},{16,8},{24,0},{1,25},{9,17},{17,9},{25,1},{2,26},{10... | collective-permute-start | bytes 884744 | tf_op jit(solution)/shard_map/ppermute | solution.py:363

commit v7 on v6

--- a/solution.py
+++ b/solution.py
@@ -16,8 +16,8 @@
 MIB = 1024 * 1024
 
 
-def build_bands(first, sources, group, kernel, off, band):
-    acq, taps = off.shape[0], kernel.shape[0]
+def build_bands(first, sources, group, kernel, shift, band):
+    acq, taps = band.shape[0], kernel.shape[0]
     gains = kernel[...].astype(jnp.float32) * 0.125
     lane = lax.broadcasted_iota(jnp.int32, gains.shape, 1)
     rows = sum(count for _, count in sources)
@@ -34,7 +34,7 @@
     blocks = CHUNK // LOOK_R
     order = jnp.where(col == (row % blocks) * LOOK_R + row // blocks, 1.0, 0.0).astype(jnp.bfloat16)
     for a in range(acq):
-        tap = base - off[a : a + 1, first : first + CHUNK]
+        tap = base - shift(a)
         total = jnp.zeros((rows, CHUNK), jnp.float32)
         gain = jnp.sum(jnp.where(lane == group[0] * acq + a, gains, 0.0), axis=1, keepdims=True)
         for k in range(taps):
@@ -46,8 +46,8 @@
         band[a] = turned.astype(jnp.bfloat16)
 
 
-def first_kernel(first, groups, group, kernel, off, slc, *rest):
-    outs, (head, tail, slab, band, gains, shifts, sems) = rest[:groups], rest[groups:]
+def first_kernel(first, groups, group, side, kernel, off, slc, *rest):
+    outs, (inner, outer, slab, band, gains, shifts, sems) = rest[:groups], rest[groups:]
     acq, _, lines, cols = slc.shape
     width = cols // groups
 
@@ -68,7 +68,7 @@
         copies[s].start()
     for copy in small:
         copy.wait()
-    build_bands(first, [(0, lines)], group, gains, shifts, band)
+    build_bands(first, [(0, lines)], group, gains, lambda a: shifts[a : a + 1, first : first + CHUNK], band)
     for s in order:
         copies[s].wait()
         at = columns(s)
@@ -76,23 +76,35 @@
             for x in range(2):
                 total = jnp.dot(band[a], slab[a, x, :, at], preferred_element_type=jnp.float32)
                 outs[s][a, x] = total.astype(jnp.bfloat16)
-    head[...] = slab[:, :, :HALO, :]
-    tail[...] = slab[:, :, lines - HALO :, :]
-
-
-def edge_kernel(first, groups, begin, count, halo_at, group, kernel, off, slab, halo, *rest):
+    for even, head, tail in ((0, outer, inner), (1, inner, outer)):
+
+        @pl.when(side[0] == even)
+        def _(head=head, tail=tail):
+            head[...] = slab[:, :, :HALO, :]
+            tail[...] = slab[:, :, lines - HALO :, :]
+
+
+def edge_kernel(groups, parity, count, group, side, kernel, off, slab, halo, *rest):
     outs, band = rest[:groups], rest[groups]
-    acq, _, _, cols = slab.shape
+    acq, _, lines, cols = slab.shape
     width = cols // groups
-    build_bands(first, [(begin, count), (halo_at, HALO)], group, kernel, off, band)
+    bottom = side[0] == parity
+    first = jnp.where(bottom, lines - CHUNK, 0)
+    begin = pl.multiple_of(jnp.where(bottom, lines - count, 0), TILE)
+    outside = jnp.where(bottom, lines, -HALO)
+
+    def shift(a):
+        return jnp.where(bottom, off[a : a + 1, lines - CHUNK :], off[a : a + 1, :CHUNK])
+
+    build_bands(first, [(begin, count), (outside, HALO)], group, kernel, shift, band)
     for s in [*range(1, groups), 0]:
         at = pl.ds(pl.multiple_of((group[0] ^ s) * width, width), width)
         for a in range(acq):
             for x in range(2):
-                lines = jnp.concatenate(
-                    [slab[a, x, begin : begin + count, at], halo[a, x, :, at]], axis=0
+                lines_in = jnp.concatenate(
+                    [slab[a, x, pl.ds(begin, count), at], halo[a, x, :, at]], axis=0
                 )
-                total = jnp.dot(band[a], lines, preferred_element_type=jnp.float32)
+                total = jnp.dot(band[a], lines_in, preferred_element_type=jnp.float32)
                 outs[s][a, x] = total.astype(jnp.bfloat16)
 
 
@@ -109,14 +121,14 @@
     )
 
 
-def resample_first(first, group, kernel, offsets, slc, groups):
+def resample_first(first, group, side, kernel, offsets, slc, groups):
     acq, _, lines, cols = slc.shape
     piece = pltpu.VMEM((acq, 2, CHUNK, cols // groups), jnp.bfloat16)
     halo = pltpu.VMEM((acq, 2, HALO, cols), jnp.bfloat16)
     slab = pltpu.VMEM(slc.shape, jnp.bfloat16)
     return pl.pallas_call(
         functools.partial(first_kernel, first, groups),
-        in_specs=[SMEM, ANY, ANY, ANY],
+        in_specs=[SMEM, SMEM, ANY, ANY, ANY],
         out_specs=[VMEM] * (groups + 3),
         out_shape=[piece] * groups + [halo, halo, slab],
         scratch_shapes=[
@@ -128,22 +140,22 @@
         compiler_params=pltpu.CompilerParams(vmem_limit_bytes=16 * MIB),
         cost_estimate=resample_cost(acq, cols, lines),
         name="resample_first",
-    )(group, kernel, offsets, slc)
-
-
-def resample_edge(first, begin, count, halo_at, group, kernel, offsets, slab, halo, groups):
+    )(group, side, kernel, offsets, slc)
+
+
+def resample_edge(parity, count, group, side, kernel, offsets, slab, halo, groups):
     acq, _, lines, cols = slab.shape
     piece = pltpu.VMEM((acq, 2, CHUNK, cols // groups), jnp.bfloat16)
     return pl.pallas_call(
-        functools.partial(edge_kernel, first, groups, begin, count, halo_at),
-        in_specs=[SMEM, VMEM, VMEM, VMEM, VMEM],
+        functools.partial(edge_kernel, groups, parity, count),
+        in_specs=[SMEM, SMEM, VMEM, VMEM, VMEM, VMEM],
         out_specs=[VMEM] * groups,
         out_shape=[piece] * groups,
         scratch_shapes=[pltpu.VMEM((acq, CHUNK, count + HALO), jnp.bfloat16)],
         compiler_params=pltpu.CompilerParams(vmem_limit_bytes=16 * MIB),
         cost_estimate=resample_cost(acq, cols, count + HALO),
         name="resample_edge",
-    )(group, kernel, offsets, slab, halo)
+    )(group, side, kernel, offsets, slab, halo)
 
 
 def slot_of(low, high):
@@ -240,7 +252,7 @@
     look_sums(blocks, 0, parts, terms, sums, 0, slot_of(0, groups * acq) * 2 * looks)
 
 
-def interfere_kernel(groups, known, place, table, *rest):
+def interfere_kernel(groups, known, spot, table, *rest):
     blocks, rest = rest[:groups], rest[groups:]
     out, parts, terms, sums, flat, inverse, slab, sem = rest[-8:]
     acq, _, lines, width = blocks[0].shape
@@ -268,12 +280,14 @@
         return carry
 
     lax.fori_loop(0, count, select, 0, unroll=max(b for b in range(1, 7) if count % b == 0))
-    for x in range(2):
-        for g in range(looks):
+    copies = []
+    for g in range(looks):
+        for x in range(2):
             slab[x, g] = flat[pl.ds(x * looks + g, count, stride=both), :].T
-    copy = pltpu.make_async_copy(slab, out.at[:, pl.ds(place * looks, looks)], sem)
-    copy.start()
-    copy.wait()
+        copies.append(pltpu.make_async_copy(slab.at[:, g], out.at[:, spot[0] * looks + g], sem.at[g]))
+        copies[-1].start()
+    for copy in copies:
+        copy.wait()
 
 
 def work_space(groups, known, acq, lines, looks):
@@ -318,8 +332,8 @@
     near = [] if near is None else [near]
     extra = [] if before is None else [before]
     return pl.pallas_call(
-        functools.partial(interfere_kernel, groups, known, place),
-        in_specs=[SMEM] + [VMEM] * (groups + len(near)) + [ANY] * len(extra),
+        functools.partial(interfere_kernel, groups, known),
+        in_specs=[SMEM, SMEM] + [VMEM] * (groups + len(near)) + [ANY] * len(extra),
         out_specs=ANY,
         out_shape=pltpu.HBM((2, chunks * looks, windows, count), jnp.float32),
         scratch_shapes=work_space(groups, known, acq, lines, looks)
@@ -328,13 +342,13 @@
             pltpu.VMEM((count * 2 * looks, windows), jnp.float32),
             pltpu.VMEM((total * looks, windows), jnp.float32),
             pltpu.VMEM((2, looks, windows, count), jnp.float32),
-            pltpu.SemaphoreType.DMA,
+            pltpu.SemaphoreType.DMA((looks,)),
         ],
-        input_output_aliases={} if before is None else {1 + groups + len(near): 0},
+        input_output_aliases={} if before is None else {2 + groups + len(near): 0},
         compiler_params=pltpu.CompilerParams(vmem_limit_bytes=16 * MIB),
         cost_estimate=interfere_cost(count, total, lines, width),
         name="interfere",
-    )(table, *blocks, *near, *extra)
+    )(place, table, *blocks, *near, *extra)
 
 
 def pair_table(pairs, groups, acq, mine):
@@ -348,14 +362,14 @@
     acq, _, lines, cols = slc.shape
     groups = lax.axis_size("acq")
     size = lax.axis_size("pix")
+    row = lax.axis_index("pix")
+    odd = row % 2
     group = jnp.reshape(lax.axis_index("acq"), (1,)).astype(jnp.int32)
+    side = jnp.reshape(odd, (1,)).astype(jnp.int32)
     kernel = weights.T
     table = pair_table(pairs, groups, acq, group[0])
     chunks = lines // CHUNK
     reach = CHUNK + TILE * 2
-
-    up = [(i, i + 1) for i in range(size - 1)]
-    down = [(j, i) for i, j in up]
 
     def send(blocks):
         moved = [blocks[0]]
@@ -363,22 +377,29 @@
             moved.append(lax.ppermute(blocks[s], "acq", [(i, i ^ s) for i in range(groups)]))
         return moved
 
-    *blocks, head, tail, slab = resample_first(
-        CHUNK, group, *[pltpu.with_memory_space_constraint(t, pltpu.HBM) for t in (kernel, offsets, slc)], groups
+    def swap(halo, begin):
+        pairs_up = [(i, i + 1) for i in range(begin, size - 1, 2)]
+        return lax.ppermute(halo, "pix", pairs_up + [(j, i) for i, j in pairs_up])
+
+    *blocks, inner, outer, slab = resample_first(
+        CHUNK, group, side, *[pltpu.with_memory_space_constraint(t, pltpu.HBM) for t in (kernel, offsets, slc)], groups
     )
-    above = lax.ppermute(tail, "pix", up)
-    below = lax.ppermute(head, "pix", down)
-    above, below = lax.optimization_barrier((above, below))
+    inside = swap(inner, 0)
+    across = swap(outer, 1)
     middle = send(blocks)
-    top = send(
-        resample_edge(0, 0, reach, -HALO, group, kernel, offsets, slab, above, groups)
+    pieces = resample_edge(0, reach, group, side, kernel, offsets, slab, inside, groups)
+    *pieces, slab = lax.optimization_barrier((*pieces, slab))
+    second = send(pieces)
+    third = send(resample_edge(1, reach, group, side, kernel, offsets, slab, across, groups))
+    low, high = jnp.zeros_like(odd), jnp.full_like(odd, chunks - 1)
+    spots = (
+        jnp.full_like(odd, 1),
+        jnp.where(odd == 0, high, low),
+        jnp.where(odd == 0, low, high),
     )
-    late = resample_edge(
-        lines - CHUNK, lines - reach, reach, lines, group, kernel, offsets, slab, below, groups
-    )
-    bottom = send(late)
     result = None
-    for place, moved, known in ((1, middle, 0), (0, top, 0), (2, bottom, groups - 1)):
+    for spot, moved, known in zip(spots, (middle, second, third), (0, 0, groups - 1)):
+        place = jnp.reshape(spot, (1,)).astype(jnp.int32)
         near = None
         if known:
             mine, result = lax.optimization_barrier((moved[0], result))

time: 56.4 us -> 56.7 us (level)
  waiting for transfers between devices: 19.1 us -> 14.7 us
  Pallas kernels: 21.1 us -> 24.8 us
  local copies, waits for them, and re-layouts: 0.01 us -> 2.89 us
  starting transfers between devices: 15.9 us -> 13.8 us
    ppermute x2, waiting for transfers between devices: 10 us -> 4.43 us  [swap(): return lax.ppermute(halo, 'pix', pairs_up + [(j, i) for i, j in pairs_up])]
    unnamed x6 -> x20, local copies, waits for them, and re-layouts: 0.01 us -> 2.89 us
    pallas_call x5, Pallas kernels: 16.3 us -> 18.9 us  [the longest x3 15.5 us: interfere(): pl.pallas_call(functools.partial(interfere_kernel, groups, known), in_spe...]
    ppermute x2, starting transfers between devices: 5.69 us -> 3.74 us  [swap(): return lax.ppermute(halo, 'pix', pairs_up + [(j, i) for i, j in pairs_up])]
    pallas_call x1, Pallas kernels: 2.46 us -> 3.67 us  [resample_first(): pl.pallas_call(functools.partial(first_kernel, first, groups), in_specs=[...]
    ppermute x9, waiting for transfers between devices: 9.13 us -> 10.3 us  [send(): lax.ppermute(blocks[s], 'acq', [(i, i ^ s) for i in range(groups)])]
  transfers between devices with their start and end apart: 11 -> 11, of which waited for: 4 -> 4; matrix products, arithmetic and copies ran while one was open for 0% -> 0% of each run, Pallas kernels for 26% -> 31%
where the time goes in v7:
time: 56.7 us; the launch traced here: 56.4 us
  Pallas kernels  24.8 us (44%)
  waiting for transfers between devices  14.7 us (26%)
  starting transfers between devices  13.8 us (24%)
  local copies, waits for them, and re-layouts  2.89 us (5%)
    pallas_call x3, Pallas kernels, interfere(): pl.pallas_call(functools.partial(interfere_kernel, groups, known), in_spe...  15.5 us
    ppermute x9, waiting for transfers between devices, send(): lax.ppermute(blocks[s], 'acq', [(i, i ^ s) for i in range(groups)])  10.3 us
    ppermute x9, starting transfers between devices, send(): lax.ppermute(blocks[s], 'acq', [(i, i ^ s) for i in range(groups)])  10 us
    ppermute x2, waiting for transfers between devices, swap(): return lax.ppermute(halo, 'pix', pairs_up + [(j, i) for i, j in pairs_up])  4.43 us
    ppermute x2, starting transfers between devices, swap(): return lax.ppermute(halo, 'pix', pairs_up + [(j, i) for i, j in pairs_up])  3.74 us
    pallas_call x1, Pallas kernels, resample_first(): pl.pallas_call(functools.partial(first_kernel, first, groups), in_specs=[...  3.67 us
    pallas_call x2, Pallas kernels, resample_edge(): pl.pallas_call(functools.partial(edge_kernel, groups, parity, count), in_...  3.34 us
    unnamed x20, local copies, waits for them, and re-layouts  2.89 us
  transfers between devices with their start and end apart: 11, of which 4 were waited for; matrix products, arithmetic and copies ran while one was open for 0% of the time, Pallas kernels for 31%

profile of v7, /device:TPU:9, one launch (start us, length us, event | category | flops | bytes accessed | tf_op | source)
XLA Modules:
  0.0 56.4 jit_solution(16792591643992434559)
XLA Ops:
  0.0 0.0 copy-start.5
  0.0 3.7 %resample_first.1 = (bf16[3,2,32,768]{3,2,1,0:T(8,128)(2,1)S(1)}, bf16[3,2,32,768]{3,2,1,0:T(8,128)(2,1)}, bf16[3,2,32,768]{3,2,1,0:T(8,128)(2,1)}, bf16[3,2,32,...) custom-call(s32[1]{0:T(128)} %bitcast.3.group, ...), custom_call_target="tpu_custom_call" | custom-call | flops 113246208 | bytes 4718592 | tf_op jit(solution)/shard_map/resample_first/pallas_call | solution.py:129
  3.7 0.0 copy-start
  3.7 0.7 %copy-done = bf16[3,2,32,768]{3,2,1,0:T(8,128)(2,1)} copy-done((bf16[3,2,32,768]{3,2,1,0:T(8,128)(2,1)}, bf16[3,2,32,768]{3,2,1,0:T(8,128)(2,1)S(1)}, u32[]{:S(2)}) %copy-start) | copy-done | bytes 294936
  4.4 0.7 %collective-permute-start = (bf16[3,2,24,3072]{3,2,1,0:T(8,128)(2,1)S(1)}, bf16[3,2,24,3072]{3,2,1,0:T(8,128)(2,1)S(1)}, u32[]{:S(2)}, u32[]{:S(2)}) collective-permute-start(bf16[3,2,24,3072]{3,2,1,0:T(8,128)(2,1)S(1)} %get-tuple-element.28), channel_id=1, source_target_pairs={{0,1},{2,3},{4,5},{6,7},{1,0},{3,2},{5,4},{7,6},{8,9},{10,11},{12,... | collective-permute-start | bytes 2654216 | tf_op jit(solution)/shard_map/ppermute | solution.py:382
  5.1 3.1 %collective-permute-start.1 = (bf16[3,2,24,3072]{3,2,1,0:T(8,128)(2,1)}, bf16[3,2,24,3072]{3,2,1,0:T(8,128)(2,1)}, u32[]{:S(2)}, u32[]{:S(2)}) collective-permute-start(bf16[3,2,24,3072]{3,2,1,0:T(8,128)(2,1)} %get-tuple-element.34), channel_id=1, source_target_pairs={{1,2},{3,4},{5,6},{2,1},{4,3},{6,5},{9,10},{11,12},{13,14},{10,9},... | collective-permute-start | bytes 2654216 | tf_op jit(solution)/shard_map/ppermute | solution.py:382
  8.2 1.3 %collective-permute-start.8 = (bf16[3,2,32,768]{3,2,1,0:T(8,128)(2,1)}, bf16[3,2,32,768]{3,2,1,0:T(8,128)(2,1)}, u32[]{:S(2)}, u32[]{:S(2)}) collective-permute-start(bf16[3,2,32,768]{3,2,1,0:T(8,128)(2,1)} %get-tuple-element.44), channel_id=1, source_target_pairs={{0,8},{8,0},{16,24},{24,16},{1,9},{9,1},{17,25},{25,17},{2,10},{10... | collective-permute-start | bytes 884744 | tf_op jit(solution)/shard_map/ppermute | solution.py:377
  9.4 1.2 %collective-permute-start.9 = (bf16[3,2,32,768]{3,2,1,0:T(8,128)(2,1)}, bf16[3,2,32,768]{3,2,1,0:T(8,128)(2,1)}, u32[]{:S(2)}, u32[]{:S(2)}) collective-permute-start(bf16[3,2,32,768]{3,2,1,0:T(8,128)(2,1)} %get-tuple-element.45), channel_id=1, source_target_pairs={{0,16},{8,24},{16,0},{24,8},{1,17},{9,25},{17,1},{25,9},{2,18},{10... | collective-permute-start | bytes 884744 | tf_op jit(solution)/shard_map/ppermute | solution.py:377
  10.7 0.2 collective-permute-start.10
  10.9 0.0 collective-permute-done.halo
  10.9 0.0 copy-done.4
  10.9 0.0 copy-done.5
  10.9 0.0 copy-start.9
  10.9 1.3 %resample_edge.2 = (bf16[3,2,32,768]{3,2,1,0:T(8,128)(2,1)S(1)}, bf16[3,2,32,768]{3,2,1,0:T(8,128)(2,1)}, bf16[3,2,32,768]{3,2,1,0:T(8,128)(2,1)S(1)}, bf16[3,2,32,768]{3,2,1,0:T(8,128)(2,1)S(1)}) custom-call(s32[1]{0:T(128)} %bitcast.3.group, s32[1]{0:T(128)} %bitcast.4.side, bf16[8,12]{1,0:T(8,128)(2,1)S(1)} %bitcast.19, s32[3,96]{1,0:T(4,128)S(1)} %copy-done.5, ...), custom_call_target="tpu_custom_call" | custom-call | flops 103809024 | bytes 4423680 | tf_op jit(solution)/shard_map/resample_edge/pallas_call | solution.py:149
  12.2 0.0 copy-start.2
  12.2 0.7 %copy-done.2 = bf16[3,2,32,768]{3,2,1,0:T(8,128)(2,1)} copy-done((bf16[3,2,32,768]{3,2,1,0:T(8,128)(2,1)}, bf16[3,2,32,768]{3,2,1,0:T(8,128)(2,1)S(1)}, u32[]{:S(2)}) %copy-start.2) | copy-done | bytes 294936
  12.9 0.0 copy-start.6
  12.9 0.7 %copy-done.6 = bf16[3,2,32,768]{3,2,1,0:T(8,128)(2,1)} copy-done((bf16[3,2,32,768]{3,2,1,0:T(8,128)(2,1)}, bf16[3,2,32,768]{3,2,1,0:T(8,128)(2,1)S(1)}, u32[]{:S(2)}) %copy-start.6) | copy-done | bytes 294936
  13.6 0.0 copy-start.8
  13.6 0.7 %copy-done.8 = bf16[3,2,32,768]{3,2,1,0:T(8,128)(2,1)} copy-done((bf16[3,2,32,768]{3,2,1,0:T(8,128)(2,1)}, bf16[3,2,32,768]{3,2,1,0:T(8,128)(2,1)S(1)}, u32[]{:S(2)}) %copy-start.8) | copy-done | bytes 294936
  14.3 1.2 %collective-permute-start.5 = (bf16[3,2,32,768]{3,2,1,0:T(8,128)(2,1)}, bf16[3,2,32,768]{3,2,1,0:T(8,128)(2,1)}, u32[]{:S(2)}, u32[]{:S(2)}) collective-permute-start(bf16[3,2,32,768]{3,2,1,0:T(8,128)(2,1)} %get-tuple-element.40), channel_id=1, source_target_pairs={{0,8},{8,0},{16,24},{24,16},{1,9},{9,1},{17,25},{25,17},{2,10},{10... | collective-permute-start | bytes 884744 | tf_op jit(solution)/shard_map/ppermute | solution.py:377
  15.5 0.0 copy-done.9
  15.6 0.0 copy-start.7
  15.6 0.0 copy-start.1
  15.6 4.4 %collective-permute-done.1.halo = bf16[3,2,24,3072]{3,2,1,0:T(8,128)(2,1)} collective-permute-done((bf16[3,2,24,3072]{3,2,1,0:T(8,128)(2,1)}, bf16[3,2,24,3072]{3,2,1,0:T(8,128)(2,1)}, u32[]{:S(2)}, u32[]{:S(2)}) %collective-permute-start.1) | collective-permute-done | bytes 884768 | tf_op jit(solution)/shard_map/ppermute | solution.py:382
  20.0 1.2 %collective-permute-start.6 = (bf16[3,2,32,768]{3,2,1,0:T(8,128)(2,1)}, bf16[3,2,32,768]{3,2,1,0:T(8,128)(2,1)S(1)}, u32[]{:S(2)}, u32[]{:S(2)}) collective-permute-start(bf16[3,2,32,768]{3,2,1,0:T(8,128)(2,1)} %copy-done.8), channel_id=1, source_target_pairs={{0,16},{8,24},{16,0},{24,8},{1,17},{9,25},{17,1},{25,9},{2,18},{10... | collective-permute-start | bytes 884744 | tf_op jit(solution)/shard_map/ppermute | solution.py:377
  21.3 2.1 %resample_edge.3 = (bf16[3,2,32,768]{3,2,1,0:T(8,128)(2,1)S(1)}, bf16[3,2,32,768]{3,2,1,0:T(8,128)(2,1)S(1)}, bf16[3,2,32,768]{3,2,1,0:T(8,128)(2,1)S(1)}, bf16[3,2,32,768]{3,2,1,0:T(8,128)(2,1)S(1)}) custom-call(s32[1]{0:T(128)} %bitcast.3.group, s32[1]{0:T(128)} %bitcast.4.side, bf16[8,12]{1,0:T(8,128)(2,1)S(1)} %bitcast.20, s32[3,96]{1,0:T(4,128)S(1)} %copy-done.5, ...), custom_call_target="tpu_custom_call" | custom-call | flops 103809024 | bytes 4423680 | tf_op jit(solution)/shard_map/resample_edge/pallas_call | solution.py:149
  23.3 0.0 collective-permute-done.8.rest_1_
  23.4 0.0 copy-done.7
  23.4 1.2 %collective-permute-start.7 = (bf16[3,2,32,768]{3,2,1,0:T(8,128)(2,1)S(1)}, bf16[3,2,32,768]{3,2,1,0:T(8,128)(2,1)S(1)}, u32[]{:S(2)}, u32[]{:S(2)}) collective-permute-start(bf16[3,2,32,768]{3,2,1,0:T(8,128)(2,1)S(1)} %copy-done.7), channel_id=1, source_target_pairs={{0,24},{8,16},{16,8},{24,0},{1,25},{9,17},{17,9},{25,1},{2,26},{10... | collective-permute-start | bytes 884744 | tf_op jit(solution)/shard_map/ppermute | solution.py:377
  24.6 0.4 collective-permute-done.9.rest_2_
  25.0 0.0 collective-permute-start.2
  25.0 0.0 collective-permute-done.10.rest_3_
  25.0 1.5 %collective-permute-start.3 = (bf16[3,2,32,768]{3,2,1,0:T(8,128)(2,1)S(1)}, bf16[3,2,32,768]{3,2,1,0:T(8,128)(2,1)S(1)}, u32[]{:S(2)}, u32[]{:S(2)}) collective-permute-start(bf16[3,2,32,768]{3,2,1,0:T(8,128)(2,1)S(1)} %get-tuple-element.37), channel_id=1, source_target_pairs={{0,16},{8,24},{16,0},{24,8},{1,17},{9,25},{17,1},{25,9},{2,18},{10... | collective-permute-start | bytes 884744 | tf_op jit(solution)/shard_map/ppermute | solution.py:377
  26.5 3.6 %collective-permute-done.5.rest_1_ = bf16[3,2,32,768]{3,2,1,0:T(8,128)(2,1)} collective-permute-done((bf16[3,2,32,768]{3,2,1,0:T(8,128)(2,1)}, bf16[3,2,32,768]{3,2,1,0:T(8,128)(2,1)}, u32[]{:S(2)}, u32[]{:S(2)}) %collective-permute-start.5) | collective-permute-done | bytes 294944 | tf_op jit(solution)/shard_map/ppermute | solution.py:377
  30.1 2.2 %collective-permute-start.4 = (bf16[3,2,32,768]{3,2,1,0:T(8,128)(2,1)S(1)}, bf16[3,2,32,768]{3,2,1,0:T(8,128)(2,1)S(1)}, u32[]{:S(2)}, u32[]{:S(2)}) collective-permute-start(bf16[3,2,32,768]{3,2,1,0:T(8,128)(2,1)S(1)} %get-tuple-element.38), channel_id=1, source_target_pairs={{0,24},{8,16},{16,8},{24,0},{1,25},{9,17},{17,9},{25,1},{2,26},{10... | collective-permute-start | bytes 884744 | tf_op jit(solution)/shard_map/ppermute | solution.py:377
  32.3 0.0 copy-done.1
  32.3 0.0 copy-start.3
  32.3 5.9 %interfere.3.rest_4_ = f32[2,24,48,60]{3,2,1,0:T(8,128)} custom-call(s32[1]{0:T(128)} %constant.56.clone.1.spot, s32[4,60]{1,0:T(4,128)S(1)} %pad_add_fusion.table, bf16[3,2,32,768]{3,2,1,0:T(8,128)(2,1)S(1)} %copy-done.1, bf16[3,2,32,768]{3,2,1,0:T(8,128)(2,1)} %collective-permute-done.8.rest_1_, bf16[3,2,32,768]{3,2,1,0:T(8,128)(2,1)} %collective-permute-done.9.rest_2_, ...), custom_call_target="tpu_custom_call" | custom-call | flops 11796480 | bytes 14155776 | tf_op jit(solution)/shard_map/interfere/pallas_call | solution.py:334
  38.2 0.0 collective-permute-done.6.rest_2_
  38.2 0.0 collective-permute-done.7.rest_3_
  38.2 0.0 copy-done.3
  38.2 5.7 %interfere.4.rest_5_ = f32[2,24,48,60]{3,2,1,0:T(8,128)} custom-call(s32[1]{0:T(128)} %bitcast.6.spot, s32[4,60]{1,0:T(4,128)S(1)} %pad_add_fusion.table, bf16[3,2,32,768]{3,2,1,0:T(8,128)(2,1)S(1)} %copy-done.3, bf16[3,2,32,768]{3,2,1,0:T(8,128)(2,1)} %collective-permute-done.5.rest_1_, ...), custom_call_target="tpu_custom_call", output_to_operand_aliasing={{}: (6, {})} | custom-call | flops 11796480 | bytes 14155776 | tf_op jit(solution)/shard_map/interfere/pallas_call | solution.py:334
  43.9 0.0 collective-permute-done.2.rest_1_
  43.9 6.2 %collective-permute-done.3.rest_2_ = bf16[3,2,32,768]{3,2,1,0:T(8,128)(2,1)S(1)} collective-permute-done((bf16[3,2,32,768]{3,2,1,0:T(8,128)(2,1)S(1)}, bf16[3,2,32,768]{3,2,1,0:T(8,128)(2,1)S(1)}, u32[]{:S(2)}, u32[]{:S(2)}) %collective-permute-start.3) | collective-permute-done | bytes 294944 | tf_op jit(solution)/shard_map/ppermute | solution.py:377
  50.2 2.3 %interfere_near.1.rest_4_ = f32[648,48]{1,0:T(8,128)S(1)} custom-call(bf16[3,2,32,768]{3,2,1,0:T(8,128)(2,1)S(1)} %get-tuple-element.47.rest_0_, bf16[3,2,32,768]{3,2,1,0:T(8,128)(2,1)S(1)} %collective-permute-done.2.rest_1_, bf16[3,2,32,768]{3,2,1,0:T(8,128)(2,1)S(1)} %collective-permute-done.3.rest_2_), custom_call_target="tpu_custom_call" | custom-call | flops 7077888 | bytes 10616832 | tf_op jit(solution)/shard_map/interfere_near/pallas_call | solution.py:315
  52.5 0.0 collective-permute-done.4.rest_3_
  52.5 3.9 %interfere.5 = f32[2,24,48,60]{3,2,1,0:T(8,128)} custom-call(s32[1]{0:T(128)} %bitcast.spot, s32[4,60]{1,0:T(4,128)S(1)} %pad_add_fusion.table, bf16[3,2,32,768]{3,2,1,0:T(8,128)(2,1)S(1)} %get-tuple-element.47.rest_0_, bf16[3,2,32,768]{3,2,1,0:T(8,128)(2,1)S(1)} %collective-permute-done.2.rest_1_, ...), custom_call_target="tpu_custom_call", output_to_operand_aliasing={{}: (7, {})} | custom-call | flops 11796480 | bytes 14155776 | tf_op jit(solution)/shard_map/interfere/pallas_call | solution.py:334
  (5 shorter events, 0.1 us)
Async XLA Ops:
  0.0 10.9 %copy-start.4 = (bf16[12,8]{0,1:T(8,128)(2,1)S(1)}, bf16[12,8]{0,1:T(8,128)(2,1)}, u32[]{:S(2)}) copy-start(bf16[12,8]{0,1:T(8,128)(2,1)} %param.6) | copy-start | bytes 580
  0.0 10.9 %copy-start.5 = (s32[3,96]{1,0:T(4,128)S(1)}, s32[3,96]{1,0:T(4,128)}, u32[]{:S(2)}) copy-start(s32[3,96]{1,0:T(4,128)} %off.5) | copy-start | bytes 3460
  3.7 0.7 %copy-start = (bf16[3,2,32,768]{3,2,1,0:T(8,128)(2,1)}, bf16[3,2,32,768]{3,2,1,0:T(8,128)(2,1)S(1)}, u32[]{:S(2)}) copy-start(bf16[3,2,32,768]{3,2,1,0:T(8,128)(2,1)S(1)} %get-tuple-element.43.rest_0_) | copy-start | bytes 884740
  4.4 6.5 %collective-permute-start = (bf16[3,2,24,3072]{3,2,1,0:T(8,128)(2,1)S(1)}, bf16[3,2,24,3072]{3,2,1,0:T(8,128)(2,1)S(1)}, u32[]{:S(2)}, u32[]{:S(2)}) collective-permute-start(bf16[3,2,24,3072]{3,2,1,0:T(8,128)(2,1)S(1)} %get-tuple-element.28), channel_id=1, source_target_pairs={{0,1},{2,3},{4,5},{6,7},{1,0},{3,2},{5,4},{7,6},{8,9},{10,11},{12,... | collective-permute-start | bytes 2654216 | tf_op jit(solution)/shard_map/ppermute | solution.py:382
  5.1 15.0 %collective-permute-start.1 = (bf16[3,2,24,3072]{3,2,1,0:T(8,128)(2,1)}, bf16[3,2,24,3072]{3,2,1,0:T(8,128)(2,1)}, u32[]{:S(2)}, u32[]{:S(2)}) collective-permute-start(bf16[3,2,24,3072]{3,2,1,0:T(8,128)(2,1)} %get-tuple-element.34), channel_id=1, source_target_pairs={{1,2},{3,4},{5,6},{2,1},{4,3},{6,5},{9,10},{11,12},{13,14},{10,9},... | collective-permute-start | bytes 2654216 | tf_op jit(solution)/shard_map/ppermute | solution.py:382
  8.2 15.2 %collective-permute-start.8 = (bf16[3,2,32,768]{3,2,1,0:T(8,128)(2,1)}, bf16[3,2,32,768]{3,2,1,0:T(8,128)(2,1)}, u32[]{:S(2)}, u32[]{:S(2)}) collective-permute-start(bf16[3,2,32,768]{3,2,1,0:T(8,128)(2,1)} %get-tuple-element.44), channel_id=1, source_target_pairs={{0,8},{8,0},{16,24},{24,16},{1,9},{9,1},{17,25},{25,17},{2,10},{10... | collective-permute-start | bytes 884744 | tf_op jit(solution)/shard_map/ppermute | solution.py:377
  9.4 15.5 %collective-permute-start.9 = (bf16[3,2,32,768]{3,2,1,0:T(8,128)(2,1)}, bf16[3,2,32,768]{3,2,1,0:T(8,128)(2,1)}, u32[]{:S(2)}, u32[]{:S(2)}) collective-permute-start(bf16[3,2,32,768]{3,2,1,0:T(8,128)(2,1)} %get-tuple-element.45), channel_id=1, source_target_pairs={{0,16},{8,24},{16,0},{24,8},{1,17},{9,25},{17,1},{25,9},{2,18},{10... | collective-permute-start | bytes 884744 | tf_op jit(solution)/shard_map/ppermute | solution.py:377
  10.7 14.3 %collective-permute-start.10 = (bf16[3,2,32,768]{3,2,1,0:T(8,128)(2,1)}, bf16[3,2,32,768]{3,2,1,0:T(8,128)(2,1)}, u32[]{:S(2)}, u32[]{:S(2)}) collective-permute-start(bf16[3,2,32,768]{3,2,1,0:T(8,128)(2,1)} %get-tuple-element.46), channel_id=1, source_target_pairs={{0,24},{8,16},{16,8},{24,0},{1,25},{9,17},{17,9},{25,1},{2,26},{10... | collective-permute-start | bytes 884744 | tf_op jit(solution)/shard_map/ppermute | solution.py:377
  10.9 4.7 %copy-start.9 = (s32[60,2]{0,1:T(2,128)S(1)}, s32[60,2]{0,1:T(2,128)}, u32[]{:S(2)}) copy-start(s32[60,2]{0,1:T(2,128)} %param.7) | copy-start | bytes 1444
  12.2 0.7 %copy-start.2 = (bf16[3,2,32,768]{3,2,1,0:T(8,128)(2,1)}, bf16[3,2,32,768]{3,2,1,0:T(8,128)(2,1)S(1)}, u32[]{:S(2)}) copy-start(bf16[3,2,32,768]{3,2,1,0:T(8,128)(2,1)S(1)} %get-tuple-element.39.rest_0_) | copy-start | bytes 884740
  12.9 0.7 %copy-start.6 = (bf16[3,2,32,768]{3,2,1,0:T(8,128)(2,1)}, bf16[3,2,32,768]{3,2,1,0:T(8,128)(2,1)S(1)}, u32[]{:S(2)}) copy-start(bf16[3,2,32,768]{3,2,1,0:T(8,128)(2,1)S(1)} %get-tuple-element.42) | copy-start | bytes 884740
  13.6 0.7 %copy-start.8 = (bf16[3,2,32,768]{3,2,1,0:T(8,128)(2,1)}, bf16[3,2,32,768]{3,2,1,0:T(8,128)(2,1)S(1)}, u32[]{:S(2)}) copy-start(bf16[3,2,32,768]{3,2,1,0:T(8,128)(2,1)S(1)} %get-tuple-element.41) | copy-start | bytes 884740
  14.3 15.8 %collective-permute-start.5 = (bf16[3,2,32,768]{3,2,1,0:T(8,128)(2,1)}, bf16[3,2,32,768]{3,2,1,0:T(8,128)(2,1)}, u32[]{:S(2)}, u32[]{:S(2)}) collective-permute-start(bf16[3,2,32,768]{3,2,1,0:T(8,128)(2,1)} %get-tuple-element.40), channel_id=1, source_target_pairs={{0,8},{8,0},{16,24},{24,16},{1,9},{9,1},{17,25},{25,17},{2,10},{10... | collective-permute-start | bytes 884744 | tf_op jit(solution)/shard_map/ppermute | solution.py:377
  15.6 7.8 %copy-start.7 = (bf16[3,2,32,768]{3,2,1,0:T(8,128)(2,1)S(1)}, bf16[3,2,32,768]{3,2,1,0:T(8,128)(2,1)}, u32[]{:S(2)}) copy-start(bf16[3,2,32,768]{3,2,1,0:T(8,128)(2,1)} %copy-done.6) | copy-start | bytes 884740
  15.6 16.7 %copy-start.1 = (bf16[3,2,32,768]{3,2,1,0:T(8,128)(2,1)S(1)}, bf16[3,2,32,768]{3,2,1,0:T(8,128)(2,1)}, u32[]{:S(2)}) copy-start(bf16[3,2,32,768]{3,2,1,0:T(8,128)(2,1)} %copy-done) | copy-start | bytes 884740
  20.0 18.2 %collective-permute-start.6 = (bf16[3,2,32,768]{3,2,1,0:T(8,128)(2,1)}, bf16[3,2,32,768]{3,2,1,0:T(8,128)(2,1)S(1)}, u32[]{:S(2)}, u32[]{:S(2)}) collective-permute-start(bf16[3,2,32,768]{3,2,1,0:T(8,128)(2,1)} %copy-done.8), channel_id=1, source_target_pairs={{0,16},{8,24},{16,0},{24,8},{1,17},{9,25},{17,1},{25,9},{2,18},{10... | collective-permute-start | bytes 884744 | tf_op jit(solution)/shard_map/ppermute | solution.py:377
  23.4 14.8 %collective-permute-start.7 = (bf16[3,2,32,768]{3,2,1,0:T(8,128)(2,1)S(1)}, bf16[3,2,32,768]{3,2,1,0:T(8,128)(2,1)S(1)}, u32[]{:S(2)}, u32[]{:S(2)}) collective-permute-start(bf16[3,2,32,768]{3,2,1,0:T(8,128)(2,1)S(1)} %copy-done.7), channel_id=1, source_target_pairs={{0,24},{8,16},{16,8},{24,0},{1,25},{9,17},{17,9},{25,1},{2,26},{10... | collective-permute-start | bytes 884744 | tf_op jit(solution)/shard_map/ppermute | solution.py:377
  25.0 18.9 %collective-permute-start.2 = (bf16[3,2,32,768]{3,2,1,0:T(8,128)(2,1)S(1)}, bf16[3,2,32,768]{3,2,1,0:T(8,128)(2,1)S(1)}, u32[]{:S(2)}, u32[]{:S(2)}) collective-permute-start(bf16[3,2,32,768]{3,2,1,0:T(8,128)(2,1)S(1)} %get-tuple-element.36), channel_id=1, source_target_pairs={{0,8},{8,0},{16,24},{24,16},{1,9},{9,1},{17,25},{25,17},{2,10},{10... | collective-permute-start | bytes 884744 | tf_op jit(solution)/shard_map/ppermute | solution.py:377
  25.0 25.2 %collective-permute-start.3 = (bf16[3,2,32,768]{3,2,1,0:T(8,128)(2,1)S(1)}, bf16[3,2,32,768]{3,2,1,0:T(8,128)(2,1)S(1)}, u32[]{:S(2)}, u32[]{:S(2)}) collective-permute-start(bf16[3,2,32,768]{3,2,1,0:T(8,128)(2,1)S(1)} %get-tuple-element.37), channel_id=1, source_target_pairs={{0,16},{8,24},{16,0},{24,8},{1,17},{9,25},{17,1},{25,9},{2,18},{10... | collective-permute-start | bytes 884744 | tf_op jit(solution)/shard_map/ppermute | solution.py:377
  30.1 22.4 %collective-permute-start.4 = (bf16[3,2,32,768]{3,2,1,0:T(8,128)(2,1)S(1)}, bf16[3,2,32,768]{3,2,1,0:T(8,128)(2,1)S(1)}, u32[]{:S(2)}, u32[]{:S(2)}) collective-permute-start(bf16[3,2,32,768]{3,2,1,0:T(8,128)(2,1)S(1)} %get-tuple-element.38), channel_id=1, source_target_pairs={{0,24},{8,16},{16,8},{24,0},{1,25},{9,17},{17,9},{25,1},{2,26},{10... | collective-permute-start | bytes 884744 | tf_op jit(solution)/shard_map/ppermute | solution.py:377
  32.3 5.9 %copy-start.3 = (bf16[3,2,32,768]{3,2,1,0:T(8,128)(2,1)S(1)}, bf16[3,2,32,768]{3,2,1,0:T(8,128)(2,1)}, u32[]{:S(2)}) copy-start(bf16[3,2,32,768]{3,2,1,0:T(8,128)(2,1)} %copy-done.2) | copy-start | bytes 884740

commit v8 on v7

--- a/solution.py
+++ b/solution.py
@@ -46,6 +46,18 @@
         band[a] = turned.astype(jnp.bfloat16)
 
 
+def copy_edge(bottom, slab, halo):
+    lines = slab.shape[2]
+
+    @pl.when(bottom)
+    def _():
+        halo[...] = slab[:, :, lines - HALO :, :]
+
+    @pl.when(jnp.logical_not(bottom))
+    def _():
+        halo[...] = slab[:, :, :HALO, :]
+
+
 def first_kernel(first, groups, group, side, kernel, off, slc, *rest):
     outs, (inner, outer, slab, band, gains, shifts, sems) = rest[:groups], rest[groups:]
     acq, _, lines, cols = slc.shape
@@ -76,16 +88,12 @@
             for x in range(2):
                 total = jnp.dot(band[a], slab[a, x, :, at], preferred_element_type=jnp.float32)
                 outs[s][a, x] = total.astype(jnp.bfloat16)
-    for even, head, tail in ((0, outer, inner), (1, inner, outer)):
-
-        @pl.when(side[0] == even)
-        def _(head=head, tail=tail):
-            head[...] = slab[:, :, :HALO, :]
-            tail[...] = slab[:, :, lines - HALO :, :]
-
-
-def edge_kernel(groups, parity, count, group, side, kernel, off, slab, halo, *rest):
-    outs, band = rest[:groups], rest[groups]
+    copy_edge(side[0] == 0, slab, inner)
+    copy_edge(side[0] == 1, slab, outer)
+
+
+def edge_kernel(groups, parity, count, group, side, kernel, off, slab, halo, _, *rest):
+    outs, band = rest[:groups], rest[-1]
     acq, _, lines, cols = slab.shape
     width = cols // groups
     bottom = side[0] == parity
@@ -137,25 +145,25 @@
             pltpu.VMEM(offsets.shape, offsets.dtype),
             pltpu.SemaphoreType.DMA((groups + 2,)),
         ],
-        compiler_params=pltpu.CompilerParams(vmem_limit_bytes=16 * MIB),
+        compiler_params=pltpu.CompilerParams(vmem_limit_bytes=10 * MIB),
         cost_estimate=resample_cost(acq, cols, lines),
         name="resample_first",
     )(group, side, kernel, offsets, slc)
 
 
-def resample_edge(parity, count, group, side, kernel, offsets, slab, halo, groups):
+def resample_edge(parity, count, group, side, kernel, offsets, slab, halo, after, groups):
     acq, _, lines, cols = slab.shape
     piece = pltpu.VMEM((acq, 2, CHUNK, cols // groups), jnp.bfloat16)
     return pl.pallas_call(
         functools.partial(edge_kernel, groups, parity, count),
-        in_specs=[SMEM, SMEM, VMEM, VMEM, VMEM, VMEM],
+        in_specs=[SMEM, SMEM, VMEM, VMEM, VMEM, VMEM, ANY],
         out_specs=[VMEM] * groups,
         out_shape=[piece] * groups,
         scratch_shapes=[pltpu.VMEM((acq, CHUNK, count + HALO), jnp.bfloat16)],
-        compiler_params=pltpu.CompilerParams(vmem_limit_bytes=16 * MIB),
+        compiler_params=pltpu.CompilerParams(vmem_limit_bytes=10 * MIB),
         cost_estimate=resample_cost(acq, cols, count + HALO),
         name="resample_edge",
-    )(group, side, kernel, offsets, slab, halo)
+    )(group, side, kernel, offsets, slab, halo, after)
 
 
 def slot_of(low, high):
@@ -318,7 +326,7 @@
         out_specs=VMEM,
         out_shape=pltpu.VMEM(((slot_of(0, total) * 2 + total) * looks, windows), jnp.float32),
         scratch_shapes=work_space(groups, 0, acq, lines, looks),
-        compiler_params=pltpu.CompilerParams(vmem_limit_bytes=16 * MIB),
+        compiler_params=pltpu.CompilerParams(vmem_limit_bytes=8 * MIB),
         cost_estimate=interfere_cost(slot_of(0, total), total, lines, width),
         name="interfere_near",
     )(*blocks)
@@ -345,7 +353,7 @@
             pltpu.SemaphoreType.DMA((looks,)),
         ],
         input_output_aliases={} if before is None else {2 + groups + len(near): 0},
-        compiler_params=pltpu.CompilerParams(vmem_limit_bytes=16 * MIB),
+        compiler_params=pltpu.CompilerParams(vmem_limit_bytes=8 * MIB),
         cost_estimate=interfere_cost(count, total, lines, width),
         name="interfere",
     )(place, table, *blocks, *near, *extra)
@@ -385,12 +393,13 @@
         CHUNK, group, side, *[pltpu.with_memory_space_constraint(t, pltpu.HBM) for t in (kernel, offsets, slc)], groups
     )
     inside = swap(inner, 0)
+    middle = send(blocks)
+    pieces = resample_edge(0, reach, group, side, kernel, offsets, slab, inside, inner, groups)
     across = swap(outer, 1)
-    middle = send(blocks)
-    pieces = resample_edge(0, reach, group, side, kernel, offsets, slab, inside, groups)
-    *pieces, slab = lax.optimization_barrier((*pieces, slab))
     second = send(pieces)
-    third = send(resample_edge(1, reach, group, side, kernel, offsets, slab, across, groups))
+    third = send(
+        resample_edge(1, reach, group, side, kernel, offsets, slab, across, middle[3], groups)
+    )
     low, high = jnp.zeros_like(odd), jnp.full_like(odd, chunks - 1)
     spots = (
         jnp.full_like(odd, 1),

time: 56.7 us -> 53.9 us (0.951); the launches traced: 56.4 us -> 53 us
  waiting for transfers between devices: 14.7 us -> 10.6 us
  starting transfers between devices: 13.8 us -> 14.5 us
    ppermute x2, waiting for transfers between devices: 4.43 us -> 0.58 us  [swap(): return lax.ppermute(halo, 'pix', pairs_up + [(j, i) for i, j in pairs_up])]
    ppermute x9, starting transfers between devices: 10 us -> 10.8 us  [send(): lax.ppermute(blocks[s], 'acq', [(i, i ^ s) for i in range(groups)])]
    unnamed x20 -> x18, local copies, waits for them, and re-layouts: 2.89 us -> 2.87 us
  transfers between devices with their start and end apart: 11 -> 11, of which waited for: 4 -> 4; matrix products, arithmetic and copies ran while one was open for 0% -> 0% of each run, Pallas kernels for 31% -> 33%
where the time goes in v8:
time: 53.9 us; the launch traced here: 53 us
  Pallas kernels  24.8 us (46%)
  starting transfers between devices  14.5 us (27%)
  waiting for transfers between devices  10.6 us (20%)
  local copies, waits for them, and re-layouts  2.88 us (5%)
    pallas_call x3, Pallas kernels, interfere(): pl.pallas_call(functools.partial(interfere_kernel, groups, known), in_spe...  15.5 us
    ppermute x9, starting transfers between devices, send(): lax.ppermute(blocks[s], 'acq', [(i, i ^ s) for i in range(groups)])  10.8 us
    ppermute x9, waiting for transfers between devices, send(): lax.ppermute(blocks[s], 'acq', [(i, i ^ s) for i in range(groups)])  9.99 us
    ppermute x2, starting transfers between devices, swap(): return lax.ppermute(halo, 'pix', pairs_up + [(j, i) for i, j in pairs_up])  3.74 us
    pallas_call x1, Pallas kernels, resample_first(): pl.pallas_call(functools.partial(first_kernel, first, groups), in_specs=[...  3.67 us
    pallas_call x2, Pallas kernels, resample_edge(): pl.pallas_call(functools.partial(edge_kernel, groups, parity, count), in_...  3.37 us
    unnamed x18, local copies, waits for them, and re-layouts  2.87 us
    pallas_call x1, Pallas kernels, interfere_near(): pl.pallas_call(functools.partial(near_kernel, groups), in_specs=[VMEM] *...  2.3 us
  transfers between devices with their start and end apart: 11, of which 4 were waited for; matrix products, arithmetic and copies ran while one was open for 0% of the time, Pallas kernels for 33%

profile of v8, /device:TPU:9, one launch (start us, length us, event | category | flops | bytes accessed | tf_op | source)
XLA Modules:
  0.0 53.0 jit_solution(1540594551626798430)
XLA Ops:
  0.0 0.0 copy-start.4
  0.0 0.0 copy-start.5
  0.0 3.7 %resample_first.1 = (bf16[3,2,32,768]{3,2,1,0:T(8,128)(2,1)S(1)}, bf16[3,2,32,768]{3,2,1,0:T(8,128)(2,1)}, bf16[3,2,32,768]{3,2,1,0:T(8,128)(2,1)}, bf16[3,2,32,...) custom-call(s32[1]{0:T(128)} %bitcast.3.group, ...), custom_call_target="tpu_custom_call" | custom-call | flops 113246208 | bytes 4718592 | tf_op jit(solution)/shard_map/resample_first/pallas_call | solution.py:137
  3.7 0.0 copy-start
  3.7 0.7 %copy-done = bf16[3,2,32,768]{3,2,1,0:T(8,128)(2,1)} copy-done((bf16[3,2,32,768]{3,2,1,0:T(8,128)(2,1)}, bf16[3,2,32,768]{3,2,1,0:T(8,128)(2,1)S(1)}, u32[]{:S(2)}) %copy-start) | copy-done | bytes 294936
  4.4 0.7 %collective-permute-start.5 = (bf16[3,2,24,3072]{3,2,1,0:T(8,128)(2,1)S(1)}, bf16[3,2,24,3072]{3,2,1,0:T(8,128)(2,1)S(1)}, u32[]{:S(2)}, u32[]{:S(2)}) collective-permute-start(bf16[3,2,24,3072]{3,2,1,0:T(8,128)(2,1)S(1)} %get-tuple-element.29._), channel_id=1, source_target_pairs={{0,1},{2,3},{4,5},{6,7},{1,0},{3,2},{5,4},{7,6},{8,9},{10,11},{12,... | collective-permute-start | bytes 2654216 | tf_op jit(solution)/shard_map/ppermute | solution.py:390
  5.0 3.1 %collective-permute-start = (bf16[3,2,24,3072]{3,2,1,0:T(8,128)(2,1)}, bf16[3,2,24,3072]{3,2,1,0:T(8,128)(2,1)}, u32[]{:S(2)}, u32[]{:S(2)}) collective-permute-start(bf16[3,2,24,3072]{3,2,1,0:T(8,128)(2,1)} %get-tuple-element.23), channel_id=1, source_target_pairs={{1,2},{3,4},{5,6},{2,1},{4,3},{6,5},{9,10},{11,12},{13,14},{10,9},... | collective-permute-start | bytes 2654216 | tf_op jit(solution)/shard_map/ppermute | solution.py:390
  8.1 2.2 %collective-permute-start.1 = (bf16[3,2,32,768]{3,2,1,0:T(8,128)(2,1)}, bf16[3,2,32,768]{3,2,1,0:T(8,128)(2,1)}, u32[]{:S(2)}, u32[]{:S(2)}) collective-permute-start(bf16[3,2,32,768]{3,2,1,0:T(8,128)(2,1)} %get-tuple-element.24), channel_id=1, source_target_pairs={{0,24},{8,16},{16,8},{24,0},{1,25},{9,17},{17,9},{25,1},{2,26},{10... | collective-permute-start | bytes 884744 | tf_op jit(solution)/shard_map/ppermute | solution.py:385
  10.4 0.2 collective-permute-start.10
  10.6 0.2 collective-permute-start.9
  10.9 0.0 collective-permute-done.5.halo
  10.9 0.0 copy-done.4
  10.9 0.0 copy-done.5
  10.9 0.0 copy-start.8
  10.9 1.3 %resample_edge.3 = (bf16[3,2,32,768]{3,2,1,0:T(8,128)(2,1)S(1)}, bf16[3,2,32,768]{3,2,1,0:T(8,128)(2,1)}, bf16[3,2,32,768]{3,2,1,0:T(8,128)(2,1)S(1)}, bf16[3,2,32,768]{3,2,1,0:T(8,128)(2,1)S(1)}) custom-call(s32[1]{0:T(128)} %bitcast.3.group, s32[1]{0:T(128)} %bitcast.4.side, bf16[8,12]{1,0:T(8,128)(2,1)S(1)} %bitcast.19, s32[3,96]{1,0:T(4,128)S(1)} %copy-done.5, ...), custom_call_target="tpu_custom_call" | custom-call | flops 103809024 | bytes 4423680 | tf_op jit(solution)/shard_map/resample_edge/pallas_call | solution.py:157
  12.2 0.0 copy-start.2
  12.2 0.7 %copy-done.2 = bf16[3,2,32,768]{3,2,1,0:T(8,128)(2,1)} copy-done((bf16[3,2,32,768]{3,2,1,0:T(8,128)(2,1)}, bf16[3,2,32,768]{3,2,1,0:T(8,128)(2,1)S(1)}, u32[]{:S(2)}) %copy-start.2) | copy-done | bytes 294936
  12.9 0.0 copy-start.6
  12.9 0.7 %copy-done.6 = bf16[3,2,32,768]{3,2,1,0:T(8,128)(2,1)} copy-done((bf16[3,2,32,768]{3,2,1,0:T(8,128)(2,1)}, bf16[3,2,32,768]{3,2,1,0:T(8,128)(2,1)S(1)}, u32[]{:S(2)}) %copy-start.6) | copy-done | bytes 294936
  13.6 0.0 copy-start.7
  13.6 0.7 %copy-done.7 = bf16[3,2,32,768]{3,2,1,0:T(8,128)(2,1)} copy-done((bf16[3,2,32,768]{3,2,1,0:T(8,128)(2,1)}, bf16[3,2,32,768]{3,2,1,0:T(8,128)(2,1)S(1)}, u32[]{:S(2)}) %copy-start.7) | copy-done | bytes 294936
  14.3 1.2 %collective-permute-start.6 = (bf16[3,2,32,768]{3,2,1,0:T(8,128)(2,1)}, bf16[3,2,32,768]{3,2,1,0:T(8,128)(2,1)}, u32[]{:S(2)}, u32[]{:S(2)}) collective-permute-start(bf16[3,2,32,768]{3,2,1,0:T(8,128)(2,1)} %get-tuple-element.31), channel_id=1, source_target_pairs={{0,8},{8,0},{16,24},{24,16},{1,9},{9,1},{17,25},{25,17},{2,10},{10... | collective-permute-start | bytes 884744 | tf_op jit(solution)/shard_map/ppermute | solution.py:385
  15.6 0.0 copy-done.8
  15.6 2.5 %collective-permute-done.1._.rest_3_ = bf16[3,2,32,768]{3,2,1,0:T(8,128)(2,1)} collective-permute-done((bf16[3,2,32,768]{3,2,1,0:T(8,128)(2,1)}, bf16[3,2,32,768]{3,2,1,0:T(8,128)(2,1)}, u32[]{:S(2)}, u32[]{:S(2)}) %collective-permute-start.1) | collective-permute-done | bytes 294944 | tf_op jit(solution)/shard_map/ppermute | solution.py:385
  18.1 1.3 %collective-permute-start.7 = (bf16[3,2,32,768]{3,2,1,0:T(8,128)(2,1)}, bf16[3,2,32,768]{3,2,1,0:T(8,128)(2,1)S(1)}, u32[]{:S(2)}, u32[]{:S(2)}) collective-permute-start(bf16[3,2,32,768]{3,2,1,0:T(8,128)(2,1)} %copy-done.7), channel_id=1, source_target_pairs={{0,16},{8,24},{16,0},{24,8},{1,17},{9,25},{17,1},{25,9},{2,18},{10... | collective-permute-start | bytes 884744 | tf_op jit(solution)/shard_map/ppermute | solution.py:385
  19.4 0.6 %collective-permute-done.halo = bf16[3,2,24,3072]{3,2,1,0:T(8,128)(2,1)} collective-permute-done((bf16[3,2,24,3072]{3,2,1,0:T(8,128)(2,1)}, bf16[3,2,24,3072]{3,2,1,0:T(8,128)(2,1)}, u32[]{:S(2)}, u32[]{:S(2)}) %collective-permute-start) | collective-permute-done | bytes 884768 | tf_op jit(solution)/shard_map/ppermute | solution.py:390
  20.0 0.0 copy-start.1
  20.0 2.2 %collective-permute-start.8 = (bf16[3,2,32,768]{3,2,1,0:T(8,128)(2,1)}, bf16[3,2,32,768]{3,2,1,0:T(8,128)(2,1)S(1)}, u32[]{:S(2)}, u32[]{:S(2)}) collective-permute-start(bf16[3,2,32,768]{3,2,1,0:T(8,128)(2,1)} %copy-done.6), channel_id=1, source_target_pairs={{0,24},{8,16},{16,8},{24,0},{1,25},{9,17},{17,9},{25,1},{2,26},{10... | collective-permute-start | bytes 884744 | tf_op jit(solution)/shard_map/ppermute | solution.py:385
  22.2 2.1 %resample_edge.2 = (bf16[3,2,32,768]{3,2,1,0:T(8,128)(2,1)S(1)}, bf16[3,2,32,768]{3,2,1,0:T(8,128)(2,1)S(1)}, bf16[3,2,32,768]{3,2,1,0:T(8,128)(2,1)S(1)}, bf16[3,2,32,768]{3,2,1,0:T(8,128)(2,1)S(1)}) custom-call(s32[1]{0:T(128)} %bitcast.3.group, s32[1]{0:T(128)} %bitcast.4.side, bf16[8,12]{1,0:T(8,128)(2,1)S(1)} %bitcast.20, s32[3,96]{1,0:T(4,128)S(1)} %copy-done.5, ...), custom_call_target="tpu_custom_call" | custom-call | flops 103809024 | bytes 4423680 | tf_op jit(solution)/shard_map/resample_edge/pallas_call | solution.py:157
  24.3 0.0 collective-permute-done.10.rest_2_
  24.3 1.5 %collective-permute-start.2 = (bf16[3,2,32,768]{3,2,1,0:T(8,128)(2,1)S(1)}, bf16[3,2,32,768]{3,2,1,0:T(8,128)(2,1)S(1)}, u32[]{:S(2)}, u32[]{:S(2)}) collective-permute-start(bf16[3,2,32,768]{3,2,1,0:T(8,128)(2,1)S(1)} %get-tuple-element.26), channel_id=1, source_target_pairs={{0,8},{8,0},{16,24},{24,16},{1,9},{9,1},{17,25},{25,17},{2,10},{10... | collective-permute-start | bytes 884744 | tf_op jit(solution)/shard_map/ppermute | solution.py:385
  25.8 0.0 collective-permute-done.9.rest_1_
  25.8 0.7 %collective-permute-start.3 = (bf16[3,2,32,768]{3,2,1,0:T(8,128)(2,1)S(1)}, bf16[3,2,32,768]{3,2,1,0:T(8,128)(2,1)S(1)}, u32[]{:S(2)}, u32[]{:S(2)}) collective-permute-start(bf16[3,2,32,768]{3,2,1,0:T(8,128)(2,1)S(1)} %get-tuple-element.27), channel_id=1, source_target_pairs={{0,16},{8,24},{16,0},{24,8},{1,17},{9,25},{17,1},{25,9},{2,18},{10... | collective-permute-start | bytes 884744 | tf_op jit(solution)/shard_map/ppermute | solution.py:385
  26.5 4.6 %collective-permute-done.6.rest_1_ = bf16[3,2,32,768]{3,2,1,0:T(8,128)(2,1)} collective-permute-done((bf16[3,2,32,768]{3,2,1,0:T(8,128)(2,1)}, bf16[3,2,32,768]{3,2,1,0:T(8,128)(2,1)}, u32[]{:S(2)}, u32[]{:S(2)}) %collective-permute-start.6) | collective-permute-done | bytes 294944 | tf_op jit(solution)/shard_map/ppermute | solution.py:385
  31.1 1.2 %collective-permute-start.4 = (bf16[3,2,32,768]{3,2,1,0:T(8,128)(2,1)S(1)}, bf16[3,2,32,768]{3,2,1,0:T(8,128)(2,1)S(1)}, u32[]{:S(2)}, u32[]{:S(2)}) collective-permute-start(bf16[3,2,32,768]{3,2,1,0:T(8,128)(2,1)S(1)} %get-tuple-element.28), channel_id=1, source_target_pairs={{0,24},{8,16},{16,8},{24,0},{1,25},{9,17},{17,9},{25,1},{2,26},{10... | collective-permute-start | bytes 884744 | tf_op jit(solution)/shard_map/ppermute | solution.py:385
  32.3 0.0 copy-done.1
  32.3 0.0 copy-start.3
  32.3 5.9 %interfere.3.rest_4_ = f32[2,24,48,60]{3,2,1,0:T(8,128)} custom-call(s32[1]{0:T(128)} %constant.56.clone.1.spot, s32[4,60]{1,0:T(4,128)S(1)} %pad_add_fusion.table, bf16[3,2,32,768]{3,2,1,0:T(8,128)(2,1)S(1)} %copy-done.1, bf16[3,2,32,768]{3,2,1,0:T(8,128)(2,1)} %collective-permute-done.9.rest_1_, bf16[3,2,32,768]{3,2,1,0:T(8,128)(2,1)} %collective-permute-done.10.rest_2_, ...), custom_call_target="tpu_custom_call" | custom-call | flops 11796480 | bytes 14155776 | tf_op jit(solution)/shard_map/interfere/pallas_call | solution.py:342
  38.2 0.0 collective-permute-done.7.rest_2_
  38.2 0.0 collective-permute-done.8.rest_3_
  38.2 0.0 copy-done.3
  38.2 5.7 %interfere.4.rest_5_ = f32[2,24,48,60]{3,2,1,0:T(8,128)} custom-call(s32[1]{0:T(128)} %bitcast.6.spot, s32[4,60]{1,0:T(4,128)S(1)} %pad_add_fusion.table, bf16[3,2,32,768]{3,2,1,0:T(8,128)(2,1)S(1)} %copy-done.3, bf16[3,2,32,768]{3,2,1,0:T(8,128)(2,1)} %collective-permute-done.6.rest_1_, ...), custom_call_target="tpu_custom_call", output_to_operand_aliasing={{}: (6, {})} | custom-call | flops 11796480 | bytes 14155776 | tf_op jit(solution)/shard_map/interfere/pallas_call | solution.py:342
  43.9 0.0 collective-permute-done.2.rest_1_
  43.9 0.0 collective-permute-done.3.rest_2_
  43.9 2.3 %interfere_near.1.rest_4_ = f32[648,48]{1,0:T(8,128)S(1)} custom-call(bf16[3,2,32,768]{3,2,1,0:T(8,128)(2,1)S(1)} %get-tuple-element.37.rest_0_, bf16[3,2,32,768]{3,2,1,0:T(8,128)(2,1)S(1)} %collective-permute-done.2.rest_1_, bf16[3,2,32,768]{3,2,1,0:T(8,128)(2,1)S(1)} %collective-permute-done.3.rest_2_), custom_call_target="tpu_custom_call" | custom-call | flops 7077888 | bytes 10616832 | tf_op jit(solution)/shard_map/interfere_near/pallas_call | solution.py:323
  46.2 2.9 %collective-permute-done.4.rest_3_ = bf16[3,2,32,768]{3,2,1,0:T(8,128)(2,1)S(1)} collective-permute-done((bf16[3,2,32,768]{3,2,1,0:T(8,128)(2,1)S(1)}, bf16[3,2,32,768]{3,2,1,0:T(8,128)(2,1)S(1)}, u32[]{:S(2)}, u32[]{:S(2)}) %collective-permute-start.4) | collective-permute-done | bytes 294944 | tf_op jit(solution)/shard_map/ppermute | solution.py:385
  49.1 3.9 %interfere.5 = f32[2,24,48,60]{3,2,1,0:T(8,128)} custom-call(s32[1]{0:T(128)} %bitcast.spot, s32[4,60]{1,0:T(4,128)S(1)} %pad_add_fusion.table, bf16[3,2,32,768]{3,2,1,0:T(8,128)(2,1)S(1)} %get-tuple-element.37.rest_0_, bf16[3,2,32,768]{3,2,1,0:T(8,128)(2,1)S(1)} %collective-permute-done.2.rest_1_, ...), custom_call_target="tpu_custom_call", output_to_operand_aliasing={{}: (7, {})} | custom-call | flops 11796480 | bytes 14155776 | tf_op jit(solution)/shard_map/interfere/pallas_call | solution.py:342
  (4 shorter events, 0.0 us)
Async XLA Ops:
  0.0 10.9 %copy-start.4 = (bf16[12,8]{0,1:T(8,128)(2,1)S(1)}, bf16[12,8]{0,1:T(8,128)(2,1)}, u32[]{:S(2)}) copy-start(bf16[12,8]{0,1:T(8,128)(2,1)} %param.6) | copy-start | bytes 580
  0.0 10.9 %copy-start.5 = (s32[3,96]{1,0:T(4,128)S(1)}, s32[3,96]{1,0:T(4,128)}, u32[]{:S(2)}) copy-start(s32[3,96]{1,0:T(4,128)} %off.5) | copy-start | bytes 3460
  3.7 0.7 %copy-start = (bf16[3,2,32,768]{3,2,1,0:T(8,128)(2,1)}, bf16[3,2,32,768]{3,2,1,0:T(8,128)(2,1)S(1)}, u32[]{:S(2)}) copy-start(bf16[3,2,32,768]{3,2,1,0:T(8,128)(2,1)S(1)} %get-tuple-element.34.rest_0_) | copy-start | bytes 884740
  4.4 6.5 %collective-permute-start.5 = (bf16[3,2,24,3072]{3,2,1,0:T(8,128)(2,1)S(1)}, bf16[3,2,24,3072]{3,2,1,0:T(8,128)(2,1)S(1)}, u32[]{:S(2)}, u32[]{:S(2)}) collective-permute-start(bf16[3,2,24,3072]{3,2,1,0:T(8,128)(2,1)S(1)} %get-tuple-element.29._), channel_id=1, source_target_pairs={{0,1},{2,3},{4,5},{6,7},{1,0},{3,2},{5,4},{7,6},{8,9},{10,11},{12,... | collective-permute-start | bytes 2654216 | tf_op jit(solution)/shard_map/ppermute | solution.py:390
  5.0 15.0 %collective-permute-start = (bf16[3,2,24,3072]{3,2,1,0:T(8,128)(2,1)}, bf16[3,2,24,3072]{3,2,1,0:T(8,128)(2,1)}, u32[]{:S(2)}, u32[]{:S(2)}) collective-permute-start(bf16[3,2,24,3072]{3,2,1,0:T(8,128)(2,1)} %get-tuple-element.23), channel_id=1, source_target_pairs={{1,2},{3,4},{5,6},{2,1},{4,3},{6,5},{9,10},{11,12},{13,14},{10,9},... | collective-permute-start | bytes 2654216 | tf_op jit(solution)/shard_map/ppermute | solution.py:390
  8.1 10.0 %collective-permute-start.1 = (bf16[3,2,32,768]{3,2,1,0:T(8,128)(2,1)}, bf16[3,2,32,768]{3,2,1,0:T(8,128)(2,1)}, u32[]{:S(2)}, u32[]{:S(2)}) collective-permute-start(bf16[3,2,32,768]{3,2,1,0:T(8,128)(2,1)} %get-tuple-element.24), channel_id=1, source_target_pairs={{0,24},{8,16},{16,8},{24,0},{1,25},{9,17},{17,9},{25,1},{2,26},{10... | collective-permute-start | bytes 884744 | tf_op jit(solution)/shard_map/ppermute | solution.py:385
  10.4 13.9 %collective-permute-start.10 = (bf16[3,2,32,768]{3,2,1,0:T(8,128)(2,1)}, bf16[3,2,32,768]{3,2,1,0:T(8,128)(2,1)}, u32[]{:S(2)}, u32[]{:S(2)}) collective-permute-start(bf16[3,2,32,768]{3,2,1,0:T(8,128)(2,1)} %get-tuple-element.36), channel_id=1, source_target_pairs={{0,16},{8,24},{16,0},{24,8},{1,17},{9,25},{17,1},{25,9},{2,18},{10... | collective-permute-start | bytes 884744 | tf_op jit(solution)/shard_map/ppermute | solution.py:385
  10.6 15.2 %collective-permute-start.9 = (bf16[3,2,32,768]{3,2,1,0:T(8,128)(2,1)}, bf16[3,2,32,768]{3,2,1,0:T(8,128)(2,1)}, u32[]{:S(2)}, u32[]{:S(2)}) collective-permute-start(bf16[3,2,32,768]{3,2,1,0:T(8,128)(2,1)} %get-tuple-element.35), channel_id=1, source_target_pairs={{0,8},{8,0},{16,24},{24,16},{1,9},{9,1},{17,25},{25,17},{2,10},{10... | collective-permute-start | bytes 884744 | tf_op jit(solution)/shard_map/ppermute | solution.py:385
  10.9 4.7 %copy-start.8 = (s32[60,2]{0,1:T(2,128)S(1)}, s32[60,2]{0,1:T(2,128)}, u32[]{:S(2)}) copy-start(s32[60,2]{0,1:T(2,128)} %param.7) | copy-start | bytes 1444
  12.2 0.7 %copy-start.2 = (bf16[3,2,32,768]{3,2,1,0:T(8,128)(2,1)}, bf16[3,2,32,768]{3,2,1,0:T(8,128)(2,1)S(1)}, u32[]{:S(2)}) copy-start(bf16[3,2,32,768]{3,2,1,0:T(8,128)(2,1)S(1)} %get-tuple-element.30.rest_0_) | copy-start | bytes 884740
  12.9 0.7 %copy-start.6 = (bf16[3,2,32,768]{3,2,1,0:T(8,128)(2,1)}, bf16[3,2,32,768]{3,2,1,0:T(8,128)(2,1)S(1)}, u32[]{:S(2)}) copy-start(bf16[3,2,32,768]{3,2,1,0:T(8,128)(2,1)S(1)} %get-tuple-element.33) | copy-start | bytes 884740
  13.6 0.7 %copy-start.7 = (bf16[3,2,32,768]{3,2,1,0:T(8,128)(2,1)}, bf16[3,2,32,768]{3,2,1,0:T(8,128)(2,1)S(1)}, u32[]{:S(2)}) copy-start(bf16[3,2,32,768]{3,2,1,0:T(8,128)(2,1)S(1)} %get-tuple-element.32) | copy-start | bytes 884740
  14.3 16.7 %collective-permute-start.6 = (bf16[3,2,32,768]{3,2,1,0:T(8,128)(2,1)}, bf16[3,2,32,768]{3,2,1,0:T(8,128)(2,1)}, u32[]{:S(2)}, u32[]{:S(2)}) collective-permute-start(bf16[3,2,32,768]{3,2,1,0:T(8,128)(2,1)} %get-tuple-element.31), channel_id=1, source_target_pairs={{0,8},{8,0},{16,24},{24,16},{1,9},{9,1},{17,25},{25,17},{2,10},{10... | collective-permute-start | bytes 884744 | tf_op jit(solution)/shard_map/ppermute | solution.py:385
  18.1 20.0 %collective-permute-start.7 = (bf16[3,2,32,768]{3,2,1,0:T(8,128)(2,1)}, bf16[3,2,32,768]{3,2,1,0:T(8,128)(2,1)S(1)}, u32[]{:S(2)}, u32[]{:S(2)}) collective-permute-start(bf16[3,2,32,768]{3,2,1,0:T(8,128)(2,1)} %copy-done.7), channel_id=1, source_target_pairs={{0,16},{8,24},{16,0},{24,8},{1,17},{9,25},{17,1},{25,9},{2,18},{10... | collective-permute-start | bytes 884744 | tf_op jit(solution)/shard_map/ppermute | solution.py:385
  20.0 12.3 %copy-start.1 = (bf16[3,2,32,768]{3,2,1,0:T(8,128)(2,1)S(1)}, bf16[3,2,32,768]{3,2,1,0:T(8,128)(2,1)}, u32[]{:S(2)}) copy-start(bf16[3,2,32,768]{3,2,1,0:T(8,128)(2,1)} %copy-done) | copy-start | bytes 884740
  20.0 18.2 %collective-permute-start.8 = (bf16[3,2,32,768]{3,2,1,0:T(8,128)(2,1)}, bf16[3,2,32,768]{3,2,1,0:T(8,128)(2,1)S(1)}, u32[]{:S(2)}, u32[]{:S(2)}) collective-permute-start(bf16[3,2,32,768]{3,2,1,0:T(8,128)(2,1)} %copy-done.6), channel_id=1, source_target_pairs={{0,24},{8,16},{16,8},{24,0},{1,25},{9,17},{17,9},{25,1},{2,26},{10... | collective-permute-start | bytes 884744 | tf_op jit(solution)/shard_map/ppermute | solution.py:385
  24.3 19.6 %collective-permute-start.2 = (bf16[3,2,32,768]{3,2,1,0:T(8,128)(2,1)S(1)}, bf16[3,2,32,768]{3,2,1,0:T(8,128)(2,1)S(1)}, u32[]{:S(2)}, u32[]{:S(2)}) collective-permute-start(bf16[3,2,32,768]{3,2,1,0:T(8,128)(2,1)S(1)} %get-tuple-element.26), channel_id=1, source_target_pairs={{0,8},{8,0},{16,24},{24,16},{1,9},{9,1},{17,25},{25,17},{2,10},{10... | collective-permute-start | bytes 884744 | tf_op jit(solution)/shard_map/ppermute | solution.py:385
  25.8 18.1 %collective-permute-start.3 = (bf16[3,2,32,768]{3,2,1,0:T(8,128)(2,1)S(1)}, bf16[3,2,32,768]{3,2,1,0:T(8,128)(2,1)S(1)}, u32[]{:S(2)}, u32[]{:S(2)}) collective-permute-start(bf16[3,2,32,768]{3,2,1,0:T(8,128)(2,1)S(1)} %get-tuple-element.27), channel_id=1, source_target_pairs={{0,16},{8,24},{16,0},{24,8},{1,17},{9,25},{17,1},{25,9},{2,18},{10... | collective-permute-start | bytes 884744 | tf_op jit(solution)/shard_map/ppermute | solution.py:385
  31.1 18.0 %collective-permute-start.4 = (bf16[3,2,32,768]{3,2,1,0:T(8,128)(2,1)S(1)}, bf16[3,2,32,768]{3,2,1,0:T(8,128)(2,1)S(1)}, u32[]{:S(2)}, u32[]{:S(2)}) collective-permute-start(bf16[3,2,32,768]{3,2,1,0:T(8,128)(2,1)S(1)} %get-tuple-element.28), channel_id=1, source_target_pairs={{0,24},{8,16},{16,8},{24,0},{1,25},{9,17},{17,9},{25,1},{2,26},{10... | collective-permute-start | bytes 884744 | tf_op jit(solution)/shard_map/ppermute | solution.py:385
  32.3 5.9 %copy-start.3 = (bf16[3,2,32,768]{3,2,1,0:T(8,128)(2,1)S(1)}, bf16[3,2,32,768]{3,2,1,0:T(8,128)(2,1)}, u32[]{:S(2)}) copy-start(bf16[3,2,32,768]{3,2,1,0:T(8,128)(2,1)} %copy-done.2) | copy-start | bytes 884740

commit v9 on v8

--- a/solution.py
+++ b/solution.py
@@ -260,7 +260,7 @@
     look_sums(blocks, 0, parts, terms, sums, 0, slot_of(0, groups * acq) * 2 * looks)
 
 
-def interfere_kernel(groups, known, spot, table, *rest):
+def interfere_kernel(groups, known, turn, table, *rest):
     blocks, rest = rest[:groups], rest[groups:]
     out, parts, terms, sums, flat, inverse, slab, sem = rest[-8:]
     acq, _, lines, width = blocks[0].shape
@@ -292,7 +292,7 @@
     for g in range(looks):
         for x in range(2):
             slab[x, g] = flat[pl.ds(x * looks + g, count, stride=both), :].T
-        copies.append(pltpu.make_async_copy(slab.at[:, g], out.at[:, spot[0] * looks + g], sem.at[g]))
+        copies.append(pltpu.make_async_copy(slab.at[:, g], out.at[:, table[4, turn] * looks + g], sem.at[g]))
         copies[-1].start()
     for copy in copies:
         copy.wait()
@@ -332,7 +332,7 @@
     )(*blocks)
 
 
-def interfere(place, chunks, table, blocks, near, known, before):
+def interfere(turn, chunks, table, blocks, near, known, before):
     groups = len(blocks)
     acq, _, lines, width = blocks[0].shape
     looks, windows, count = lines // LOOK_R, width // LOOK_C, table.shape[1]
@@ -340,8 +340,8 @@
     near = [] if near is None else [near]
     extra = [] if before is None else [before]
     return pl.pallas_call(
-        functools.partial(interfere_kernel, groups, known),
-        in_specs=[SMEM, SMEM] + [VMEM] * (groups + len(near)) + [ANY] * len(extra),
+        functools.partial(interfere_kernel, groups, known, turn),
+        in_specs=[SMEM] + [VMEM] * (groups + len(near)) + [ANY] * len(extra),
         out_specs=ANY,
         out_shape=pltpu.HBM((2, chunks * looks, windows, count), jnp.float32),
         scratch_shapes=work_space(groups, known, acq, lines, looks)
@@ -352,18 +352,21 @@
             pltpu.VMEM((2, looks, windows, count), jnp.float32),
             pltpu.SemaphoreType.DMA((looks,)),
         ],
-        input_output_aliases={} if before is None else {2 + groups + len(near): 0},
+        input_output_aliases={} if before is None else {1 + groups + len(near): 0},
         compiler_params=pltpu.CompilerParams(vmem_limit_bytes=8 * MIB),
         cost_estimate=interfere_cost(count, total, lines, width),
         name="interfere",
-    )(place, table, *blocks, *near, *extra)
-
-
-def pair_table(pairs, groups, acq, mine):
+    )(table, *blocks, *near, *extra)
+
+
+def pair_table(pairs, groups, acq, mine, odd, chunks):
     close = ((pairs // acq) ^ mine) * acq + pairs % acq
     m, s = close[:, 0], close[:, 1]
     slot = slot_of(jnp.minimum(m, s), jnp.maximum(m, s))
-    return jnp.stack([slot, m, s, jnp.where(m < s, 1, -1)]).astype(jnp.int32)
+    turn = jnp.arange(pairs.shape[0])
+    edge = jnp.where((turn == 1) == (odd == 0), chunks - 1, 0)
+    place = jnp.where(turn == 0, 1, edge)
+    return jnp.stack([slot, m, s, jnp.where(m < s, 1, -1), place]).astype(jnp.int32)
 
 
 def local(slc, offsets, weights, pairs):
@@ -375,8 +378,8 @@
     group = jnp.reshape(lax.axis_index("acq"), (1,)).astype(jnp.int32)
     side = jnp.reshape(odd, (1,)).astype(jnp.int32)
     kernel = weights.T
-    table = pair_table(pairs, groups, acq, group[0])
     chunks = lines // CHUNK
+    table = pair_table(pairs, groups, acq, group[0], odd, chunks)
     reach = CHUNK + TILE * 2
 
     def send(blocks):
@@ -398,22 +401,15 @@
     across = swap(outer, 1)
     second = send(pieces)
     third = send(
-        resample_edge(1, reach, group, side, kernel, offsets, slab, across, middle[3], groups)
-    )
-    low, high = jnp.zeros_like(odd), jnp.full_like(odd, chunks - 1)
-    spots = (
-        jnp.full_like(odd, 1),
-        jnp.where(odd == 0, high, low),
-        jnp.where(odd == 0, low, high),
+        resample_edge(1, reach, group, side, kernel, offsets, slab, across, pieces[0], groups)
     )
     result = None
-    for spot, moved, known in zip(spots, (middle, second, third), (0, 0, groups - 1)):
-        place = jnp.reshape(spot, (1,)).astype(jnp.int32)
+    for turn, (moved, known) in enumerate(((middle, 0), (second, 0), (third, groups - 1))):
         near = None
         if known:
             mine, result = lax.optimization_barrier((moved[0], result))
             near = interfere_near([mine, *moved[1:known]])
-        result = interfere(place, chunks, table, moved, near, known, result)
+        result = interfere(turn, chunks, table, moved, near, known, result)
     return jnp.transpose(result, (0, 3, 1, 2))
 
 

time: 53.9 us -> 54.6 us (1.013); the launches traced: 53 us -> 54.4 us
  waiting for transfers between devices: 10.6 us -> 16.8 us
  Pallas kernels: 24.8 us -> 22.4 us
  local copies, waits for them, and re-layouts: 2.88 us -> 0.69 us
  starting transfers between devices: 14.5 us -> 13.8 us
    ppermute x2, waiting for transfers between devices: 0.58 us -> 6.03 us  [swap(): return lax.ppermute(halo, 'pix', pairs_up + [(j, i) for i, j in pairs_up])]
    unnamed x18 -> x6, local copies, waits for them, and re-layouts: 2.87 us -> 0.01 us
    pallas_call x1, Pallas kernels: 3.67 us -> 2.47 us  [resample_first(): pl.pallas_call(functools.partial(first_kernel, first, groups), in_specs=[...]
    pallas_call x3, Pallas kernels: 15.5 us -> 14.6 us  [interfere(): pl.pallas_call(functools.partial(interfere_kernel, groups, known, turn),...]
    ppermute x9, starting transfers between devices: 10.8 us -> 9.98 us  [send(): lax.ppermute(blocks[s], 'acq', [(i, i ^ s) for i in range(groups)])]
    ppermute x9, waiting for transfers between devices: 9.99 us -> 10.8 us  [send(): lax.ppermute(blocks[s], 'acq', [(i, i ^ s) for i in range(groups)])]
    another operation x0 -> x1, local copies, waits for them, and re-layouts: none -> 0.67 us  [pair_table(): jnp.stack([slot, m, s, jnp.where(m < s, 1, -1), place]).astype(jnp.int32)]
    select_n x0 -> x1, other arithmetic: none -> 0.55 us  [pair_table(): jnp.where(m < s, 1, -1)]
  transfers between devices with their start and end apart: 11 -> 11, of which waited for: 4 -> 4; matrix products, arithmetic and copies ran while one was open for 0% -> 2% of each run, Pallas kernels for 33% -> 29%
where the time goes in v9:
time: 54.6 us; the launch traced here: 54.4 us
  Pallas kernels  22.4 us (41%)
  waiting for transfers between devices  16.8 us (31%)
  starting transfers between devices  13.8 us (25%)
  local copies, waits for them, and re-layouts  0.69 us (1%)
  other arithmetic  0.57 us (1%)
    pallas_call x3, Pallas kernels, interfere(): pl.pallas_call(functools.partial(interfere_kernel, groups, known, turn),...  14.6 us
    ppermute x9, waiting for transfers between devices, send(): lax.ppermute(blocks[s], 'acq', [(i, i ^ s) for i in range(groups)])  10.8 us
    ppermute x9, starting transfers between devices, send(): lax.ppermute(blocks[s], 'acq', [(i, i ^ s) for i in range(groups)])  9.98 us
    ppermute x2, waiting for transfers between devices, swap(): return lax.ppermute(halo, 'pix', pairs_up + [(j, i) for i, j in pairs_up])  6.03 us
    ppermute x2, starting transfers between devices, swap(): return lax.ppermute(halo, 'pix', pairs_up + [(j, i) for i, j in pairs_up])  3.82 us
    pallas_call x2, Pallas kernels, resample_edge(): pl.pallas_call(functools.partial(edge_kernel, groups, parity, count), in_...  3.07 us
    pallas_call x1, Pallas kernels, resample_first(): pl.pallas_call(functools.partial(first_kernel, first, groups), in_specs=[...  2.47 us
    pallas_call x1, Pallas kernels, interfere_near(): pl.pallas_call(functools.partial(near_kernel, groups), in_specs=[VMEM] *...  2.3 us
  transfers between devices with their start and end apart: 11, of which 4 were waited for; matrix products, arithmetic and copies ran while one was open for 2% of the time, Pallas kernels for 29%

profile of v9, /device:TPU:9, one launch (start us, length us, event | category | flops | bytes accessed | tf_op | source)
XLA Modules:
  0.0 54.4 jit_solution(12644640689526470705)
XLA Ops:
  0.0 0.0 copy-start
  0.0 0.0 copy-start.1
  0.0 2.5 %resample_first.1 = (bf16[3,2,32,768]{3,2,1,0:T(8,128)(2,1)S(1)}, bf16[3,2,32,768]{3,2,1,0:T(8,128)(2,1)S(1)}, bf16[3,2,32,768]{3,2,1,0:T(8,128)(2,1)S(1)}, bf16...) custom-call(s32[1]{0:T(128)} %bitcast.2.group, ...), custom_call_target="tpu_custom_call" | custom-call | flops 113246208 | bytes 4718592 | tf_op jit(solution)/shard_map/resample_first/pallas_call | solution.py:137
  2.5 0.7 %collective-permute-start.1 = (bf16[3,2,24,3072]{3,2,1,0:T(8,128)(2,1)S(1)}, bf16[3,2,24,3072]{3,2,1,0:T(8,128)(2,1)S(1)}, u32[]{:S(2)}, u32[]{:S(2)}) collective-permute-start(bf16[3,2,24,3072]{3,2,1,0:T(8,128)(2,1)S(1)} %get-tuple-element.24._), channel_id=1, source_target_pairs={{0,1},{2,3},{4,5},{6,7},{1,0},{3,2},{5,4},{7,6},{8,9},{10,11},{12,... | collective-permute-start | bytes 2654216 | tf_op jit(solution)/shard_map/ppermute | solution.py:393
  3.2 3.1 %collective-permute-start = (bf16[3,2,24,3072]{3,2,1,0:T(8,128)(2,1)S(1)}, bf16[3,2,24,3072]{3,2,1,0:T(8,128)(2,1)S(1)}, u32[]{:S(2)}, u32[]{:S(2)}) collective-permute-start(bf16[3,2,24,3072]{3,2,1,0:T(8,128)(2,1)S(1)} %get-tuple-element.23), channel_id=1, source_target_pairs={{1,2},{3,4},{5,6},{2,1},{4,3},{6,5},{9,10},{11,12},{13,14},{10,9},... | collective-permute-start | bytes 2654216 | tf_op jit(solution)/shard_map/ppermute | solution.py:393
  6.3 1.3 %collective-permute-start.8 = (bf16[3,2,32,768]{3,2,1,0:T(8,128)(2,1)S(1)}, bf16[3,2,32,768]{3,2,1,0:T(8,128)(2,1)S(1)}, u32[]{:S(2)}, u32[]{:S(2)}) collective-permute-start(bf16[3,2,32,768]{3,2,1,0:T(8,128)(2,1)S(1)} %get-tuple-element.34), channel_id=1, source_target_pairs={{0,8},{8,0},{16,24},{24,16},{1,9},{9,1},{17,25},{25,17},{2,10},{10... | collective-permute-start | bytes 884744 | tf_op jit(solution)/shard_map/ppermute | solution.py:388
  7.6 1.2 %collective-permute-start.9 = (bf16[3,2,32,768]{3,2,1,0:T(8,128)(2,1)S(1)}, bf16[3,2,32,768]{3,2,1,0:T(8,128)(2,1)S(1)}, u32[]{:S(2)}, u32[]{:S(2)}) collective-permute-start(bf16[3,2,32,768]{3,2,1,0:T(8,128)(2,1)S(1)} %get-tuple-element.35), channel_id=1, source_target_pairs={{0,16},{8,24},{16,0},{24,8},{1,17},{9,25},{17,1},{25,9},{2,18},{10... | collective-permute-start | bytes 884744 | tf_op jit(solution)/shard_map/ppermute | solution.py:388
  8.8 0.2 collective-permute-start.10
  9.0 0.0 collective-permute-done.1.halo
  9.0 0.0 copy-done
  9.0 0.0 copy-done.1
  9.0 0.0 copy-start.2
  9.1 1.5 %resample_edge.2 = (bf16[3,2,32,768]{3,2,1,0:T(8,128)(2,1)S(1)}, bf16[3,2,32,768]{3,2,1,0:T(8,128)(2,1)S(1)}, bf16[3,2,32,768]{3,2,1,0:T(8,128)(2,1)}, bf16[3,2,32,768]{3,2,1,0:T(8,128)(2,1)}) custom-call(s32[1]{0:T(128)} %bitcast.2.group, s32[1]{0:T(128)} %bitcast.3.side, bf16[8,12]{1,0:T(8,128)(2,1)S(1)} %bitcast.17, s32[3,96]{1,0:T(4,128)S(1)} %copy-done.1, ...), custom_call_target="tpu_custom_call" | custom-call | flops 103809024 | bytes 4423680 | tf_op jit(solution)/shard_map/resample_edge/pallas_call | solution.py:157
  10.6 1.2 %collective-permute-start.5 = (bf16[3,2,32,768]{3,2,1,0:T(8,128)(2,1)S(1)}, bf16[3,2,32,768]{3,2,1,0:T(8,128)(2,1)S(1)}, u32[]{:S(2)}, u32[]{:S(2)}) collective-permute-start(bf16[3,2,32,768]{3,2,1,0:T(8,128)(2,1)S(1)} %get-tuple-element.30), channel_id=1, source_target_pairs={{0,8},{8,0},{16,24},{24,16},{1,9},{9,1},{17,25},{25,17},{2,10},{10... | collective-permute-start | bytes 884744 | tf_op jit(solution)/shard_map/ppermute | solution.py:388
  11.8 0.0 copy-done.2
  11.8 6.0 %collective-permute-done.halo = bf16[3,2,24,3072]{3,2,1,0:T(8,128)(2,1)S(1)} collective-permute-done((bf16[3,2,24,3072]{3,2,1,0:T(8,128)(2,1)S(1)}, bf16[3,2,24,3072]{3,2,1,0:T(8,128)(2,1)S(1)}, u32[]{:S(2)}, u32[]{:S(2)}) %collective-permute-start) | collective-permute-done | bytes 884768 | tf_op jit(solution)/shard_map/ppermute | solution.py:393
  17.8 1.2 %collective-permute-start.6 = (bf16[3,2,32,768]{3,2,1,0:T(8,128)(2,1)}, bf16[3,2,32,768]{3,2,1,0:T(8,128)(2,1)S(1)}, u32[]{:S(2)}, u32[]{:S(2)}) collective-permute-start(bf16[3,2,32,768]{3,2,1,0:T(8,128)(2,1)} %get-tuple-element.31), channel_id=1, source_target_pairs={{0,16},{8,24},{16,0},{24,8},{1,17},{9,25},{17,1},{25,9},{2,18},{10... | collective-permute-start | bytes 884744 | tf_op jit(solution)/shard_map/ppermute | solution.py:388
  19.1 1.5 %resample_edge.3 = (bf16[3,2,32,768]{3,2,1,0:T(8,128)(2,1)S(1)}, bf16[3,2,32,768]{3,2,1,0:T(8,128)(2,1)}, bf16[3,2,32,768]{3,2,1,0:T(8,128)(2,1)}, bf16[3,2,32,768]{3,2,1,0:T(8,128)(2,1)}) custom-call(s32[1]{0:T(128)} %bitcast.2.group, s32[1]{0:T(128)} %bitcast.3.side, bf16[8,12]{1,0:T(8,128)(2,1)S(1)} %bitcast.18, s32[3,96]{1,0:T(4,128)S(1)} %copy-done.1, ...), custom_call_target="tpu_custom_call" | custom-call | flops 103809024 | bytes 4423680 | tf_op jit(solution)/shard_map/resample_edge/pallas_call | solution.py:157
  20.6 0.0 collective-permute-done.8.rest_1_
  20.6 1.1 %collective-permute-start.7 = (bf16[3,2,32,768]{3,2,1,0:T(8,128)(2,1)}, bf16[3,2,32,768]{3,2,1,0:T(8,128)(2,1)S(1)}, u32[]{:S(2)}, u32[]{:S(2)}) collective-permute-start(bf16[3,2,32,768]{3,2,1,0:T(8,128)(2,1)} %get-tuple-element.32), channel_id=1, source_target_pairs={{0,24},{8,16},{16,8},{24,0},{1,25},{9,17},{17,9},{25,1},{2,26},{10... | collective-permute-start | bytes 884744 | tf_op jit(solution)/shard_map/ppermute | solution.py:388
  21.8 1.1 %collective-permute-done.9.rest_2_ = bf16[3,2,32,768]{3,2,1,0:T(8,128)(2,1)S(1)} collective-permute-done((bf16[3,2,32,768]{3,2,1,0:T(8,128)(2,1)S(1)}, bf16[3,2,32,768]{3,2,1,0:T(8,128)(2,1)S(1)}, u32[]{:S(2)}, u32[]{:S(2)}) %collective-permute-start.9) | collective-permute-done | bytes 294944 | tf_op jit(solution)/shard_map/ppermute | solution.py:388
  22.8 0.0 collective-permute-start.2
  22.8 0.0 collective-permute-done.10.rest_3_
  22.8 1.5 %collective-permute-start.3 = (bf16[3,2,32,768]{3,2,1,0:T(8,128)(2,1)}, bf16[3,2,32,768]{3,2,1,0:T(8,128)(2,1)S(1)}, u32[]{:S(2)}, u32[]{:S(2)}) collective-permute-start(bf16[3,2,32,768]{3,2,1,0:T(8,128)(2,1)} %get-tuple-element.28), channel_id=1, source_target_pairs={{0,16},{8,24},{16,0},{24,8},{1,17},{9,25},{17,1},{25,9},{2,18},{10... | collective-permute-start | bytes 884744 | tf_op jit(solution)/shard_map/ppermute | solution.py:388
  24.3 3.7 %collective-permute-done.5.rest_1_ = bf16[3,2,32,768]{3,2,1,0:T(8,128)(2,1)S(1)} collective-permute-done((bf16[3,2,32,768]{3,2,1,0:T(8,128)(2,1)S(1)}, bf16[3,2,32,768]{3,2,1,0:T(8,128)(2,1)S(1)}, u32[]{:S(2)}, u32[]{:S(2)}) %collective-permute-start.5) | collective-permute-done | bytes 294944 | tf_op jit(solution)/shard_map/ppermute | solution.py:388
  28.0 2.2 %collective-permute-start.4 = (bf16[3,2,32,768]{3,2,1,0:T(8,128)(2,1)}, bf16[3,2,32,768]{3,2,1,0:T(8,128)(2,1)S(1)}, u32[]{:S(2)}, u32[]{:S(2)}) collective-permute-start(bf16[3,2,32,768]{3,2,1,0:T(8,128)(2,1)} %get-tuple-element.29), channel_id=1, source_target_pairs={{0,24},{8,16},{16,8},{24,0},{1,25},{9,17},{17,9},{25,1},{2,26},{10... | collective-permute-start | bytes 884744 | tf_op jit(solution)/shard_map/ppermute | solution.py:388
  30.2 0.5 %compare_select_fusion.2 = (s32[1,60]{1,0:T(1,128)S(1)}, s32[1,60]{1,0:T(1,128)}, s32[1,60]{1,0:T(1,128)}) fusion(s32[60,2]{0,1:T(2,128)S(1)} %fusion, pred[]{:T(512)S(6)} %eq.43), kind=kLoop, calls=%fused_computation.2 | loop fusion | flops 1620 | bytes 1201 | tf_op jit(solution)/shard_map/jit(_where)/select_n | solution.py:369
  30.8 0.7 %stack.2.table = s32[5,60]{1,0:T(8,128)S(1)} concatenate(s32[1,60]{1,0:T(1,128)} %get-tuple-element.40, s32[1,60]{1,0:T(1,128)S(1)} %get-tuple-element.42, s32[1,60]{1,0:T(1,128)S(1)} %get-tuple-element.41, s32[1,60]{1,0:T(1,128)S(1)} %get-tuple-element.39, s32[1,60]{1,0:T(1,128)} %get-tuple-element.43), dimensions={0} | concatenate | bytes 2400 | tf_op jit(solution)/shard_map/stack | solution.py:369
  31.4 5.3 %interfere.3.rest_4_ = f32[2,24,48,60]{3,2,1,0:T(8,128)} custom-call(s32[5,60]{1,0:T(8,128)S(1)} %stack.2.table, bf16[3,2,32,768]{3,2,1,0:T(8,128)(2,1)S(1)} %get-tuple-element.33.rest_0_, bf16[3,2,32,768]{3,2,1,0:T(8,128)(2,1)S(1)} %collective-permute-done.8.rest_1_, bf16[3,2,32,768]{3,2,1,0:T(8,128)(2,1)S(1)} %collective-permute-done.9.rest_2_, ...), custom_call_target="tpu_custom_call" | custom-call | flops 11796480 | bytes 14155776 | tf_op jit(solution)/shard_map/interfere/pallas_call | solution.py:342
  36.8 0.0 collective-permute-done.6.rest_2_
  36.8 0.0 collective-permute-done.7.rest_3_
  36.8 5.3 %interfere.4.rest_5_ = f32[2,24,48,60]{3,2,1,0:T(8,128)} custom-call(s32[5,60]{1,0:T(8,128)S(1)} %stack.2.table, bf16[3,2,32,768]{3,2,1,0:T(8,128)(2,1)S(1)} %get-tuple-element.25._.rest_0_, bf16[3,2,32,768]{3,2,1,0:T(8,128)(2,1)S(1)} %collective-permute-done.5.rest_1_, ...), custom_call_target="tpu_custom_call", output_to_operand_aliasing={{}: (5, {})} | custom-call | flops 11796480 | bytes 14155776 | tf_op jit(solution)/shard_map/interfere/pallas_call | solution.py:342
  42.1 0.0 collective-permute-done.2.rest_1_
  42.1 6.0 %collective-permute-done.3.rest_2_ = bf16[3,2,32,768]{3,2,1,0:T(8,128)(2,1)S(1)} collective-permute-done((bf16[3,2,32,768]{3,2,1,0:T(8,128)(2,1)}, bf16[3,2,32,768]{3,2,1,0:T(8,128)(2,1)S(1)}, u32[]{:S(2)}, u32[]{:S(2)}) %collective-permute-start.3) | collective-permute-done | bytes 294944 | tf_op jit(solution)/shard_map/ppermute | solution.py:388
  48.1 2.3 %interfere_near.1.rest_4_ = f32[648,48]{1,0:T(8,128)S(1)} custom-call(bf16[3,2,32,768]{3,2,1,0:T(8,128)(2,1)S(1)} %get-tuple-element.37.rest_0_, bf16[3,2,32,768]{3,2,1,0:T(8,128)(2,1)S(1)} %collective-permute-done.2.rest_1_, bf16[3,2,32,768]{3,2,1,0:T(8,128)(2,1)S(1)} %collective-permute-done.3.rest_2_), custom_call_target="tpu_custom_call" | custom-call | flops 7077888 | bytes 10616832 | tf_op jit(solution)/shard_map/interfere_near/pallas_call | solution.py:323
  50.4 0.0 collective-permute-done.4.rest_3_
  50.4 4.0 %interfere.5 = f32[2,24,48,60]{3,2,1,0:T(8,128)} custom-call(s32[5,60]{1,0:T(8,128)S(1)} %stack.2.table, bf16[3,2,32,768]{3,2,1,0:T(8,128)(2,1)S(1)} %get-tuple-element.37.rest_0_, bf16[3,2,32,768]{3,2,1,0:T(8,128)(2,1)S(1)} %collective-permute-done.2.rest_1_, ...), custom_call_target="tpu_custom_call", output_to_operand_aliasing={{}: (6, {})} | custom-call | flops 11796480 | bytes 14155776 | tf_op jit(solution)/shard_map/interfere/pallas_call | solution.py:342
  (2 shorter events, 0.0 us)
Async XLA Ops:
  0.0 9.0 %copy-start = (bf16[12,8]{0,1:T(8,128)(2,1)S(1)}, bf16[12,8]{0,1:T(8,128)(2,1)}, u32[]{:S(2)}) copy-start(bf16[12,8]{0,1:T(8,128)(2,1)} %param.6) | copy-start | bytes 580
  0.0 9.0 %copy-start.1 = (s32[3,96]{1,0:T(4,128)S(1)}, s32[3,96]{1,0:T(4,128)}, u32[]{:S(2)}) copy-start(s32[3,96]{1,0:T(4,128)} %off.5) | copy-start | bytes 3460
  2.5 6.5 %collective-permute-start.1 = (bf16[3,2,24,3072]{3,2,1,0:T(8,128)(2,1)S(1)}, bf16[3,2,24,3072]{3,2,1,0:T(8,128)(2,1)S(1)}, u32[]{:S(2)}, u32[]{:S(2)}) collective-permute-start(bf16[3,2,24,3072]{3,2,1,0:T(8,128)(2,1)S(1)} %get-tuple-element.24._), channel_id=1, source_target_pairs={{0,1},{2,3},{4,5},{6,7},{1,0},{3,2},{5,4},{7,6},{8,9},{10,11},{12,... | collective-permute-start | bytes 2654216 | tf_op jit(solution)/shard_map/ppermute | solution.py:393
  3.2 14.6 %collective-permute-start = (bf16[3,2,24,3072]{3,2,1,0:T(8,128)(2,1)S(1)}, bf16[3,2,24,3072]{3,2,1,0:T(8,128)(2,1)S(1)}, u32[]{:S(2)}, u32[]{:S(2)}) collective-permute-start(bf16[3,2,24,3072]{3,2,1,0:T(8,128)(2,1)S(1)} %get-tuple-element.23), channel_id=1, source_target_pairs={{1,2},{3,4},{5,6},{2,1},{4,3},{6,5},{9,10},{11,12},{13,14},{10,9},... | collective-permute-start | bytes 2654216 | tf_op jit(solution)/shard_map/ppermute | solution.py:393
  6.3 14.3 %collective-permute-start.8 = (bf16[3,2,32,768]{3,2,1,0:T(8,128)(2,1)S(1)}, bf16[3,2,32,768]{3,2,1,0:T(8,128)(2,1)S(1)}, u32[]{:S(2)}, u32[]{:S(2)}) collective-permute-start(bf16[3,2,32,768]{3,2,1,0:T(8,128)(2,1)S(1)} %get-tuple-element.34), channel_id=1, source_target_pairs={{0,8},{8,0},{16,24},{24,16},{1,9},{9,1},{17,25},{25,17},{2,10},{10... | collective-permute-start | bytes 884744 | tf_op jit(solution)/shard_map/ppermute | solution.py:388
  7.6 15.2 %collective-permute-start.9 = (bf16[3,2,32,768]{3,2,1,0:T(8,128)(2,1)S(1)}, bf16[3,2,32,768]{3,2,1,0:T(8,128)(2,1)S(1)}, u32[]{:S(2)}, u32[]{:S(2)}) collective-permute-start(bf16[3,2,32,768]{3,2,1,0:T(8,128)(2,1)S(1)} %get-tuple-element.35), channel_id=1, source_target_pairs={{0,16},{8,24},{16,0},{24,8},{1,17},{9,25},{17,1},{25,9},{2,18},{10... | collective-permute-start | bytes 884744 | tf_op jit(solution)/shard_map/ppermute | solution.py:388
  8.8 14.0 %collective-permute-start.10 = (bf16[3,2,32,768]{3,2,1,0:T(8,128)(2,1)S(1)}, bf16[3,2,32,768]{3,2,1,0:T(8,128)(2,1)S(1)}, u32[]{:S(2)}, u32[]{:S(2)}) collective-permute-start(bf16[3,2,32,768]{3,2,1,0:T(8,128)(2,1)S(1)} %get-tuple-element.36), channel_id=1, source_target_pairs={{0,24},{8,16},{16,8},{24,0},{1,25},{9,17},{17,9},{25,1},{2,26},{10... | collective-permute-start | bytes 884744 | tf_op jit(solution)/shard_map/ppermute | solution.py:388
  9.0 2.8 %copy-start.2 = (s32[60,2]{0,1:T(2,128)S(1)}, s32[60,2]{0,1:T(2,128)}, u32[]{:S(2)}) copy-start(s32[60,2]{0,1:T(2,128)} %param.7) | copy-start | bytes 1444
  10.6 17.5 %collective-permute-start.5 = (bf16[3,2,32,768]{3,2,1,0:T(8,128)(2,1)S(1)}, bf16[3,2,32,768]{3,2,1,0:T(8,128)(2,1)S(1)}, u32[]{:S(2)}, u32[]{:S(2)}) collective-permute-start(bf16[3,2,32,768]{3,2,1,0:T(8,128)(2,1)S(1)} %get-tuple-element.30), channel_id=1, source_target_pairs={{0,8},{8,0},{16,24},{24,16},{1,9},{9,1},{17,25},{25,17},{2,10},{10... | collective-permute-start | bytes 884744 | tf_op jit(solution)/shard_map/ppermute | solution.py:388
  17.8 18.9 %collective-permute-start.6 = (bf16[3,2,32,768]{3,2,1,0:T(8,128)(2,1)}, bf16[3,2,32,768]{3,2,1,0:T(8,128)(2,1)S(1)}, u32[]{:S(2)}, u32[]{:S(2)}) collective-permute-start(bf16[3,2,32,768]{3,2,1,0:T(8,128)(2,1)} %get-tuple-element.31), channel_id=1, source_target_pairs={{0,16},{8,24},{16,0},{24,8},{1,17},{9,25},{17,1},{25,9},{2,18},{10... | collective-permute-start | bytes 884744 | tf_op jit(solution)/shard_map/ppermute | solution.py:388
  20.6 16.1 %collective-permute-start.7 = (bf16[3,2,32,768]{3,2,1,0:T(8,128)(2,1)}, bf16[3,2,32,768]{3,2,1,0:T(8,128)(2,1)S(1)}, u32[]{:S(2)}, u32[]{:S(2)}) collective-permute-start(bf16[3,2,32,768]{3,2,1,0:T(8,128)(2,1)} %get-tuple-element.32), channel_id=1, source_target_pairs={{0,24},{8,16},{16,8},{24,0},{1,25},{9,17},{17,9},{25,1},{2,26},{10... | collective-permute-start | bytes 884744 | tf_op jit(solution)/shard_map/ppermute | solution.py:388
  22.8 19.3 %collective-permute-start.2 = (bf16[3,2,32,768]{3,2,1,0:T(8,128)(2,1)}, bf16[3,2,32,768]{3,2,1,0:T(8,128)(2,1)S(1)}, u32[]{:S(2)}, u32[]{:S(2)}) collective-permute-start(bf16[3,2,32,768]{3,2,1,0:T(8,128)(2,1)} %get-tuple-element.27), channel_id=1, source_target_pairs={{0,8},{8,0},{16,24},{24,16},{1,9},{9,1},{17,25},{25,17},{2,10},{10... | collective-permute-start | bytes 884744 | tf_op jit(solution)/shard_map/ppermute | solution.py:388
  22.8 25.3 %collective-permute-start.3 = (bf16[3,2,32,768]{3,2,1,0:T(8,128)(2,1)}, bf16[3,2,32,768]{3,2,1,0:T(8,128)(2,1)S(1)}, u32[]{:S(2)}, u32[]{:S(2)}) collective-permute-start(bf16[3,2,32,768]{3,2,1,0:T(8,128)(2,1)} %get-tuple-element.28), channel_id=1, source_target_pairs={{0,16},{8,24},{16,0},{24,8},{1,17},{9,25},{17,1},{25,9},{2,18},{10... | collective-permute-start | bytes 884744 | tf_op jit(solution)/shard_map/ppermute | solution.py:388
  28.0 22.4 %collective-permute-start.4 = (bf16[3,2,32,768]{3,2,1,0:T(8,128)(2,1)}, bf16[3,2,32,768]{3,2,1,0:T(8,128)(2,1)S(1)}, u32[]{:S(2)}, u32[]{:S(2)}) collective-permute-start(bf16[3,2,32,768]{3,2,1,0:T(8,128)(2,1)} %get-tuple-element.29), channel_id=1, source_target_pairs={{0,24},{8,16},{16,8},{24,0},{1,25},{9,17},{17,9},{25,1},{2,26},{10... | collective-permute-start | bytes 884744 | tf_op jit(solution)/shard_map/ppermute | solution.py:388

commit v10 on v9

--- a/solution.py
+++ b/solution.py
@@ -11,6 +11,7 @@
 LOOK_C = 16
 CHUNK = 32
 HALO = 24
+ORDER = (0, 2, 3, 1)
 TILE = 16
 LANES = 128
 MIB = 1024 * 1024
@@ -360,7 +361,9 @@
 
 
 def pair_table(pairs, groups, acq, mine, odd, chunks):
-    close = ((pairs // acq) ^ mine) * acq + pairs % acq
+    apart = (pairs // acq) ^ mine
+    rank = sum(jnp.where(apart == s, r, 0) for r, s in enumerate(ORDER))
+    close = rank * acq + pairs % acq
     m, s = close[:, 0], close[:, 1]
     slot = slot_of(jnp.minimum(m, s), jnp.maximum(m, s))
     turn = jnp.arange(pairs.shape[0])
@@ -384,7 +387,7 @@
 
     def send(blocks):
         moved = [blocks[0]]
-        for s in range(1, groups):
+        for s in ORDER[1:]:
             moved.append(lax.ppermute(blocks[s], "acq", [(i, i ^ s) for i in range(groups)]))
         return moved
 
@@ -404,7 +407,7 @@
         resample_edge(1, reach, group, side, kernel, offsets, slab, across, pieces[0], groups)
     )
     result = None
-    for turn, (moved, known) in enumerate(((middle, 0), (second, 0), (third, groups - 1))):
+    for turn, (moved, known) in enumerate(((middle, 0), (second, 0), (third, 2))):
         near = None
         if known:
             mine, result = lax.optimization_barrier((moved[0], result))

time: 54.6 us -> 56.3 us (1.031)
  the two profiles are of different devices: /device:TPU:9 before, /device:TPU:24 now
where the time goes in v10:
time: 56.3 us; the launch traced here: 56.1 us
  Pallas kernels  22.3 us (40%)
  waiting for transfers between devices  17.4 us (31%)
  starting transfers between devices  15 us (27%)
  local copies, waits for them, and re-layouts  0.69 us (1%)
  other arithmetic  0.57 us (1%)
    pallas_call x3, Pallas kernels, interfere(): pl.pallas_call(functools.partial(interfere_kernel, groups, known, turn),...  15.3 us
    ppermute x9, starting transfers between devices, send(): lax.ppermute(blocks[s], 'acq', [(i, i ^ s) for i in range(groups)])  12.5 us
    ppermute x9, waiting for transfers between devices, send(): lax.ppermute(blocks[s], 'acq', [(i, i ^ s) for i in range(groups)])  12.1 us
    ppermute x2, waiting for transfers between devices, swap(): return lax.ppermute(halo, 'pix', pairs_up + [(j, i) for i, j in pairs_up])  5.26 us
    pallas_call x2, Pallas kernels, resample_edge(): pl.pallas_call(functools.partial(edge_kernel, groups, parity, count), in_...  3.07 us
    ppermute x2, starting transfers between devices, swap(): return lax.ppermute(halo, 'pix', pairs_up + [(j, i) for i, j in pairs_up])  2.52 us
    pallas_call x1, Pallas kernels, resample_first(): pl.pallas_call(functools.partial(first_kernel, first, groups), in_specs=[...  2.45 us
    pallas_call x1, Pallas kernels, interfere_near(): pl.pallas_call(functools.partial(near_kernel, groups), in_specs=[VMEM] *...  1.54 us
  transfers between devices with their start and end apart: 11, of which 3 were waited for; matrix products, arithmetic and copies ran while one was open for 2% of the time, Pallas kernels for 27%

profile of v10, /device:TPU:24, one launch (start us, length us, event | category | flops | bytes accessed | tf_op | source)
XLA Modules:
  0.0 56.1 jit_solution(6262364751839273410)
XLA Ops:
  0.0 0.0 copy-start
  0.0 0.0 copy-start.1
  0.0 2.4 %resample_first.1 = (bf16[3,2,32,768]{3,2,1,0:T(8,128)(2,1)S(1)}, bf16[3,2,32,768]{3,2,1,0:T(8,128)(2,1)S(1)}, bf16[3,2,32,768]{3,2,1,0:T(8,128)(2,1)S(1)}, bf16...) custom-call(s32[1]{0:T(128)} %bitcast.2.group, ...), custom_call_target="tpu_custom_call" | custom-call | flops 113246208 | bytes 4718592 | tf_op jit(solution)/shard_map/resample_first/pallas_call | solution.py:138
  2.5 0.1 collective-permute-start.1
  2.5 2.4 %collective-permute-start = (bf16[3,2,24,3072]{3,2,1,0:T(8,128)(2,1)S(1)}, bf16[3,2,24,3072]{3,2,1,0:T(8,128)(2,1)S(1)}, u32[]{:S(2)}, u32[]{:S(2)}) collective-permute-start(bf16[3,2,24,3072]{3,2,1,0:T(8,128)(2,1)S(1)} %get-tuple-element.23), channel_id=1, source_target_pairs={{1,2},{3,4},{5,6},{2,1},{4,3},{6,5},{9,10},{11,12},{13,14},{10,9},... | collective-permute-start | bytes 2654216 | tf_op jit(solution)/shard_map/ppermute | solution.py:396
  5.0 1.6 %collective-permute-start.8 = (bf16[3,2,32,768]{3,2,1,0:T(8,128)(2,1)S(1)}, bf16[3,2,32,768]{3,2,1,0:T(8,128)(2,1)S(1)}, u32[]{:S(2)}, u32[]{:S(2)}) collective-permute-start(bf16[3,2,32,768]{3,2,1,0:T(8,128)(2,1)S(1)} %get-tuple-element.34), channel_id=1, source_target_pairs={{0,16},{8,24},{16,0},{24,8},{1,17},{9,25},{17,1},{25,9},{2,18},{10... | collective-permute-start | bytes 884744 | tf_op jit(solution)/shard_map/ppermute | solution.py:391
  6.6 1.4 %collective-permute-start.9 = (bf16[3,2,32,768]{3,2,1,0:T(8,128)(2,1)S(1)}, bf16[3,2,32,768]{3,2,1,0:T(8,128)(2,1)S(1)}, u32[]{:S(2)}, u32[]{:S(2)}) collective-permute-start(bf16[3,2,32,768]{3,2,1,0:T(8,128)(2,1)S(1)} %get-tuple-element.35), channel_id=1, source_target_pairs={{0,24},{8,16},{16,8},{24,0},{1,25},{9,17},{17,9},{25,1},{2,26},{10... | collective-permute-start | bytes 884744 | tf_op jit(solution)/shard_map/ppermute | solution.py:391
  8.0 0.5 collective-permute-start.10
  8.6 0.0 collective-permute-done.1.halo
  8.6 0.0 copy-done
  8.6 0.0 copy-done.1
  8.6 0.0 copy-start.2
  8.6 1.5 %resample_edge.2 = (bf16[3,2,32,768]{3,2,1,0:T(8,128)(2,1)S(1)}, bf16[3,2,32,768]{3,2,1,0:T(8,128)(2,1)}, bf16[3,2,32,768]{3,2,1,0:T(8,128)(2,1)S(1)}, bf16[3,2,32,768]{3,2,1,0:T(8,128)(2,1)}) custom-call(s32[1]{0:T(128)} %bitcast.2.group, s32[1]{0:T(128)} %bitcast.3.side, bf16[8,12]{1,0:T(8,128)(2,1)S(1)} %bitcast.17, s32[3,96]{1,0:T(4,128)S(1)} %copy-done.1, ...), custom_call_target="tpu_custom_call" | custom-call | flops 103809024 | bytes 4423680 | tf_op jit(solution)/shard_map/resample_edge/pallas_call | solution.py:158
  10.1 1.5 %collective-permute-start.5 = (bf16[3,2,32,768]{3,2,1,0:T(8,128)(2,1)S(1)}, bf16[3,2,32,768]{3,2,1,0:T(8,128)(2,1)S(1)}, u32[]{:S(2)}, u32[]{:S(2)}) collective-permute-start(bf16[3,2,32,768]{3,2,1,0:T(8,128)(2,1)S(1)} %get-tuple-element.30), channel_id=1, source_target_pairs={{0,16},{8,24},{16,0},{24,8},{1,17},{9,25},{17,1},{25,9},{2,18},{10... | collective-permute-start | bytes 884744 | tf_op jit(solution)/shard_map/ppermute | solution.py:391
  11.6 0.0 copy-done.2
  11.7 5.3 %collective-permute-done.halo = bf16[3,2,24,3072]{3,2,1,0:T(8,128)(2,1)S(1)} collective-permute-done((bf16[3,2,24,3072]{3,2,1,0:T(8,128)(2,1)S(1)}, bf16[3,2,24,3072]{3,2,1,0:T(8,128)(2,1)S(1)}, u32[]{:S(2)}, u32[]{:S(2)}) %collective-permute-start) | collective-permute-done | bytes 884768 | tf_op jit(solution)/shard_map/ppermute | solution.py:396
  16.9 2.4 %collective-permute-start.6 = (bf16[3,2,32,768]{3,2,1,0:T(8,128)(2,1)}, bf16[3,2,32,768]{3,2,1,0:T(8,128)(2,1)S(1)}, u32[]{:S(2)}, u32[]{:S(2)}) collective-permute-start(bf16[3,2,32,768]{3,2,1,0:T(8,128)(2,1)} %get-tuple-element.31), channel_id=1, source_target_pairs={{0,24},{8,16},{16,8},{24,0},{1,25},{9,17},{17,9},{25,1},{2,26},{10... | collective-permute-start | bytes 884744 | tf_op jit(solution)/shard_map/ppermute | solution.py:391
  19.4 1.5 %resample_edge.3 = (bf16[3,2,32,768]{3,2,1,0:T(8,128)(2,1)S(1)}, bf16[3,2,32,768]{3,2,1,0:T(8,128)(2,1)}, bf16[3,2,32,768]{3,2,1,0:T(8,128)(2,1)}, bf16[3,2,32,768]{3,2,1,0:T(8,128)(2,1)}) custom-call(s32[1]{0:T(128)} %bitcast.2.group, s32[1]{0:T(128)} %bitcast.3.side, bf16[8,12]{1,0:T(8,128)(2,1)S(1)} %bitcast.18, s32[3,96]{1,0:T(4,128)S(1)} %copy-done.1, ...), custom_call_target="tpu_custom_call" | custom-call | flops 103809024 | bytes 4423680 | tf_op jit(solution)/shard_map/resample_edge/pallas_call | solution.py:158
  20.9 3.0 %collective-permute-done.8.rest_1_ = bf16[3,2,32,768]{3,2,1,0:T(8,128)(2,1)S(1)} collective-permute-done((bf16[3,2,32,768]{3,2,1,0:T(8,128)(2,1)S(1)}, bf16[3,2,32,768]{3,2,1,0:T(8,128)(2,1)S(1)}, u32[]{:S(2)}, u32[]{:S(2)}) %collective-permute-start.8) | collective-permute-done | bytes 294944 | tf_op jit(solution)/shard_map/ppermute | solution.py:391
  23.8 1.5 %collective-permute-start.7 = (bf16[3,2,32,768]{3,2,1,0:T(8,128)(2,1)}, bf16[3,2,32,768]{3,2,1,0:T(8,128)(2,1)S(1)}, u32[]{:S(2)}, u32[]{:S(2)}) collective-permute-start(bf16[3,2,32,768]{3,2,1,0:T(8,128)(2,1)} %get-tuple-element.32), channel_id=1, source_target_pairs={{0,8},{8,0},{16,24},{24,16},{1,9},{9,1},{17,25},{25,17},{2,10},{10... | collective-permute-start | bytes 884744 | tf_op jit(solution)/shard_map/ppermute | solution.py:391
  25.3 0.0 collective-permute-done.9.rest_2_
  25.3 1.9 %collective-permute-start.2 = (bf16[3,2,32,768]{3,2,1,0:T(8,128)(2,1)}, bf16[3,2,32,768]{3,2,1,0:T(8,128)(2,1)S(1)}, u32[]{:S(2)}, u32[]{:S(2)}) collective-permute-start(bf16[3,2,32,768]{3,2,1,0:T(8,128)(2,1)} %get-tuple-element.27), channel_id=1, source_target_pairs={{0,16},{8,24},{16,0},{24,8},{1,17},{9,25},{17,1},{25,9},{2,18},{10... | collective-permute-start | bytes 884744 | tf_op jit(solution)/shard_map/ppermute | solution.py:391
  27.2 0.0 collective-permute-done.10.rest_3_
  27.2 0.1 collective-permute-start.3
  27.3 9.1 %collective-permute-done.5.rest_1_ = bf16[3,2,32,768]{3,2,1,0:T(8,128)(2,1)S(1)} collective-permute-done((bf16[3,2,32,768]{3,2,1,0:T(8,128)(2,1)S(1)}, bf16[3,2,32,768]{3,2,1,0:T(8,128)(2,1)S(1)}, u32[]{:S(2)}, u32[]{:S(2)}) %collective-permute-start.5) | collective-permute-done | bytes 294944 | tf_op jit(solution)/shard_map/ppermute | solution.py:391
  36.5 1.5 %collective-permute-start.4 = (bf16[3,2,32,768]{3,2,1,0:T(8,128)(2,1)}, bf16[3,2,32,768]{3,2,1,0:T(8,128)(2,1)S(1)}, u32[]{:S(2)}, u32[]{:S(2)}) collective-permute-start(bf16[3,2,32,768]{3,2,1,0:T(8,128)(2,1)} %get-tuple-element.29), channel_id=1, source_target_pairs={{0,8},{8,0},{16,24},{24,16},{1,9},{9,1},{17,25},{25,17},{2,10},{10... | collective-permute-start | bytes 884744 | tf_op jit(solution)/shard_map/ppermute | solution.py:391
  38.0 0.5 compare_select_fusion.2
  38.5 0.7 %stack.2.table = s32[5,60]{1,0:T(8,128)S(1)} concatenate(s32[1,60]{1,0:T(1,128)} %get-tuple-element.40, s32[1,60]{1,0:T(1,128)S(1)} %get-tuple-element.42, s32[1,60]{1,0:T(1,128)S(1)} %get-tuple-element.41, s32[1,60]{1,0:T(1,128)S(1)} %get-tuple-element.39, s32[1,60]{1,0:T(1,128)} %get-tuple-element.43), dimensions={0} | concatenate | bytes 2400 | tf_op jit(solution)/shard_map/stack | solution.py:372
  39.2 5.3 %interfere.3.rest_4_ = f32[2,24,48,60]{3,2,1,0:T(8,128)} custom-call(s32[5,60]{1,0:T(8,128)S(1)} %stack.2.table, bf16[3,2,32,768]{3,2,1,0:T(8,128)(2,1)S(1)} %get-tuple-element.33.rest_0_, bf16[3,2,32,768]{3,2,1,0:T(8,128)(2,1)S(1)} %collective-permute-done.8.rest_1_, bf16[3,2,32,768]{3,2,1,0:T(8,128)(2,1)S(1)} %collective-permute-done.9.rest_2_, ...), custom_call_target="tpu_custom_call" | custom-call | flops 11796480 | bytes 14155776 | tf_op jit(solution)/shard_map/interfere/pallas_call | solution.py:343
  44.5 0.0 collective-permute-done.6.rest_2_
  44.5 0.0 collective-permute-done.7.rest_3_
  44.5 5.3 %interfere.4.rest_5_ = f32[2,24,48,60]{3,2,1,0:T(8,128)} custom-call(s32[5,60]{1,0:T(8,128)S(1)} %stack.2.table, bf16[3,2,32,768]{3,2,1,0:T(8,128)(2,1)S(1)} %get-tuple-element.25._.rest_0_, bf16[3,2,32,768]{3,2,1,0:T(8,128)(2,1)S(1)} %collective-permute-done.5.rest_1_, ...), custom_call_target="tpu_custom_call", output_to_operand_aliasing={{}: (5, {})} | custom-call | flops 11796480 | bytes 14155776 | tf_op jit(solution)/shard_map/interfere/pallas_call | solution.py:343
  49.8 0.0 collective-permute-done.2.rest_1_
  49.9 1.5 %interfere_near.1.rest_4_ = f32[288,48]{1,0:T(8,128)S(1)} custom-call(bf16[3,2,32,768]{3,2,1,0:T(8,128)(2,1)S(1)} %get-tuple-element.37.rest_0_, bf16[3,2,32,768]{3,2,1,0:T(8,128)(2,1)S(1)} %collective-permute-done.2.rest_1_), custom_call_target="tpu_custom_call" | custom-call | flops 2949120 | bytes 7077888 | tf_op jit(solution)/shard_map/interfere_near/pallas_call | solution.py:324
  51.4 0.0 collective-permute-done.3.rest_2_
  51.4 0.0 collective-permute-done.4.rest_3_
  51.4 4.7 %interfere.5 = f32[2,24,48,60]{3,2,1,0:T(8,128)} custom-call(s32[5,60]{1,0:T(8,128)S(1)} %stack.2.table, bf16[3,2,32,768]{3,2,1,0:T(8,128)(2,1)S(1)} %get-tuple-element.37.rest_0_, bf16[3,2,32,768]{3,2,1,0:T(8,128)(2,1)S(1)} %collective-permute-done.2.rest_1_, ...), custom_call_target="tpu_custom_call", output_to_operand_aliasing={{}: (6, {})} | custom-call | flops 11796480 | bytes 14155776 | tf_op jit(solution)/shard_map/interfere/pallas_call | solution.py:343
  (2 shorter events, 0.0 us)
Async XLA Ops:
  0.0 8.6 %copy-start = (bf16[12,8]{0,1:T(8,128)(2,1)S(1)}, bf16[12,8]{0,1:T(8,128)(2,1)}, u32[]{:S(2)}) copy-start(bf16[12,8]{0,1:T(8,128)(2,1)} %param.6) | copy-start | bytes 580
  0.0 8.6 %copy-start.1 = (s32[3,96]{1,0:T(4,128)S(1)}, s32[3,96]{1,0:T(4,128)}, u32[]{:S(2)}) copy-start(s32[3,96]{1,0:T(4,128)} %off.5) | copy-start | bytes 3460
  2.5 6.1 %collective-permute-start.1 = (bf16[3,2,24,3072]{3,2,1,0:T(8,128)(2,1)S(1)}, bf16[3,2,24,3072]{3,2,1,0:T(8,128)(2,1)S(1)}, u32[]{:S(2)}, u32[]{:S(2)}) collective-permute-start(bf16[3,2,24,3072]{3,2,1,0:T(8,128)(2,1)S(1)} %get-tuple-element.24._), channel_id=1, source_target_pairs={{0,1},{2,3},{4,5},{6,7},{1,0},{3,2},{5,4},{7,6},{8,9},{10,11},{12,... | collective-permute-start | bytes 2654216 | tf_op jit(solution)/shard_map/ppermute | solution.py:396
  2.5 14.4 %collective-permute-start = (bf16[3,2,24,3072]{3,2,1,0:T(8,128)(2,1)S(1)}, bf16[3,2,24,3072]{3,2,1,0:T(8,128)(2,1)S(1)}, u32[]{:S(2)}, u32[]{:S(2)}) collective-permute-start(bf16[3,2,24,3072]{3,2,1,0:T(8,128)(2,1)S(1)} %get-tuple-element.23), channel_id=1, source_target_pairs={{1,2},{3,4},{5,6},{2,1},{4,3},{6,5},{9,10},{11,12},{13,14},{10,9},... | collective-permute-start | bytes 2654216 | tf_op jit(solution)/shard_map/ppermute | solution.py:396
  5.0 18.8 %collective-permute-start.8 = (bf16[3,2,32,768]{3,2,1,0:T(8,128)(2,1)S(1)}, bf16[3,2,32,768]{3,2,1,0:T(8,128)(2,1)S(1)}, u32[]{:S(2)}, u32[]{:S(2)}) collective-permute-start(bf16[3,2,32,768]{3,2,1,0:T(8,128)(2,1)S(1)} %get-tuple-element.34), channel_id=1, source_target_pairs={{0,16},{8,24},{16,0},{24,8},{1,17},{9,25},{17,1},{25,9},{2,18},{10... | collective-permute-start | bytes 884744 | tf_op jit(solution)/shard_map/ppermute | solution.py:391
  6.6 18.8 %collective-permute-start.9 = (bf16[3,2,32,768]{3,2,1,0:T(8,128)(2,1)S(1)}, bf16[3,2,32,768]{3,2,1,0:T(8,128)(2,1)S(1)}, u32[]{:S(2)}, u32[]{:S(2)}) collective-permute-start(bf16[3,2,32,768]{3,2,1,0:T(8,128)(2,1)S(1)} %get-tuple-element.35), channel_id=1, source_target_pairs={{0,24},{8,16},{16,8},{24,0},{1,25},{9,17},{17,9},{25,1},{2,26},{10... | collective-permute-start | bytes 884744 | tf_op jit(solution)/shard_map/ppermute | solution.py:391
  8.0 19.2 %collective-permute-start.10 = (bf16[3,2,32,768]{3,2,1,0:T(8,128)(2,1)S(1)}, bf16[3,2,32,768]{3,2,1,0:T(8,128)(2,1)S(1)}, u32[]{:S(2)}, u32[]{:S(2)}) collective-permute-start(bf16[3,2,32,768]{3,2,1,0:T(8,128)(2,1)S(1)} %get-tuple-element.36), channel_id=1, source_target_pairs={{0,8},{8,0},{16,24},{24,16},{1,9},{9,1},{17,25},{25,17},{2,10},{10... | collective-permute-start | bytes 884744 | tf_op jit(solution)/shard_map/ppermute | solution.py:391
  8.6 3.1 %copy-start.2 = (s32[60,2]{0,1:T(2,128)S(1)}, s32[60,2]{0,1:T(2,128)}, u32[]{:S(2)}) copy-start(s32[60,2]{0,1:T(2,128)} %param.7) | copy-start | bytes 1444
  10.1 26.4 %collective-permute-start.5 = (bf16[3,2,32,768]{3,2,1,0:T(8,128)(2,1)S(1)}, bf16[3,2,32,768]{3,2,1,0:T(8,128)(2,1)S(1)}, u32[]{:S(2)}, u32[]{:S(2)}) collective-permute-start(bf16[3,2,32,768]{3,2,1,0:T(8,128)(2,1)S(1)} %get-tuple-element.30), channel_id=1, source_target_pairs={{0,16},{8,24},{16,0},{24,8},{1,17},{9,25},{17,1},{25,9},{2,18},{10... | collective-permute-start | bytes 884744 | tf_op jit(solution)/shard_map/ppermute | solution.py:391
  16.9 27.6 %collective-permute-start.6 = (bf16[3,2,32,768]{3,2,1,0:T(8,128)(2,1)}, bf16[3,2,32,768]{3,2,1,0:T(8,128)(2,1)S(1)}, u32[]{:S(2)}, u32[]{:S(2)}) collective-permute-start(bf16[3,2,32,768]{3,2,1,0:T(8,128)(2,1)} %get-tuple-element.31), channel_id=1, source_target_pairs={{0,24},{8,16},{16,8},{24,0},{1,25},{9,17},{17,9},{25,1},{2,26},{10... | collective-permute-start | bytes 884744 | tf_op jit(solution)/shard_map/ppermute | solution.py:391
  23.8 20.7 %collective-permute-start.7 = (bf16[3,2,32,768]{3,2,1,0:T(8,128)(2,1)}, bf16[3,2,32,768]{3,2,1,0:T(8,128)(2,1)S(1)}, u32[]{:S(2)}, u32[]{:S(2)}) collective-permute-start(bf16[3,2,32,768]{3,2,1,0:T(8,128)(2,1)} %get-tuple-element.32), channel_id=1, source_target_pairs={{0,8},{8,0},{16,24},{24,16},{1,9},{9,1},{17,25},{25,17},{2,10},{10... | collective-permute-start | bytes 884744 | tf_op jit(solution)/shard_map/ppermute | solution.py:391
  25.3 24.5 %collective-permute-start.2 = (bf16[3,2,32,768]{3,2,1,0:T(8,128)(2,1)}, bf16[3,2,32,768]{3,2,1,0:T(8,128)(2,1)S(1)}, u32[]{:S(2)}, u32[]{:S(2)}) collective-permute-start(bf16[3,2,32,768]{3,2,1,0:T(8,128)(2,1)} %get-tuple-element.27), channel_id=1, source_target_pairs={{0,16},{8,24},{16,0},{24,8},{1,17},{9,25},{17,1},{25,9},{2,18},{10... | collective-permute-start | bytes 884744 | tf_op jit(solution)/shard_map/ppermute | solution.py:391
  27.2 24.2 %collective-permute-start.3 = (bf16[3,2,32,768]{3,2,1,0:T(8,128)(2,1)}, bf16[3,2,32,768]{3,2,1,0:T(8,128)(2,1)S(1)}, u32[]{:S(2)}, u32[]{:S(2)}) collective-permute-start(bf16[3,2,32,768]{3,2,1,0:T(8,128)(2,1)} %get-tuple-element.28), channel_id=1, source_target_pairs={{0,24},{8,16},{16,8},{24,0},{1,25},{9,17},{17,9},{25,1},{2,26},{10... | collective-permute-start | bytes 884744 | tf_op jit(solution)/shard_map/ppermute | solution.py:391
  36.5 14.9 %collective-permute-start.4 = (bf16[3,2,32,768]{3,2,1,0:T(8,128)(2,1)}, bf16[3,2,32,768]{3,2,1,0:T(8,128)(2,1)S(1)}, u32[]{:S(2)}, u32[]{:S(2)}) collective-permute-start(bf16[3,2,32,768]{3,2,1,0:T(8,128)(2,1)} %get-tuple-element.29), channel_id=1, source_target_pairs={{0,8},{8,0},{16,24},{24,16},{1,9},{9,1},{17,25},{25,17},{2,10},{10... | collective-permute-start | bytes 884744 | tf_op jit(solution)/shard_map/ppermute | solution.py:391

commit v11 on v10

--- a/solution.py
+++ b/solution.py
@@ -11,7 +11,7 @@
 LOOK_C = 16
 CHUNK = 32
 HALO = 24
-ORDER = (0, 2, 3, 1)
+ORDER = (0, 1, 2, 3)
 TILE = 16
 LANES = 128
 MIB = 1024 * 1024
@@ -174,7 +174,6 @@
 def look_sums(blocks, begin, parts, terms, sums, slot_rows, power_rows):
     acq, _, lines, width = blocks[0].shape
     looks = lines // LOOK_R
-    windows = width // LOOK_C
     both = 2 * looks
     tiles = width // LANES
     total, fresh = len(blocks) * acq, begin * acq
@@ -183,8 +182,8 @@
     used = split + (total - fresh) * looks
 
     def pool(tile):
-        row = lax.broadcasted_iota(jnp.int32, (2 * LANES, windows), 0)
-        window = lax.broadcasted_iota(jnp.int32, (2 * LANES, windows), 1)
+        row = lax.broadcasted_iota(jnp.int32, (2 * LANES, LANES), 0)
+        window = lax.broadcasted_iota(jnp.int32, (2 * LANES, LANES), 1) % (LANES // 2)
         wanted = tile * (LANES // LOOK_C) + (row % LANES) // LOOK_C
         return jnp.where(wanted == window, 1.0, 0.0).astype(jnp.bfloat16)
 
@@ -275,24 +274,28 @@
         near = rest[0]
         sums[:start, :] = near[:start, :]
         sums[split : split + fresh * looks, :] = near[start : start + fresh * looks, :]
+    windows = width // LOOK_C
     look_sums(blocks, known, parts, terms, sums, start, split + fresh * looks)
     inverse[...] = lax.rsqrt(sums[split : split + total * looks, :] + 1e-6)
+
+    left = lax.broadcasted_iota(jnp.int32, (looks, LANES), 1) < LANES // 2
 
     def select(p, carry):
         at = pl.multiple_of(table[0, p] * both, both)
         m = pl.multiple_of(table[1, p] * looks, looks)
         s = pl.multiple_of(table[2, p] * looks, looks)
         scale = inverse[pl.ds(m, looks), :] * inverse[pl.ds(s, looks), :]
-        turned = scale * table[3, p].astype(jnp.float32)
-        value = sums[pl.ds(at, both), :] * jnp.concatenate([scale, turned], axis=0)
-        flat[pl.ds(pl.multiple_of(p * both, both), both), :] = value
+        imag = sums[pl.ds(at + looks, looks), :] * table[3, p].astype(jnp.float32)
+        value = jnp.where(left, sums[pl.ds(at, looks), :], imag) * scale
+        flat[pl.ds(pl.multiple_of(p * looks, looks), looks), :] = value
         return carry
 
     lax.fori_loop(0, count, select, 0, unroll=max(b for b in range(1, 7) if count % b == 0))
     copies = []
     for g in range(looks):
+        turned = flat[pl.ds(g, count, stride=looks), :].T
         for x in range(2):
-            slab[x, g] = flat[pl.ds(x * looks + g, count, stride=both), :].T
+            slab[x, g] = turned[x * (LANES // 2) : x * (LANES // 2) + windows]
         copies.append(pltpu.make_async_copy(slab.at[:, g], out.at[:, table[4, turn] * looks + g], sem.at[g]))
         copies[-1].start()
     for copy in copies:
@@ -325,7 +328,7 @@
         functools.partial(near_kernel, groups),
         in_specs=[VMEM] * groups,
         out_specs=VMEM,
-        out_shape=pltpu.VMEM(((slot_of(0, total) * 2 + total) * looks, windows), jnp.float32),
+        out_shape=pltpu.VMEM(((slot_of(0, total) * 2 + total) * looks, LANES), jnp.float32),
         scratch_shapes=work_space(groups, 0, acq, lines, looks),
         compiler_params=pltpu.CompilerParams(vmem_limit_bytes=8 * MIB),
         cost_estimate=interfere_cost(slot_of(0, total), total, lines, width),
@@ -347,9 +350,9 @@
         out_shape=pltpu.HBM((2, chunks * looks, windows, count), jnp.float32),
         scratch_shapes=work_space(groups, known, acq, lines, looks)
         + [
-            pltpu.VMEM(((slot_of(0, total) * 2 + total) * looks, windows), jnp.float32),
-            pltpu.VMEM((count * 2 * looks, windows), jnp.float32),
-            pltpu.VMEM((total * looks, windows), jnp.float32),
+            pltpu.VMEM(((slot_of(0, total) * 2 + total) * looks, LANES), jnp.float32),
+            pltpu.VMEM((count * looks, LANES), jnp.float32),
+            pltpu.VMEM((total * looks, LANES), jnp.float32),
             pltpu.VMEM((2, looks, windows, count), jnp.float32),
             pltpu.SemaphoreType.DMA((looks,)),
         ],

time: 56.3 us -> 53 us (0.941)
  the two profiles are of different devices: /device:TPU:24 before, /device:TPU:9 now
where the time goes in v11:
time: 53 us; the launch traced here: 52.8 us
  Pallas kernels  22.3 us (42%)
  waiting for transfers between devices  15.3 us (29%)
  starting transfers between devices  13.8 us (26%)
  local copies, waits for them, and re-layouts  0.69 us (1%)
  other arithmetic  0.57 us (1%)
    pallas_call x3, Pallas kernels, interfere(): pl.pallas_call(functools.partial(interfere_kernel, groups, known, turn),...  15.2 us
    ppermute x9, starting transfers between devices, send(): lax.ppermute(blocks[s], 'acq', [(i, i ^ s) for i in range(groups)])  9.98 us
    ppermute x9, waiting for transfers between devices, send(): lax.ppermute(blocks[s], 'acq', [(i, i ^ s) for i in range(groups)])  9.31 us
    ppermute x2, waiting for transfers between devices, swap(): return lax.ppermute(halo, 'pix', pairs_up + [(j, i) for i, j in pairs_up])  6.03 us
    ppermute x2, starting transfers between devices, swap(): return lax.ppermute(halo, 'pix', pairs_up + [(j, i) for i, j in pairs_up])  3.82 us
    pallas_call x2, Pallas kernels, resample_edge(): pl.pallas_call(functools.partial(edge_kernel, groups, parity, count), in_...  3.07 us
    pallas_call x1, Pallas kernels, resample_first(): pl.pallas_call(functools.partial(first_kernel, first, groups), in_specs=[...  2.47 us
    pallas_call x1, Pallas kernels, interfere_near(): pl.pallas_call(functools.partial(near_kernel, groups), in_specs=[VMEM] *...  1.54 us
  transfers between devices with their start and end apart: 11, of which 4 were waited for; matrix products, arithmetic and copies ran while one was open for 2% of the time, Pallas kernels for 29%

profile of v11, /device:TPU:9, one launch (start us, length us, event | category | flops | bytes accessed | tf_op | source)
XLA Modules:
  0.0 52.8 jit_solution(16180245659821309799)
XLA Ops:
  0.0 0.0 copy-start
  0.0 0.0 copy-start.1
  0.0 2.5 %resample_first.1 = (bf16[3,2,32,768]{3,2,1,0:T(8,128)(2,1)S(1)}, bf16[3,2,32,768]{3,2,1,0:T(8,128)(2,1)S(1)}, bf16[3,2,32,768]{3,2,1,0:T(8,128)(2,1)S(1)}, bf16...) custom-call(s32[1]{0:T(128)} %bitcast.2.group, ...), custom_call_target="tpu_custom_call" | custom-call | flops 113246208 | bytes 4718592 | tf_op jit(solution)/shard_map/resample_first/pallas_call | solution.py:138
  2.5 0.7 %collective-permute-start.1 = (bf16[3,2,24,3072]{3,2,1,0:T(8,128)(2,1)S(1)}, bf16[3,2,24,3072]{3,2,1,0:T(8,128)(2,1)S(1)}, u32[]{:S(2)}, u32[]{:S(2)}) collective-permute-start(bf16[3,2,24,3072]{3,2,1,0:T(8,128)(2,1)S(1)} %get-tuple-element.24._), channel_id=1, source_target_pairs={{0,1},{2,3},{4,5},{6,7},{1,0},{3,2},{5,4},{7,6},{8,9},{10,11},{12,... | collective-permute-start | bytes 2654216 | tf_op jit(solution)/shard_map/ppermute | solution.py:399
  3.2 3.1 %collective-permute-start = (bf16[3,2,24,3072]{3,2,1,0:T(8,128)(2,1)S(1)}, bf16[3,2,24,3072]{3,2,1,0:T(8,128)(2,1)S(1)}, u32[]{:S(2)}, u32[]{:S(2)}) collective-permute-start(bf16[3,2,24,3072]{3,2,1,0:T(8,128)(2,1)S(1)} %get-tuple-element.23), channel_id=1, source_target_pairs={{1,2},{3,4},{5,6},{2,1},{4,3},{6,5},{9,10},{11,12},{13,14},{10,9},... | collective-permute-start | bytes 2654216 | tf_op jit(solution)/shard_map/ppermute | solution.py:399
  6.3 1.3 %collective-permute-start.8 = (bf16[3,2,32,768]{3,2,1,0:T(8,128)(2,1)S(1)}, bf16[3,2,32,768]{3,2,1,0:T(8,128)(2,1)S(1)}, u32[]{:S(2)}, u32[]{:S(2)}) collective-permute-start(bf16[3,2,32,768]{3,2,1,0:T(8,128)(2,1)S(1)} %get-tuple-element.34), channel_id=1, source_target_pairs={{0,8},{8,0},{16,24},{24,16},{1,9},{9,1},{17,25},{25,17},{2,10},{10... | collective-permute-start | bytes 884744 | tf_op jit(solution)/shard_map/ppermute | solution.py:394
  7.6 1.2 %collective-permute-start.9 = (bf16[3,2,32,768]{3,2,1,0:T(8,128)(2,1)S(1)}, bf16[3,2,32,768]{3,2,1,0:T(8,128)(2,1)S(1)}, u32[]{:S(2)}, u32[]{:S(2)}) collective-permute-start(bf16[3,2,32,768]{3,2,1,0:T(8,128)(2,1)S(1)} %get-tuple-element.35), channel_id=1, source_target_pairs={{0,16},{8,24},{16,0},{24,8},{1,17},{9,25},{17,1},{25,9},{2,18},{10... | collective-permute-start | bytes 884744 | tf_op jit(solution)/shard_map/ppermute | solution.py:394
  8.8 0.2 collective-permute-start.10
  9.0 0.0 collective-permute-done.1.halo
  9.0 0.0 copy-done
  9.0 0.0 copy-done.1
  9.0 0.0 copy-start.2
  9.1 1.5 %resample_edge.2 = (bf16[3,2,32,768]{3,2,1,0:T(8,128)(2,1)S(1)}, bf16[3,2,32,768]{3,2,1,0:T(8,128)(2,1)S(1)}, bf16[3,2,32,768]{3,2,1,0:T(8,128)(2,1)}, bf16[3,2,32,768]{3,2,1,0:T(8,128)(2,1)}) custom-call(s32[1]{0:T(128)} %bitcast.2.group, s32[1]{0:T(128)} %bitcast.3.side, bf16[8,12]{1,0:T(8,128)(2,1)S(1)} %bitcast.17, s32[3,96]{1,0:T(4,128)S(1)} %copy-done.1, ...), custom_call_target="tpu_custom_call" | custom-call | flops 103809024 | bytes 4423680 | tf_op jit(solution)/shard_map/resample_edge/pallas_call | solution.py:158
  10.6 1.2 %collective-permute-start.5 = (bf16[3,2,32,768]{3,2,1,0:T(8,128)(2,1)S(1)}, bf16[3,2,32,768]{3,2,1,0:T(8,128)(2,1)S(1)}, u32[]{:S(2)}, u32[]{:S(2)}) collective-permute-start(bf16[3,2,32,768]{3,2,1,0:T(8,128)(2,1)S(1)} %get-tuple-element.30), channel_id=1, source_target_pairs={{0,8},{8,0},{16,24},{24,16},{1,9},{9,1},{17,25},{25,17},{2,10},{10... | collective-permute-start | bytes 884744 | tf_op jit(solution)/shard_map/ppermute | solution.py:394
  11.8 0.0 copy-done.2
  11.8 6.0 %collective-permute-done.halo = bf16[3,2,24,3072]{3,2,1,0:T(8,128)(2,1)S(1)} collective-permute-done((bf16[3,2,24,3072]{3,2,1,0:T(8,128)(2,1)S(1)}, bf16[3,2,24,3072]{3,2,1,0:T(8,128)(2,1)S(1)}, u32[]{:S(2)}, u32[]{:S(2)}) %collective-permute-start) | collective-permute-done | bytes 884768 | tf_op jit(solution)/shard_map/ppermute | solution.py:399
  17.8 1.2 %collective-permute-start.6 = (bf16[3,2,32,768]{3,2,1,0:T(8,128)(2,1)}, bf16[3,2,32,768]{3,2,1,0:T(8,128)(2,1)S(1)}, u32[]{:S(2)}, u32[]{:S(2)}) collective-permute-start(bf16[3,2,32,768]{3,2,1,0:T(8,128)(2,1)} %get-tuple-element.31), channel_id=1, source_target_pairs={{0,16},{8,24},{16,0},{24,8},{1,17},{9,25},{17,1},{25,9},{2,18},{10... | collective-permute-start | bytes 884744 | tf_op jit(solution)/shard_map/ppermute | solution.py:394
  19.1 1.5 %resample_edge.3 = (bf16[3,2,32,768]{3,2,1,0:T(8,128)(2,1)S(1)}, bf16[3,2,32,768]{3,2,1,0:T(8,128)(2,1)}, bf16[3,2,32,768]{3,2,1,0:T(8,128)(2,1)}, bf16[3,2,32,768]{3,2,1,0:T(8,128)(2,1)}) custom-call(s32[1]{0:T(128)} %bitcast.2.group, s32[1]{0:T(128)} %bitcast.3.side, bf16[8,12]{1,0:T(8,128)(2,1)S(1)} %bitcast.18, s32[3,96]{1,0:T(4,128)S(1)} %copy-done.1, ...), custom_call_target="tpu_custom_call" | custom-call | flops 103809024 | bytes 4423680 | tf_op jit(solution)/shard_map/resample_edge/pallas_call | solution.py:158
  20.6 0.0 collective-permute-done.8.rest_1_
  20.6 1.1 %collective-permute-start.7 = (bf16[3,2,32,768]{3,2,1,0:T(8,128)(2,1)}, bf16[3,2,32,768]{3,2,1,0:T(8,128)(2,1)S(1)}, u32[]{:S(2)}, u32[]{:S(2)}) collective-permute-start(bf16[3,2,32,768]{3,2,1,0:T(8,128)(2,1)} %get-tuple-element.32), channel_id=1, source_target_pairs={{0,24},{8,16},{16,8},{24,0},{1,25},{9,17},{17,9},{25,1},{2,26},{10... | collective-permute-start | bytes 884744 | tf_op jit(solution)/shard_map/ppermute | solution.py:394
  21.8 1.1 %collective-permute-done.9.rest_2_ = bf16[3,2,32,768]{3,2,1,0:T(8,128)(2,1)S(1)} collective-permute-done((bf16[3,2,32,768]{3,2,1,0:T(8,128)(2,1)S(1)}, bf16[3,2,32,768]{3,2,1,0:T(8,128)(2,1)S(1)}, u32[]{:S(2)}, u32[]{:S(2)}) %collective-permute-start.9) | collective-permute-done | bytes 294944 | tf_op jit(solution)/shard_map/ppermute | solution.py:394
  22.8 0.0 collective-permute-start.2
  22.8 0.0 collective-permute-done.10.rest_3_
  22.8 1.5 %collective-permute-start.3 = (bf16[3,2,32,768]{3,2,1,0:T(8,128)(2,1)}, bf16[3,2,32,768]{3,2,1,0:T(8,128)(2,1)S(1)}, u32[]{:S(2)}, u32[]{:S(2)}) collective-permute-start(bf16[3,2,32,768]{3,2,1,0:T(8,128)(2,1)} %get-tuple-element.28), channel_id=1, source_target_pairs={{0,16},{8,24},{16,0},{24,8},{1,17},{9,25},{17,1},{25,9},{2,18},{10... | collective-permute-start | bytes 884744 | tf_op jit(solution)/shard_map/ppermute | solution.py:394
  24.3 3.7 %collective-permute-done.5.rest_1_ = bf16[3,2,32,768]{3,2,1,0:T(8,128)(2,1)S(1)} collective-permute-done((bf16[3,2,32,768]{3,2,1,0:T(8,128)(2,1)S(1)}, bf16[3,2,32,768]{3,2,1,0:T(8,128)(2,1)S(1)}, u32[]{:S(2)}, u32[]{:S(2)}) %collective-permute-start.5) | collective-permute-done | bytes 294944 | tf_op jit(solution)/shard_map/ppermute | solution.py:394
  28.0 2.2 %collective-permute-start.4 = (bf16[3,2,32,768]{3,2,1,0:T(8,128)(2,1)}, bf16[3,2,32,768]{3,2,1,0:T(8,128)(2,1)S(1)}, u32[]{:S(2)}, u32[]{:S(2)}) collective-permute-start(bf16[3,2,32,768]{3,2,1,0:T(8,128)(2,1)} %get-tuple-element.29), channel_id=1, source_target_pairs={{0,24},{8,16},{16,8},{24,0},{1,25},{9,17},{17,9},{25,1},{2,26},{10... | collective-permute-start | bytes 884744 | tf_op jit(solution)/shard_map/ppermute | solution.py:394
  30.2 0.5 %compare_select_fusion.2 = (s32[1,60]{1,0:T(1,128)S(1)}, s32[1,60]{1,0:T(1,128)}, s32[1,60]{1,0:T(1,128)}) fusion(s32[60,2]{0,1:T(2,128)S(1)} %fusion.3, pred[]{:T(512)S(6)} %eq.62), kind=kLoop, calls=%fused_computation.2 | loop fusion | flops 1620 | bytes 1201 | tf_op jit(solution)/shard_map/jit(_where)/select_n | solution.py:375
  30.8 0.7 %stack.2.table = s32[5,60]{1,0:T(8,128)S(1)} concatenate(s32[1,60]{1,0:T(1,128)} %get-tuple-element.40, s32[1,60]{1,0:T(1,128)S(1)} %get-tuple-element.42, s32[1,60]{1,0:T(1,128)S(1)} %get-tuple-element.41, s32[1,60]{1,0:T(1,128)S(1)} %get-tuple-element.39, s32[1,60]{1,0:T(1,128)} %get-tuple-element.43), dimensions={0} | concatenate | bytes 2400 | tf_op jit(solution)/shard_map/stack | solution.py:375
  31.4 5.3 %interfere.3.rest_4_ = f32[2,24,48,60]{3,2,1,0:T(8,128)} custom-call(s32[5,60]{1,0:T(8,128)S(1)} %stack.2.table, bf16[3,2,32,768]{3,2,1,0:T(8,128)(2,1)S(1)} %get-tuple-element.33.rest_0_, bf16[3,2,32,768]{3,2,1,0:T(8,128)(2,1)S(1)} %collective-permute-done.8.rest_1_, bf16[3,2,32,768]{3,2,1,0:T(8,128)(2,1)S(1)} %collective-permute-done.9.rest_2_, ...), custom_call_target="tpu_custom_call" | custom-call | flops 11796480 | bytes 14155776 | tf_op jit(solution)/shard_map/interfere/pallas_call | solution.py:346
  36.7 0.0 collective-permute-done.6.rest_2_
  36.7 0.0 collective-permute-done.7.rest_3_
  36.8 5.3 %interfere.4.rest_5_ = f32[2,24,48,60]{3,2,1,0:T(8,128)} custom-call(s32[5,60]{1,0:T(8,128)S(1)} %stack.2.table, bf16[3,2,32,768]{3,2,1,0:T(8,128)(2,1)S(1)} %get-tuple-element.25._.rest_0_, bf16[3,2,32,768]{3,2,1,0:T(8,128)(2,1)S(1)} %collective-permute-done.5.rest_1_, ...), custom_call_target="tpu_custom_call", output_to_operand_aliasing={{}: (5, {})} | custom-call | flops 11796480 | bytes 14155776 | tf_op jit(solution)/shard_map/interfere/pallas_call | solution.py:346
  42.0 0.0 collective-permute-done.2.rest_1_
  42.1 1.5 %interfere_near.1.rest_4_ = f32[288,128]{1,0:T(8,128)S(1)} custom-call(bf16[3,2,32,768]{3,2,1,0:T(8,128)(2,1)S(1)} %get-tuple-element.37.rest_0_, bf16[3,2,32,768]{3,2,1,0:T(8,128)(2,1)S(1)} %collective-permute-done.2.rest_1_), custom_call_target="tpu_custom_call" | custom-call | flops 2949120 | bytes 7077888 | tf_op jit(solution)/shard_map/interfere_near/pallas_call | solution.py:327
  43.6 4.5 %collective-permute-done.3.rest_2_ = bf16[3,2,32,768]{3,2,1,0:T(8,128)(2,1)S(1)} collective-permute-done((bf16[3,2,32,768]{3,2,1,0:T(8,128)(2,1)}, bf16[3,2,32,768]{3,2,1,0:T(8,128)(2,1)S(1)}, u32[]{:S(2)}, u32[]{:S(2)}) %collective-permute-start.3) | collective-permute-done | bytes 294944 | tf_op jit(solution)/shard_map/ppermute | solution.py:394
  48.1 0.0 collective-permute-done.4.rest_3_
  48.1 4.7 %interfere.5 = f32[2,24,48,60]{3,2,1,0:T(8,128)} custom-call(s32[5,60]{1,0:T(8,128)S(1)} %stack.2.table, bf16[3,2,32,768]{3,2,1,0:T(8,128)(2,1)S(1)} %get-tuple-element.37.rest_0_, bf16[3,2,32,768]{3,2,1,0:T(8,128)(2,1)S(1)} %collective-permute-done.2.rest_1_, ...), custom_call_target="tpu_custom_call", output_to_operand_aliasing={{}: (6, {})} | custom-call | flops 11796480 | bytes 14155776 | tf_op jit(solution)/shard_map/interfere/pallas_call | solution.py:346
  (2 shorter events, 0.0 us)
Async XLA Ops:
  0.0 9.0 %copy-start = (bf16[12,8]{0,1:T(8,128)(2,1)S(1)}, bf16[12,8]{0,1:T(8,128)(2,1)}, u32[]{:S(2)}) copy-start(bf16[12,8]{0,1:T(8,128)(2,1)} %param.6) | copy-start | bytes 580
  0.0 9.0 %copy-start.1 = (s32[3,96]{1,0:T(4,128)S(1)}, s32[3,96]{1,0:T(4,128)}, u32[]{:S(2)}) copy-start(s32[3,96]{1,0:T(4,128)} %off.5) | copy-start | bytes 3460
  2.5 6.5 %collective-permute-start.1 = (bf16[3,2,24,3072]{3,2,1,0:T(8,128)(2,1)S(1)}, bf16[3,2,24,3072]{3,2,1,0:T(8,128)(2,1)S(1)}, u32[]{:S(2)}, u32[]{:S(2)}) collective-permute-start(bf16[3,2,24,3072]{3,2,1,0:T(8,128)(2,1)S(1)} %get-tuple-element.24._), channel_id=1, source_target_pairs={{0,1},{2,3},{4,5},{6,7},{1,0},{3,2},{5,4},{7,6},{8,9},{10,11},{12,... | collective-permute-start | bytes 2654216 | tf_op jit(solution)/shard_map/ppermute | solution.py:399
  3.2 14.6 %collective-permute-start = (bf16[3,2,24,3072]{3,2,1,0:T(8,128)(2,1)S(1)}, bf16[3,2,24,3072]{3,2,1,0:T(8,128)(2,1)S(1)}, u32[]{:S(2)}, u32[]{:S(2)}) collective-permute-start(bf16[3,2,24,3072]{3,2,1,0:T(8,128)(2,1)S(1)} %get-tuple-element.23), channel_id=1, source_target_pairs={{1,2},{3,4},{5,6},{2,1},{4,3},{6,5},{9,10},{11,12},{13,14},{10,9},... | collective-permute-start | bytes 2654216 | tf_op jit(solution)/shard_map/ppermute | solution.py:399
  6.3 14.3 %collective-permute-start.8 = (bf16[3,2,32,768]{3,2,1,0:T(8,128)(2,1)S(1)}, bf16[3,2,32,768]{3,2,1,0:T(8,128)(2,1)S(1)}, u32[]{:S(2)}, u32[]{:S(2)}) collective-permute-start(bf16[3,2,32,768]{3,2,1,0:T(8,128)(2,1)S(1)} %get-tuple-element.34), channel_id=1, source_target_pairs={{0,8},{8,0},{16,24},{24,16},{1,9},{9,1},{17,25},{25,17},{2,10},{10... | collective-permute-start | bytes 884744 | tf_op jit(solution)/shard_map/ppermute | solution.py:394
  7.6 15.2 %collective-permute-start.9 = (bf16[3,2,32,768]{3,2,1,0:T(8,128)(2,1)S(1)}, bf16[3,2,32,768]{3,2,1,0:T(8,128)(2,1)S(1)}, u32[]{:S(2)}, u32[]{:S(2)}) collective-permute-start(bf16[3,2,32,768]{3,2,1,0:T(8,128)(2,1)S(1)} %get-tuple-element.35), channel_id=1, source_target_pairs={{0,16},{8,24},{16,0},{24,8},{1,17},{9,25},{17,1},{25,9},{2,18},{10... | collective-permute-start | bytes 884744 | tf_op jit(solution)/shard_map/ppermute | solution.py:394
  8.8 14.0 %collective-permute-start.10 = (bf16[3,2,32,768]{3,2,1,0:T(8,128)(2,1)S(1)}, bf16[3,2,32,768]{3,2,1,0:T(8,128)(2,1)S(1)}, u32[]{:S(2)}, u32[]{:S(2)}) collective-permute-start(bf16[3,2,32,768]{3,2,1,0:T(8,128)(2,1)S(1)} %get-tuple-element.36), channel_id=1, source_target_pairs={{0,24},{8,16},{16,8},{24,0},{1,25},{9,17},{17,9},{25,1},{2,26},{10... | collective-permute-start | bytes 884744 | tf_op jit(solution)/shard_map/ppermute | solution.py:394
  9.0 2.8 %copy-start.2 = (s32[60,2]{0,1:T(2,128)S(1)}, s32[60,2]{0,1:T(2,128)}, u32[]{:S(2)}) copy-start(s32[60,2]{0,1:T(2,128)} %param.7) | copy-start | bytes 1444
  10.6 17.5 %collective-permute-start.5 = (bf16[3,2,32,768]{3,2,1,0:T(8,128)(2,1)S(1)}, bf16[3,2,32,768]{3,2,1,0:T(8,128)(2,1)S(1)}, u32[]{:S(2)}, u32[]{:S(2)}) collective-permute-start(bf16[3,2,32,768]{3,2,1,0:T(8,128)(2,1)S(1)} %get-tuple-element.30), channel_id=1, source_target_pairs={{0,8},{8,0},{16,24},{24,16},{1,9},{9,1},{17,25},{25,17},{2,10},{10... | collective-permute-start | bytes 884744 | tf_op jit(solution)/shard_map/ppermute | solution.py:394
  17.8 18.9 %collective-permute-start.6 = (bf16[3,2,32,768]{3,2,1,0:T(8,128)(2,1)}, bf16[3,2,32,768]{3,2,1,0:T(8,128)(2,1)S(1)}, u32[]{:S(2)}, u32[]{:S(2)}) collective-permute-start(bf16[3,2,32,768]{3,2,1,0:T(8,128)(2,1)} %get-tuple-element.31), channel_id=1, source_target_pairs={{0,16},{8,24},{16,0},{24,8},{1,17},{9,25},{17,1},{25,9},{2,18},{10... | collective-permute-start | bytes 884744 | tf_op jit(solution)/shard_map/ppermute | solution.py:394
  20.6 16.1 %collective-permute-start.7 = (bf16[3,2,32,768]{3,2,1,0:T(8,128)(2,1)}, bf16[3,2,32,768]{3,2,1,0:T(8,128)(2,1)S(1)}, u32[]{:S(2)}, u32[]{:S(2)}) collective-permute-start(bf16[3,2,32,768]{3,2,1,0:T(8,128)(2,1)} %get-tuple-element.32), channel_id=1, source_target_pairs={{0,24},{8,16},{16,8},{24,0},{1,25},{9,17},{17,9},{25,1},{2,26},{10... | collective-permute-start | bytes 884744 | tf_op jit(solution)/shard_map/ppermute | solution.py:394
  22.8 19.2 %collective-permute-start.2 = (bf16[3,2,32,768]{3,2,1,0:T(8,128)(2,1)}, bf16[3,2,32,768]{3,2,1,0:T(8,128)(2,1)S(1)}, u32[]{:S(2)}, u32[]{:S(2)}) collective-permute-start(bf16[3,2,32,768]{3,2,1,0:T(8,128)(2,1)} %get-tuple-element.27), channel_id=1, source_target_pairs={{0,8},{8,0},{16,24},{24,16},{1,9},{9,1},{17,25},{25,17},{2,10},{10... | collective-permute-start | bytes 884744 | tf_op jit(solution)/shard_map/ppermute | solution.py:394
  22.8 25.3 %collective-permute-start.3 = (bf16[3,2,32,768]{3,2,1,0:T(8,128)(2,1)}, bf16[3,2,32,768]{3,2,1,0:T(8,128)(2,1)S(1)}, u32[]{:S(2)}, u32[]{:S(2)}) collective-permute-start(bf16[3,2,32,768]{3,2,1,0:T(8,128)(2,1)} %get-tuple-element.28), channel_id=1, source_target_pairs={{0,16},{8,24},{16,0},{24,8},{1,17},{9,25},{17,1},{25,9},{2,18},{10... | collective-permute-start | bytes 884744 | tf_op jit(solution)/shard_map/ppermute | solution.py:394
  28.0 20.1 %collective-permute-start.4 = (bf16[3,2,32,768]{3,2,1,0:T(8,128)(2,1)}, bf16[3,2,32,768]{3,2,1,0:T(8,128)(2,1)S(1)}, u32[]{:S(2)}, u32[]{:S(2)}) collective-permute-start(bf16[3,2,32,768]{3,2,1,0:T(8,128)(2,1)} %get-tuple-element.29), channel_id=1, source_target_pairs={{0,24},{8,16},{16,8},{24,0},{1,25},{9,17},{17,9},{25,1},{2,26},{10... | collective-permute-start | bytes 884744 | tf_op jit(solution)/shard_map/ppermute | solution.py:394

commit v12 on v11

--- a/solution.py
+++ b/solution.py
@@ -260,8 +260,9 @@
     look_sums(blocks, 0, parts, terms, sums, 0, slot_of(0, groups * acq) * 2 * looks)
 
 
-def interfere_kernel(groups, known, turn, table, *rest):
-    blocks, rest = rest[:groups], rest[groups:]
+def interfere_kernel(via, known, turn, table, *rest):
+    groups = len(via)
+    blocks, rest = [rest[via.index(r)] for r in range(groups)], rest[groups:]
     out, parts, terms, sums, flat, inverse, slab, sem = rest[-8:]
     acq, _, lines, width = blocks[0].shape
     looks = lines // LOOK_R
@@ -336,7 +337,7 @@
     )(*blocks)
 
 
-def interfere(turn, chunks, table, blocks, near, known, before):
+def interfere(turn, chunks, table, blocks, via, near, known, before):
     groups = len(blocks)
     acq, _, lines, width = blocks[0].shape
     looks, windows, count = lines // LOOK_R, width // LOOK_C, table.shape[1]
@@ -344,7 +345,7 @@
     near = [] if near is None else [near]
     extra = [] if before is None else [before]
     return pl.pallas_call(
-        functools.partial(interfere_kernel, groups, known, turn),
+        functools.partial(interfere_kernel, via, known, turn),
         in_specs=[SMEM] + [VMEM] * (groups + len(near)) + [ANY] * len(extra),
         out_specs=ANY,
         out_shape=pltpu.HBM((2, chunks * looks, windows, count), jnp.float32),
@@ -360,7 +361,7 @@
         compiler_params=pltpu.CompilerParams(vmem_limit_bytes=8 * MIB),
         cost_estimate=interfere_cost(count, total, lines, width),
         name="interfere",
-    )(table, *blocks, *near, *extra)
+    )(table, *[blocks[r] for r in via], *near, *extra)
 
 
 def pair_table(pairs, groups, acq, mine, odd, chunks):
@@ -415,7 +416,7 @@
         if known:
             mine, result = lax.optimization_barrier((moved[0], result))
             near = interfere_near([mine, *moved[1:known]])
-        result = interfere(turn, chunks, table, moved, near, known, result)
+        result = interfere(turn, chunks, table, moved, ((0, 2, 1, 3), (0, 2, 1, 3), (0, 2, 1, 3))[turn], near, known, result)
     return jnp.transpose(result, (0, 3, 1, 2))
 
 

time: 53 us -> 53 us (level)
  waiting for transfers between devices: 15.3 us -> 14.6 us
    ppermute x9, waiting for transfers between devices: 9.31 us -> 8.61 us  [send(): lax.ppermute(blocks[s], 'acq', [(i, i ^ s) for i in range(groups)])]
where the time goes in v12:
time: 53 us; the launch traced here: 52.3 us
  Pallas kernels  22.3 us (42%)
  waiting for transfers between devices  14.6 us (28%)
  starting transfers between devices  14.1 us (27%)
  local copies, waits for them, and re-layouts  0.69 us (1%)
  other arithmetic  0.57 us (1%)
    pallas_call x3, Pallas kernels, interfere(): pl.pallas_call(functools.partial(interfere_kernel, via, known, turn), in_...  15.2 us
    ppermute x9, starting transfers between devices, send(): lax.ppermute(blocks[s], 'acq', [(i, i ^ s) for i in range(groups)])  10.2 us
    ppermute x9, waiting for transfers between devices, send(): lax.ppermute(blocks[s], 'acq', [(i, i ^ s) for i in range(groups)])  8.61 us
    ppermute x2, waiting for transfers between devices, swap(): return lax.ppermute(halo, 'pix', pairs_up + [(j, i) for i, j in pairs_up])  6 us
    ppermute x2, starting transfers between devices, swap(): return lax.ppermute(halo, 'pix', pairs_up + [(j, i) for i, j in pairs_up])  3.82 us
    pallas_call x2, Pallas kernels, resample_edge(): pl.pallas_call(functools.partial(edge_kernel, groups, parity, count), in_...  3.07 us
    pallas_call x1, Pallas kernels, resample_first(): pl.pallas_call(functools.partial(first_kernel, first, groups), in_specs=[...  2.47 us
    pallas_call x1, Pallas kernels, interfere_near(): pl.pallas_call(functools.partial(near_kernel, groups), in_specs=[VMEM] *...  1.54 us
  transfers between devices with their start and end apart: 11, of which 4 were waited for; matrix products, arithmetic and copies ran while one was open for 2% of the time, Pallas kernels for 29%

profile of v12, /device:TPU:9, one launch (start us, length us, event | category | flops | bytes accessed | tf_op | source)
XLA Modules:
  0.0 52.3 jit_solution(7868582489275226278)
XLA Ops:
  0.0 0.0 copy-start
  0.0 0.0 copy-start.1
  0.0 2.5 %resample_first.1 = (bf16[3,2,32,768]{3,2,1,0:T(8,128)(2,1)S(1)}, bf16[3,2,32,768]{3,2,1,0:T(8,128)(2,1)S(1)}, bf16[3,2,32,768]{3,2,1,0:T(8,128)(2,1)S(1)}, bf16...) custom-call(s32[1]{0:T(128)} %bitcast.2.group, ...), custom_call_target="tpu_custom_call" | custom-call | flops 113246208 | bytes 4718592 | tf_op jit(solution)/shard_map/resample_first/pallas_call | solution.py:138
  2.5 0.7 %collective-permute-start.1 = (bf16[3,2,24,3072]{3,2,1,0:T(8,128)(2,1)S(1)}, bf16[3,2,24,3072]{3,2,1,0:T(8,128)(2,1)S(1)}, u32[]{:S(2)}, u32[]{:S(2)}) collective-permute-start(bf16[3,2,24,3072]{3,2,1,0:T(8,128)(2,1)S(1)} %get-tuple-element.24._), channel_id=1, source_target_pairs={{0,1},{2,3},{4,5},{6,7},{1,0},{3,2},{5,4},{7,6},{8,9},{10,11},{12,... | collective-permute-start | bytes 2654216 | tf_op jit(solution)/shard_map/ppermute | solution.py:400
  3.2 3.1 %collective-permute-start = (bf16[3,2,24,3072]{3,2,1,0:T(8,128)(2,1)S(1)}, bf16[3,2,24,3072]{3,2,1,0:T(8,128)(2,1)S(1)}, u32[]{:S(2)}, u32[]{:S(2)}) collective-permute-start(bf16[3,2,24,3072]{3,2,1,0:T(8,128)(2,1)S(1)} %get-tuple-element.23), channel_id=1, source_target_pairs={{1,2},{3,4},{5,6},{2,1},{4,3},{6,5},{9,10},{11,12},{13,14},{10,9},... | collective-permute-start | bytes 2654216 | tf_op jit(solution)/shard_map/ppermute | solution.py:400
  6.3 1.3 %collective-permute-start.8 = (bf16[3,2,32,768]{3,2,1,0:T(8,128)(2,1)S(1)}, bf16[3,2,32,768]{3,2,1,0:T(8,128)(2,1)S(1)}, u32[]{:S(2)}, u32[]{:S(2)}) collective-permute-start(bf16[3,2,32,768]{3,2,1,0:T(8,128)(2,1)S(1)} %get-tuple-element.34), channel_id=1, source_target_pairs={{0,16},{8,24},{16,0},{24,8},{1,17},{9,25},{17,1},{25,9},{2,18},{10... | collective-permute-start | bytes 884744 | tf_op jit(solution)/shard_map/ppermute | solution.py:395
  7.6 1.2 %collective-permute-start.9 = (bf16[3,2,32,768]{3,2,1,0:T(8,128)(2,1)S(1)}, bf16[3,2,32,768]{3,2,1,0:T(8,128)(2,1)S(1)}, u32[]{:S(2)}, u32[]{:S(2)}) collective-permute-start(bf16[3,2,32,768]{3,2,1,0:T(8,128)(2,1)S(1)} %get-tuple-element.35), channel_id=1, source_target_pairs={{0,8},{8,0},{16,24},{24,16},{1,9},{9,1},{17,25},{25,17},{2,10},{10... | collective-permute-start | bytes 884744 | tf_op jit(solution)/shard_map/ppermute | solution.py:395
  8.8 0.2 collective-permute-start.10
  9.0 0.0 collective-permute-done.1.halo
  9.0 0.0 copy-done
  9.0 0.0 copy-done.1
  9.0 0.0 copy-start.2
  9.1 1.5 %resample_edge.2 = (bf16[3,2,32,768]{3,2,1,0:T(8,128)(2,1)S(1)}, bf16[3,2,32,768]{3,2,1,0:T(8,128)(2,1)}, bf16[3,2,32,768]{3,2,1,0:T(8,128)(2,1)S(1)}, bf16[3,2,32,768]{3,2,1,0:T(8,128)(2,1)}) custom-call(s32[1]{0:T(128)} %bitcast.2.group, s32[1]{0:T(128)} %bitcast.3.side, bf16[8,12]{1,0:T(8,128)(2,1)S(1)} %bitcast.17, s32[3,96]{1,0:T(4,128)S(1)} %copy-done.1, ...), custom_call_target="tpu_custom_call" | custom-call | flops 103809024 | bytes 4423680 | tf_op jit(solution)/shard_map/resample_edge/pallas_call | solution.py:158
  10.6 1.2 %collective-permute-start.5 = (bf16[3,2,32,768]{3,2,1,0:T(8,128)(2,1)S(1)}, bf16[3,2,32,768]{3,2,1,0:T(8,128)(2,1)S(1)}, u32[]{:S(2)}, u32[]{:S(2)}) collective-permute-start(bf16[3,2,32,768]{3,2,1,0:T(8,128)(2,1)S(1)} %get-tuple-element.30), channel_id=1, source_target_pairs={{0,16},{8,24},{16,0},{24,8},{1,17},{9,25},{17,1},{25,9},{2,18},{10... | collective-permute-start | bytes 884744 | tf_op jit(solution)/shard_map/ppermute | solution.py:395
  11.8 0.0 copy-done.2
  11.9 6.0 %collective-permute-done.halo = bf16[3,2,24,3072]{3,2,1,0:T(8,128)(2,1)S(1)} collective-permute-done((bf16[3,2,24,3072]{3,2,1,0:T(8,128)(2,1)S(1)}, bf16[3,2,24,3072]{3,2,1,0:T(8,128)(2,1)S(1)}, u32[]{:S(2)}, u32[]{:S(2)}) %collective-permute-start) | collective-permute-done | bytes 884768 | tf_op jit(solution)/shard_map/ppermute | solution.py:400
  17.8 1.2 %collective-permute-start.6 = (bf16[3,2,32,768]{3,2,1,0:T(8,128)(2,1)}, bf16[3,2,32,768]{3,2,1,0:T(8,128)(2,1)S(1)}, u32[]{:S(2)}, u32[]{:S(2)}) collective-permute-start(bf16[3,2,32,768]{3,2,1,0:T(8,128)(2,1)} %get-tuple-element.31), channel_id=1, source_target_pairs={{0,8},{8,0},{16,24},{24,16},{1,9},{9,1},{17,25},{25,17},{2,10},{10... | collective-permute-start | bytes 884744 | tf_op jit(solution)/shard_map/ppermute | solution.py:395
  19.1 1.5 %resample_edge.3 = (bf16[3,2,32,768]{3,2,1,0:T(8,128)(2,1)S(1)}, bf16[3,2,32,768]{3,2,1,0:T(8,128)(2,1)}, bf16[3,2,32,768]{3,2,1,0:T(8,128)(2,1)}, bf16[3,2,32,768]{3,2,1,0:T(8,128)(2,1)}) custom-call(s32[1]{0:T(128)} %bitcast.2.group, s32[1]{0:T(128)} %bitcast.3.side, bf16[8,12]{1,0:T(8,128)(2,1)S(1)} %bitcast.18, s32[3,96]{1,0:T(4,128)S(1)} %copy-done.1, ...), custom_call_target="tpu_custom_call" | custom-call | flops 103809024 | bytes 4423680 | tf_op jit(solution)/shard_map/resample_edge/pallas_call | solution.py:158
  20.6 0.0 collective-permute-done.8.rest_1_
  20.6 1.2 %collective-permute-start.7 = (bf16[3,2,32,768]{3,2,1,0:T(8,128)(2,1)}, bf16[3,2,32,768]{3,2,1,0:T(8,128)(2,1)S(1)}, u32[]{:S(2)}, u32[]{:S(2)}) collective-permute-start(bf16[3,2,32,768]{3,2,1,0:T(8,128)(2,1)} %get-tuple-element.32), channel_id=1, source_target_pairs={{0,24},{8,16},{16,8},{24,0},{1,25},{9,17},{17,9},{25,1},{2,26},{10... | collective-permute-start | bytes 884744 | tf_op jit(solution)/shard_map/ppermute | solution.py:395
  21.8 0.0 collective-permute-done.9.rest_2_
  21.8 0.2 collective-permute-start.2
  22.0 0.6 %collective-permute-done.10.rest_3_ = bf16[3,2,32,768]{3,2,1,0:T(8,128)(2,1)S(1)} collective-permute-done((bf16[3,2,32,768]{3,2,1,0:T(8,128)(2,1)S(1)}, bf16[3,2,32,768]{3,2,1,0:T(8,128)(2,1)S(1)}, u32[]{:S(2)}, u32[]{:S(2)}) %collective-permute-start.10) | collective-permute-done | bytes 294944 | tf_op jit(solution)/shard_map/ppermute | solution.py:395
  22.7 1.4 %collective-permute-start.3 = (bf16[3,2,32,768]{3,2,1,0:T(8,128)(2,1)}, bf16[3,2,32,768]{3,2,1,0:T(8,128)(2,1)S(1)}, u32[]{:S(2)}, u32[]{:S(2)}) collective-permute-start(bf16[3,2,32,768]{3,2,1,0:T(8,128)(2,1)} %get-tuple-element.28), channel_id=1, source_target_pairs={{0,8},{8,0},{16,24},{24,16},{1,9},{9,1},{17,25},{25,17},{2,10},{10... | collective-permute-start | bytes 884744 | tf_op jit(solution)/shard_map/ppermute | solution.py:395
  24.1 3.9 %collective-permute-done.5.rest_1_ = bf16[3,2,32,768]{3,2,1,0:T(8,128)(2,1)S(1)} collective-permute-done((bf16[3,2,32,768]{3,2,1,0:T(8,128)(2,1)S(1)}, bf16[3,2,32,768]{3,2,1,0:T(8,128)(2,1)S(1)}, u32[]{:S(2)}, u32[]{:S(2)}) %collective-permute-start.5) | collective-permute-done | bytes 294944 | tf_op jit(solution)/shard_map/ppermute | solution.py:395
  28.0 2.2 %collective-permute-start.4 = (bf16[3,2,32,768]{3,2,1,0:T(8,128)(2,1)}, bf16[3,2,32,768]{3,2,1,0:T(8,128)(2,1)S(1)}, u32[]{:S(2)}, u32[]{:S(2)}) collective-permute-start(bf16[3,2,32,768]{3,2,1,0:T(8,128)(2,1)} %get-tuple-element.29), channel_id=1, source_target_pairs={{0,24},{8,16},{16,8},{24,0},{1,25},{9,17},{17,9},{25,1},{2,26},{10... | collective-permute-start | bytes 884744 | tf_op jit(solution)/shard_map/ppermute | solution.py:395
  30.2 0.5 %compare_select_fusion.2 = (s32[1,60]{1,0:T(1,128)S(1)}, s32[1,60]{1,0:T(1,128)}, s32[1,60]{1,0:T(1,128)}) fusion(s32[60,2]{0,1:T(2,128)S(1)} %fusion.3, pred[]{:T(512)S(6)} %eq.62), kind=kLoop, calls=%fused_computation.2 | loop fusion | flops 1620 | bytes 1201 | tf_op jit(solution)/shard_map/jit(_where)/select_n | solution.py:376
  30.8 0.7 %stack.2.table = s32[5,60]{1,0:T(8,128)S(1)} concatenate(s32[1,60]{1,0:T(1,128)} %get-tuple-element.40, s32[1,60]{1,0:T(1,128)S(1)} %get-tuple-element.42, s32[1,60]{1,0:T(1,128)S(1)} %get-tuple-element.41, s32[1,60]{1,0:T(1,128)S(1)} %get-tuple-element.39, s32[1,60]{1,0:T(1,128)} %get-tuple-element.43), dimensions={0} | concatenate | bytes 2400 | tf_op jit(solution)/shard_map/stack | solution.py:376
  31.4 5.3 %interfere.3.rest_4_ = f32[2,24,48,60]{3,2,1,0:T(8,128)} custom-call(s32[5,60]{1,0:T(8,128)S(1)} %stack.2.table, bf16[3,2,32,768]{3,2,1,0:T(8,128)(2,1)S(1)} %get-tuple-element.33.rest_0_, bf16[3,2,32,768]{3,2,1,0:T(8,128)(2,1)S(1)} %collective-permute-done.8.rest_1_, bf16[3,2,32,768]{3,2,1,0:T(8,128)(2,1)S(1)} %collective-permute-done.9.rest_2_, ...), custom_call_target="tpu_custom_call" | custom-call | flops 11796480 | bytes 14155776 | tf_op jit(solution)/shard_map/interfere/pallas_call | solution.py:347
  36.7 0.0 collective-permute-done.6.rest_2_
  36.7 0.0 collective-permute-done.7.rest_3_
  36.7 5.3 %interfere.4.rest_5_ = f32[2,24,48,60]{3,2,1,0:T(8,128)} custom-call(s32[5,60]{1,0:T(8,128)S(1)} %stack.2.table, bf16[3,2,32,768]{3,2,1,0:T(8,128)(2,1)S(1)} %get-tuple-element.25._.rest_0_, bf16[3,2,32,768]{3,2,1,0:T(8,128)(2,1)S(1)} %collective-permute-done.5.rest_1_, ...), custom_call_target="tpu_custom_call", output_to_operand_aliasing={{}: (5, {})} | custom-call | flops 11796480 | bytes 14155776 | tf_op jit(solution)/shard_map/interfere/pallas_call | solution.py:347
  42.0 0.0 collective-permute-done.3.rest_1_.rest_2_
  42.0 1.5 %interfere_near.1.rest_4_ = f32[288,128]{1,0:T(8,128)S(1)} custom-call(bf16[3,2,32,768]{3,2,1,0:T(8,128)(2,1)S(1)} %get-tuple-element.37.rest_0_, bf16[3,2,32,768]{3,2,1,0:T(8,128)(2,1)S(1)} %collective-permute-done.3.rest_1_.rest_2_), custom_call_target="tpu_custom_call" | custom-call | flops 2949120 | bytes 7077888 | tf_op jit(solution)/shard_map/interfere_near/pallas_call | solution.py:328
  43.6 0.0 collective-permute-done.2.rest_1_
  43.6 4.0 %collective-permute-done.4.rest_3_ = bf16[3,2,32,768]{3,2,1,0:T(8,128)(2,1)S(1)} collective-permute-done((bf16[3,2,32,768]{3,2,1,0:T(8,128)(2,1)}, bf16[3,2,32,768]{3,2,1,0:T(8,128)(2,1)S(1)}, u32[]{:S(2)}, u32[]{:S(2)}) %collective-permute-start.4) | collective-permute-done | bytes 294944 | tf_op jit(solution)/shard_map/ppermute | solution.py:395
  47.7 4.7 %interfere.5 = f32[2,24,48,60]{3,2,1,0:T(8,128)} custom-call(s32[5,60]{1,0:T(8,128)S(1)} %stack.2.table, bf16[3,2,32,768]{3,2,1,0:T(8,128)(2,1)S(1)} %get-tuple-element.37.rest_0_, bf16[3,2,32,768]{3,2,1,0:T(8,128)(2,1)S(1)} %collective-permute-done.2.rest_1_, ...), custom_call_target="tpu_custom_call", output_to_operand_aliasing={{}: (6, {})} | custom-call | flops 11796480 | bytes 14155776 | tf_op jit(solution)/shard_map/interfere/pallas_call | solution.py:347
  (2 shorter events, 0.0 us)
Async XLA Ops:
  0.0 9.0 %copy-start = (bf16[12,8]{0,1:T(8,128)(2,1)S(1)}, bf16[12,8]{0,1:T(8,128)(2,1)}, u32[]{:S(2)}) copy-start(bf16[12,8]{0,1:T(8,128)(2,1)} %param.6) | copy-start | bytes 580
  0.0 9.0 %copy-start.1 = (s32[3,96]{1,0:T(4,128)S(1)}, s32[3,96]{1,0:T(4,128)}, u32[]{:S(2)}) copy-start(s32[3,96]{1,0:T(4,128)} %off.5) | copy-start | bytes 3460
  2.5 6.5 %collective-permute-start.1 = (bf16[3,2,24,3072]{3,2,1,0:T(8,128)(2,1)S(1)}, bf16[3,2,24,3072]{3,2,1,0:T(8,128)(2,1)S(1)}, u32[]{:S(2)}, u32[]{:S(2)}) collective-permute-start(bf16[3,2,24,3072]{3,2,1,0:T(8,128)(2,1)S(1)} %get-tuple-element.24._), channel_id=1, source_target_pairs={{0,1},{2,3},{4,5},{6,7},{1,0},{3,2},{5,4},{7,6},{8,9},{10,11},{12,... | collective-permute-start | bytes 2654216 | tf_op jit(solution)/shard_map/ppermute | solution.py:400
  3.2 14.6 %collective-permute-start = (bf16[3,2,24,3072]{3,2,1,0:T(8,128)(2,1)S(1)}, bf16[3,2,24,3072]{3,2,1,0:T(8,128)(2,1)S(1)}, u32[]{:S(2)}, u32[]{:S(2)}) collective-permute-start(bf16[3,2,24,3072]{3,2,1,0:T(8,128)(2,1)S(1)} %get-tuple-element.23), channel_id=1, source_target_pairs={{1,2},{3,4},{5,6},{2,1},{4,3},{6,5},{9,10},{11,12},{13,14},{10,9},... | collective-permute-start | bytes 2654216 | tf_op jit(solution)/shard_map/ppermute | solution.py:400
  6.3 14.3 %collective-permute-start.8 = (bf16[3,2,32,768]{3,2,1,0:T(8,128)(2,1)S(1)}, bf16[3,2,32,768]{3,2,1,0:T(8,128)(2,1)S(1)}, u32[]{:S(2)}, u32[]{:S(2)}) collective-permute-start(bf16[3,2,32,768]{3,2,1,0:T(8,128)(2,1)S(1)} %get-tuple-element.34), channel_id=1, source_target_pairs={{0,16},{8,24},{16,0},{24,8},{1,17},{9,25},{17,1},{25,9},{2,18},{10... | collective-permute-start | bytes 884744 | tf_op jit(solution)/shard_map/ppermute | solution.py:395
  7.6 14.2 %collective-permute-start.9 = (bf16[3,2,32,768]{3,2,1,0:T(8,128)(2,1)S(1)}, bf16[3,2,32,768]{3,2,1,0:T(8,128)(2,1)S(1)}, u32[]{:S(2)}, u32[]{:S(2)}) collective-permute-start(bf16[3,2,32,768]{3,2,1,0:T(8,128)(2,1)S(1)} %get-tuple-element.35), channel_id=1, source_target_pairs={{0,8},{8,0},{16,24},{24,16},{1,9},{9,1},{17,25},{25,17},{2,10},{10... | collective-permute-start | bytes 884744 | tf_op jit(solution)/shard_map/ppermute | solution.py:395
  8.8 13.8 %collective-permute-start.10 = (bf16[3,2,32,768]{3,2,1,0:T(8,128)(2,1)S(1)}, bf16[3,2,32,768]{3,2,1,0:T(8,128)(2,1)S(1)}, u32[]{:S(2)}, u32[]{:S(2)}) collective-permute-start(bf16[3,2,32,768]{3,2,1,0:T(8,128)(2,1)S(1)} %get-tuple-element.36), channel_id=1, source_target_pairs={{0,24},{8,16},{16,8},{24,0},{1,25},{9,17},{17,9},{25,1},{2,26},{10... | collective-permute-start | bytes 884744 | tf_op jit(solution)/shard_map/ppermute | solution.py:395
  9.0 2.8 %copy-start.2 = (s32[60,2]{0,1:T(2,128)S(1)}, s32[60,2]{0,1:T(2,128)}, u32[]{:S(2)}) copy-start(s32[60,2]{0,1:T(2,128)} %param.7) | copy-start | bytes 1444
  10.6 17.4 %collective-permute-start.5 = (bf16[3,2,32,768]{3,2,1,0:T(8,128)(2,1)S(1)}, bf16[3,2,32,768]{3,2,1,0:T(8,128)(2,1)S(1)}, u32[]{:S(2)}, u32[]{:S(2)}) collective-permute-start(bf16[3,2,32,768]{3,2,1,0:T(8,128)(2,1)S(1)} %get-tuple-element.30), channel_id=1, source_target_pairs={{0,16},{8,24},{16,0},{24,8},{1,17},{9,25},{17,1},{25,9},{2,18},{10... | collective-permute-start | bytes 884744 | tf_op jit(solution)/shard_map/ppermute | solution.py:395
  17.8 18.9 %collective-permute-start.6 = (bf16[3,2,32,768]{3,2,1,0:T(8,128)(2,1)}, bf16[3,2,32,768]{3,2,1,0:T(8,128)(2,1)S(1)}, u32[]{:S(2)}, u32[]{:S(2)}) collective-permute-start(bf16[3,2,32,768]{3,2,1,0:T(8,128)(2,1)} %get-tuple-element.31), channel_id=1, source_target_pairs={{0,8},{8,0},{16,24},{24,16},{1,9},{9,1},{17,25},{25,17},{2,10},{10... | collective-permute-start | bytes 884744 | tf_op jit(solution)/shard_map/ppermute | solution.py:395
  20.6 16.1 %collective-permute-start.7 = (bf16[3,2,32,768]{3,2,1,0:T(8,128)(2,1)}, bf16[3,2,32,768]{3,2,1,0:T(8,128)(2,1)S(1)}, u32[]{:S(2)}, u32[]{:S(2)}) collective-permute-start(bf16[3,2,32,768]{3,2,1,0:T(8,128)(2,1)} %get-tuple-element.32), channel_id=1, source_target_pairs={{0,24},{8,16},{16,8},{24,0},{1,25},{9,17},{17,9},{25,1},{2,26},{10... | collective-permute-start | bytes 884744 | tf_op jit(solution)/shard_map/ppermute | solution.py:395
  21.8 21.8 %collective-permute-start.2 = (bf16[3,2,32,768]{3,2,1,0:T(8,128)(2,1)}, bf16[3,2,32,768]{3,2,1,0:T(8,128)(2,1)S(1)}, u32[]{:S(2)}, u32[]{:S(2)}) collective-permute-start(bf16[3,2,32,768]{3,2,1,0:T(8,128)(2,1)} %get-tuple-element.27), channel_id=1, source_target_pairs={{0,16},{8,24},{16,0},{24,8},{1,17},{9,25},{17,1},{25,9},{2,18},{10... | collective-permute-start | bytes 884744 | tf_op jit(solution)/shard_map/ppermute | solution.py:395
  22.7 19.4 %collective-permute-start.3 = (bf16[3,2,32,768]{3,2,1,0:T(8,128)(2,1)}, bf16[3,2,32,768]{3,2,1,0:T(8,128)(2,1)S(1)}, u32[]{:S(2)}, u32[]{:S(2)}) collective-permute-start(bf16[3,2,32,768]{3,2,1,0:T(8,128)(2,1)} %get-tuple-element.28), channel_id=1, source_target_pairs={{0,8},{8,0},{16,24},{24,16},{1,9},{9,1},{17,25},{25,17},{2,10},{10... | collective-permute-start | bytes 884744 | tf_op jit(solution)/shard_map/ppermute | solution.py:395
  28.0 19.7 %collective-permute-start.4 = (bf16[3,2,32,768]{3,2,1,0:T(8,128)(2,1)}, bf16[3,2,32,768]{3,2,1,0:T(8,128)(2,1)S(1)}, u32[]{:S(2)}, u32[]{:S(2)}) collective-permute-start(bf16[3,2,32,768]{3,2,1,0:T(8,128)(2,1)} %get-tuple-element.29), channel_id=1, source_target_pairs={{0,24},{8,16},{16,8},{24,0},{1,25},{9,17},{17,9},{25,1},{2,26},{10... | collective-permute-start | bytes 884744 | tf_op jit(solution)/shard_map/ppermute | solution.py:395

commit v13 on v12

--- a/solution.py
+++ b/solution.py
@@ -291,7 +291,7 @@
         flat[pl.ds(pl.multiple_of(p * looks, looks), looks), :] = value
         return carry
 
-    lax.fori_loop(0, count, select, 0, unroll=max(b for b in range(1, 7) if count % b == 0))
+    lax.fori_loop(0, count, select, 0, unroll=max(b for b in range(1, 31) if count % b == 0))
     copies = []
     for g in range(looks):
         turned = flat[pl.ds(g, count, stride=looks), :].T
@@ -411,7 +411,7 @@
         resample_edge(1, reach, group, side, kernel, offsets, slab, across, pieces[0], groups)
     )
     result = None
-    for turn, (moved, known) in enumerate(((middle, 0), (second, 0), (third, 2))):
+    for turn, (moved, known) in enumerate(((middle, 0), (second, 0), (third, 3))):
         near = None
         if known:
             mine, result = lax.optimization_barrier((moved[0], result))

time: 53 us -> 52.5 us (level)
  waiting for transfers between devices: 14.6 us -> 14 us
    pallas_call x3, Pallas kernels: 15.2 us -> 14.3 us  [interfere(): pl.pallas_call(functools.partial(interfere_kernel, via, known, turn), in_...]
    pallas_call x1, Pallas kernels: 1.54 us -> 2.29 us  [interfere_near(): pl.pallas_call(functools.partial(near_kernel, groups), in_specs=[VMEM] *...]
    ppermute x9, waiting for transfers between devices: 8.61 us -> 7.96 us  [send(): lax.ppermute(blocks[s], 'acq', [(i, i ^ s) for i in range(groups)])]
  transfers between devices with their start and end apart: 11 -> 11, of which waited for: 4 -> 4; matrix products, arithmetic and copies ran while one was open for 2% -> 2% of each run, Pallas kernels for 29% -> 31%
where the time goes in v13:
time: 52.5 us; the launch traced here: 51.5 us
  Pallas kernels  22.2 us (42%)
  starting transfers between devices  14.1 us (27%)
  waiting for transfers between devices  14 us (27%)
  local copies, waits for them, and re-layouts  0.69 us (1%)
  other arithmetic  0.57 us (1%)
    pallas_call x3, Pallas kernels, interfere(): pl.pallas_call(functools.partial(interfere_kernel, via, known, turn), in_...  14.3 us
    ppermute x9, starting transfers between devices, send(): lax.ppermute(blocks[s], 'acq', [(i, i ^ s) for i in range(groups)])  10.2 us
    ppermute x9, waiting for transfers between devices, send(): lax.ppermute(blocks[s], 'acq', [(i, i ^ s) for i in range(groups)])  7.96 us
    ppermute x2, waiting for transfers between devices, swap(): return lax.ppermute(halo, 'pix', pairs_up + [(j, i) for i, j in pairs_up])  6 us
    ppermute x2, starting transfers between devices, swap(): return lax.ppermute(halo, 'pix', pairs_up + [(j, i) for i, j in pairs_up])  3.82 us
    pallas_call x2, Pallas kernels, resample_edge(): pl.pallas_call(functools.partial(edge_kernel, groups, parity, count), in_...  3.07 us
    pallas_call x1, Pallas kernels, resample_first(): pl.pallas_call(functools.partial(first_kernel, first, groups), in_specs=[...  2.47 us
    pallas_call x1, Pallas kernels, interfere_near(): pl.pallas_call(functools.partial(near_kernel, groups), in_specs=[VMEM] *...  2.29 us
  transfers between devices with their start and end apart: 11, of which 4 were waited for; matrix products, arithmetic and copies ran while one was open for 2% of the time, Pallas kernels for 31%

profile of v13, /device:TPU:9, one launch (start us, length us, event | category | flops | bytes accessed | tf_op | source)
XLA Modules:
  0.0 51.5 jit_solution(1863897818565611563)
XLA Ops:
  0.0 0.0 copy-start
  0.0 0.0 copy-start.1
  0.0 2.5 %resample_first.1 = (bf16[3,2,32,768]{3,2,1,0:T(8,128)(2,1)S(1)}, bf16[3,2,32,768]{3,2,1,0:T(8,128)(2,1)S(1)}, bf16[3,2,32,768]{3,2,1,0:T(8,128)(2,1)S(1)}, bf16...) custom-call(s32[1]{0:T(128)} %bitcast.2.group, ...), custom_call_target="tpu_custom_call" | custom-call | flops 113246208 | bytes 4718592 | tf_op jit(solution)/shard_map/resample_first/pallas_call | solution.py:138
  2.5 0.7 %collective-permute-start.1 = (bf16[3,2,24,3072]{3,2,1,0:T(8,128)(2,1)S(1)}, bf16[3,2,24,3072]{3,2,1,0:T(8,128)(2,1)S(1)}, u32[]{:S(2)}, u32[]{:S(2)}) collective-permute-start(bf16[3,2,24,3072]{3,2,1,0:T(8,128)(2,1)S(1)} %get-tuple-element.24._), channel_id=1, source_target_pairs={{0,1},{2,3},{4,5},{6,7},{1,0},{3,2},{5,4},{7,6},{8,9},{10,11},{12,... | collective-permute-start | bytes 2654216 | tf_op jit(solution)/shard_map/ppermute | solution.py:400
  3.2 3.1 %collective-permute-start = (bf16[3,2,24,3072]{3,2,1,0:T(8,128)(2,1)S(1)}, bf16[3,2,24,3072]{3,2,1,0:T(8,128)(2,1)S(1)}, u32[]{:S(2)}, u32[]{:S(2)}) collective-permute-start(bf16[3,2,24,3072]{3,2,1,0:T(8,128)(2,1)S(1)} %get-tuple-element.23), channel_id=1, source_target_pairs={{1,2},{3,4},{5,6},{2,1},{4,3},{6,5},{9,10},{11,12},{13,14},{10,9},... | collective-permute-start | bytes 2654216 | tf_op jit(solution)/shard_map/ppermute | solution.py:400
  6.3 1.3 %collective-permute-start.8 = (bf16[3,2,32,768]{3,2,1,0:T(8,128)(2,1)S(1)}, bf16[3,2,32,768]{3,2,1,0:T(8,128)(2,1)S(1)}, u32[]{:S(2)}, u32[]{:S(2)}) collective-permute-start(bf16[3,2,32,768]{3,2,1,0:T(8,128)(2,1)S(1)} %get-tuple-element.34), channel_id=1, source_target_pairs={{0,16},{8,24},{16,0},{24,8},{1,17},{9,25},{17,1},{25,9},{2,18},{10... | collective-permute-start | bytes 884744 | tf_op jit(solution)/shard_map/ppermute | solution.py:395
  7.6 1.2 %collective-permute-start.9 = (bf16[3,2,32,768]{3,2,1,0:T(8,128)(2,1)S(1)}, bf16[3,2,32,768]{3,2,1,0:T(8,128)(2,1)S(1)}, u32[]{:S(2)}, u32[]{:S(2)}) collective-permute-start(bf16[3,2,32,768]{3,2,1,0:T(8,128)(2,1)S(1)} %get-tuple-element.35), channel_id=1, source_target_pairs={{0,8},{8,0},{16,24},{24,16},{1,9},{9,1},{17,25},{25,17},{2,10},{10... | collective-permute-start | bytes 884744 | tf_op jit(solution)/shard_map/ppermute | solution.py:395
  8.8 0.2 collective-permute-start.10
  9.0 0.0 collective-permute-done.1.halo
  9.0 0.0 copy-done
  9.0 0.0 copy-done.1
  9.0 0.0 copy-start.2
  9.1 1.5 %resample_edge.2 = (bf16[3,2,32,768]{3,2,1,0:T(8,128)(2,1)S(1)}, bf16[3,2,32,768]{3,2,1,0:T(8,128)(2,1)}, bf16[3,2,32,768]{3,2,1,0:T(8,128)(2,1)S(1)}, bf16[3,2,32,768]{3,2,1,0:T(8,128)(2,1)}) custom-call(s32[1]{0:T(128)} %bitcast.2.group, s32[1]{0:T(128)} %bitcast.3.side, bf16[8,12]{1,0:T(8,128)(2,1)S(1)} %bitcast.17, s32[3,96]{1,0:T(4,128)S(1)} %copy-done.1, ...), custom_call_target="tpu_custom_call" | custom-call | flops 103809024 | bytes 4423680 | tf_op jit(solution)/shard_map/resample_edge/pallas_call | solution.py:158
  10.6 1.2 %collective-permute-start.5 = (bf16[3,2,32,768]{3,2,1,0:T(8,128)(2,1)S(1)}, bf16[3,2,32,768]{3,2,1,0:T(8,128)(2,1)S(1)}, u32[]{:S(2)}, u32[]{:S(2)}) collective-permute-start(bf16[3,2,32,768]{3,2,1,0:T(8,128)(2,1)S(1)} %get-tuple-element.30), channel_id=1, source_target_pairs={{0,16},{8,24},{16,0},{24,8},{1,17},{9,25},{17,1},{25,9},{2,18},{10... | collective-permute-start | bytes 884744 | tf_op jit(solution)/shard_map/ppermute | solution.py:395
  11.8 0.0 copy-done.2
  11.9 6.0 %collective-permute-done.halo = bf16[3,2,24,3072]{3,2,1,0:T(8,128)(2,1)S(1)} collective-permute-done((bf16[3,2,24,3072]{3,2,1,0:T(8,128)(2,1)S(1)}, bf16[3,2,24,3072]{3,2,1,0:T(8,128)(2,1)S(1)}, u32[]{:S(2)}, u32[]{:S(2)}) %collective-permute-start) | collective-permute-done | bytes 884768 | tf_op jit(solution)/shard_map/ppermute | solution.py:400
  17.8 1.2 %collective-permute-start.6 = (bf16[3,2,32,768]{3,2,1,0:T(8,128)(2,1)}, bf16[3,2,32,768]{3,2,1,0:T(8,128)(2,1)S(1)}, u32[]{:S(2)}, u32[]{:S(2)}) collective-permute-start(bf16[3,2,32,768]{3,2,1,0:T(8,128)(2,1)} %get-tuple-element.31), channel_id=1, source_target_pairs={{0,8},{8,0},{16,24},{24,16},{1,9},{9,1},{17,25},{25,17},{2,10},{10... | collective-permute-start | bytes 884744 | tf_op jit(solution)/shard_map/ppermute | solution.py:395
  19.1 1.5 %resample_edge.3 = (bf16[3,2,32,768]{3,2,1,0:T(8,128)(2,1)S(1)}, bf16[3,2,32,768]{3,2,1,0:T(8,128)(2,1)}, bf16[3,2,32,768]{3,2,1,0:T(8,128)(2,1)}, bf16[3,2,32,768]{3,2,1,0:T(8,128)(2,1)}) custom-call(s32[1]{0:T(128)} %bitcast.2.group, s32[1]{0:T(128)} %bitcast.3.side, bf16[8,12]{1,0:T(8,128)(2,1)S(1)} %bitcast.18, s32[3,96]{1,0:T(4,128)S(1)} %copy-done.1, ...), custom_call_target="tpu_custom_call" | custom-call | flops 103809024 | bytes 4423680 | tf_op jit(solution)/shard_map/resample_edge/pallas_call | solution.py:158
  20.6 0.0 collective-permute-done.8.rest_1_
  20.6 1.2 %collective-permute-start.7 = (bf16[3,2,32,768]{3,2,1,0:T(8,128)(2,1)}, bf16[3,2,32,768]{3,2,1,0:T(8,128)(2,1)S(1)}, u32[]{:S(2)}, u32[]{:S(2)}) collective-permute-start(bf16[3,2,32,768]{3,2,1,0:T(8,128)(2,1)} %get-tuple-element.32), channel_id=1, source_target_pairs={{0,24},{8,16},{16,8},{24,0},{1,25},{9,17},{17,9},{25,1},{2,26},{10... | collective-permute-start | bytes 884744 | tf_op jit(solution)/shard_map/ppermute | solution.py:395
  21.8 0.0 collective-permute-done.9.rest_2_
  21.8 0.2 collective-permute-start.2
  22.0 0.6 %collective-permute-done.10.rest_3_ = bf16[3,2,32,768]{3,2,1,0:T(8,128)(2,1)S(1)} collective-permute-done((bf16[3,2,32,768]{3,2,1,0:T(8,128)(2,1)S(1)}, bf16[3,2,32,768]{3,2,1,0:T(8,128)(2,1)S(1)}, u32[]{:S(2)}, u32[]{:S(2)}) %collective-permute-start.10) | collective-permute-done | bytes 294944 | tf_op jit(solution)/shard_map/ppermute | solution.py:395
  22.7 1.4 %collective-permute-start.3 = (bf16[3,2,32,768]{3,2,1,0:T(8,128)(2,1)}, bf16[3,2,32,768]{3,2,1,0:T(8,128)(2,1)S(1)}, u32[]{:S(2)}, u32[]{:S(2)}) collective-permute-start(bf16[3,2,32,768]{3,2,1,0:T(8,128)(2,1)} %get-tuple-element.28), channel_id=1, source_target_pairs={{0,8},{8,0},{16,24},{24,16},{1,9},{9,1},{17,25},{25,17},{2,10},{10... | collective-permute-start | bytes 884744 | tf_op jit(solution)/shard_map/ppermute | solution.py:395
  24.1 3.9 %collective-permute-done.5.rest_1_ = bf16[3,2,32,768]{3,2,1,0:T(8,128)(2,1)S(1)} collective-permute-done((bf16[3,2,32,768]{3,2,1,0:T(8,128)(2,1)S(1)}, bf16[3,2,32,768]{3,2,1,0:T(8,128)(2,1)S(1)}, u32[]{:S(2)}, u32[]{:S(2)}) %collective-permute-start.5) | collective-permute-done | bytes 294944 | tf_op jit(solution)/shard_map/ppermute | solution.py:395
  28.0 2.2 %collective-permute-start.4 = (bf16[3,2,32,768]{3,2,1,0:T(8,128)(2,1)}, bf16[3,2,32,768]{3,2,1,0:T(8,128)(2,1)S(1)}, u32[]{:S(2)}, u32[]{:S(2)}) collective-permute-start(bf16[3,2,32,768]{3,2,1,0:T(8,128)(2,1)} %get-tuple-element.29), channel_id=1, source_target_pairs={{0,24},{8,16},{16,8},{24,0},{1,25},{9,17},{17,9},{25,1},{2,26},{10... | collective-permute-start | bytes 884744 | tf_op jit(solution)/shard_map/ppermute | solution.py:395
  30.2 0.5 %compare_select_fusion.2 = (s32[1,60]{1,0:T(1,128)S(1)}, s32[1,60]{1,0:T(1,128)}, s32[1,60]{1,0:T(1,128)}) fusion(s32[60,2]{0,1:T(2,128)S(1)} %fusion.3, pred[]{:T(512)S(6)} %eq.62), kind=kLoop, calls=%fused_computation.2 | loop fusion | flops 1620 | bytes 1201 | tf_op jit(solution)/shard_map/jit(_where)/select_n | solution.py:376
  30.8 0.7 %stack.2.table = s32[5,60]{1,0:T(8,128)S(1)} concatenate(s32[1,60]{1,0:T(1,128)} %get-tuple-element.40, s32[1,60]{1,0:T(1,128)S(1)} %get-tuple-element.42, s32[1,60]{1,0:T(1,128)S(1)} %get-tuple-element.41, s32[1,60]{1,0:T(1,128)S(1)} %get-tuple-element.39, s32[1,60]{1,0:T(1,128)} %get-tuple-element.43), dimensions={0} | concatenate | bytes 2400 | tf_op jit(solution)/shard_map/stack | solution.py:376
  31.4 5.2 %interfere.3.rest_4_ = f32[2,24,48,60]{3,2,1,0:T(8,128)} custom-call(s32[5,60]{1,0:T(8,128)S(1)} %stack.2.table, bf16[3,2,32,768]{3,2,1,0:T(8,128)(2,1)S(1)} %get-tuple-element.33.rest_0_, bf16[3,2,32,768]{3,2,1,0:T(8,128)(2,1)S(1)} %collective-permute-done.8.rest_1_, bf16[3,2,32,768]{3,2,1,0:T(8,128)(2,1)S(1)} %collective-permute-done.9.rest_2_, ...), custom_call_target="tpu_custom_call" | custom-call | flops 11796480 | bytes 14155776 | tf_op jit(solution)/shard_map/interfere/pallas_call | solution.py:347
  36.7 0.0 collective-permute-done.6.rest_2_
  36.7 0.0 collective-permute-done.7.rest_3_
  36.7 5.2 %interfere.4.rest_5_ = f32[2,24,48,60]{3,2,1,0:T(8,128)} custom-call(s32[5,60]{1,0:T(8,128)S(1)} %stack.2.table, bf16[3,2,32,768]{3,2,1,0:T(8,128)(2,1)S(1)} %get-tuple-element.25._.rest_0_, bf16[3,2,32,768]{3,2,1,0:T(8,128)(2,1)S(1)} %collective-permute-done.5.rest_1_, ...), custom_call_target="tpu_custom_call", output_to_operand_aliasing={{}: (5, {})} | custom-call | flops 11796480 | bytes 14155776 | tf_op jit(solution)/shard_map/interfere/pallas_call | solution.py:347
  41.9 0.0 collective-permute-done.2.rest_2_.rest_1_
  41.9 0.0 collective-permute-done.3.rest_1_.rest_2_
  42.0 2.3 %interfere_near.1.rest_4_ = f32[648,128]{1,0:T(8,128)S(1)} custom-call(bf16[3,2,32,768]{3,2,1,0:T(8,128)(2,1)S(1)} %get-tuple-element.37.rest_0_, bf16[3,2,32,768]{3,2,1,0:T(8,128)(2,1)S(1)} %collective-permute-done.3.rest_1_.rest_2_, bf16[3,2,32,768]{3,2,1,0:T(8,128)(2,1)S(1)} %collective-permute-done.2.rest_2_.rest_1_), custom_call_target="tpu_custom_call" | custom-call | flops 7077888 | bytes 10616832 | tf_op jit(solution)/shard_map/interfere_near/pallas_call | solution.py:328
  44.3 3.4 %collective-permute-done.4.rest_3_ = bf16[3,2,32,768]{3,2,1,0:T(8,128)(2,1)S(1)} collective-permute-done((bf16[3,2,32,768]{3,2,1,0:T(8,128)(2,1)}, bf16[3,2,32,768]{3,2,1,0:T(8,128)(2,1)S(1)}, u32[]{:S(2)}, u32[]{:S(2)}) %collective-permute-start.4) | collective-permute-done | bytes 294944 | tf_op jit(solution)/shard_map/ppermute | solution.py:395
  47.7 3.9 %interfere.5 = f32[2,24,48,60]{3,2,1,0:T(8,128)} custom-call(s32[5,60]{1,0:T(8,128)S(1)} %stack.2.table, bf16[3,2,32,768]{3,2,1,0:T(8,128)(2,1)S(1)} %get-tuple-element.37.rest_0_, bf16[3,2,32,768]{3,2,1,0:T(8,128)(2,1)S(1)} %collective-permute-done.2.rest_2_.rest_1_, ...), custom_call_target="tpu_custom_call", output_to_operand_aliasing={{}: (6, {})} | custom-call | flops 11796480 | bytes 14155776 | tf_op jit(solution)/shard_map/interfere/pallas_call | solution.py:347
  (2 shorter events, 0.0 us)
Async XLA Ops:
  0.0 9.0 %copy-start = (bf16[12,8]{0,1:T(8,128)(2,1)S(1)}, bf16[12,8]{0,1:T(8,128)(2,1)}, u32[]{:S(2)}) copy-start(bf16[12,8]{0,1:T(8,128)(2,1)} %param.6) | copy-start | bytes 580
  0.0 9.0 %copy-start.1 = (s32[3,96]{1,0:T(4,128)S(1)}, s32[3,96]{1,0:T(4,128)}, u32[]{:S(2)}) copy-start(s32[3,96]{1,0:T(4,128)} %off.5) | copy-start | bytes 3460
  2.5 6.5 %collective-permute-start.1 = (bf16[3,2,24,3072]{3,2,1,0:T(8,128)(2,1)S(1)}, bf16[3,2,24,3072]{3,2,1,0:T(8,128)(2,1)S(1)}, u32[]{:S(2)}, u32[]{:S(2)}) collective-permute-start(bf16[3,2,24,3072]{3,2,1,0:T(8,128)(2,1)S(1)} %get-tuple-element.24._), channel_id=1, source_target_pairs={{0,1},{2,3},{4,5},{6,7},{1,0},{3,2},{5,4},{7,6},{8,9},{10,11},{12,... | collective-permute-start | bytes 2654216 | tf_op jit(solution)/shard_map/ppermute | solution.py:400
  3.2 14.6 %collective-permute-start = (bf16[3,2,24,3072]{3,2,1,0:T(8,128)(2,1)S(1)}, bf16[3,2,24,3072]{3,2,1,0:T(8,128)(2,1)S(1)}, u32[]{:S(2)}, u32[]{:S(2)}) collective-permute-start(bf16[3,2,24,3072]{3,2,1,0:T(8,128)(2,1)S(1)} %get-tuple-element.23), channel_id=1, source_target_pairs={{1,2},{3,4},{5,6},{2,1},{4,3},{6,5},{9,10},{11,12},{13,14},{10,9},... | collective-permute-start | bytes 2654216 | tf_op jit(solution)/shard_map/ppermute | solution.py:400
  6.3 14.3 %collective-permute-start.8 = (bf16[3,2,32,768]{3,2,1,0:T(8,128)(2,1)S(1)}, bf16[3,2,32,768]{3,2,1,0:T(8,128)(2,1)S(1)}, u32[]{:S(2)}, u32[]{:S(2)}) collective-permute-start(bf16[3,2,32,768]{3,2,1,0:T(8,128)(2,1)S(1)} %get-tuple-element.34), channel_id=1, source_target_pairs={{0,16},{8,24},{16,0},{24,8},{1,17},{9,25},{17,1},{25,9},{2,18},{10... | collective-permute-start | bytes 884744 | tf_op jit(solution)/shard_map/ppermute | solution.py:395
  7.6 14.2 %collective-permute-start.9 = (bf16[3,2,32,768]{3,2,1,0:T(8,128)(2,1)S(1)}, bf16[3,2,32,768]{3,2,1,0:T(8,128)(2,1)S(1)}, u32[]{:S(2)}, u32[]{:S(2)}) collective-permute-start(bf16[3,2,32,768]{3,2,1,0:T(8,128)(2,1)S(1)} %get-tuple-element.35), channel_id=1, source_target_pairs={{0,8},{8,0},{16,24},{24,16},{1,9},{9,1},{17,25},{25,17},{2,10},{10... | collective-permute-start | bytes 884744 | tf_op jit(solution)/shard_map/ppermute | solution.py:395
  8.8 13.8 %collective-permute-start.10 = (bf16[3,2,32,768]{3,2,1,0:T(8,128)(2,1)S(1)}, bf16[3,2,32,768]{3,2,1,0:T(8,128)(2,1)S(1)}, u32[]{:S(2)}, u32[]{:S(2)}) collective-permute-start(bf16[3,2,32,768]{3,2,1,0:T(8,128)(2,1)S(1)} %get-tuple-element.36), channel_id=1, source_target_pairs={{0,24},{8,16},{16,8},{24,0},{1,25},{9,17},{17,9},{25,1},{2,26},{10... | collective-permute-start | bytes 884744 | tf_op jit(solution)/shard_map/ppermute | solution.py:395
  9.0 2.8 %copy-start.2 = (s32[60,2]{0,1:T(2,128)S(1)}, s32[60,2]{0,1:T(2,128)}, u32[]{:S(2)}) copy-start(s32[60,2]{0,1:T(2,128)} %param.7) | copy-start | bytes 1444
  10.6 17.4 %collective-permute-start.5 = (bf16[3,2,32,768]{3,2,1,0:T(8,128)(2,1)S(1)}, bf16[3,2,32,768]{3,2,1,0:T(8,128)(2,1)S(1)}, u32[]{:S(2)}, u32[]{:S(2)}) collective-permute-start(bf16[3,2,32,768]{3,2,1,0:T(8,128)(2,1)S(1)} %get-tuple-element.30), channel_id=1, source_target_pairs={{0,16},{8,24},{16,0},{24,8},{1,17},{9,25},{17,1},{25,9},{2,18},{10... | collective-permute-start | bytes 884744 | tf_op jit(solution)/shard_map/ppermute | solution.py:395
  17.8 18.8 %collective-permute-start.6 = (bf16[3,2,32,768]{3,2,1,0:T(8,128)(2,1)}, bf16[3,2,32,768]{3,2,1,0:T(8,128)(2,1)S(1)}, u32[]{:S(2)}, u32[]{:S(2)}) collective-permute-start(bf16[3,2,32,768]{3,2,1,0:T(8,128)(2,1)} %get-tuple-element.31), channel_id=1, source_target_pairs={{0,8},{8,0},{16,24},{24,16},{1,9},{9,1},{17,25},{25,17},{2,10},{10... | collective-permute-start | bytes 884744 | tf_op jit(solution)/shard_map/ppermute | solution.py:395
  20.6 16.1 %collective-permute-start.7 = (bf16[3,2,32,768]{3,2,1,0:T(8,128)(2,1)}, bf16[3,2,32,768]{3,2,1,0:T(8,128)(2,1)S(1)}, u32[]{:S(2)}, u32[]{:S(2)}) collective-permute-start(bf16[3,2,32,768]{3,2,1,0:T(8,128)(2,1)} %get-tuple-element.32), channel_id=1, source_target_pairs={{0,24},{8,16},{16,8},{24,0},{1,25},{9,17},{17,9},{25,1},{2,26},{10... | collective-permute-start | bytes 884744 | tf_op jit(solution)/shard_map/ppermute | solution.py:395
  21.8 20.1 %collective-permute-start.2 = (bf16[3,2,32,768]{3,2,1,0:T(8,128)(2,1)}, bf16[3,2,32,768]{3,2,1,0:T(8,128)(2,1)S(1)}, u32[]{:S(2)}, u32[]{:S(2)}) collective-permute-start(bf16[3,2,32,768]{3,2,1,0:T(8,128)(2,1)} %get-tuple-element.27), channel_id=1, source_target_pairs={{0,16},{8,24},{16,0},{24,8},{1,17},{9,25},{17,1},{25,9},{2,18},{10... | collective-permute-start | bytes 884744 | tf_op jit(solution)/shard_map/ppermute | solution.py:395
  22.7 19.3 %collective-permute-start.3 = (bf16[3,2,32,768]{3,2,1,0:T(8,128)(2,1)}, bf16[3,2,32,768]{3,2,1,0:T(8,128)(2,1)S(1)}, u32[]{:S(2)}, u32[]{:S(2)}) collective-permute-start(bf16[3,2,32,768]{3,2,1,0:T(8,128)(2,1)} %get-tuple-element.28), channel_id=1, source_target_pairs={{0,8},{8,0},{16,24},{24,16},{1,9},{9,1},{17,25},{25,17},{2,10},{10... | collective-permute-start | bytes 884744 | tf_op jit(solution)/shard_map/ppermute | solution.py:395
  28.0 19.7 %collective-permute-start.4 = (bf16[3,2,32,768]{3,2,1,0:T(8,128)(2,1)}, bf16[3,2,32,768]{3,2,1,0:T(8,128)(2,1)S(1)}, u32[]{:S(2)}, u32[]{:S(2)}) collective-permute-start(bf16[3,2,32,768]{3,2,1,0:T(8,128)(2,1)} %get-tuple-element.29), channel_id=1, source_target_pairs={{0,24},{8,16},{16,8},{24,0},{1,25},{9,17},{17,9},{25,1},{2,26},{10... | collective-permute-start | bytes 884744 | tf_op jit(solution)/shard_map/ppermute | solution.py:395

commit v14 on v13

--- a/solution.py
+++ b/solution.py
@@ -206,7 +206,8 @@
                 parts[r * acq + a, 0] = real
                 parts[r * acq + a, 1] = imag
                 parts[r * acq + a, 2] = real + imag
-                parts[r * acq + a, 3] = real - imag
+                if r >= begin:
+                    parts[r * acq + a, 3] = real - imag
 
     def cross(pairs):
         totals = {pair: [0.0, 0.0, 0.0] for pair in pairs}
@@ -416,7 +417,7 @@
         if known:
             mine, result = lax.optimization_barrier((moved[0], result))
             near = interfere_near([mine, *moved[1:known]])
-        result = interfere(turn, chunks, table, moved, ((0, 2, 1, 3), (0, 2, 1, 3), (0, 2, 1, 3))[turn], near, known, result)
+        result = interfere(turn, chunks, table, moved, ((0, 2, 3, 1), (0, 2, 1, 3), (0, 2, 1, 3))[turn], near, known, result)
     return jnp.transpose(result, (0, 3, 1, 2))
 
 

time: 52.5 us -> 53.5 us (1.019)
  waiting for transfers between devices: 14 us -> 15 us
    ppermute x9, waiting for transfers between devices: 7.96 us -> 9.02 us  [send(): lax.ppermute(blocks[s], 'acq', [(i, i ^ s) for i in range(groups)])]
  transfers between devices with their start and end apart: 11 -> 11, of which waited for: 4 -> 4; matrix products, arithmetic and copies ran while one was open for 2% -> 2% of each run, Pallas kernels for 31% -> 30%
where the time goes in v14:
time: 53.5 us; the launch traced here: 53 us
  Pallas kernels  22.2 us (41%)
  waiting for transfers between devices  15 us (28%)
  starting transfers between devices  14.5 us (27%)
  local copies, waits for them, and re-layouts  0.69 us (1%)
  other arithmetic  0.57 us (1%)
    pallas_call x3, Pallas kernels, interfere(): pl.pallas_call(functools.partial(interfere_kernel, via, known, turn), in_...  14.3 us
    ppermute x9, starting transfers between devices, send(): lax.ppermute(blocks[s], 'acq', [(i, i ^ s) for i in range(groups)])  10.7 us
    ppermute x9, waiting for transfers between devices, send(): lax.ppermute(blocks[s], 'acq', [(i, i ^ s) for i in range(groups)])  9.02 us
    ppermute x2, waiting for transfers between devices, swap(): return lax.ppermute(halo, 'pix', pairs_up + [(j, i) for i, j in pairs_up])  6 us
    ppermute x2, starting transfers between devices, swap(): return lax.ppermute(halo, 'pix', pairs_up + [(j, i) for i, j in pairs_up])  3.82 us
    pallas_call x2, Pallas kernels, resample_edge(): pl.pallas_call(functools.partial(edge_kernel, groups, parity, count), in_...  3.07 us
    pallas_call x1, Pallas kernels, resample_first(): pl.pallas_call(functools.partial(first_kernel, first, groups), in_specs=[...  2.47 us
    pallas_call x1, Pallas kernels, interfere_near(): pl.pallas_call(functools.partial(near_kernel, groups), in_specs=[VMEM] *...  2.29 us
  transfers between devices with their start and end apart: 11, of which 4 were waited for; matrix products, arithmetic and copies ran while one was open for 2% of the time, Pallas kernels for 30%

profile of v14, /device:TPU:9, one launch (start us, length us, event | category | flops | bytes accessed | tf_op | source)
XLA Modules:
  0.0 53.0 jit_solution(1470830206846561054)
XLA Ops:
  0.0 0.0 copy-start
  0.0 0.0 copy-start.1
  0.0 2.5 %resample_first.1 = (bf16[3,2,32,768]{3,2,1,0:T(8,128)(2,1)S(1)}, bf16[3,2,32,768]{3,2,1,0:T(8,128)(2,1)S(1)}, bf16[3,2,32,768]{3,2,1,0:T(8,128)(2,1)S(1)}, bf16...) custom-call(s32[1]{0:T(128)} %bitcast.2.group, ...), custom_call_target="tpu_custom_call" | custom-call | flops 113246208 | bytes 4718592 | tf_op jit(solution)/shard_map/resample_first/pallas_call | solution.py:138
  2.5 0.7 %collective-permute-start.1 = (bf16[3,2,24,3072]{3,2,1,0:T(8,128)(2,1)S(1)}, bf16[3,2,24,3072]{3,2,1,0:T(8,128)(2,1)S(1)}, u32[]{:S(2)}, u32[]{:S(2)}) collective-permute-start(bf16[3,2,24,3072]{3,2,1,0:T(8,128)(2,1)S(1)} %get-tuple-element.24._), channel_id=1, source_target_pairs={{0,1},{2,3},{4,5},{6,7},{1,0},{3,2},{5,4},{7,6},{8,9},{10,11},{12,... | collective-permute-start | bytes 2654216 | tf_op jit(solution)/shard_map/ppermute | solution.py:401
  3.2 3.1 %collective-permute-start = (bf16[3,2,24,3072]{3,2,1,0:T(8,128)(2,1)S(1)}, bf16[3,2,24,3072]{3,2,1,0:T(8,128)(2,1)S(1)}, u32[]{:S(2)}, u32[]{:S(2)}) collective-permute-start(bf16[3,2,24,3072]{3,2,1,0:T(8,128)(2,1)S(1)} %get-tuple-element.23), channel_id=1, source_target_pairs={{1,2},{3,4},{5,6},{2,1},{4,3},{6,5},{9,10},{11,12},{13,14},{10,9},... | collective-permute-start | bytes 2654216 | tf_op jit(solution)/shard_map/ppermute | solution.py:401
  6.3 1.3 %collective-permute-start.8 = (bf16[3,2,32,768]{3,2,1,0:T(8,128)(2,1)S(1)}, bf16[3,2,32,768]{3,2,1,0:T(8,128)(2,1)S(1)}, u32[]{:S(2)}, u32[]{:S(2)}) collective-permute-start(bf16[3,2,32,768]{3,2,1,0:T(8,128)(2,1)S(1)} %get-tuple-element.34), channel_id=1, source_target_pairs={{0,16},{8,24},{16,0},{24,8},{1,17},{9,25},{17,1},{25,9},{2,18},{10... | collective-permute-start | bytes 884744 | tf_op jit(solution)/shard_map/ppermute | solution.py:396
  7.6 1.2 %collective-permute-start.9 = (bf16[3,2,32,768]{3,2,1,0:T(8,128)(2,1)S(1)}, bf16[3,2,32,768]{3,2,1,0:T(8,128)(2,1)S(1)}, u32[]{:S(2)}, u32[]{:S(2)}) collective-permute-start(bf16[3,2,32,768]{3,2,1,0:T(8,128)(2,1)S(1)} %get-tuple-element.35), channel_id=1, source_target_pairs={{0,24},{8,16},{16,8},{24,0},{1,25},{9,17},{17,9},{25,1},{2,26},{10... | collective-permute-start | bytes 884744 | tf_op jit(solution)/shard_map/ppermute | solution.py:396
  8.8 0.3 collective-permute-start.10
  9.0 0.0 collective-permute-done.1.halo
  9.0 0.0 copy-done
  9.0 0.0 copy-done.1
  9.0 0.0 copy-start.2
  9.1 1.5 %resample_edge.2 = (bf16[3,2,32,768]{3,2,1,0:T(8,128)(2,1)S(1)}, bf16[3,2,32,768]{3,2,1,0:T(8,128)(2,1)}, bf16[3,2,32,768]{3,2,1,0:T(8,128)(2,1)S(1)}, bf16[3,2,32,768]{3,2,1,0:T(8,128)(2,1)}) custom-call(s32[1]{0:T(128)} %bitcast.2.group, s32[1]{0:T(128)} %bitcast.3.side, bf16[8,12]{1,0:T(8,128)(2,1)S(1)} %bitcast.17, s32[3,96]{1,0:T(4,128)S(1)} %copy-done.1, ...), custom_call_target="tpu_custom_call" | custom-call | flops 103809024 | bytes 4423680 | tf_op jit(solution)/shard_map/resample_edge/pallas_call | solution.py:158
  10.6 1.2 %collective-permute-start.5 = (bf16[3,2,32,768]{3,2,1,0:T(8,128)(2,1)S(1)}, bf16[3,2,32,768]{3,2,1,0:T(8,128)(2,1)S(1)}, u32[]{:S(2)}, u32[]{:S(2)}) collective-permute-start(bf16[3,2,32,768]{3,2,1,0:T(8,128)(2,1)S(1)} %get-tuple-element.30), channel_id=1, source_target_pairs={{0,16},{8,24},{16,0},{24,8},{1,17},{9,25},{17,1},{25,9},{2,18},{10... | collective-permute-start | bytes 884744 | tf_op jit(solution)/shard_map/ppermute | solution.py:396
  11.8 0.0 copy-done.2
  11.9 6.0 %collective-permute-done.halo = bf16[3,2,24,3072]{3,2,1,0:T(8,128)(2,1)S(1)} collective-permute-done((bf16[3,2,24,3072]{3,2,1,0:T(8,128)(2,1)S(1)}, bf16[3,2,24,3072]{3,2,1,0:T(8,128)(2,1)S(1)}, u32[]{:S(2)}, u32[]{:S(2)}) %collective-permute-start) | collective-permute-done | bytes 884768 | tf_op jit(solution)/shard_map/ppermute | solution.py:401
  17.8 1.2 %collective-permute-start.6 = (bf16[3,2,32,768]{3,2,1,0:T(8,128)(2,1)}, bf16[3,2,32,768]{3,2,1,0:T(8,128)(2,1)S(1)}, u32[]{:S(2)}, u32[]{:S(2)}) collective-permute-start(bf16[3,2,32,768]{3,2,1,0:T(8,128)(2,1)} %get-tuple-element.31), channel_id=1, source_target_pairs={{0,8},{8,0},{16,24},{24,16},{1,9},{9,1},{17,25},{25,17},{2,10},{10... | collective-permute-start | bytes 884744 | tf_op jit(solution)/shard_map/ppermute | solution.py:396
  19.1 1.5 %resample_edge.3 = (bf16[3,2,32,768]{3,2,1,0:T(8,128)(2,1)S(1)}, bf16[3,2,32,768]{3,2,1,0:T(8,128)(2,1)}, bf16[3,2,32,768]{3,2,1,0:T(8,128)(2,1)}, bf16[3,2,32,768]{3,2,1,0:T(8,128)(2,1)}) custom-call(s32[1]{0:T(128)} %bitcast.2.group, s32[1]{0:T(128)} %bitcast.3.side, bf16[8,12]{1,0:T(8,128)(2,1)S(1)} %bitcast.18, s32[3,96]{1,0:T(4,128)S(1)} %copy-done.1, ...), custom_call_target="tpu_custom_call" | custom-call | flops 103809024 | bytes 4423680 | tf_op jit(solution)/shard_map/resample_edge/pallas_call | solution.py:158
  20.6 1.1 %collective-permute-done.8.rest_1_ = bf16[3,2,32,768]{3,2,1,0:T(8,128)(2,1)S(1)} collective-permute-done((bf16[3,2,32,768]{3,2,1,0:T(8,128)(2,1)S(1)}, bf16[3,2,32,768]{3,2,1,0:T(8,128)(2,1)S(1)}, u32[]{:S(2)}, u32[]{:S(2)}) %collective-permute-start.8) | collective-permute-done | bytes 294944 | tf_op jit(solution)/shard_map/ppermute | solution.py:396
  21.7 2.2 %collective-permute-start.7 = (bf16[3,2,32,768]{3,2,1,0:T(8,128)(2,1)}, bf16[3,2,32,768]{3,2,1,0:T(8,128)(2,1)S(1)}, u32[]{:S(2)}, u32[]{:S(2)}) collective-permute-start(bf16[3,2,32,768]{3,2,1,0:T(8,128)(2,1)} %get-tuple-element.32), channel_id=1, source_target_pairs={{0,24},{8,16},{16,8},{24,0},{1,25},{9,17},{17,9},{25,1},{2,26},{10... | collective-permute-start | bytes 884744 | tf_op jit(solution)/shard_map/ppermute | solution.py:396
  23.9 0.0 collective-permute-done.9.rest_2_
  23.9 0.2 collective-permute-start.2
  24.1 0.0 collective-permute-done.10.rest_3_
  24.1 0.2 collective-permute-start.3
  24.3 3.0 %collective-permute-done.5.rest_1_ = bf16[3,2,32,768]{3,2,1,0:T(8,128)(2,1)S(1)} collective-permute-done((bf16[3,2,32,768]{3,2,1,0:T(8,128)(2,1)S(1)}, bf16[3,2,32,768]{3,2,1,0:T(8,128)(2,1)S(1)}, u32[]{:S(2)}, u32[]{:S(2)}) %collective-permute-start.5) | collective-permute-done | bytes 294944 | tf_op jit(solution)/shard_map/ppermute | solution.py:396
  27.4 2.8 %collective-permute-start.4 = (bf16[3,2,32,768]{3,2,1,0:T(8,128)(2,1)}, bf16[3,2,32,768]{3,2,1,0:T(8,128)(2,1)S(1)}, u32[]{:S(2)}, u32[]{:S(2)}) collective-permute-start(bf16[3,2,32,768]{3,2,1,0:T(8,128)(2,1)} %get-tuple-element.29), channel_id=1, source_target_pairs={{0,24},{8,16},{16,8},{24,0},{1,25},{9,17},{17,9},{25,1},{2,26},{10... | collective-permute-start | bytes 884744 | tf_op jit(solution)/shard_map/ppermute | solution.py:396
  30.2 0.5 %compare_select_fusion.2 = (s32[1,60]{1,0:T(1,128)S(1)}, s32[1,60]{1,0:T(1,128)}, s32[1,60]{1,0:T(1,128)}) fusion(s32[60,2]{0,1:T(2,128)S(1)} %fusion.3, pred[]{:T(512)S(6)} %eq.62), kind=kLoop, calls=%fused_computation.2 | loop fusion | flops 1620 | bytes 1201 | tf_op jit(solution)/shard_map/jit(_where)/select_n | solution.py:377
  30.8 0.7 %stack.2.table = s32[5,60]{1,0:T(8,128)S(1)} concatenate(s32[1,60]{1,0:T(1,128)} %get-tuple-element.40, s32[1,60]{1,0:T(1,128)S(1)} %get-tuple-element.42, s32[1,60]{1,0:T(1,128)S(1)} %get-tuple-element.41, s32[1,60]{1,0:T(1,128)S(1)} %get-tuple-element.39, s32[1,60]{1,0:T(1,128)} %get-tuple-element.43), dimensions={0} | concatenate | bytes 2400 | tf_op jit(solution)/shard_map/stack | solution.py:377
  31.4 5.2 %interfere.3.rest_4_ = f32[2,24,48,60]{3,2,1,0:T(8,128)} custom-call(s32[5,60]{1,0:T(8,128)S(1)} %stack.2.table, bf16[3,2,32,768]{3,2,1,0:T(8,128)(2,1)S(1)} %get-tuple-element.33.rest_0_, bf16[3,2,32,768]{3,2,1,0:T(8,128)(2,1)S(1)} %collective-permute-done.8.rest_1_, bf16[3,2,32,768]{3,2,1,0:T(8,128)(2,1)S(1)} %collective-permute-done.9.rest_2_, ...), custom_call_target="tpu_custom_call" | custom-call | flops 11796480 | bytes 14155776 | tf_op jit(solution)/shard_map/interfere/pallas_call | solution.py:348
  36.7 0.0 collective-permute-done.6.rest_2_
  36.7 0.0 collective-permute-done.7.rest_3_
  36.7 5.2 %interfere.4.rest_5_ = f32[2,24,48,60]{3,2,1,0:T(8,128)} custom-call(s32[5,60]{1,0:T(8,128)S(1)} %stack.2.table, bf16[3,2,32,768]{3,2,1,0:T(8,128)(2,1)S(1)} %get-tuple-element.25._.rest_0_, bf16[3,2,32,768]{3,2,1,0:T(8,128)(2,1)S(1)} %collective-permute-done.5.rest_1_, ...), custom_call_target="tpu_custom_call", output_to_operand_aliasing={{}: (5, {})} | custom-call | flops 11796480 | bytes 14155776 | tf_op jit(solution)/shard_map/interfere/pallas_call | solution.py:348
  41.9 0.0 collective-permute-done.2.rest_2_.rest_1_
  41.9 0.0 collective-permute-done.3.rest_1_.rest_2_
  42.0 2.3 %interfere_near.1.rest_4_ = f32[648,128]{1,0:T(8,128)S(1)} custom-call(bf16[3,2,32,768]{3,2,1,0:T(8,128)(2,1)S(1)} %get-tuple-element.37.rest_0_, bf16[3,2,32,768]{3,2,1,0:T(8,128)(2,1)S(1)} %collective-permute-done.3.rest_1_.rest_2_, bf16[3,2,32,768]{3,2,1,0:T(8,128)(2,1)S(1)} %collective-permute-done.2.rest_2_.rest_1_), custom_call_target="tpu_custom_call" | custom-call | flops 7077888 | bytes 10616832 | tf_op jit(solution)/shard_map/interfere_near/pallas_call | solution.py:329
  44.3 4.9 %collective-permute-done.4.rest_3_ = bf16[3,2,32,768]{3,2,1,0:T(8,128)(2,1)S(1)} collective-permute-done((bf16[3,2,32,768]{3,2,1,0:T(8,128)(2,1)}, bf16[3,2,32,768]{3,2,1,0:T(8,128)(2,1)S(1)}, u32[]{:S(2)}, u32[]{:S(2)}) %collective-permute-start.4) | collective-permute-done | bytes 294944 | tf_op jit(solution)/shard_map/ppermute | solution.py:396
  49.1 3.9 %interfere.5 = f32[2,24,48,60]{3,2,1,0:T(8,128)} custom-call(s32[5,60]{1,0:T(8,128)S(1)} %stack.2.table, bf16[3,2,32,768]{3,2,1,0:T(8,128)(2,1)S(1)} %get-tuple-element.37.rest_0_, bf16[3,2,32,768]{3,2,1,0:T(8,128)(2,1)S(1)} %collective-permute-done.2.rest_2_.rest_1_, ...), custom_call_target="tpu_custom_call", output_to_operand_aliasing={{}: (6, {})} | custom-call | flops 11796480 | bytes 14155776 | tf_op jit(solution)/shard_map/interfere/pallas_call | solution.py:348
  (2 shorter events, 0.0 us)
Async XLA Ops:
  0.0 9.0 %copy-start = (bf16[12,8]{0,1:T(8,128)(2,1)S(1)}, bf16[12,8]{0,1:T(8,128)(2,1)}, u32[]{:S(2)}) copy-start(bf16[12,8]{0,1:T(8,128)(2,1)} %param.6) | copy-start | bytes 580
  0.0 9.0 %copy-start.1 = (s32[3,96]{1,0:T(4,128)S(1)}, s32[3,96]{1,0:T(4,128)}, u32[]{:S(2)}) copy-start(s32[3,96]{1,0:T(4,128)} %off.5) | copy-start | bytes 3460
  2.5 6.6 %collective-permute-start.1 = (bf16[3,2,24,3072]{3,2,1,0:T(8,128)(2,1)S(1)}, bf16[3,2,24,3072]{3,2,1,0:T(8,128)(2,1)S(1)}, u32[]{:S(2)}, u32[]{:S(2)}) collective-permute-start(bf16[3,2,24,3072]{3,2,1,0:T(8,128)(2,1)S(1)} %get-tuple-element.24._), channel_id=1, source_target_pairs={{0,1},{2,3},{4,5},{6,7},{1,0},{3,2},{5,4},{7,6},{8,9},{10,11},{12,... | collective-permute-start | bytes 2654216 | tf_op jit(solution)/shard_map/ppermute | solution.py:401
  3.2 14.6 %collective-permute-start = (bf16[3,2,24,3072]{3,2,1,0:T(8,128)(2,1)S(1)}, bf16[3,2,24,3072]{3,2,1,0:T(8,128)(2,1)S(1)}, u32[]{:S(2)}, u32[]{:S(2)}) collective-permute-start(bf16[3,2,24,3072]{3,2,1,0:T(8,128)(2,1)S(1)} %get-tuple-element.23), channel_id=1, source_target_pairs={{1,2},{3,4},{5,6},{2,1},{4,3},{6,5},{9,10},{11,12},{13,14},{10,9},... | collective-permute-start | bytes 2654216 | tf_op jit(solution)/shard_map/ppermute | solution.py:401
  6.3 15.4 %collective-permute-start.8 = (bf16[3,2,32,768]{3,2,1,0:T(8,128)(2,1)S(1)}, bf16[3,2,32,768]{3,2,1,0:T(8,128)(2,1)S(1)}, u32[]{:S(2)}, u32[]{:S(2)}) collective-permute-start(bf16[3,2,32,768]{3,2,1,0:T(8,128)(2,1)S(1)} %get-tuple-element.34), channel_id=1, source_target_pairs={{0,16},{8,24},{16,0},{24,8},{1,17},{9,25},{17,1},{25,9},{2,18},{10... | collective-permute-start | bytes 884744 | tf_op jit(solution)/shard_map/ppermute | solution.py:396
  7.6 16.3 %collective-permute-start.9 = (bf16[3,2,32,768]{3,2,1,0:T(8,128)(2,1)S(1)}, bf16[3,2,32,768]{3,2,1,0:T(8,128)(2,1)S(1)}, u32[]{:S(2)}, u32[]{:S(2)}) collective-permute-start(bf16[3,2,32,768]{3,2,1,0:T(8,128)(2,1)S(1)} %get-tuple-element.35), channel_id=1, source_target_pairs={{0,24},{8,16},{16,8},{24,0},{1,25},{9,17},{17,9},{25,1},{2,26},{10... | collective-permute-start | bytes 884744 | tf_op jit(solution)/shard_map/ppermute | solution.py:396
  8.8 15.4 %collective-permute-start.10 = (bf16[3,2,32,768]{3,2,1,0:T(8,128)(2,1)S(1)}, bf16[3,2,32,768]{3,2,1,0:T(8,128)(2,1)S(1)}, u32[]{:S(2)}, u32[]{:S(2)}) collective-permute-start(bf16[3,2,32,768]{3,2,1,0:T(8,128)(2,1)S(1)} %get-tuple-element.36), channel_id=1, source_target_pairs={{0,8},{8,0},{16,24},{24,16},{1,9},{9,1},{17,25},{25,17},{2,10},{10... | collective-permute-start | bytes 884744 | tf_op jit(solution)/shard_map/ppermute | solution.py:396
  9.0 2.8 %copy-start.2 = (s32[60,2]{0,1:T(2,128)S(1)}, s32[60,2]{0,1:T(2,128)}, u32[]{:S(2)}) copy-start(s32[60,2]{0,1:T(2,128)} %param.7) | copy-start | bytes 1444
  10.6 16.8 %collective-permute-start.5 = (bf16[3,2,32,768]{3,2,1,0:T(8,128)(2,1)S(1)}, bf16[3,2,32,768]{3,2,1,0:T(8,128)(2,1)S(1)}, u32[]{:S(2)}, u32[]{:S(2)}) collective-permute-start(bf16[3,2,32,768]{3,2,1,0:T(8,128)(2,1)S(1)} %get-tuple-element.30), channel_id=1, source_target_pairs={{0,16},{8,24},{16,0},{24,8},{1,17},{9,25},{17,1},{25,9},{2,18},{10... | collective-permute-start | bytes 884744 | tf_op jit(solution)/shard_map/ppermute | solution.py:396
  17.8 18.8 %collective-permute-start.6 = (bf16[3,2,32,768]{3,2,1,0:T(8,128)(2,1)}, bf16[3,2,32,768]{3,2,1,0:T(8,128)(2,1)S(1)}, u32[]{:S(2)}, u32[]{:S(2)}) collective-permute-start(bf16[3,2,32,768]{3,2,1,0:T(8,128)(2,1)} %get-tuple-element.31), channel_id=1, source_target_pairs={{0,8},{8,0},{16,24},{24,16},{1,9},{9,1},{17,25},{25,17},{2,10},{10... | collective-permute-start | bytes 884744 | tf_op jit(solution)/shard_map/ppermute | solution.py:396
  21.7 15.0 %collective-permute-start.7 = (bf16[3,2,32,768]{3,2,1,0:T(8,128)(2,1)}, bf16[3,2,32,768]{3,2,1,0:T(8,128)(2,1)S(1)}, u32[]{:S(2)}, u32[]{:S(2)}) collective-permute-start(bf16[3,2,32,768]{3,2,1,0:T(8,128)(2,1)} %get-tuple-element.32), channel_id=1, source_target_pairs={{0,24},{8,16},{16,8},{24,0},{1,25},{9,17},{17,9},{25,1},{2,26},{10... | collective-permute-start | bytes 884744 | tf_op jit(solution)/shard_map/ppermute | solution.py:396
  23.9 18.0 %collective-permute-start.2 = (bf16[3,2,32,768]{3,2,1,0:T(8,128)(2,1)}, bf16[3,2,32,768]{3,2,1,0:T(8,128)(2,1)S(1)}, u32[]{:S(2)}, u32[]{:S(2)}) collective-permute-start(bf16[3,2,32,768]{3,2,1,0:T(8,128)(2,1)} %get-tuple-element.27), channel_id=1, source_target_pairs={{0,16},{8,24},{16,0},{24,8},{1,17},{9,25},{17,1},{25,9},{2,18},{10... | collective-permute-start | bytes 884744 | tf_op jit(solution)/shard_map/ppermute | solution.py:396
  24.1 17.8 %collective-permute-start.3 = (bf16[3,2,32,768]{3,2,1,0:T(8,128)(2,1)}, bf16[3,2,32,768]{3,2,1,0:T(8,128)(2,1)S(1)}, u32[]{:S(2)}, u32[]{:S(2)}) collective-permute-start(bf16[3,2,32,768]{3,2,1,0:T(8,128)(2,1)} %get-tuple-element.28), channel_id=1, source_target_pairs={{0,8},{8,0},{16,24},{24,16},{1,9},{9,1},{17,25},{25,17},{2,10},{10... | collective-permute-start | bytes 884744 | tf_op jit(solution)/shard_map/ppermute | solution.py:396
  27.4 21.8 %collective-permute-start.4 = (bf16[3,2,32,768]{3,2,1,0:T(8,128)(2,1)}, bf16[3,2,32,768]{3,2,1,0:T(8,128)(2,1)S(1)}, u32[]{:S(2)}, u32[]{:S(2)}) collective-permute-start(bf16[3,2,32,768]{3,2,1,0:T(8,128)(2,1)} %get-tuple-element.29), channel_id=1, source_target_pairs={{0,24},{8,16},{16,8},{24,0},{1,25},{9,17},{17,9},{25,1},{2,26},{10... | collective-permute-start | bytes 884744 | tf_op jit(solution)/shard_map/ppermute | solution.py:396
